TPU v7x, 256 devices: a whole 4x4x8 slice. The times are simulated.
256 devices in a mesh: batch: 4 (over y), ctx: 16 (over z, core), tower: 4 (over x).
Axes of the slice: x: 4, y: 4, z: 8, core: 2. Of those that a mesh axis runs over, the one named last changes fastest.
Arguments:
- video_q: bfloat16 [4, 8192, 1536], P('batch', ('ctx', 'tower')), may hold values from -20 to 20
- video_k: bfloat16 [4, 8192, 1536], P('batch', ('ctx', 'tower')), may hold values from -20 to 20
- video_v: bfloat16 [4, 8192, 1536], P('batch', ('ctx', 'tower')), may hold values from -6 to 6
- audio_q: bfloat16 [4, 1536, 1536], P('batch', 'tower'), may hold values from -20 to 20
- audio_k: bfloat16 [4, 1536, 1536], P('batch', 'tower'), may hold values from -20 to 20
- audio_v: bfloat16 [4, 1536, 1536], P('batch', 'tower'), may hold values from -6 to 6
- margin: int32 [4, 64, 3], P('batch'), may hold values from 0 to 63, as said below
- out_weight: bfloat16 [3, 12, 128, 3072], P(None, 'tower', 'batch'), may hold values from -0.21875 to 0.21875
- gate_gains: float32 [4, 2, 3072], P('batch'), may hold values from 0.5 to 1.5
Outputs:
- video_out: bfloat16 [4, 8192, 3072], P('batch', ('ctx', 'tower'))
- audio_out: bfloat16 [4, 1536, 3072], P('batch', ('ctx', 'tower'))
Inputs may be any that keep to these rules, and one draw needn't show every extreme that they name: margin[c, i, 0] = i, and every entry of margin[c, i, :] lies within 2 of i.
All inputs are finite; a program needn't handle non-finite values.
Results may differ from a plain program's by a relative error of at most 0.017.
Values may be sent and summed in bfloat16 or wider, within the bound.
No kernel may reach another device: no remote copies, remote signals or barrier semaphores. Data moves between devices by JAX's collectives and lax.ppermute only.
A program may use at most 128 MiB of HBM per device.

v0:
```python
import functools

import jax
import jax.numpy as jnp
from jax import lax
from jax.experimental import pallas as pl
from jax.experimental.pallas import tpu as pltpu
from jax.sharding import PartitionSpec as P

H = 12
HD = 128
VBLK = 128
ABLK = 24
TOWERS = 4
CHIPS = 8
LOCAL = H // TOWERS
GW = LOCAL * HD
NEG = -1e30
SCALE2 = HD**-0.5 * 1.4426950408889634
MIB = 1024 * 1024
VMEM = 60 * MIB


def nt_dot(a, b):
    return lax.dot_general(a, b, (((1,), (1,)), ((), ())), preferred_element_type=jnp.float32)


def nn_dot(a, b):
    return jnp.dot(a, b, preferred_element_type=jnp.float32)


def full(shape):
    return pl.BlockSpec(shape, lambda *_: (0,) * len(shape))


def pack_video_kernel(q_ref, k_ref, v_ref, kv_out, q_out):
    kv_out[0, 0] = k_ref[...]
    kv_out[0, 1] = v_ref[...]
    q_out[0] = q_ref[...]


def pack_video(q, k, v):
    rows = q.shape[0]
    group = pl.BlockSpec((rows, GW), lambda g: (0, g))
    return pl.pallas_call(
        pack_video_kernel,
        out_shape=[
            jax.ShapeDtypeStruct((TOWERS, 2, rows, GW), jnp.bfloat16),
            jax.ShapeDtypeStruct((TOWERS, rows, GW), jnp.bfloat16),
        ],
        grid=(TOWERS,),
        in_specs=[group] * 3,
        out_specs=[
            pl.BlockSpec((1, 2, rows, GW), lambda g: (g, 0, 0, 0)),
            pl.BlockSpec((1, rows, GW), lambda g: (g, 0, 0)),
        ],
        compiler_params=pltpu.CompilerParams(vmem_limit_bytes=VMEM),
        name="pack_video",
    )(q, k, v)


WIN = 192
HALO = 48
QROWS = 96
QAT = 2 * WIN
HAT = QAT + QROWS
AROWS = HAT + 2 * HALO


def main_first(ctx):
    return jnp.clip(lax.rem(ctx, 4) * QROWS - HALO, 0, 384 - WIN)


def edge_tower(ctx):
    return jnp.clip(jnp.where(lax.rem(ctx, 4) == 0, ctx // 4 - 1, ctx // 4 + 1), 0, TOWERS - 1)


def pack_audio_kernel(place, q_ref, k_ref, v_ref, out):
    ctx = place[0]
    phase = lax.rem(ctx, 4)
    main = pl.multiple_of(main_first(ctx), 16)
    mine = pl.multiple_of(phase * QROWS, 16)
    halo = pl.multiple_of(jnp.where(phase == 0, 384 - HALO, 0), 16)
    out[0, pl.ds(0, WIN), :] = k_ref[pl.ds(main, WIN), :]
    out[0, pl.ds(WIN, WIN), :] = v_ref[pl.ds(main, WIN), :]
    out[0, pl.ds(QAT, QROWS), :] = q_ref[pl.ds(mine, QROWS), :]
    out[0, pl.ds(HAT, HALO), :] = k_ref[pl.ds(halo, HALO), :]
    out[0, pl.ds(HAT + HALO, HALO), :] = v_ref[pl.ds(halo, HALO), :]


def pack_audio(place, q, k, v):
    group = pl.BlockSpec((q.shape[0], GW), lambda g, *_: (0, g))
    return pl.pallas_call(
        pack_audio_kernel,
        out_shape=jax.ShapeDtypeStruct((TOWERS, AROWS, GW), jnp.bfloat16),
        grid_spec=pltpu.PrefetchScalarGridSpec(
            num_scalar_prefetch=1,
            grid=(TOWERS,),
            in_specs=[group] * 3,
            out_specs=pl.BlockSpec((1, AROWS, GW), lambda g, *_: (g, 0, 0)),
        ),
        compiler_params=pltpu.CompilerParams(vmem_limit_bytes=VMEM),
        name="pack_audio",
    )(place, q, k, v)


def rows_of(kv_ref, which):
    return jnp.concatenate([kv_ref[r, which] for r in range(TOWERS)], axis=0)


def flash_kernel(kv_count, first, last, *refs):
    q_ref = refs[0]
    kv_refs = refs[1 : 1 + kv_count]
    rest = refs[1 + kv_count :]
    if first:
        outs = rest
    else:
        acc_in, stat_in = rest[:2]
        outs = rest[2:]
    size = 2 * VBLK
    for tile in range(TOWERS // 2):
        rows = pl.ds(tile * size, size)
        query = q_ref[rows, :]
        scores = [nt_dot(query, rows_of(kv, 0)) for kv in kv_refs]
        top = functools.reduce(
            jnp.maximum, [jnp.max(s, axis=1, keepdims=True) for s in scores]
        ) * SCALE2
        if not first:
            stat = stat_in[rows, :]
            old_top, old_total = stat[:, 0:1], stat[:, 64:65]
            top = jnp.maximum(top, old_top)
            factor = jnp.exp2(old_top - top)
        total = None
        acc = None
        for s, kv in zip(scores, kv_refs):
            weights = jnp.exp2(s * SCALE2 - top)
            part = jnp.sum(weights, axis=1, keepdims=True)
            total = part if total is None else total + part
            part = nn_dot(weights.astype(jnp.bfloat16), rows_of(kv, 1))
            acc = part if acc is None else acc + part
        if not first:
            total = total + old_total * factor
            acc = acc + acc_in[rows, :] * factor
        if last:
            outs[0][rows, :] = (acc / total).astype(jnp.bfloat16)
        else:
            outs[0][rows, :] = acc
            lane = lax.broadcasted_iota(jnp.int32, (size, HD), 1)
            outs[1][rows, :] = jnp.where(lane < 64, top, total)


def flash(query, kvs, state, last):
    rows = TOWERS * VBLK
    keys = rows * len(kvs)
    wide = jax.ShapeDtypeStruct((rows, GW), jnp.float32)
    head = pl.BlockSpec((rows, HD), lambda h: (0, h))
    if last:
        out_shape = jax.ShapeDtypeStruct((rows, GW), jnp.bfloat16)
        out_specs = head
    else:
        out_shape = [wide, wide]
        out_specs = [head, head]
    shard = pl.BlockSpec((TOWERS, 2, VBLK, HD), lambda h: (0, 0, 0, h))
    return pl.pallas_call(
        functools.partial(flash_kernel, len(kvs), state is None, last),
        out_shape=out_shape,
        grid=(LOCAL,),
        in_specs=[head] + [shard] * len(kvs) + ([] if state is None else [head, head]),
        out_specs=out_specs,
        compiler_params=pltpu.CompilerParams(vmem_limit_bytes=VMEM),
        cost_estimate=pl.CostEstimate(
            flops=8 * rows * keys * GW,
            bytes_accessed=4 * keys * GW + 16 * rows * GW,
            transcendentals=rows * keys * LOCAL,
        ),
        name="flash",
    )(query, *kvs, *(() if state is None else state))


def cross_kernel(place, margin, q_ref, main, edge, out):
    ctx = place[0]
    phase = lax.rem(ctx, 4)
    base = (ctx - phase) * 4
    lane = lax.broadcasted_iota(jnp.int32, (1, 256), 1)
    halo_base = jnp.where(phase == 0, base - 2, jnp.where(phase == 3, base + 16, -100))
    main_base = base + lax.div(main_first(ctx), ABLK)
    ids = jnp.where(lane < WIN, lane // ABLK + main_base, lane // ABLK - WIN // ABLK + halo_base)
    ids = jnp.where(lane < WIN + HALO, ids, -100)
    spare = jnp.zeros((256 - WIN - HALO, HD), jnp.bfloat16)
    keys = jnp.concatenate([main[0, pl.ds(0, WIN), :], edge[0, pl.ds(HAT, HALO), :], spare], axis=0)
    values = jnp.concatenate(
        [main[0, pl.ds(WIN, WIN), :], edge[0, pl.ds(HAT + HALO, HALO), :], spare], axis=0
    )
    scores = nt_dot(q_ref[...], keys) * SCALE2
    parts = []
    for r in range(TOWERS):
        block = ctx * 4 + r
        hit = (ids == margin[block, 0]) | (ids == margin[block, 1]) | (ids == margin[block, 2])
        parts.append(jnp.where(hit, scores[r * VBLK : (r + 1) * VBLK], NEG))
    scores = jnp.concatenate(parts, axis=0)
    weights = jnp.exp2(scores - jnp.max(scores, axis=1, keepdims=True))
    total = jnp.sum(weights, axis=1, keepdims=True)
    out[...] = (nn_dot(weights.astype(jnp.bfloat16), values) / total).astype(jnp.bfloat16)


def cross(place, margin, query, audio):
    rows = query.shape[0]
    head = pl.BlockSpec((rows, HD), lambda h, *_: (0, h))
    return pl.pallas_call(
        cross_kernel,
        out_shape=jax.ShapeDtypeStruct((rows, GW), jnp.bfloat16),
        grid_spec=pltpu.PrefetchScalarGridSpec(
            num_scalar_prefetch=2,
            grid=(LOCAL,),
            in_specs=[
                head,
                pl.BlockSpec((1, AROWS, HD), lambda h, place, margin: (place[2], 0, h)),
                pl.BlockSpec((1, AROWS, HD), lambda h, place, margin: (place[3], 0, h)),
            ],
            out_specs=head,
        ),
        compiler_params=pltpu.CompilerParams(vmem_limit_bytes=VMEM),
        cost_estimate=pl.CostEstimate(
            flops=8 * rows * 256 * GW, bytes_accessed=2 * MIB, transcendentals=rows * 256 * 3
        ),
        name="cross",
    )(place, margin, query, audio, audio)


def audio_kernel(place, margin, audio, own, sibling, third, out):
    ctx = place[0]
    core = lax.rem(ctx, 2)
    owners = (ctx, ctx + 1 - 2 * core, lax.rem(ctx - 1 + 2 * core + 16, 16))
    row_block = lax.broadcasted_iota(jnp.int32, (QROWS, 1), 0) // ABLK + ctx * 4
    query = audio[0, pl.ds(QAT, QROWS), :]
    scores = []
    for owner, kv in zip(owners, (own, sibling, third)):
        s = nt_dot(query, rows_of(kv, 0)) * SCALE2
        for r in range(TOWERS):
            block = owner * 4 + r
            hit = (
                (row_block == margin[block, 0])
                | (row_block == margin[block, 1])
                | (row_block == margin[block, 2])
            )
            scores.append(jnp.where(hit, s[:, r * VBLK : (r + 1) * VBLK], NEG))
    scores = jnp.concatenate(scores, axis=1)
    weights = jnp.exp2(scores - jnp.max(scores, axis=1, keepdims=True))
    total = jnp.sum(weights, axis=1, keepdims=True)
    values = jnp.concatenate([rows_of(kv, 1) for kv in (own, sibling, third)], axis=0)
    out[...] = (nn_dot(weights.astype(jnp.bfloat16), values) / total).astype(jnp.bfloat16)


def audio_mix(place, margin, audio, kvs):
    shard = pl.BlockSpec((TOWERS, 2, VBLK, HD), lambda h, *_: (0, 0, 0, h))
    return pl.pallas_call(
        audio_kernel,
        out_shape=jax.ShapeDtypeStruct((QROWS, GW), jnp.bfloat16),
        grid_spec=pltpu.PrefetchScalarGridSpec(
            num_scalar_prefetch=2,
            grid=(LOCAL,),
            in_specs=[pl.BlockSpec((1, AROWS, HD), lambda h, place, margin: (place[2], 0, h))]
            + [shard] * 3,
            out_specs=pl.BlockSpec((QROWS, HD), lambda h, *_: (0, h)),
        ),
        compiler_params=pltpu.CompilerParams(vmem_limit_bytes=VMEM),
        cost_estimate=pl.CostEstimate(
            flops=8 * 96 * 1536 * GW, bytes_accessed=3 * MIB, transcendentals=96 * 1536 * 3
        ),
        name="audio_mix",
    )(place, margin, audio, *kvs)


def project_kernel(has_base, place, a_ref, mine, other, *refs):
    step = pl.program_id(0)

    def part(w_ref):
        acc = None
        for t in range(TOWERS):
            w = jnp.concatenate(
                [w_ref[b * TOWERS + t, 0, h] for h in range(LOCAL) for b in range(4)], axis=0
            )
            term = nn_dot(a_ref[t], w)
            acc = term if acc is None else acc + term
        if has_base:
            base, gain, out = refs
            out[...] = (gain[...] * (acc + base[...])).astype(out.dtype)
        else:
            refs[0][...] = acc

    @pl.when(step < 3)
    def _():
        part(mine)

    @pl.when(step >= 3)
    def _():
        part(other)


def project(place, a, mine, other, kind, base=None, gain=None):
    width = mine.shape[-1]
    tile = width // 3

    def column(i, place):
        return jnp.where(i < 3, place[4] * 3 + i, (1 - place[4]) * 3 + i - 3)

    block = (16, 1, LOCAL, HD // 4, tile)
    rows = pl.BlockSpec((VBLK, tile), lambda i, place: (0, column(i, place)))
    extra = [] if base is None else [rows, pl.BlockSpec((1, tile), lambda i, place: (0, column(i, place)))]
    dtype = jnp.float32 if base is None else jnp.bfloat16
    return pl.pallas_call(
        functools.partial(project_kernel, base is not None),
        out_shape=jax.ShapeDtypeStruct((VBLK, 2 * width), dtype),
        grid_spec=pltpu.PrefetchScalarGridSpec(
            num_scalar_prefetch=1,
            grid=(6,),
            in_specs=[
                full(a.shape),
                pl.BlockSpec(block, lambda i, place: (0, kind, 0, 0, jnp.minimum(i, 2))),
                pl.BlockSpec(block, lambda i, place: (0, kind, 0, 0, jnp.maximum(i - 3, 0))),
            ]
            + extra,
            out_specs=rows,
        ),
        compiler_params=pltpu.CompilerParams(vmem_limit_bytes=VMEM),
        cost_estimate=pl.CostEstimate(
            flops=2 * VBLK * 1536 * 3072, bytes_accessed=12 * MIB, transcendentals=0
        ),
        name="project",
    )(place, a, mine, other, *(() if base is None else (base, gain)))


def gate_kernel(*refs):
    pass


def gate(value, *after):
    anywhere = pl.BlockSpec(memory_space=pl.ANY)
    return pl.pallas_call(
        gate_kernel,
        out_shape=jax.ShapeDtypeStruct(value.shape, value.dtype),
        in_specs=[anywhere] * (1 + len(after)),
        out_specs=anywhere,
        input_output_aliases={0: 0},
        name="gate",
    )(value, *after)


def exchange_towers(value):
    return lax.all_to_all(value, "tower", split_axis=0, concat_axis=0, tiled=True)


def hop(value):
    total = 2 * CHIPS
    return lax.ppermute(value, "ctx", [(i, (i + 2 - 4 * (i % 2)) % total) for i in range(total)])


def swap_core(value):
    return lax.ppermute(value, "ctx", [(i, i ^ 1) for i in range(2 * CHIPS)])


def shards(video_q, video_k, video_v, audio_q, audio_k, audio_v, margin, out_weight, gate_gains):
    ctx = lax.axis_index("ctx")
    tower = lax.axis_index("tower")
    core = lax.rem(ctx, 2)
    place = jnp.stack([ctx, tower, ctx // 4, edge_tower(ctx), core]).astype(jnp.int32)
    gains = gate_gains[0]
    margins = margin[0]

    kv_parts, q_parts = pack_video(video_q[0], video_k[0], video_v[0])
    own = exchange_towers(kv_parts)
    sibling = swap_core(own)
    near, far = hop(own), hop(sibling)

    half = out_weight.shape[-1] // 2
    narrow = lax.dynamic_slice_in_dim(out_weight[:2], core * half, half, 3)
    w_mine = lax.all_gather(narrow, ("batch", "tower"), axis=0, tiled=False)
    w_audio = lax.all_gather(out_weight[2], "batch", axis=1, tiled=True)

    query = exchange_towers(q_parts).reshape(TOWERS * VBLK, GW)
    state = flash(query, [own, sibling], None, False)
    audio = exchange_towers(pack_audio(place, audio_q[0], audio_k[0], audio_v[0]))
    video_cross = cross(place, margins, query, audio)
    mixed = audio_mix(place, margins, audio, (own, sibling, far))
    near = gate(near, state[1])

    for step in range(1, 4):
        now = [near, far, swap_core(near), swap_core(far)]
        near, far = hop(near), (hop(far) if step < 3 else None)
        state = flash(query, now, state, False)
        if step == 1:
            near = gate(near, state[1], video_cross, mixed)
        if step == 2:
            near = gate(near, state[1])
            w_mine = gate(w_mine, state[1])
    video_self = flash(query, [near, swap_core(near)], state, True)

    w_other = swap_core(w_mine)
    cross_all = exchange_towers(video_cross.reshape(TOWERS, VBLK, GW))
    base = project(place, cross_all, w_mine, w_other, 1)
    self_all = exchange_towers(video_self.reshape(TOWERS, VBLK, GW))
    video_out = project(place, self_all, w_mine, w_other, 0, base, gains[0][None])

    audio_part = nn_dot(mixed, w_audio.reshape(GW, -1)).astype(jnp.bfloat16)
    audio_part = exchange_towers(audio_part.reshape(TOWERS, ABLK, -1))
    audio_sum = jnp.sum(audio_part.astype(jnp.float32), axis=0)
    audio_out = (gains[1][None] * audio_sum).astype(jnp.bfloat16)
    return (video_out[None], audio_out[None])


def solution(mesh):
    return jax.shard_map(
        shards,
        mesh=mesh,
        in_specs=(
            P("batch", ("ctx", "tower"), None),
            P("batch", ("ctx", "tower"), None),
            P("batch", ("ctx", "tower"), None),
            P("batch", "tower", None),
            P("batch", "tower", None),
            P("batch", "tower", None),
            P("batch", None, None),
            P(None, "tower", "batch", None),
            P("batch", None, None),
        ),
        out_specs=(P("batch", ("ctx", "tower"), None), P("batch", ("ctx", "tower"), None)),
        check_vma=False,
    )
```

profile of v0, /device:TPU:1, one launch (start us, length us, event | category | flops | bytes accessed | tf_op | source)
XLA Modules:
  0.0 229.6 jit_solution(16527475564826800363)
XLA Ops:
  10.2 3.5 %pack_video.1 = (bf16[4,2,128,384]{3,2,1,0:T(8,128)(2,1)}, bf16[4,128,384]{2,1,0:T(8,128)(2,1)}) custom-call(bf16[128,1536]{1,0:T(8,128)(2,1)} %bitcast.41, bf16[128,1536]{1,0:T(8,128)(2,1)} %bitcast.42, bf16[128,1536]{1,0:T(8,128)(2,1)} %bitcast.43), custom_call_target="tpu_custom_call" | custom-call | tf_op jit(solution)/shard_map/pack_video/pallas_call | solution.py:45
  13.7 15.3 %all_to_all.30.refs_1_.own = bf16[4,2,128,384]{3,2,1,0:T(8,128)(2,1)S(1)} all-to-all(bf16[4,2,128,384]{3,2,1,0:T(8,128)(2,1)} %get-tuple-element.13), channel_id=1, replica_groups=mesh['batch'=4,'ctx'=16,'tower'=4] {'tower'}, dimensions={0} | all-to-all | bytes 1572864 | tf_op jit(solution)/shard_map/all_to_all | solution.py:350
  31.7 3.5 %all-to-all-start = ((bf16[4,128,384]{2,1,0:T(8,128)(2,1)}), bf16[4,128,384]{2,1,0:T(8,128)(2,1)S(1)}, u32[]{:S(2)}, u32[]{:S(2)}) async-start(bf16[4,128,384]{2,1,0:T(8,128)(2,1)} %get-tuple-element.12), calls=%async_computation | async-start | bytes 786432 | tf_op jit(solution)/shard_map/all_to_all | solution.py:350
  35.2 8.7 %collective-permute-start = (bf16[4,2,128,384]{3,2,1,0:T(8,128)(2,1)S(1)}, bf16[4,2,128,384]{3,2,1,0:T(8,128)(2,1)}, u32[]{:S(2)}, u32[]{:S(2)}) collective-permute-start(bf16[4,2,128,384]{3,2,1,0:T(8,128)(2,1)S(1)} %all_to_all.30.refs_1_.own), channel_id=1, source_target_pairs={{0,8},{4,60},{8,16},{12,4},{16,24},{20,12},{24,32},{28,20},{32,40}... | collective-permute-start | bytes 2359304 | tf_op jit(solution)/shard_map/ppermute | solution.py:355
  44.7 4.7 %pack_audio.1 = bf16[4,576,384]{2,1,0:T(8,128)(2,1)} custom-call(s32[5]{0:T(128)} %stack.23.place, bf16[384,1536]{1,0:T(8,128)(2,1)} %bitcast.36, bf16[384,1536]{1,0:T(8,128)(2,1)} %bitcast.37, bf16[384,1536]{1,0:T(8,128)(2,1)} %bitcast.38), custom_call_target="tpu_custom_call" | custom-call | tf_op jit(solution)/shard_map/pack_audio/pallas_call | solution.py:93
  50.2 4.1 %all-to-all-start.2 = ((bf16[4,576,384]{2,1,0:T(8,128)(2,1)}), bf16[4,576,384]{2,1,0:T(8,128)(2,1)S(1)}, u32[]{:S(2)}, u32[]{:S(2)}) async-start(bf16[4,576,384]{2,1,0:T(8,128)(2,1)} %pack_audio.1), calls=%async_computation.2 | async-start | bytes 3538944 | tf_op jit(solution)/shard_map/all_to_all | solution.py:350
  54.3 5.4 %flash.5 = (f32[512,384]{1,0:T(8,128)}, f32[512,384]{1,0:T(8,128)}) custom-call(bf16[512,384]{1,0:T(8,128)(2,1)} %bitcast.30, bf16[4,2,128,384]{3,2,1,0:T(8,128)(2,1)} %copy-done.1, bf16[4,2,128,384]{3,2,1,0:T(8,128)(2,1)} %collective-permute-done.1.refs_2_.sibling), custom_call_target="tpu_custom_call" | custom-call | flops 1610612736 | bytes 4718592 | tf_op jit(solution)/shard_map/flash/pallas_call | solution.py:164
  65.5 28.5 %all-to-all-done.2.main.edge.audio = bf16[4,576,384]{2,1,0:T(8,128)(2,1)S(1)} async-done(((bf16[4,576,384]{2,1,0:T(8,128)(2,1)}), bf16[4,576,384]{2,1,0:T(8,128)(2,1)S(1)}, u32[]{:S(2)}, u32[]{:S(2)}) %all-to-all-start.2) | async-done | bytes 1769504 | tf_op jit(solution)/shard_map/all_to_all | solution.py:350
  95.2 5.1 %cross.1.refs_2_ = bf16[512,384]{1,0:T(8,128)(2,1)} custom-call(s32[5]{0:T(128)} %stack.23.place, s32[64,3]{1,0:T(8,128)} %bitcast.44, bf16[512,384]{1,0:T(8,128)(2,1)} %bitcast.31, bf16[4,576,384]{2,1,0:T(8,128)(2,1)} %copy-done, bf16[4,576,384]{2,1,0:T(8,128)(2,1)} %copy-done), custom_call_target="tpu_custom_call" | custom-call | flops 402653184 | bytes 2097152 | tf_op jit(solution)/shard_map/cross/pallas_call | solution.py:209
  100.3 5.5 %audio_mix.1.refs_3_ = bf16[96,384]{1,0:T(8,128)(2,1)} custom-call(s32[5]{0:T(128)} %stack.23.place, s32[64,3]{1,0:T(8,128)} %bitcast.45, bf16[4,576,384]{2,1,0:T(8,128)(2,1)} %copy-done, bf16[4,2,128,384]{3,2,1,0:T(8,128)(2,1)} %copy-done.1, bf16[4,2,128,384]{3,2,1,0:T(8,128)(2,1)} %collective-permute-done.1.refs_2_.sibling, ...), custom_call_target="tpu_custom_call" | custom-call | flops 452984832 | bytes 3145728 | tf_op jit(solution)/shard_map/audio_mix/pallas_call | solution.py:256
  105.8 8.7 %flash.6 = (f32[512,384]{1,0:T(8,128)}, f32[512,384]{1,0:T(8,128)}) custom-call(bf16[512,384]{1,0:T(8,128)(2,1)} %bitcast.32, bf16[4,2,128,384]{3,2,1,0:T(8,128)(2,1)} %gate.4.refs_1_, bf16[4,2,128,384]{3,2,1,0:T(8,128)(2,1)} %collective-permute-done.3.refs_2_.third, bf16[4,2,128,384]{3,2,1,0:T(8,128)(2,1)} %collective-permute-done.4.refs_3_, ...), custom_call_target="tpu_custom_call" | custom-call | flops 3221225472 | bytes 6291456 | tf_op jit(solution)/shard_map/flash/pallas_call | solution.py:164
  119.8 8.6 %flash.7 = (f32[512,384]{1,0:T(8,128)}, f32[512,384]{1,0:T(8,128)}) custom-call(bf16[512,384]{1,0:T(8,128)(2,1)} %bitcast.33, bf16[4,2,128,384]{3,2,1,0:T(8,128)(2,1)} %gate.5.refs_1_, bf16[4,2,128,384]{3,2,1,0:T(8,128)(2,1)} %copy-done.13, bf16[4,2,128,384]{3,2,1,0:T(8,128)(2,1)} %copy-done.15, bf16[4,2,128,384]{3,2,1,0:T(8,128)(2,1)} %copy-done.16, ...), custom_call_target="tpu_custom_call" | custom-call | flops 3221225472 | bytes 6291456 | tf_op jit(solution)/shard_map/flash/pallas_call | solution.py:164
  130.8 4.4 %collective-permute-start.6 = (bf16[4,2,128,384]{3,2,1,0:T(8,128)(2,1)S(1)}, bf16[4,2,128,384]{3,2,1,0:T(8,128)(2,1)S(1)}, u32[]{:S(2)}, u32[]{:S(2)}) collective-permute-start(bf16[4,2,128,384]{3,2,1,0:T(8,128)(2,1)S(1)} %copy-done.7), channel_id=1, source_target_pairs={{0,8},{4,60},{8,16},{12,4},{16,24},{20,12},{24,32},{28,20},{32,40}... | collective-permute-start | bytes 2359304 | tf_op jit(solution)/shard_map/ppermute | solution.py:355
  135.3 8.8 %collective-permute-done.6.refs_0_ = bf16[4,2,128,384]{3,2,1,0:T(8,128)(2,1)S(1)} collective-permute-done((bf16[4,2,128,384]{3,2,1,0:T(8,128)(2,1)S(1)}, bf16[4,2,128,384]{3,2,1,0:T(8,128)(2,1)S(1)}, u32[]{:S(2)}, u32[]{:S(2)}) %collective-permute-start.6) | collective-permute-done | bytes 786464 | tf_op jit(solution)/shard_map/ppermute | solution.py:355
  148.2 16.8 %all-gather.7.cloned.1.call-done = bf16[1,3,128,3072]{3,2,1,0:T(8,128)(2,1)} async-done(((bf16[1,3,32,3072]{3,2,1,0:T(8,128)(2,1)}), bf16[1,3,128,3072]{3,2,1,0:T(8,128)(2,1)}) %all-gather.7.cloned.1.call-update) | async-done | bytes 2359312 | tf_op jit(solution)/shard_map/all_gather | solution.py:378
  165.0 3.2 %convolution_convert_fusion = bf16[96,3072]{1,0:T(8,128)(2,1)} fusion(bf16[96,384]{1,0:T(8,128)(2,1)S(1)} %copy-done.10, bf16[384,3072]{1,0:T(8,128)(2,1)} %bitcast.29), kind=kOutput, calls=%fused_computation | convolution fusion | flops 226787328 | bytes 3022848 | tf_op jit(solution)/shard_map/dot_general | solution.py:29
  168.2 4.0 %all-to-all-start.5 = ((bf16[4,24,3072]{2,1,0:T(8,128)(2,1)}), bf16[4,24,3072]{2,1,0:T(8,128)(2,1)S(1)}, u32[]{:S(2)}, u32[]{:S(2)}) async-start(bf16[4,24,3072]{2,1,0:T(8,128)(2,1)} %bitcast.20), calls=%async_computation.5 | async-start | bytes 1179648 | tf_op jit(solution)/shard_map/all_to_all | solution.py:350
  174.4 6.7 %all-to-all-done.5 = bf16[4,24,3072]{2,1,0:T(8,128)(2,1)S(1)} async-done(((bf16[4,24,3072]{2,1,0:T(8,128)(2,1)}), bf16[4,24,3072]{2,1,0:T(8,128)(2,1)S(1)}, u32[]{:S(2)}, u32[]{:S(2)}) %all-to-all-start.5) | async-done | bytes 589856 | tf_op jit(solution)/shard_map/all_to_all | solution.py:350
  181.0 3.5 %all-to-all-start.4 = ((bf16[4,128,384]{2,1,0:T(8,128)(2,1)}), bf16[4,128,384]{2,1,0:T(8,128)(2,1)S(1)}, u32[]{:S(2)}, u32[]{:S(2)}) async-start(bf16[4,128,384]{2,1,0:T(8,128)(2,1)} %bitcast.15), calls=%async_computation.4 | async-start | bytes 786432 | tf_op jit(solution)/shard_map/all_to_all | solution.py:350
  184.6 8.7 %flash.8 = (f32[512,384]{1,0:T(8,128)}, f32[512,384]{1,0:T(8,128)}) custom-call(bf16[512,384]{1,0:T(8,128)(2,1)} %bitcast.34, bf16[4,2,128,384]{3,2,1,0:T(8,128)(2,1)} %gate.6.refs_1_, bf16[4,2,128,384]{3,2,1,0:T(8,128)(2,1)} %collective-permute-done.12.refs_2_, bf16[4,2,128,384]{3,2,1,0:T(8,128)(2,1)} %collective-permute-done.13.refs_3_, ...), custom_call_target="tpu_custom_call" | custom-call | flops 3221225472 | bytes 6291456 | tf_op jit(solution)/shard_map/flash/pallas_call | solution.py:164
  193.3 6.0 %flash.9 = bf16[512,384]{1,0:T(8,128)(2,1)} custom-call(bf16[512,384]{1,0:T(8,128)(2,1)} %bitcast.35, bf16[4,2,128,384]{3,2,1,0:T(8,128)(2,1)} %copy-done.14, bf16[4,2,128,384]{3,2,1,0:T(8,128)(2,1)} %collective-permute-done.11.refs_2_, f32[512,384]{1,0:T(8,128)} %get-tuple-element.20.refs_3_, f32[512,384]{1,0:T(8,128)} %get-tuple-element.21.refs_4_), custom_call_target="tpu_custom_call" | custom-call | flops 1610612736 | bytes 4718592 | tf_op jit(solution)/shard_map/flash/pallas_call | solution.py:164
  199.3 4.2 %all-to-all-start.3 = ((bf16[4,128,384]{2,1,0:T(8,128)(2,1)}), bf16[4,128,384]{2,1,0:T(8,128)(2,1)S(1)}, u32[]{:S(2)}, u32[]{:S(2)}) async-start(bf16[4,128,384]{2,1,0:T(8,128)(2,1)} %bitcast.40), calls=%async_computation.3 | async-start | bytes 786432 | tf_op jit(solution)/shard_map/all_to_all | solution.py:350
  204.2 8.6 %project.2.refs_0_ = f32[128,3072]{1,0:T(8,128)} custom-call(s32[5]{0:T(128)} %stack.23.place, bf16[4,128,384]{2,1,0:T(8,128)(2,1)} %copy-done.4, bf16[16,2,3,32,1536]{4,3,2,1,0:T(8,128)(2,1)} %gate.7.mine, bf16[16,2,3,32,1536]{4,3,2,1,0:T(8,128)(2,1)} %collective-permute-done.15.other), custom_call_target="tpu_custom_call" | custom-call | flops 1207959552 | bytes 12582912 | tf_op jit(solution)/shard_map/project/pallas_call | solution.py:311
  213.5 8.6 %project.3 = bf16[128,3072]{1,0:T(8,128)(2,1)} custom-call(s32[5]{0:T(128)} %stack.23.place, bf16[4,128,384]{2,1,0:T(8,128)(2,1)} %copy-done.5, bf16[16,2,3,32,1536]{4,3,2,1,0:T(8,128)(2,1)} %gate.7.mine, bf16[16,2,3,32,1536]{4,3,2,1,0:T(8,128)(2,1)} %collective-permute-done.15.other, f32[128,3072]{1,0:T(8,128)} %project.2.refs_0_, ...), custom_call_target="tpu_custom_call" | custom-call | flops 1207959552 | bytes 12582912 | tf_op jit(solution)/shard_map/project/pallas_call | solution.py:311
  (84 shorter events, 28.9 us)
Async XLA Ops:
  8.0 120.4 %all-gather.5.cloned.1.call-start = ((), (), s32[]{:S(2)}) async-start(), calls=%async_computation.6 | async-start | bytes 10027008 | tf_op jit(solution)/shard_map/all_gather | solution.py:377
  29.0 14.9 %collective-permute-start.1 = (bf16[4,2,128,384]{3,2,1,0:T(8,128)(2,1)S(1)}, bf16[4,2,128,384]{3,2,1,0:T(8,128)(2,1)}, u32[]{:S(2)}, u32[]{:S(2)}) collective-permute-start(bf16[4,2,128,384]{3,2,1,0:T(8,128)(2,1)S(1)} %all_to_all.30.refs_1_.own), channel_id=1, source_target_pairs={{0,4},{4,0},{8,12},{12,8},{16,20},{20,16},{24,28},{28,24},{32,36},... | collective-permute-start | bytes 2359304 | tf_op jit(solution)/shard_map/ppermute | solution.py:359
  31.7 17.7 %all-to-all-start = ((bf16[4,128,384]{2,1,0:T(8,128)(2,1)}), bf16[4,128,384]{2,1,0:T(8,128)(2,1)S(1)}, u32[]{:S(2)}, u32[]{:S(2)}) async-start(bf16[4,128,384]{2,1,0:T(8,128)(2,1)} %get-tuple-element.12), calls=%async_computation | async-start | bytes 786432 | tf_op jit(solution)/shard_map/all_to_all | solution.py:350
  35.2 24.5 %collective-permute-start = (bf16[4,2,128,384]{3,2,1,0:T(8,128)(2,1)S(1)}, bf16[4,2,128,384]{3,2,1,0:T(8,128)(2,1)}, u32[]{:S(2)}, u32[]{:S(2)}) collective-permute-start(bf16[4,2,128,384]{3,2,1,0:T(8,128)(2,1)S(1)} %all_to_all.30.refs_1_.own), channel_id=1, source_target_pairs={{0,8},{4,60},{8,16},{12,4},{16,24},{20,12},{24,32},{28,20},{32,40}... | collective-permute-start | bytes 2359304 | tf_op jit(solution)/shard_map/ppermute | solution.py:355
  43.9 17.5 %collective-permute-start.3 = (bf16[4,2,128,384]{3,2,1,0:T(8,128)(2,1)}, bf16[4,2,128,384]{3,2,1,0:T(8,128)(2,1)}, u32[]{:S(2)}, u32[]{:S(2)}) collective-permute-start(bf16[4,2,128,384]{3,2,1,0:T(8,128)(2,1)} %collective-permute-done.1.refs_2_.sibling), channel_id=1, source_target_pairs={{0,8},{4,60},{8,16},{12,4},{16,24},{20,12},{24,32},{28,20},{32,40}... | collective-permute-start | bytes 2359304 | tf_op jit(solution)/shard_map/ppermute | solution.py:355
  50.2 43.8 %all-to-all-start.2 = ((bf16[4,576,384]{2,1,0:T(8,128)(2,1)}), bf16[4,576,384]{2,1,0:T(8,128)(2,1)S(1)}, u32[]{:S(2)}, u32[]{:S(2)}) async-start(bf16[4,576,384]{2,1,0:T(8,128)(2,1)} %pack_audio.1), calls=%async_computation.2 | async-start | bytes 3538944 | tf_op jit(solution)/shard_map/all_to_all | solution.py:350
  54.3 110.7 %all-gather.7.cloned.1.call-start = ((), (), s32[]{:S(2)}) async-start(), calls=%async_computation.7 | async-start | bytes 2949120 | tf_op jit(solution)/shard_map/all_gather | solution.py:378
  59.7 46.1 %collective-permute-start.4 = (bf16[4,2,128,384]{3,2,1,0:T(8,128)(2,1)}, bf16[4,2,128,384]{3,2,1,0:T(8,128)(2,1)}, u32[]{:S(2)}, u32[]{:S(2)}) collective-permute-start(bf16[4,2,128,384]{3,2,1,0:T(8,128)(2,1)} %gate.4.refs_1_), channel_id=1, source_target_pairs={{0,4},{4,0},{8,12},{12,8},{16,20},{20,16},{24,28},{28,24},{32,36},... | collective-permute-start | bytes 2359304 | tf_op jit(solution)/shard_map/ppermute | solution.py:359
  61.4 44.5 %collective-permute-start.5 = (bf16[4,2,128,384]{3,2,1,0:T(8,128)(2,1)}, bf16[4,2,128,384]{3,2,1,0:T(8,128)(2,1)}, u32[]{:S(2)}, u32[]{:S(2)}) collective-permute-start(bf16[4,2,128,384]{3,2,1,0:T(8,128)(2,1)} %collective-permute-done.3.refs_2_.third), channel_id=1, source_target_pairs={{0,4},{4,0},{8,12},{12,8},{16,20},{20,16},{24,28},{28,24},{32,36},... | collective-permute-start | bytes 2359304 | tf_op jit(solution)/shard_map/ppermute | solution.py:359
  62.7 51.9 %collective-permute-start.2 = (bf16[4,2,128,384]{3,2,1,0:T(8,128)(2,1)}, bf16[4,2,128,384]{3,2,1,0:T(8,128)(2,1)S(1)}, u32[]{:S(2)}, u32[]{:S(2)}) collective-permute-start(bf16[4,2,128,384]{3,2,1,0:T(8,128)(2,1)} %gate.4.refs_1_), channel_id=1, source_target_pairs={{0,8},{4,60},{8,16},{12,4},{16,24},{20,12},{24,32},{28,20},{32,40}... | collective-permute-start | bytes 2359304 | tf_op jit(solution)/shard_map/ppermute | solution.py:355
  64.8 50.7 %collective-permute-start.7 = (bf16[4,2,128,384]{3,2,1,0:T(8,128)(2,1)}, bf16[4,2,128,384]{3,2,1,0:T(8,128)(2,1)S(1)}, u32[]{:S(2)}, u32[]{:S(2)}) collective-permute-start(bf16[4,2,128,384]{3,2,1,0:T(8,128)(2,1)} %collective-permute-done.3.refs_2_.third), channel_id=1, source_target_pairs={{0,8},{4,60},{8,16},{12,4},{16,24},{20,12},{24,32},{28,20},{32,40}... | collective-permute-start | bytes 2359304 | tf_op jit(solution)/shard_map/ppermute | solution.py:355
  115.4 2.5 %collective-permute-start.8 = (bf16[4,2,128,384]{3,2,1,0:T(8,128)(2,1)}, bf16[4,2,128,384]{3,2,1,0:T(8,128)(2,1)S(1)}, u32[]{:S(2)}, u32[]{:S(2)}) collective-permute-start(bf16[4,2,128,384]{3,2,1,0:T(8,128)(2,1)} %gate.5.refs_1_), channel_id=1, source_target_pairs={{0,4},{4,0},{8,12},{12,8},{16,20},{20,16},{24,28},{28,24},{32,36},... | collective-permute-start | bytes 2359304 | tf_op jit(solution)/shard_map/ppermute | solution.py:359
  115.4 3.4 %collective-permute-start.9 = (bf16[4,2,128,384]{3,2,1,0:T(8,128)(2,1)S(1)}, bf16[4,2,128,384]{3,2,1,0:T(8,128)(2,1)S(1)}, u32[]{:S(2)}, u32[]{:S(2)}) collective-permute-start(bf16[4,2,128,384]{3,2,1,0:T(8,128)(2,1)S(1)} %collective-permute-done.7.refs_2_), channel_id=1, source_target_pairs={{0,4},{4,0},{8,12},{12,8},{16,20},{20,16},{24,28},{28,24},{32,36},... | collective-permute-start | bytes 2359304 | tf_op jit(solution)/shard_map/ppermute | solution.py:359
  128.5 75.7 %collective-permute-start.15 = (bf16[16,2,3,32,1536]{4,3,2,1,0:T(8,128)(2,1)}, bf16[16,2,3,32,1536]{4,3,2,1,0:T(8,128)(2,1)}, u32[]{:S(2)}, u32[]{:S(2)}) collective-permute-start(bf16[16,2,3,32,1536]{4,3,2,1,0:T(8,128)(2,1)} %gate.7.mine), channel_id=1, source_target_pairs={{0,4},{4,0},{8,12},{12,8},{16,20},{20,16},{24,28},{28,24},{32,36},... | collective-permute-start | bytes 28311560 | tf_op jit(solution)/shard_map/ppermute | solution.py:359
  130.8 34.2 %copy-start.10 = (bf16[96,384]{1,0:T(8,128)(2,1)S(1)}, bf16[96,384]{1,0:T(8,128)(2,1)}, u32[]{:S(2)}) copy-start(bf16[96,384]{1,0:T(8,128)(2,1)} %audio_mix.1.refs_3_) | copy-start | bytes 221188
  130.8 13.3 %collective-permute-start.6 = (bf16[4,2,128,384]{3,2,1,0:T(8,128)(2,1)S(1)}, bf16[4,2,128,384]{3,2,1,0:T(8,128)(2,1)S(1)}, u32[]{:S(2)}, u32[]{:S(2)}) collective-permute-start(bf16[4,2,128,384]{3,2,1,0:T(8,128)(2,1)S(1)} %copy-done.7), channel_id=1, source_target_pairs={{0,8},{4,60},{8,16},{12,4},{16,24},{20,12},{24,32},{28,20},{32,40}... | collective-permute-start | bytes 2359304 | tf_op jit(solution)/shard_map/ppermute | solution.py:355
  135.2 38.0 %collective-permute-start.12 = (bf16[4,2,128,384]{3,2,1,0:T(8,128)(2,1)}, bf16[4,2,128,384]{3,2,1,0:T(8,128)(2,1)}, u32[]{:S(2)}, u32[]{:S(2)}) collective-permute-start(bf16[4,2,128,384]{3,2,1,0:T(8,128)(2,1)} %copy-done.13), channel_id=1, source_target_pairs={{0,8},{4,60},{8,16},{12,4},{16,24},{20,12},{24,32},{28,20},{32,40}... | collective-permute-start | bytes 2359304 | tf_op jit(solution)/shard_map/ppermute | solution.py:355
  145.0 28.3 %collective-permute-start.10 = (bf16[4,2,128,384]{3,2,1,0:T(8,128)(2,1)}, bf16[4,2,128,384]{3,2,1,0:T(8,128)(2,1)S(1)}, u32[]{:S(2)}, u32[]{:S(2)}) collective-permute-start(bf16[4,2,128,384]{3,2,1,0:T(8,128)(2,1)} %gate.6.refs_1_), channel_id=1, source_target_pairs={{0,8},{4,60},{8,16},{12,4},{16,24},{20,12},{24,32},{28,20},{32,40}... | collective-permute-start | bytes 2359304 | tf_op jit(solution)/shard_map/ppermute | solution.py:355
  168.2 12.8 %all-to-all-start.5 = ((bf16[4,24,3072]{2,1,0:T(8,128)(2,1)}), bf16[4,24,3072]{2,1,0:T(8,128)(2,1)S(1)}, u32[]{:S(2)}, u32[]{:S(2)}) async-start(bf16[4,24,3072]{2,1,0:T(8,128)(2,1)} %bitcast.20), calls=%async_computation.5 | async-start | bytes 1179648 | tf_op jit(solution)/shard_map/all_to_all | solution.py:350
  172.2 12.4 %collective-permute-start.13 = (bf16[4,2,128,384]{3,2,1,0:T(8,128)(2,1)S(1)}, bf16[4,2,128,384]{3,2,1,0:T(8,128)(2,1)}, u32[]{:S(2)}, u32[]{:S(2)}) collective-permute-start(bf16[4,2,128,384]{3,2,1,0:T(8,128)(2,1)S(1)} %copy-done.9), channel_id=1, source_target_pairs={{0,4},{4,0},{8,12},{12,8},{16,20},{20,16},{24,28},{28,24},{32,36},... | collective-permute-start | bytes 2359304 | tf_op jit(solution)/shard_map/ppermute | solution.py:359
  173.2 11.4 %collective-permute-start.14 = (bf16[4,2,128,384]{3,2,1,0:T(8,128)(2,1)}, bf16[4,2,128,384]{3,2,1,0:T(8,128)(2,1)}, u32[]{:S(2)}, u32[]{:S(2)}) collective-permute-start(bf16[4,2,128,384]{3,2,1,0:T(8,128)(2,1)} %collective-permute-done.12.refs_2_), channel_id=1, source_target_pairs={{0,4},{4,0},{8,12},{12,8},{16,20},{20,16},{24,28},{28,24},{32,36},... | collective-permute-start | bytes 2359304 | tf_op jit(solution)/shard_map/ppermute | solution.py:359
  173.3 20.0 %collective-permute-start.11 = (bf16[4,2,128,384]{3,2,1,0:T(8,128)(2,1)S(1)}, bf16[4,2,128,384]{3,2,1,0:T(8,128)(2,1)}, u32[]{:S(2)}, u32[]{:S(2)}) collective-permute-start(bf16[4,2,128,384]{3,2,1,0:T(8,128)(2,1)S(1)} %collective-permute-done.10.refs_1_), channel_id=1, source_target_pairs={{0,4},{4,0},{8,12},{12,8},{16,20},{20,16},{24,28},{28,24},{32,36},... | collective-permute-start | bytes 2359304 | tf_op jit(solution)/shard_map/ppermute | solution.py:359
  181.0 18.3 %all-to-all-start.4 = ((bf16[4,128,384]{2,1,0:T(8,128)(2,1)}), bf16[4,128,384]{2,1,0:T(8,128)(2,1)S(1)}, u32[]{:S(2)}, u32[]{:S(2)}) async-start(bf16[4,128,384]{2,1,0:T(8,128)(2,1)} %bitcast.15), calls=%async_computation.4 | async-start | bytes 786432 | tf_op jit(solution)/shard_map/all_to_all | solution.py:350
  199.3 13.5 %all-to-all-start.3 = ((bf16[4,128,384]{2,1,0:T(8,128)(2,1)}), bf16[4,128,384]{2,1,0:T(8,128)(2,1)S(1)}, u32[]{:S(2)}, u32[]{:S(2)}) async-start(bf16[4,128,384]{2,1,0:T(8,128)(2,1)} %bitcast.40), calls=%async_computation.3 | async-start | bytes 786432 | tf_op jit(solution)/shard_map/all_to_all | solution.py:350
  (17 other events, 81.2 us)
Sparse Core Ops, SparseCore 0:
  11.3 102.5 all-gather.4
Sparse Core Ops, SparseCore 1:
  130.9 34.0 all-gather.6
where the time goes:
time: 233 us; the launch traced here: 230 us
  Pallas kernels  73.4 us (32%)
  waiting for transfers between devices  65.3 us (28%)
  starting transfers between devices  44.4 us (19%)
  between operations  15.7 us (7%)
  blocking collectives  15.3 us (7%)
  local copies, waits for them, and re-layouts  11.6 us (5%)
  matrix products  3.18 us (1%)
    pallas_call x5, Pallas kernels, flash(): pl.pallas_call(functools.partial(flash_kernel, len(kvs), state is None, l...  37.4 us
    all_to_all x5, waiting for transfers between devices, exchange_towers(): lax.all_to_all(value, 'tower', split_axis=0, concat_axis=0, tiled=True)  35.1 us
    all_to_all x5, starting transfers between devices, exchange_towers(): lax.all_to_all(value, 'tower', split_axis=0, concat_axis=0, tiled=True)  19.2 us
    ppermute x7, starting transfers between devices, hop(): lax.ppermute(value, 'ctx', [(i, (i + 2 - 4 * (i % 2)) % total) for i in r...  18.6 us
    pallas_call x2, Pallas kernels, project(): pl.pallas_call(functools.partial(project_kernel, base is not None), out_s...  17.2 us
    all_gather x1, waiting for transfers between devices, shards(): w_audio = lax.all_gather(out_weight[2], 'batch', axis=1, tiled=True)  16.8 us
    all_to_all x1, blocking collectives, exchange_towers(): lax.all_to_all(value, 'tower', split_axis=0, concat_axis=0, tiled=True)  15.3 us
    ppermute x7, waiting for transfers between devices, hop(): lax.ppermute(value, 'ctx', [(i, (i + 2 - 4 * (i % 2)) % total) for i in r...  10.4 us
  transfers between devices with their start and end apart: 23, of which 7 were waited for; matrix products, arithmetic and copies ran while one was open for 3% of the time, Pallas kernels for 28%

commit v1 on v0

v1 whole, which is shorter than its diff:
```python
import functools

import jax
import jax.numpy as jnp
from jax import lax
from jax.experimental import pallas as pl
from jax.experimental.pallas import tpu as pltpu
from jax.sharding import PartitionSpec as P

H = 12
HD = 128
VBLK = 128
ABLK = 24
TOWERS = 4
CHIPS = 8
LOCAL = H // TOWERS
GW = LOCAL * HD
NEG = -1e30
SCALE2 = HD**-0.5 * 1.4426950408889634
MIB = 1024 * 1024


def nt_dot(a, b):
    return lax.dot_general(a, b, (((1,), (1,)), ((), ())), preferred_element_type=jnp.float32)


def nn_dot(a, b):
    return jnp.dot(a, b, preferred_element_type=jnp.float32)


def full(shape):
    return pl.BlockSpec(shape, lambda *_: (0,) * len(shape))


ANY = pl.BlockSpec(memory_space=pl.ANY)


def start_copies(pairs, sem, first):
    copies = [pltpu.make_async_copy(a, b, sem.at[first + i]) for i, (a, b) in enumerate(pairs)]
    for copy in copies:
        copy.start()
    return copies


def pack_video_kernel(place, k_ref, v_ref, q_ref, w_ref, kv_out, q_out, self_out, rest_out, rows, w_rows, sem):
    half = w_ref.shape[3] // 2
    columns = pl.ds(pl.multiple_of(place[4] * half, 128), half)
    coming = start_copies([(ref, rows.at[i]) for i, ref in enumerate((k_ref, v_ref, q_ref))], sem, 0)
    coming += start_copies([(w_ref.at[:, :, :, columns], w_rows)], sem, 3)
    going = []
    for i in range(3):
        coming[i].wait()
        pairs = []
        for g in range(TOWERS):
            target = q_out.at[g] if i == 2 else kv_out.at[g, i]
            pairs.append((rows.at[i, :, pl.ds(g * GW, GW)], target))
        going += start_copies(pairs, sem, 4 + i * TOWERS)
    coming[3].wait()
    going += start_copies([(w_rows.at[0], self_out), (w_rows.at[pl.ds(1, 2)], rest_out)], sem, 16)
    for copy in going:
        copy.wait()


def pack_video(place, k, v, q, w):
    rows = k.shape[0]
    narrow = (LOCAL, w.shape[2], w.shape[3] // 2)
    shapes = [(TOWERS, 2, rows, GW), (TOWERS, rows, GW), narrow, (2,) + narrow]
    return pl.pallas_call(
        pack_video_kernel,
        out_shape=[jax.ShapeDtypeStruct(shape, jnp.bfloat16) for shape in shapes],
        grid_spec=pltpu.PrefetchScalarGridSpec(
            num_scalar_prefetch=1,
            grid=(1,),
            in_specs=[ANY] * 4,
            out_specs=[ANY] * 4,
            scratch_shapes=[
                pltpu.VMEM((3,) + k.shape, jnp.bfloat16),
                pltpu.VMEM((3,) + narrow, jnp.bfloat16),
                pltpu.SemaphoreType.DMA((18,)),
            ],
        ),
        compiler_params=pltpu.CompilerParams(vmem_limit_bytes=60 * MIB),
        name="pack_video",
    )(place, k, v, q, w)


WIN = 192
HALO = 48
QROWS = 96
QAT = 2 * WIN
HAT = QAT + QROWS
AROWS = HAT + 2 * HALO


def main_first(ctx):
    return jnp.clip(lax.rem(ctx, 4) * QROWS - HALO, 0, 384 - WIN)


def edge_tower(ctx):
    return jnp.clip(jnp.where(lax.rem(ctx, 4) == 0, ctx // 4 - 1, ctx // 4 + 1), 0, TOWERS - 1)


def pack_audio_kernel(place, q_ref, k_ref, v_ref, out, rows, sem):
    ctx = place[0]
    phase = lax.rem(ctx, 4)
    main = pl.ds(pl.multiple_of(main_first(ctx), 16), WIN)
    mine = pl.ds(pl.multiple_of(phase * QROWS, 16), QROWS)
    halo = pl.ds(pl.multiple_of(jnp.where(phase == 0, 384 - HALO, 0), 16), HALO)
    coming = start_copies(
        [
            (k_ref.at[main], rows.at[pl.ds(0, WIN)]),
            (v_ref.at[main], rows.at[pl.ds(WIN, WIN)]),
            (q_ref.at[mine], rows.at[pl.ds(QAT, QROWS)]),
            (k_ref.at[halo], rows.at[pl.ds(HAT, HALO)]),
            (v_ref.at[halo], rows.at[pl.ds(HAT + HALO, HALO)]),
        ],
        sem,
        0,
    )
    for copy in coming:
        copy.wait()
    going = start_copies(
        [(rows.at[:, pl.ds(g * GW, GW)], out.at[g]) for g in range(TOWERS)], sem, 5
    )
    for copy in going:
        copy.wait()


def pack_audio(place, q, k, v):
    return pl.pallas_call(
        pack_audio_kernel,
        out_shape=jax.ShapeDtypeStruct((TOWERS, AROWS, GW), jnp.bfloat16),
        grid_spec=pltpu.PrefetchScalarGridSpec(
            num_scalar_prefetch=1,
            grid=(1,),
            in_specs=[ANY] * 3,
            out_specs=ANY,
            scratch_shapes=[
                pltpu.VMEM((AROWS, q.shape[1]), jnp.bfloat16),
                pltpu.SemaphoreType.DMA((9,)),
            ],
        ),
        compiler_params=pltpu.CompilerParams(vmem_limit_bytes=60 * MIB),
        name="pack_audio",
    )(place, q, k, v)


def rows_of(kv_ref, which):
    return jnp.concatenate([kv_ref[r, which] for r in range(TOWERS)], axis=0)


def flash_kernel(kv_count, first, last, *refs):
    q_ref = refs[0]
    kv_refs = refs[1 : 1 + kv_count]
    rest = refs[1 + kv_count :]
    if first:
        outs = rest
    else:
        acc_in, stat_in = rest[:2]
        outs = rest[2:]
    size = TOWERS * VBLK
    scaled = q_ref[...].astype(jnp.float32) * SCALE2
    high = scaled.astype(jnp.bfloat16)
    low = (scaled - high.astype(jnp.float32)).astype(jnp.bfloat16)
    query = jnp.concatenate([high, low], axis=1)
    scores = []
    for kv in kv_refs:
        keys = rows_of(kv, 0)
        scores.append(nt_dot(query, jnp.concatenate([keys, keys], axis=1)))
    top = functools.reduce(jnp.maximum, [jnp.max(s, axis=1, keepdims=True) for s in scores])
    if not first:
        stat = stat_in[...]
        old_top, old_total = stat[:, 0:1], stat[:, 64:65]
        top = jnp.maximum(top, old_top)
        factor = jnp.exp2(old_top - top)
    acc = None
    for s, kv in zip(scores, kv_refs):
        weights = jnp.exp2(s - top).astype(jnp.bfloat16)
        values = rows_of(kv, 1)
        part = nn_dot(weights, jnp.concatenate([values, jnp.ones_like(values)], axis=1))
        acc = part if acc is None else acc + part
    acc, total = acc[:, :HD], acc[:, HD:]
    if not first:
        total = total + old_total * factor
        acc = acc + acc_in[...] * factor
    if last:
        outs[0][...] = (acc / total).astype(jnp.bfloat16)
    else:
        outs[0][...] = acc
        lane = lax.broadcasted_iota(jnp.int32, (size, HD), 1)
        outs[1][...] = jnp.where(lane < 64, top, total)
        outs[2][...] = total[:8]


def flash(query, kvs, state, last):
    rows = TOWERS * VBLK
    keys = rows * len(kvs)
    wide = jax.ShapeDtypeStruct((rows, GW), jnp.float32)
    head = pl.BlockSpec((rows, HD), lambda h: (0, h))
    if last:
        out_shape = jax.ShapeDtypeStruct((rows, GW), jnp.bfloat16)
        out_specs = head
    else:
        out_shape = [wide, wide, jax.ShapeDtypeStruct((8, HD), jnp.float32)]
        out_specs = [head, head, pl.BlockSpec((8, HD), lambda h: (0, 0))]
    shard = pl.BlockSpec((TOWERS, 2, VBLK, HD), lambda h: (0, 0, 0, h))
    return pl.pallas_call(
        functools.partial(flash_kernel, len(kvs), state is None, last),
        out_shape=out_shape,
        grid=(LOCAL,),
        in_specs=[head] + [shard] * len(kvs) + ([] if state is None else [head, head]),
        out_specs=out_specs,
        compiler_params=pltpu.CompilerParams(vmem_limit_bytes=60 * MIB),
        cost_estimate=pl.CostEstimate(
            flops=8 * rows * keys * GW,
            bytes_accessed=4 * keys * GW + 16 * rows * GW,
            transcendentals=rows * keys * LOCAL,
        ),
        name="flash",
    )(query, *kvs, *(() if state is None else state[:2]))


AUDIO_ROWS = 32
BOTH = VBLK + AUDIO_ROWS


def audio_rows(place, margin, audio, own, sibling, third):
    ctx = place[0]
    core = lax.rem(ctx, 2)
    row_block = lax.broadcasted_iota(jnp.int32, (QROWS, 1), 0) // ABLK + ctx * 4
    query = audio[0, pl.ds(QAT, QROWS), :]
    pieces = [(own, r, ctx * 4 + r) for r in range(TOWERS)]
    after = lax.rem(ctx + 1, 16) * 4
    before = lax.rem(ctx + 15, 16) * 4 + 2
    for r in range(2):
        pieces.append((sibling, 2 * core + r, jnp.where(core == 0, after, before) + r))
        pieces.append((third, 2 - 2 * core + r, jnp.where(core == 0, before, after) + r))
    keys = jnp.concatenate([ref[r, 0] for ref, r, _ in pieces], axis=0)
    values = jnp.concatenate([ref[r, 1] for ref, r, _ in pieces], axis=0)
    raw = nt_dot(query, keys) * SCALE2
    scores = []
    for i, (_, _, block) in enumerate(pieces):
        hit = (
            (row_block == margin[block, 0])
            | (row_block == margin[block, 1])
            | (row_block == margin[block, 2])
        )
        scores.append(jnp.where(hit, raw[:, i * VBLK : (i + 1) * VBLK], NEG))
    scores = jnp.concatenate(scores, axis=1)
    weights = jnp.exp2(scores - jnp.max(scores, axis=1, keepdims=True))
    total = jnp.sum(weights, axis=1, keepdims=True)
    return nn_dot(weights.astype(jnp.bfloat16), values) / total


def cross_kernel(place, margin, q_ref, main, edge, own, sibling, third, out):
    ctx = place[0]
    phase = lax.rem(ctx, 4)
    base = (ctx - phase) * 4
    lane = lax.broadcasted_iota(jnp.int32, (1, 256), 1)
    halo_base = jnp.where(phase == 0, base - 2, jnp.where(phase == 3, base + 16, -100))
    main_base = base + lax.div(main_first(ctx), ABLK)
    ids = jnp.where(lane < WIN, lane // ABLK + main_base, lane // ABLK - WIN // ABLK + halo_base)
    ids = jnp.where(lane < WIN + HALO, ids, -100)
    spare = jnp.zeros((256 - WIN - HALO, HD), jnp.bfloat16)
    keys = jnp.concatenate([main[0, pl.ds(0, WIN), :], edge[0, pl.ds(HAT, HALO), :], spare], axis=0)
    values = jnp.concatenate(
        [main[0, pl.ds(WIN, WIN), :], edge[0, pl.ds(HAT + HALO, HALO), :], spare], axis=0
    )
    scores = nt_dot(q_ref[...], keys) * SCALE2
    parts = []
    for r in range(TOWERS):
        block = ctx * 4 + r
        hit = (ids == margin[block, 0]) | (ids == margin[block, 1]) | (ids == margin[block, 2])
        parts.append(jnp.where(hit, scores[r * VBLK : (r + 1) * VBLK], NEG))
    scores = jnp.concatenate(parts, axis=0)
    weights = jnp.exp2(scores - jnp.max(scores, axis=1, keepdims=True))
    total = jnp.sum(weights, axis=1, keepdims=True)
    result = (nn_dot(weights.astype(jnp.bfloat16), values) / total).astype(jnp.bfloat16)
    mixed = audio_rows(place, margin, main, own, sibling, third)
    for r in range(TOWERS):
        out[r, pl.ds(0, VBLK), :] = result[r * VBLK : (r + 1) * VBLK]
        padded = jnp.concatenate(
            [mixed[r * ABLK : (r + 1) * ABLK], jnp.zeros((AUDIO_ROWS - ABLK, HD), jnp.float32)], axis=0
        )
        out[r, pl.ds(VBLK, AUDIO_ROWS), :] = padded.astype(jnp.bfloat16)


def cross(place, margin, query, audio, own, sibling, third):
    rows = query.shape[0]
    shard = pl.BlockSpec((TOWERS, 2, VBLK, HD), lambda h, *_: (0, 0, 0, h))
    return pl.pallas_call(
        cross_kernel,
        out_shape=jax.ShapeDtypeStruct((TOWERS, BOTH, GW), jnp.bfloat16),
        grid_spec=pltpu.PrefetchScalarGridSpec(
            num_scalar_prefetch=2,
            grid=(LOCAL,),
            in_specs=[
                pl.BlockSpec((rows, HD), lambda h, *_: (0, h)),
                pl.BlockSpec((1, AROWS, HD), lambda h, place, margin: (place[2], 0, h)),
                pl.BlockSpec((1, AROWS, HD), lambda h, place, margin: (place[3], 0, h)),
                shard,
                shard,
                shard,
            ],
            out_specs=pl.BlockSpec((TOWERS, BOTH, HD), lambda h, *_: (0, 0, h)),
        ),
        compiler_params=pltpu.CompilerParams(vmem_limit_bytes=60 * MIB),
        cost_estimate=pl.CostEstimate(
            flops=8 * rows * 1024 * GW, bytes_accessed=4 * MIB, transcendentals=rows * 512 * 3
        ),
        name="cross",
    )(place, margin, query, audio, audio, own, sibling, third)


def weight_rows(pieces):
    return jnp.concatenate([piece(h) for h in range(LOCAL) for piece in pieces], axis=0)


def project_cross_kernel(place, own, sibling, w_ref, *outs):
    towers = [lax.rem(place[1] + step, TOWERS) for step in range(TOWERS)]
    pairs = [(step, ref) for step in range(TOWERS) for ref in (own, sibling)]
    for kind, (first, count) in enumerate(((0, VBLK), (VBLK, AUDIO_ROWS))):
        w = weight_rows([functools.partial(lambda b, h: w_ref[b, kind, h], b) for b in range(4)])
        a = jnp.concatenate([ref[towers[step], pl.ds(first, count), :] for step, ref in pairs], axis=0)
        y = nn_dot(a, w).astype(jnp.bfloat16)
        for i, (step, ref) in enumerate(pairs):
            at = first + (BOTH if ref is sibling else 0)
            outs[step][pl.ds(at, count), :] = y[i * count : (i + 1) * count]


def project_cross(place, own, sibling, w):
    width = w.shape[-1]
    tile = width // 3
    return pl.pallas_call(
        project_cross_kernel,
        out_shape=[jax.ShapeDtypeStruct((2 * BOTH, width), jnp.bfloat16)] * TOWERS,
        grid_spec=pltpu.PrefetchScalarGridSpec(
            num_scalar_prefetch=1,
            grid=(3,),
            in_specs=[
                full(own.shape),
                full(own.shape),
                pl.BlockSpec(w.shape[:-1] + (tile,), lambda i, place: (0, 0, 0, 0, i)),
            ],
            out_specs=[pl.BlockSpec((2 * BOTH, tile), lambda i, place: (0, i))] * TOWERS,
        ),
        compiler_params=pltpu.CompilerParams(vmem_limit_bytes=60 * MIB),
        cost_estimate=pl.CostEstimate(
            flops=2 * 1280 * GW * width, bytes_accessed=8 * MIB, transcendentals=0
        ),
        name="project_cross",
    )(place, own, sibling, w)


def project_self_kernel(place, own, sibling, w_ref, *refs):
    base_refs, (gain, own_out, sibling_out) = refs[:TOWERS], refs[TOWERS:]
    a = jnp.concatenate(
        [jnp.concatenate([ref[t] for t in range(TOWERS)], axis=1) for ref in (own, sibling)], axis=0
    )
    w = jnp.concatenate(
        [
            weight_rows([functools.partial(lambda b, h: w_ref[b * TOWERS + t, h], b) for b in range(4)])
            for t in range(TOWERS)
        ],
        axis=0,
    )
    acc = nn_dot(a, w)
    base = functools.reduce(jnp.add, [ref[...].astype(jnp.float32) for ref in base_refs])
    for i, out in enumerate((own_out, sibling_out)):
        video = acc[i * VBLK : (i + 1) * VBLK] + base[i * BOTH : i * BOTH + VBLK]
        audio = base[i * BOTH + VBLK : (i + 1) * BOTH]
        out[pl.ds(0, VBLK), :] = (gain[0:1] * video).astype(jnp.bfloat16)
        out[pl.ds(VBLK, AUDIO_ROWS), :] = (gain[1:2] * audio).astype(jnp.bfloat16)


def project_self(place, own, sibling, w, base, gains):
    width = w.shape[-1]
    tile = width // 3
    rows = pl.BlockSpec((BOTH, tile), lambda i, place: (0, i))
    return pl.pallas_call(
        project_self_kernel,
        out_shape=[jax.ShapeDtypeStruct((BOTH, width), jnp.bfloat16)] * 2,
        grid_spec=pltpu.PrefetchScalarGridSpec(
            num_scalar_prefetch=1,
            grid=(3,),
            in_specs=[
                full(own.shape),
                full(own.shape),
                pl.BlockSpec(w.shape[:-1] + (tile,), lambda i, place: (0, 0, 0, i)),
            ]
            + [pl.BlockSpec((2 * BOTH, tile), lambda i, place: (0, i))] * TOWERS
            + [pl.BlockSpec((2, tile), lambda i, place: (0, place[4] * 3 + i))],
            out_specs=[rows] * 2,
        ),
        compiler_params=pltpu.CompilerParams(vmem_limit_bytes=60 * MIB),
        cost_estimate=pl.CostEstimate(
            flops=4 * VBLK * 1536 * width, bytes_accessed=10 * MIB, transcendentals=0
        ),
        name="project_self",
    )(place, own, sibling, w, *base, gains)


def gate_kernel(*refs):
    pass


def gate(value, *after):
    return pl.pallas_call(
        gate_kernel,
        out_shape=jax.ShapeDtypeStruct(value.shape, value.dtype),
        in_specs=[ANY] * (1 + len(after)),
        out_specs=ANY,
        input_output_aliases={0: 0},
        compiler_params=pltpu.CompilerParams(vmem_limit_bytes=60 * MIB),
        name="gate",
    )(value, *after)


def exchange_towers(value):
    return lax.all_to_all(value, "tower", split_axis=0, concat_axis=0, tiled=True)


def shift_tower(value, step):
    return lax.ppermute(value, "tower", [(i, (i + step) % TOWERS) for i in range(TOWERS)])


def hop(value):
    total = 2 * CHIPS
    return lax.ppermute(value, "ctx", [(i, (i + 2 - 4 * (i % 2)) % total) for i in range(total)])


def swap_core(value):
    return lax.ppermute(value, "ctx", [(i, i ^ 1) for i in range(2 * CHIPS)])


def shards(video_q, video_k, video_v, audio_q, audio_k, audio_v, margin, out_weight, gate_gains):
    ctx = lax.axis_index("ctx")
    tower = lax.axis_index("tower")
    core = lax.rem(ctx, 2)
    place = jnp.stack([ctx, tower, ctx // 4, edge_tower(ctx), core]).astype(jnp.int32)
    gains = gate_gains[0]
    margins = margin[0]

    kv_parts, q_parts, w_self, w_rest = pack_video(
        place, video_k[0], video_v[0], video_q[0], out_weight
    )
    w_rest = lax.all_gather(w_rest, "batch", axis=0, tiled=False)
    w_self = lax.all_gather(w_self, ("batch", "tower"), axis=0, tiled=False)
    own = exchange_towers(kv_parts)
    sibling = swap_core(own)
    near, far = hop(own), hop(sibling)
    third = far

    query = exchange_towers(q_parts).reshape(TOWERS * VBLK, GW)
    audio = exchange_towers(pack_audio(place, audio_q[0], audio_k[0], audio_v[0]))
    state = flash(query, [own, sibling], None, False)
    started = state[2]

    for step in range(1, 4):
        now = [near, far, swap_core(near), swap_core(far)]
        near, far = hop(near), (hop(far) if step < 3 else None)
        state = flash(query, now, state, False)
        if step == 1:
            near = gate(near, started)
            audio = gate(audio, state[2])
        if step == 2:
            crossed = cross(place, margins, query, audio, own, sibling, third)
            parts = project_cross(place, crossed, swap_core(crossed), w_rest)
            base = [parts[0]] + [shift_tower(parts[i], i) for i in (1, 2, 3)]
            near = gate(near, state[2], parts[0])
    video_self = flash(query, [near, swap_core(near)], state, True)
    self_all = exchange_towers(video_self.reshape(TOWERS, VBLK, GW))
    mine, theirs = project_self(place, self_all, swap_core(self_all), w_self, base, gains)
    theirs = swap_core(theirs)
    outs = []
    for first, count in ((0, VBLK), (VBLK, ABLK)):
        a, b = mine[first : first + count], theirs[first : first + count]
        outs.append(
            jnp.where(core == 0, jnp.concatenate([a, b], axis=1), jnp.concatenate([b, a], axis=1))[None]
        )
    return tuple(outs)


def solution(mesh):
    return jax.shard_map(
        shards,
        mesh=mesh,
        in_specs=(
            P("batch", ("ctx", "tower"), None),
            P("batch", ("ctx", "tower"), None),
            P("batch", ("ctx", "tower"), None),
            P("batch", "tower", None),
            P("batch", "tower", None),
            P("batch", "tower", None),
            P("batch", None, None),
            P(None, "tower", "batch", None),
            P("batch", None, None),
        ),
        out_specs=(P("batch", ("ctx", "tower"), None), P("batch", ("ctx", "tower"), None)),
        check_vma=False,
    )
```

time: 233 us -> 201 us (0.86); the launches traced: 230 us -> 200 us
  waiting for transfers between devices: 65.3 us -> 21.1 us
  blocking collectives: 15.3 us -> 42.2 us
  starting transfers between devices: 44.4 us -> 38.7 us
  matrix products: 3.18 us -> 0 us
    all_to_all x5 -> x2, waiting for transfers between devices: 35.1 us -> 2.75 us  [exchange_towers(): lax.all_to_all(value, 'tower', split_axis=0, concat_axis=0, tiled=True)]
    all_to_all x1 -> x2, blocking collectives: 15.3 us -> 42.2 us  [exchange_towers(): lax.all_to_all(value, 'tower', split_axis=0, concat_axis=0, tiled=True)]
    all_gather x2, waiting for transfers between devices: 16.9 us -> 0.01 us  [the longest x1 0.01 us: shards(): w_rest = lax.all_gather(w_rest, 'batch', axis=0, tiled=False)]
    all_to_all x5 -> x2, starting transfers between devices: 19.2 us -> 7.04 us  [exchange_towers(): lax.all_to_all(value, 'tower', split_axis=0, concat_axis=0, tiled=True)]
    pallas_call x5, Pallas kernels: 37.4 us -> 46.2 us  [flash(): pl.pallas_call(functools.partial(flash_kernel, len(kvs), state is None, l...]
    pallas_call x5 -> x4, Pallas kernels: 31.3 us -> 23.2 us  [the longest x1 6.91 us: project_self(): pl.pallas_call(project_self_kernel, out_shape=[jax.ShapeDtypeStruct((BOTH...]
    ppermute x7, waiting for transfers between devices: 10.4 us -> 16.2 us  [hop(): lax.ppermute(value, 'ctx', [(i, (i + 2 - 4 * (i % 2)) % total) for i in r...]
    ppermute x0 -> x3, starting transfers between devices: none -> 5.43 us  [shift_tower(): lax.ppermute(value, 'tower', [(i, (i + step) % TOWERS) for i in range(TOW...]
  transfers between devices with their start and end apart: 23 -> 25, of which waited for: 7 -> 5; matrix products, arithmetic and copies ran while one was open for 3% -> 1% of each run, Pallas kernels for 28% -> 31%
where the time goes in v1:
time: 201 us; the launch traced here: 200 us
  Pallas kernels  72.9 us (36%)
  blocking collectives  42.2 us (21%)
  starting transfers between devices  38.7 us (19%)
  waiting for transfers between devices  21.1 us (10%)
  between operations  14.3 us (7%)
  local copies, waits for them, and re-layouts  9.28 us (5%)
    pallas_call x5, Pallas kernels, flash(): pl.pallas_call(functools.partial(flash_kernel, len(kvs), state is None, l...  46.2 us
    all_to_all x2, blocking collectives, exchange_towers(): lax.all_to_all(value, 'tower', split_axis=0, concat_axis=0, tiled=True)  42.2 us
    ppermute x7, waiting for transfers between devices, hop(): lax.ppermute(value, 'ctx', [(i, (i + 2 - 4 * (i % 2)) % total) for i in r...  16.2 us
    ppermute x7, starting transfers between devices, hop(): lax.ppermute(value, 'ctx', [(i, (i + 2 - 4 * (i % 2)) % total) for i in r...  15.8 us
    ppermute x11, starting transfers between devices, swap_core(): return lax.ppermute(value, 'ctx', [(i, i ^ 1) for i in range(2 * CHIPS)])  10.4 us
    all_to_all x2, starting transfers between devices, exchange_towers(): lax.all_to_all(value, 'tower', split_axis=0, concat_axis=0, tiled=True)  7.04 us
    pallas_call x1, Pallas kernels, project_self(): pl.pallas_call(project_self_kernel, out_shape=[jax.ShapeDtypeStruct((BOTH...  6.91 us
    unnamed x29, local copies, waits for them, and re-layouts  6.76 us
  transfers between devices with their start and end apart: 25, of which 5 were waited for; matrix products, arithmetic and copies ran while one was open for 1% of the time, Pallas kernels for 31%

profile of v1, /device:TPU:1, one launch (start us, length us, event | category | flops | bytes accessed | tf_op | source)
XLA Modules:
  0.0 200.2 jit_solution(16712539135926359872)
XLA Ops:
  7.8 3.3 %pack_video.1 = (bf16[4,2,128,384]{3,2,1,0:T(8,128)(2,1)}, bf16[4,128,384]{2,1,0:T(8,128)(2,1)}, bf16[3,32,1536]{2,1,0:T(8,128)(2,1)}, bf16[2,3,32,1536]{3,2,1,0:T(8,128)(2,1)}) custom-call(s32[5]{0:T(128)} %stack.23.place, bf16[128,1536]{1,0:T(8,128)(2,1)} %bitcast.35, bf16[128,1536]{1,0:T(8,128)(2,1)} %bitcast.36, bf16[128,1536]{1,0:T(8,128)(2,1)} %bitcast.37, ...), custom_call_target="tpu_custom_call" | custom-call | tf_op jit(solution)/shard_map/pack_video/pallas_call | solution.py:68
  11.9 15.3 %all_to_all.20.refs_1_.own = bf16[4,2,128,384]{3,2,1,0:T(8,128)(2,1)S(1)} all-to-all(bf16[4,2,128,384]{3,2,1,0:T(8,128)(2,1)} %get-tuple-element.24), channel_id=1, replica_groups=mesh['batch'=4,'ctx'=16,'tower'=4] {'tower'}, dimensions={0} | all-to-all | bytes 1572864 | tf_op jit(solution)/shard_map/all_to_all | solution.py:420
  27.2 2.8 %collective-permute-start.2 = (bf16[4,2,128,384]{3,2,1,0:T(8,128)(2,1)S(1)}, bf16[4,2,128,384]{3,2,1,0:T(8,128)(2,1)}, u32[]{:S(2)}, u32[]{:S(2)}) collective-permute-start(bf16[4,2,128,384]{3,2,1,0:T(8,128)(2,1)S(1)} %all_to_all.20.refs_1_.own), channel_id=1, source_target_pairs={{0,4},{4,0},{8,12},{12,8},{16,20},{20,16},{24,28},{28,24},{32,36},... | collective-permute-start | bytes 2359304 | tf_op jit(solution)/shard_map/ppermute | solution.py:433
  30.0 5.6 %collective-permute-start = (bf16[4,2,128,384]{3,2,1,0:T(8,128)(2,1)S(1)}, bf16[4,2,128,384]{3,2,1,0:T(8,128)(2,1)}, u32[]{:S(2)}, u32[]{:S(2)}) collective-permute-start(bf16[4,2,128,384]{3,2,1,0:T(8,128)(2,1)S(1)} %all_to_all.20.refs_1_.own), channel_id=1, source_target_pairs={{0,8},{4,60},{8,16},{12,4},{16,24},{20,12},{24,32},{28,20},{32,40}... | collective-permute-start | bytes 2359304 | tf_op jit(solution)/shard_map/ppermute | solution.py:429
  35.5 2.0 %collective-permute-start.4 = (bf16[4,2,128,384]{3,2,1,0:T(8,128)(2,1)}, bf16[4,2,128,384]{3,2,1,0:T(8,128)(2,1)}, u32[]{:S(2)}, u32[]{:S(2)}) collective-permute-start(bf16[4,2,128,384]{3,2,1,0:T(8,128)(2,1)} %collective-permute-done.2.refs_2_.sibling), channel_id=1, source_target_pairs={{0,8},{4,60},{8,16},{12,4},{16,24},{20,12},{24,32},{28,20},{32,40}... | collective-permute-start | bytes 2359304 | tf_op jit(solution)/shard_map/ppermute | solution.py:429
  37.6 3.5 %all-to-all-start = ((bf16[4,128,384]{2,1,0:T(8,128)(2,1)}), bf16[4,128,384]{2,1,0:T(8,128)(2,1)S(1)}, u32[]{:S(2)}, u32[]{:S(2)}) async-start(bf16[4,128,384]{2,1,0:T(8,128)(2,1)} %get-tuple-element.23), calls=%async_computation | async-start | bytes 786432 | tf_op jit(solution)/shard_map/all_to_all | solution.py:420
  41.0 3.5 %pack_audio.1 = bf16[4,576,384]{2,1,0:T(8,128)(2,1)} custom-call(s32[5]{0:T(128)} %stack.23.place, bf16[384,1536]{1,0:T(8,128)(2,1)} %bitcast.32, bf16[384,1536]{1,0:T(8,128)(2,1)} %bitcast.33, bf16[384,1536]{1,0:T(8,128)(2,1)} %bitcast.34), custom_call_target="tpu_custom_call" | custom-call | tf_op jit(solution)/shard_map/pack_audio/pallas_call | solution.py:130
  44.5 2.7 %all-to-all-done = bf16[4,128,384]{2,1,0:T(8,128)(2,1)S(1)} async-done(((bf16[4,128,384]{2,1,0:T(8,128)(2,1)}), bf16[4,128,384]{2,1,0:T(8,128)(2,1)S(1)}, u32[]{:S(2)}, u32[]{:S(2)}) %all-to-all-start) | async-done | bytes 393248 | tf_op jit(solution)/shard_map/all_to_all | solution.py:420
  48.0 3.6 %all-to-all-start.2 = ((bf16[4,576,384]{2,1,0:T(8,128)(2,1)}), bf16[4,576,384]{2,1,0:T(8,128)(2,1)S(1)}, u32[]{:S(2)}, u32[]{:S(2)}) async-start(bf16[4,576,384]{2,1,0:T(8,128)(2,1)} %pack_audio.1), calls=%async_computation.2 | async-start | bytes 3538944 | tf_op jit(solution)/shard_map/all_to_all | solution.py:420
  51.6 3.1 %collective-permute-start.1 = (bf16[4,2,128,384]{3,2,1,0:T(8,128)(2,1)}, bf16[4,2,128,384]{3,2,1,0:T(8,128)(2,1)S(1)}, u32[]{:S(2)}, u32[]{:S(2)}) collective-permute-start(bf16[4,2,128,384]{3,2,1,0:T(8,128)(2,1)} %collective-permute-done.refs_1_), channel_id=1, source_target_pairs={{0,8},{4,60},{8,16},{12,4},{16,24},{20,12},{24,32},{28,20},{32,40}... | collective-permute-start | bytes 2359304 | tf_op jit(solution)/shard_map/ppermute | solution.py:429
  57.3 6.1 %flash.5 = (f32[512,384]{1,0:T(8,128)}, f32[512,384]{1,0:T(8,128)}, f32[8,128]{1,0:T(8,128)}) custom-call(bf16[512,384]{1,0:T(8,128)(2,1)} %bitcast.26, bf16[4,2,128,384]{3,2,1,0:T(8,128)(2,1)} %copy-done.1, bf16[4,2,128,384]{3,2,1,0:T(8,128)(2,1)} %collective-permute-done.2.refs_2_.sibling), custom_call_target="tpu_custom_call" | custom-call | flops 1610612736 | bytes 4718592 | tf_op jit(solution)/shard_map/flash/pallas_call | solution.py:207
  66.5 5.8 %collective-permute-done.5.refs_2_ = bf16[4,2,128,384]{3,2,1,0:T(8,128)(2,1)} collective-permute-done((bf16[4,2,128,384]{3,2,1,0:T(8,128)(2,1)}, bf16[4,2,128,384]{3,2,1,0:T(8,128)(2,1)}, u32[]{:S(2)}, u32[]{:S(2)}) %collective-permute-start.5) | collective-permute-done | bytes 786464 | tf_op jit(solution)/shard_map/ppermute | solution.py:429
  74.2 11.0 %flash.6 = (f32[512,384]{1,0:T(8,128)}, f32[512,384]{1,0:T(8,128)}, f32[8,128]{1,0:T(8,128)}) custom-call(bf16[512,384]{1,0:T(8,128)(2,1)} %bitcast.27, bf16[4,2,128,384]{3,2,1,0:T(8,128)(2,1)} %collective-permute-done.refs_1_, bf16[4,2,128,384]{3,2,1,0:T(8,128)(2,1)} %collective-permute-done.4.refs_2_.third, ...), custom_call_target="tpu_custom_call" | custom-call | flops 3221225472 | bytes 6291456 | tf_op jit(solution)/shard_map/flash/pallas_call | solution.py:207
  86.5 6.6 %cross.1.own = bf16[4,160,384]{2,1,0:T(8,128)(2,1)} custom-call(s32[5]{0:T(128)} %stack.23.place, s32[64,3]{1,0:T(8,128)} %bitcast.39, bf16[512,384]{1,0:T(8,128)(2,1)} %bitcast.28, bf16[4,576,384]{2,1,0:T(8,128)(2,1)} %gate.4.main.edge, bf16[4,576,384]{2,1,0:T(8,128)(2,1)} %gate.4.main.edge, bf16[4,2,128,384]{3,2,1,0:T(8,128)(2,1)} %copy-done.1, ...), custom_call_target="tpu_custom_call" | custom-call | flops 1610612736 | bytes 4194304 | tf_op jit(solution)/shard_map/cross/pallas_call | solution.py:291
  93.0 2.0 collective-permute-start.3
  95.6 6.5 %project_cross.1 = (bf16[320,1536]{1,0:T(8,128)(2,1)}, bf16[320,1536]{1,0:T(8,128)(2,1)}, bf16[320,1536]{1,0:T(8,128)(2,1)}, bf16[320,1536]{1,0:T(8,128)(2,1)}) custom-call(s32[5]{0:T(128)} %stack.23.place, bf16[4,160,384]{2,1,0:T(8,128)(2,1)} %cross.1.own, bf16[4,160,384]{2,1,0:T(8,128)(2,1)} %collective-permute-done.10.sibling, ...), custom_call_target="tpu_custom_call" | custom-call | flops 1509949440 | bytes 8388608 | tf_op jit(solution)/shard_map/project_cross/pallas_call | solution.py:334
  103.3 10.9 %flash.7 = (f32[512,384]{1,0:T(8,128)}, f32[512,384]{1,0:T(8,128)}, f32[8,128]{1,0:T(8,128)}) custom-call(bf16[512,384]{1,0:T(8,128)(2,1)} %bitcast.29, bf16[4,2,128,384]{3,2,1,0:T(8,128)(2,1)} %gate.3.refs_1_, bf16[4,2,128,384]{3,2,1,0:T(8,128)(2,1)} %collective-permute-done.5.refs_2_, bf16[4,2,128,384]{3,2,1,0:T(8,128)(2,1)} %copy-done.11, ...), custom_call_target="tpu_custom_call" | custom-call | flops 3221225472 | bytes 6291456 | tf_op jit(solution)/shard_map/flash/pallas_call | solution.py:207
  116.7 9.8 %collective-permute-done.11.refs_1_ = bf16[4,2,128,384]{3,2,1,0:T(8,128)(2,1)} collective-permute-done((bf16[4,2,128,384]{3,2,1,0:T(8,128)(2,1)}, bf16[4,2,128,384]{3,2,1,0:T(8,128)(2,1)}, u32[]{:S(2)}, u32[]{:S(2)}) %collective-permute-start.11) | collective-permute-done | bytes 786464 | tf_op jit(solution)/shard_map/ppermute | solution.py:429
  128.3 1.9 collective-permute-start.17
  130.2 2.4 %collective-permute-start.18 = (bf16[320,1536]{1,0:T(8,128)(2,1)}, bf16[320,1536]{1,0:T(8,128)(2,1)S(1)}, u32[]{:S(2)}, u32[]{:S(2)}) collective-permute-start(bf16[320,1536]{1,0:T(8,128)(2,1)} %get-tuple-element.40), channel_id=1, source_target_pairs={{0,2},{1,3},{2,0},{3,1},{4,6},{5,7},{6,4},{7,5},{8,10},{9,11},{10,... | collective-permute-start | bytes 2949128 | tf_op jit(solution)/shard_map/ppermute | solution.py:424
  134.7 11.0 %flash.8 = (f32[512,384]{1,0:T(8,128)}, f32[512,384]{1,0:T(8,128)}, f32[8,128]{1,0:T(8,128)}) custom-call(bf16[512,384]{1,0:T(8,128)(2,1)} %bitcast.30, bf16[4,2,128,384]{3,2,1,0:T(8,128)(2,1)} %gate.5.refs_1_, bf16[4,2,128,384]{3,2,1,0:T(8,128)(2,1)} %collective-permute-done.13.refs_2_, bf16[4,2,128,384]{3,2,1,0:T(8,128)(2,1)} %copy-done.13, ...), custom_call_target="tpu_custom_call" | custom-call | flops 3221225472 | bytes 6291456 | tf_op jit(solution)/shard_map/flash/pallas_call | solution.py:207
  145.6 7.3 %flash.9 = bf16[512,384]{1,0:T(8,128)(2,1)} custom-call(bf16[512,384]{1,0:T(8,128)(2,1)} %bitcast.31, bf16[4,2,128,384]{3,2,1,0:T(8,128)(2,1)} %collective-permute-done.11.refs_1_, bf16[4,2,128,384]{3,2,1,0:T(8,128)(2,1)} %collective-permute-done.12.refs_2_, f32[512,384]{1,0:T(8,128)} %get-tuple-element.36.refs_3_, f32[512,384]{1,0:T(8,128)} %get-tuple-element.37.refs_4_), custom_call_target="tpu_custom_call" | custom-call | flops 1610612736 | bytes 4718592 | tf_op jit(solution)/shard_map/flash/pallas_call | solution.py:207
  153.0 26.9 %all_to_all.21.own = bf16[4,128,384]{2,1,0:T(8,128)(2,1)S(1)} all-to-all(bf16[4,128,384]{2,1,0:T(8,128)(2,1)} %bitcast.38), channel_id=1, replica_groups=mesh['batch'=4,'ctx'=16,'tower'=4] {'tower'}, dimensions={0} | all-to-all | bytes 786432 | tf_op jit(solution)/shard_map/all_to_all | solution.py:420
  182.5 6.9 %project_self.1 = (bf16[160,1536]{1,0:T(8,128)(2,1)}, bf16[160,1536]{1,0:T(8,128)(2,1)}) custom-call(s32[5]{0:T(128)} %stack.23.place, bf16[4,128,384]{2,1,0:T(8,128)(2,1)} %copy-done.2, bf16[4,128,384]{2,1,0:T(8,128)(2,1)} %collective-permute-done.16.sibling, bf16[16,3,32,1536]{3,2,1,0:T(8,128)(2,1)} %bitcast.25, ...), custom_call_target="tpu_custom_call" | custom-call | flops 1207959552 | bytes 10485760 | tf_op jit(solution)/shard_map/project_self/pallas_call | solution.py:380
  (79 shorter events, 25.8 us)
Async XLA Ops:
  7.2 88.5 %all-gather.5.cloned.1.call-start = ((), (), s32[]{:S(2)}) async-start(), calls=%async_computation.4 | async-start | bytes 2949120 | tf_op jit(solution)/shard_map/all_gather | solution.py:447
  11.1 171.2 %all-gather.7.cloned.1.call-start = ((), (), s32[]{:S(2)}) async-start(), calls=%async_computation.5 | async-start | bytes 5013504 | tf_op jit(solution)/shard_map/all_gather | solution.py:448
  27.2 8.4 %collective-permute-start.2 = (bf16[4,2,128,384]{3,2,1,0:T(8,128)(2,1)S(1)}, bf16[4,2,128,384]{3,2,1,0:T(8,128)(2,1)}, u32[]{:S(2)}, u32[]{:S(2)}) collective-permute-start(bf16[4,2,128,384]{3,2,1,0:T(8,128)(2,1)S(1)} %all_to_all.20.refs_1_.own), channel_id=1, source_target_pairs={{0,4},{4,0},{8,12},{12,8},{16,20},{20,16},{24,28},{28,24},{32,36},... | collective-permute-start | bytes 2359304 | tf_op jit(solution)/shard_map/ppermute | solution.py:433
  30.0 21.7 %collective-permute-start = (bf16[4,2,128,384]{3,2,1,0:T(8,128)(2,1)S(1)}, bf16[4,2,128,384]{3,2,1,0:T(8,128)(2,1)}, u32[]{:S(2)}, u32[]{:S(2)}) collective-permute-start(bf16[4,2,128,384]{3,2,1,0:T(8,128)(2,1)S(1)} %all_to_all.20.refs_1_.own), channel_id=1, source_target_pairs={{0,8},{4,60},{8,16},{12,4},{16,24},{20,12},{24,32},{28,20},{32,40}... | collective-permute-start | bytes 2359304 | tf_op jit(solution)/shard_map/ppermute | solution.py:429
  35.5 19.2 %collective-permute-start.4 = (bf16[4,2,128,384]{3,2,1,0:T(8,128)(2,1)}, bf16[4,2,128,384]{3,2,1,0:T(8,128)(2,1)}, u32[]{:S(2)}, u32[]{:S(2)}) collective-permute-start(bf16[4,2,128,384]{3,2,1,0:T(8,128)(2,1)} %collective-permute-done.2.refs_2_.sibling), channel_id=1, source_target_pairs={{0,8},{4,60},{8,16},{12,4},{16,24},{20,12},{24,32},{28,20},{32,40}... | collective-permute-start | bytes 2359304 | tf_op jit(solution)/shard_map/ppermute | solution.py:429
  37.6 9.7 %all-to-all-start = ((bf16[4,128,384]{2,1,0:T(8,128)(2,1)}), bf16[4,128,384]{2,1,0:T(8,128)(2,1)S(1)}, u32[]{:S(2)}, u32[]{:S(2)}) async-start(bf16[4,128,384]{2,1,0:T(8,128)(2,1)} %get-tuple-element.23), calls=%async_computation | async-start | bytes 786432 | tf_op jit(solution)/shard_map/all_to_all | solution.py:420
  48.0 37.1 %all-to-all-start.2 = ((bf16[4,576,384]{2,1,0:T(8,128)(2,1)}), bf16[4,576,384]{2,1,0:T(8,128)(2,1)S(1)}, u32[]{:S(2)}, u32[]{:S(2)}) async-start(bf16[4,576,384]{2,1,0:T(8,128)(2,1)} %pack_audio.1), calls=%async_computation.2 | async-start | bytes 3538944 | tf_op jit(solution)/shard_map/all_to_all | solution.py:420
  51.6 12.3 %collective-permute-start.1 = (bf16[4,2,128,384]{3,2,1,0:T(8,128)(2,1)}, bf16[4,2,128,384]{3,2,1,0:T(8,128)(2,1)S(1)}, u32[]{:S(2)}, u32[]{:S(2)}) collective-permute-start(bf16[4,2,128,384]{3,2,1,0:T(8,128)(2,1)} %collective-permute-done.refs_1_), channel_id=1, source_target_pairs={{0,8},{4,60},{8,16},{12,4},{16,24},{20,12},{24,32},{28,20},{32,40}... | collective-permute-start | bytes 2359304 | tf_op jit(solution)/shard_map/ppermute | solution.py:429
  54.7 17.7 %collective-permute-start.5 = (bf16[4,2,128,384]{3,2,1,0:T(8,128)(2,1)}, bf16[4,2,128,384]{3,2,1,0:T(8,128)(2,1)}, u32[]{:S(2)}, u32[]{:S(2)}) collective-permute-start(bf16[4,2,128,384]{3,2,1,0:T(8,128)(2,1)} %collective-permute-done.4.refs_2_.third), channel_id=1, source_target_pairs={{0,8},{4,60},{8,16},{12,4},{16,24},{20,12},{24,32},{28,20},{32,40}... | collective-permute-start | bytes 2359304 | tf_op jit(solution)/shard_map/ppermute | solution.py:429
  56.1 18.1 %collective-permute-start.8 = (bf16[4,2,128,384]{3,2,1,0:T(8,128)(2,1)}, bf16[4,2,128,384]{3,2,1,0:T(8,128)(2,1)}, u32[]{:S(2)}, u32[]{:S(2)}) collective-permute-start(bf16[4,2,128,384]{3,2,1,0:T(8,128)(2,1)} %collective-permute-done.refs_1_), channel_id=1, source_target_pairs={{0,4},{4,0},{8,12},{12,8},{16,20},{20,16},{24,28},{28,24},{32,36},... | collective-permute-start | bytes 2359304 | tf_op jit(solution)/shard_map/ppermute | solution.py:433
  56.1 18.1 %collective-permute-start.9 = (bf16[4,2,128,384]{3,2,1,0:T(8,128)(2,1)}, bf16[4,2,128,384]{3,2,1,0:T(8,128)(2,1)}, u32[]{:S(2)}, u32[]{:S(2)}) collective-permute-start(bf16[4,2,128,384]{3,2,1,0:T(8,128)(2,1)} %collective-permute-done.4.refs_2_.third), channel_id=1, source_target_pairs={{0,4},{4,0},{8,12},{12,8},{16,20},{20,16},{24,28},{28,24},{32,36},... | collective-permute-start | bytes 2359304 | tf_op jit(solution)/shard_map/ppermute | solution.py:433
  64.8 37.3 %collective-permute-start.6 = (bf16[4,2,128,384]{3,2,1,0:T(8,128)(2,1)}, bf16[4,2,128,384]{3,2,1,0:T(8,128)(2,1)S(1)}, u32[]{:S(2)}, u32[]{:S(2)}) collective-permute-start(bf16[4,2,128,384]{3,2,1,0:T(8,128)(2,1)} %gate.3.refs_1_), channel_id=1, source_target_pairs={{0,4},{4,0},{8,12},{12,8},{16,20},{20,16},{24,28},{28,24},{32,36},... | collective-permute-start | bytes 2359304 | tf_op jit(solution)/shard_map/ppermute | solution.py:433
  72.4 29.8 %collective-permute-start.7 = (bf16[4,2,128,384]{3,2,1,0:T(8,128)(2,1)}, bf16[4,2,128,384]{3,2,1,0:T(8,128)(2,1)S(1)}, u32[]{:S(2)}, u32[]{:S(2)}) collective-permute-start(bf16[4,2,128,384]{3,2,1,0:T(8,128)(2,1)} %collective-permute-done.5.refs_2_), channel_id=1, source_target_pairs={{0,4},{4,0},{8,12},{12,8},{16,20},{20,16},{24,28},{28,24},{32,36},... | collective-permute-start | bytes 2359304 | tf_op jit(solution)/shard_map/ppermute | solution.py:433
  93.0 2.6 %collective-permute-start.10 = (bf16[4,160,384]{2,1,0:T(8,128)(2,1)}, bf16[4,160,384]{2,1,0:T(8,128)(2,1)}, u32[]{:S(2)}, u32[]{:S(2)}) collective-permute-start(bf16[4,160,384]{2,1,0:T(8,128)(2,1)} %cross.1.own), channel_id=1, source_target_pairs={{0,4},{4,0},{8,12},{12,8},{16,20},{20,16},{24,28},{28,24},{32,36},... | collective-permute-start | bytes 1474568 | tf_op jit(solution)/shard_map/ppermute | solution.py:433
  93.0 21.2 %collective-permute-start.3 = (bf16[4,2,128,384]{3,2,1,0:T(8,128)(2,1)S(1)}, bf16[4,2,128,384]{3,2,1,0:T(8,128)(2,1)S(1)}, u32[]{:S(2)}, u32[]{:S(2)}) collective-permute-start(bf16[4,2,128,384]{3,2,1,0:T(8,128)(2,1)S(1)} %copy-done.8), channel_id=1, source_target_pairs={{0,8},{4,60},{8,16},{12,4},{16,24},{20,12},{24,32},{28,20},{32,40}... | collective-permute-start | bytes 2359304 | tf_op jit(solution)/shard_map/ppermute | solution.py:429
  95.0 21.2 %collective-permute-start.13 = (bf16[4,2,128,384]{3,2,1,0:T(8,128)(2,1)}, bf16[4,2,128,384]{3,2,1,0:T(8,128)(2,1)}, u32[]{:S(2)}, u32[]{:S(2)}) collective-permute-start(bf16[4,2,128,384]{3,2,1,0:T(8,128)(2,1)} %collective-permute-done.5.refs_2_), channel_id=1, source_target_pairs={{0,8},{4,60},{8,16},{12,4},{16,24},{20,12},{24,32},{28,20},{32,40}... | collective-permute-start | bytes 2359304 | tf_op jit(solution)/shard_map/ppermute | solution.py:429
  115.1 11.5 %collective-permute-start.11 = (bf16[4,2,128,384]{3,2,1,0:T(8,128)(2,1)}, bf16[4,2,128,384]{3,2,1,0:T(8,128)(2,1)}, u32[]{:S(2)}, u32[]{:S(2)}) collective-permute-start(bf16[4,2,128,384]{3,2,1,0:T(8,128)(2,1)} %gate.5.refs_1_), channel_id=1, source_target_pairs={{0,8},{4,60},{8,16},{12,4},{16,24},{20,12},{24,32},{28,20},{32,40}... | collective-permute-start | bytes 2359304 | tf_op jit(solution)/shard_map/ppermute | solution.py:429
  116.2 16.4 %collective-permute-start.14 = (bf16[4,2,128,384]{3,2,1,0:T(8,128)(2,1)}, bf16[4,2,128,384]{3,2,1,0:T(8,128)(2,1)S(1)}, u32[]{:S(2)}, u32[]{:S(2)}) collective-permute-start(bf16[4,2,128,384]{3,2,1,0:T(8,128)(2,1)} %gate.5.refs_1_), channel_id=1, source_target_pairs={{0,4},{4,0},{8,12},{12,8},{16,20},{20,16},{24,28},{28,24},{32,36},... | collective-permute-start | bytes 2359304 | tf_op jit(solution)/shard_map/ppermute | solution.py:433
  116.2 18.5 %collective-permute-start.15 = (bf16[4,2,128,384]{3,2,1,0:T(8,128)(2,1)}, bf16[4,2,128,384]{3,2,1,0:T(8,128)(2,1)}, u32[]{:S(2)}, u32[]{:S(2)}) collective-permute-start(bf16[4,2,128,384]{3,2,1,0:T(8,128)(2,1)} %collective-permute-done.13.refs_2_), channel_id=1, source_target_pairs={{0,4},{4,0},{8,12},{12,8},{16,20},{20,16},{24,28},{28,24},{32,36},... | collective-permute-start | bytes 2359304 | tf_op jit(solution)/shard_map/ppermute | solution.py:433
  126.5 19.1 %collective-permute-start.12 = (bf16[4,2,128,384]{3,2,1,0:T(8,128)(2,1)}, bf16[4,2,128,384]{3,2,1,0:T(8,128)(2,1)}, u32[]{:S(2)}, u32[]{:S(2)}) collective-permute-start(bf16[4,2,128,384]{3,2,1,0:T(8,128)(2,1)} %collective-permute-done.11.refs_1_), channel_id=1, source_target_pairs={{0,4},{4,0},{8,12},{12,8},{16,20},{20,16},{24,28},{28,24},{32,36},... | collective-permute-start | bytes 2359304 | tf_op jit(solution)/shard_map/ppermute | solution.py:433
  128.3 52.5 %collective-permute-start.17 = (bf16[320,1536]{1,0:T(8,128)(2,1)}, bf16[320,1536]{1,0:T(8,128)(2,1)S(1)}, u32[]{:S(2)}, u32[]{:S(2)}) collective-permute-start(bf16[320,1536]{1,0:T(8,128)(2,1)} %get-tuple-element.39), channel_id=1, source_target_pairs={{0,1},{1,2},{2,3},{3,0},{4,5},{5,6},{6,7},{7,4},{8,9},{9,10},{10,1... | collective-permute-start | bytes 2949128 | tf_op jit(solution)/shard_map/ppermute | solution.py:424
  130.2 50.6 %collective-permute-start.18 = (bf16[320,1536]{1,0:T(8,128)(2,1)}, bf16[320,1536]{1,0:T(8,128)(2,1)S(1)}, u32[]{:S(2)}, u32[]{:S(2)}) collective-permute-start(bf16[320,1536]{1,0:T(8,128)(2,1)} %get-tuple-element.40), channel_id=1, source_target_pairs={{0,2},{1,3},{2,0},{3,1},{4,6},{5,7},{6,4},{7,5},{8,10},{9,11},{10,... | collective-permute-start | bytes 2949128 | tf_op jit(solution)/shard_map/ppermute | solution.py:424
  133.5 47.4 %collective-permute-start.19 = (bf16[320,1536]{1,0:T(8,128)(2,1)}, bf16[320,1536]{1,0:T(8,128)(2,1)S(1)}, u32[]{:S(2)}, u32[]{:S(2)}) collective-permute-start(bf16[320,1536]{1,0:T(8,128)(2,1)} %get-tuple-element.41), channel_id=1, source_target_pairs={{0,3},{1,0},{2,1},{3,2},{4,7},{5,4},{6,5},{7,6},{8,11},{9,8},{10,9... | collective-permute-start | bytes 2949128 | tf_op jit(solution)/shard_map/ppermute | solution.py:424
  179.8 2.5 %collective-permute-start.16 = (bf16[4,128,384]{2,1,0:T(8,128)(2,1)S(1)}, bf16[4,128,384]{2,1,0:T(8,128)(2,1)}, u32[]{:S(2)}, u32[]{:S(2)}) collective-permute-start(bf16[4,128,384]{2,1,0:T(8,128)(2,1)S(1)} %all_to_all.21.own), channel_id=1, source_target_pairs={{0,4},{4,0},{8,12},{12,8},{16,20},{20,16},{24,28},{28,24},{32,36},... | collective-permute-start | bytes 1179656 | tf_op jit(solution)/shard_map/ppermute | solution.py:433
  (15 other events, 52.0 us)
Sparse Core Ops, SparseCore 0:
  11.2 39.3 all-gather.4
  53.1 60.3 all-gather.6

commit v2 on v1

--- a/solution.py
+++ b/solution.py
@@ -32,6 +32,7 @@
     return pl.BlockSpec(shape, lambda *_: (0,) * len(shape))
 
 
+BRIEF = pl.CostEstimate(flops=1, bytes_accessed=1, transcendentals=0)
 ANY = pl.BlockSpec(memory_space=pl.ANY)
 
 
@@ -42,21 +43,26 @@
     return copies
 
 
-def pack_video_kernel(place, k_ref, v_ref, q_ref, w_ref, kv_out, q_out, self_out, rest_out, rows, w_rows, sem):
+def pack_video_kernel(place, k_ref, v_ref, q_ref, w_ref, out, self_out, rest_out, rows, turned, w_rows, sem):
     half = w_ref.shape[3] // 2
     columns = pl.ds(pl.multiple_of(place[4] * half, 128), half)
     coming = start_copies([(ref, rows.at[i]) for i, ref in enumerate((k_ref, v_ref, q_ref))], sem, 0)
     coming += start_copies([(w_ref.at[:, :, :, columns], w_rows)], sem, 3)
+    heads = [(g, h) for g in range(TOWERS) for h in range(LOCAL)]
     going = []
-    for i in range(3):
+    for i in (1, 2):
         coming[i].wait()
-        pairs = []
-        for g in range(TOWERS):
-            target = q_out.at[g] if i == 2 else kv_out.at[g, i]
-            pairs.append((rows.at[i, :, pl.ds(g * GW, GW)], target))
-        going += start_copies(pairs, sem, 4 + i * TOWERS)
+        pairs = [
+            (rows.at[i, :, pl.ds((g * LOCAL + h) * HD, HD)], out.at[g, i, h]) for g, h in heads
+        ]
+        going += start_copies(pairs, sem, 4 + (i - 1) * H)
+    coming[0].wait()
+    for g, h in heads:
+        block = rows[0, :, pl.ds((g * LOCAL + h) * HD, HD)]
+        turned[g, h] = block.astype(jnp.float32).T.astype(jnp.bfloat16)
+    going += start_copies([(turned.at[g], out.at[g, 0]) for g in range(TOWERS)], sem, 28)
     coming[3].wait()
-    going += start_copies([(w_rows.at[0], self_out), (w_rows.at[pl.ds(1, 2)], rest_out)], sem, 16)
+    going += start_copies([(w_rows.at[0], self_out), (w_rows.at[pl.ds(1, 2)], rest_out)], sem, 32)
     for copy in going:
         copy.wait()
 
@@ -64,7 +70,7 @@
 def pack_video(place, k, v, q, w):
     rows = k.shape[0]
     narrow = (LOCAL, w.shape[2], w.shape[3] // 2)
-    shapes = [(TOWERS, 2, rows, GW), (TOWERS, rows, GW), narrow, (2,) + narrow]
+    shapes = [(TOWERS, 3, LOCAL, rows, HD), narrow, (2,) + narrow]
     return pl.pallas_call(
         pack_video_kernel,
         out_shape=[jax.ShapeDtypeStruct(shape, jnp.bfloat16) for shape in shapes],
@@ -72,11 +78,12 @@
             num_scalar_prefetch=1,
             grid=(1,),
             in_specs=[ANY] * 4,
-            out_specs=[ANY] * 4,
+            out_specs=[ANY] * 3,
             scratch_shapes=[
                 pltpu.VMEM((3,) + k.shape, jnp.bfloat16),
+                pltpu.VMEM((TOWERS, LOCAL, HD, rows), jnp.bfloat16),
                 pltpu.VMEM((3,) + narrow, jnp.bfloat16),
-                pltpu.SemaphoreType.DMA((18,)),
+                pltpu.SemaphoreType.DMA((34,)),
             ],
         ),
         compiler_params=pltpu.CompilerParams(vmem_limit_bytes=60 * MIB),
@@ -145,8 +152,12 @@
     )(place, q, k, v)
 
 
+def keys_of(kv_ref):
+    return jnp.concatenate([kv_ref[r, 0, 0] for r in range(TOWERS)], axis=1)
+
+
 def rows_of(kv_ref, which):
-    return jnp.concatenate([kv_ref[r, which] for r in range(TOWERS)], axis=0)
+    return jnp.concatenate([kv_ref[r, which, 0] for r in range(TOWERS)], axis=0)
 
 
 def flash_kernel(kv_count, first, last, *refs):
@@ -159,27 +170,24 @@
         acc_in, stat_in = rest[:2]
         outs = rest[2:]
     size = TOWERS * VBLK
-    scaled = q_ref[...].astype(jnp.float32) * SCALE2
-    high = scaled.astype(jnp.bfloat16)
-    low = (scaled - high.astype(jnp.float32)).astype(jnp.bfloat16)
-    query = jnp.concatenate([high, low], axis=1)
-    scores = []
-    for kv in kv_refs:
-        keys = rows_of(kv, 0)
-        scores.append(nt_dot(query, jnp.concatenate([keys, keys], axis=1)))
-    top = functools.reduce(jnp.maximum, [jnp.max(s, axis=1, keepdims=True) for s in scores])
+    query = rows_of(q_ref, 0)
+    scores = [nn_dot(query, keys_of(kv)) for kv in kv_refs]
+    top = functools.reduce(
+        jnp.maximum, [jnp.max(s, axis=1, keepdims=True) for s in scores]
+    ) * SCALE2
     if not first:
         stat = stat_in[...]
         old_top, old_total = stat[:, 0:1], stat[:, 64:65]
         top = jnp.maximum(top, old_top)
         factor = jnp.exp2(old_top - top)
+    total = None
     acc = None
     for s, kv in zip(scores, kv_refs):
-        weights = jnp.exp2(s - top).astype(jnp.bfloat16)
-        values = rows_of(kv, 1)
-        part = nn_dot(weights, jnp.concatenate([values, jnp.ones_like(values)], axis=1))
+        weights = jnp.exp2(s * SCALE2 - top)
+        part = jnp.sum(weights, axis=1, keepdims=True)
+        total = part if total is None else total + part
+        part = nn_dot(weights.astype(jnp.bfloat16), rows_of(kv, 1))
         acc = part if acc is None else acc + part
-    acc, total = acc[:, :HD], acc[:, HD:]
     if not first:
         total = total + old_total * factor
         acc = acc + acc_in[...] * factor
@@ -189,7 +197,11 @@
         outs[0][...] = acc
         lane = lax.broadcasted_iota(jnp.int32, (size, HD), 1)
         outs[1][...] = jnp.where(lane < 64, top, total)
-        outs[2][...] = total[:8]
+        outs[2][...] = total[:8] + jnp.zeros((8, HD), jnp.float32)
+
+
+QUERY = pl.BlockSpec((TOWERS, 1, 1, VBLK, HD), lambda h, *_: (0, 2, h, 0, 0))
+SHARD = pl.BlockSpec((TOWERS, 2, 1, VBLK, HD), lambda h, *_: (0, 0, h, 0, 0))
 
 
 def flash(query, kvs, state, last):
@@ -203,19 +215,14 @@
     else:
         out_shape = [wide, wide, jax.ShapeDtypeStruct((8, HD), jnp.float32)]
         out_specs = [head, head, pl.BlockSpec((8, HD), lambda h: (0, 0))]
-    shard = pl.BlockSpec((TOWERS, 2, VBLK, HD), lambda h: (0, 0, 0, h))
     return pl.pallas_call(
         functools.partial(flash_kernel, len(kvs), state is None, last),
         out_shape=out_shape,
         grid=(LOCAL,),
-        in_specs=[head] + [shard] * len(kvs) + ([] if state is None else [head, head]),
+        in_specs=[QUERY] + [SHARD] * len(kvs) + ([] if state is None else [head, head]),
         out_specs=out_specs,
         compiler_params=pltpu.CompilerParams(vmem_limit_bytes=60 * MIB),
-        cost_estimate=pl.CostEstimate(
-            flops=8 * rows * keys * GW,
-            bytes_accessed=4 * keys * GW + 16 * rows * GW,
-            transcendentals=rows * keys * LOCAL,
-        ),
+        cost_estimate=BRIEF,
         name="flash",
     )(query, *kvs, *(() if state is None else state[:2]))
 
@@ -235,9 +242,9 @@
     for r in range(2):
         pieces.append((sibling, 2 * core + r, jnp.where(core == 0, after, before) + r))
         pieces.append((third, 2 - 2 * core + r, jnp.where(core == 0, before, after) + r))
-    keys = jnp.concatenate([ref[r, 0] for ref, r, _ in pieces], axis=0)
-    values = jnp.concatenate([ref[r, 1] for ref, r, _ in pieces], axis=0)
-    raw = nt_dot(query, keys) * SCALE2
+    keys = jnp.concatenate([ref[r, 0, 0] for ref, r, _ in pieces], axis=1)
+    values = jnp.concatenate([ref[r, 1, 0] for ref, r, _ in pieces], axis=0)
+    raw = nn_dot(query, keys) * SCALE2
     scores = []
     for i, (_, _, block) in enumerate(pieces):
         hit = (
@@ -266,7 +273,7 @@
     values = jnp.concatenate(
         [main[0, pl.ds(WIN, WIN), :], edge[0, pl.ds(HAT + HALO, HALO), :], spare], axis=0
     )
-    scores = nt_dot(q_ref[...], keys) * SCALE2
+    scores = nt_dot(rows_of(q_ref, 0), keys) * SCALE2
     parts = []
     for r in range(TOWERS):
         block = ctx * 4 + r
@@ -286,8 +293,7 @@
 
 
 def cross(place, margin, query, audio, own, sibling, third):
-    rows = query.shape[0]
-    shard = pl.BlockSpec((TOWERS, 2, VBLK, HD), lambda h, *_: (0, 0, 0, h))
+    rows = TOWERS * VBLK
     return pl.pallas_call(
         cross_kernel,
         out_shape=jax.ShapeDtypeStruct((TOWERS, BOTH, GW), jnp.bfloat16),
@@ -295,19 +301,17 @@
             num_scalar_prefetch=2,
             grid=(LOCAL,),
             in_specs=[
-                pl.BlockSpec((rows, HD), lambda h, *_: (0, h)),
+                QUERY,
                 pl.BlockSpec((1, AROWS, HD), lambda h, place, margin: (place[2], 0, h)),
                 pl.BlockSpec((1, AROWS, HD), lambda h, place, margin: (place[3], 0, h)),
-                shard,
-                shard,
-                shard,
+                SHARD,
+                SHARD,
+                SHARD,
             ],
             out_specs=pl.BlockSpec((TOWERS, BOTH, HD), lambda h, *_: (0, 0, h)),
         ),
         compiler_params=pltpu.CompilerParams(vmem_limit_bytes=60 * MIB),
-        cost_estimate=pl.CostEstimate(
-            flops=8 * rows * 1024 * GW, bytes_accessed=4 * MIB, transcendentals=rows * 512 * 3
-        ),
+        cost_estimate=BRIEF,
         name="cross",
     )(place, margin, query, audio, audio, own, sibling, third)
 
@@ -316,16 +320,25 @@
     return jnp.concatenate([piece(h) for h in range(LOCAL) for piece in pieces], axis=0)
 
 
-def project_cross_kernel(place, own, sibling, w_ref, *outs):
+def project_cross_kernel(place, own, sibling, w_ref, mine, up, down, up_later, down_later):
     towers = [lax.rem(place[1] + step, TOWERS) for step in range(TOWERS)]
     pairs = [(step, ref) for step in range(TOWERS) for ref in (own, sibling)]
+    targets = (
+        (mine, 0),
+        (mine, BOTH),
+        (up_later, 0),
+        (up, BOTH),
+        (up, 0),
+        (down, BOTH),
+        (down, 0),
+        (down_later, 0),
+    )
     for kind, (first, count) in enumerate(((0, VBLK), (VBLK, AUDIO_ROWS))):
         w = weight_rows([functools.partial(lambda b, h: w_ref[b, kind, h], b) for b in range(4)])
         a = jnp.concatenate([ref[towers[step], pl.ds(first, count), :] for step, ref in pairs], axis=0)
         y = nn_dot(a, w).astype(jnp.bfloat16)
-        for i, (step, ref) in enumerate(pairs):
-            at = first + (BOTH if ref is sibling else 0)
-            outs[step][pl.ds(at, count), :] = y[i * count : (i + 1) * count]
+        for i, (out, at) in enumerate(targets):
+            out[pl.ds(at + first, count), :] = y[i * count : (i + 1) * count]
 
 
 def project_cross(place, own, sibling, w):
@@ -333,7 +346,7 @@
     tile = width // 3
     return pl.pallas_call(
         project_cross_kernel,
-        out_shape=[jax.ShapeDtypeStruct((2 * BOTH, width), jnp.bfloat16)] * TOWERS,
+        out_shape=[jax.ShapeDtypeStruct((n * BOTH, width), jnp.bfloat16) for n in (2, 2, 2, 1, 1)],
         grid_spec=pltpu.PrefetchScalarGridSpec(
             num_scalar_prefetch=1,
             grid=(3,),
@@ -342,18 +355,18 @@
                 full(own.shape),
                 pl.BlockSpec(w.shape[:-1] + (tile,), lambda i, place: (0, 0, 0, 0, i)),
             ],
-            out_specs=[pl.BlockSpec((2 * BOTH, tile), lambda i, place: (0, i))] * TOWERS,
-        ),
-        compiler_params=pltpu.CompilerParams(vmem_limit_bytes=60 * MIB),
-        cost_estimate=pl.CostEstimate(
-            flops=2 * 1280 * GW * width, bytes_accessed=8 * MIB, transcendentals=0
-        ),
+            out_specs=[
+                pl.BlockSpec((n * BOTH, tile), lambda i, place: (0, i)) for n in (2, 2, 2, 1, 1)
+            ],
+        ),
+        compiler_params=pltpu.CompilerParams(vmem_limit_bytes=60 * MIB),
+        cost_estimate=BRIEF,
         name="project_cross",
     )(place, own, sibling, w)
 
 
 def project_self_kernel(place, own, sibling, w_ref, *refs):
-    base_refs, (gain, own_out, sibling_out) = refs[:TOWERS], refs[TOWERS:]
+    mine, up, down, up_later, down_later, gain, own_out, sibling_out = refs
     a = jnp.concatenate(
         [jnp.concatenate([ref[t] for t in range(TOWERS)], axis=1) for ref in (own, sibling)], axis=0
     )
@@ -365,7 +378,11 @@
         axis=0,
     )
     acc = nn_dot(a, w)
-    base = functools.reduce(jnp.add, [ref[...].astype(jnp.float32) for ref in base_refs])
+    top = [mine[pl.ds(0, BOTH), :], down[pl.ds(0, BOTH), :], up_later[...]]
+    bottom = [mine[pl.ds(BOTH, BOTH), :], up[pl.ds(BOTH, BOTH), :], down_later[...]]
+    base = jnp.concatenate(
+        [functools.reduce(jnp.add, [x.astype(jnp.float32) for x in xs]) for xs in (top, bottom)], axis=0
+    )
     for i, out in enumerate((own_out, sibling_out)):
         video = acc[i * VBLK : (i + 1) * VBLK] + base[i * BOTH : i * BOTH + VBLK]
         audio = base[i * BOTH + VBLK : (i + 1) * BOTH]
@@ -375,29 +392,64 @@
 
 def project_self(place, own, sibling, w, base, gains):
     width = w.shape[-1]
-    tile = width // 3
+    tile = width // 6
     rows = pl.BlockSpec((BOTH, tile), lambda i, place: (0, i))
     return pl.pallas_call(
         project_self_kernel,
         out_shape=[jax.ShapeDtypeStruct((BOTH, width), jnp.bfloat16)] * 2,
         grid_spec=pltpu.PrefetchScalarGridSpec(
             num_scalar_prefetch=1,
-            grid=(3,),
+            grid=(6,),
             in_specs=[
                 full(own.shape),
                 full(own.shape),
                 pl.BlockSpec(w.shape[:-1] + (tile,), lambda i, place: (0, 0, 0, i)),
             ]
-            + [pl.BlockSpec((2 * BOTH, tile), lambda i, place: (0, i))] * TOWERS
-            + [pl.BlockSpec((2, tile), lambda i, place: (0, place[4] * 3 + i))],
+            + [pl.BlockSpec((n * BOTH, tile), lambda i, place: (0, i)) for n in (2, 2, 2, 1, 1)]
+            + [pl.BlockSpec((2, tile), lambda i, place: (0, place[4] * 6 + i))],
             out_specs=[rows] * 2,
         ),
         compiler_params=pltpu.CompilerParams(vmem_limit_bytes=60 * MIB),
-        cost_estimate=pl.CostEstimate(
-            flops=4 * VBLK * 1536 * width, bytes_accessed=10 * MIB, transcendentals=0
-        ),
+        cost_estimate=BRIEF,
         name="project_self",
     )(place, own, sibling, w, *base, gains)
+
+
+def assemble_kernel(place, mine, theirs, video, audio):
+    def put(ref):
+        video[...] = ref[pl.ds(0, VBLK), :]
+        audio[...] = ref[pl.ds(VBLK, AUDIO_ROWS), :].astype(jnp.float32)[:ABLK].astype(jnp.bfloat16)
+
+    @pl.when(pl.program_id(0) == 0)
+    def _():
+        put(mine)
+
+    @pl.when(pl.program_id(0) == 1)
+    def _():
+        put(theirs)
+
+
+def assemble(place, mine, theirs):
+    width = mine.shape[1]
+
+    def column(i, place):
+        return (0, jnp.where(i == 0, place[4], 1 - place[4]))
+
+    return pl.pallas_call(
+        assemble_kernel,
+        out_shape=[
+            jax.ShapeDtypeStruct((VBLK, 2 * width), jnp.bfloat16),
+            jax.ShapeDtypeStruct((ABLK, 2 * width), jnp.bfloat16),
+        ],
+        grid_spec=pltpu.PrefetchScalarGridSpec(
+            num_scalar_prefetch=1,
+            grid=(2,),
+            in_specs=[full(mine.shape)] * 2,
+            out_specs=[pl.BlockSpec((VBLK, width), column), pl.BlockSpec((ABLK, width), column)],
+        ),
+        compiler_params=pltpu.CompilerParams(vmem_limit_bytes=60 * MIB),
+        name="assemble",
+    )(place, mine, theirs)
 
 
 def gate_kernel(*refs):
@@ -418,6 +470,10 @@
 
 def exchange_towers(value):
     return lax.all_to_all(value, "tower", split_axis=0, concat_axis=0, tiled=True)
+
+
+def add(a, b):
+    return (a.astype(jnp.float32) + b.astype(jnp.float32)).astype(jnp.bfloat16)
 
 
 def shift_tower(value, step):
@@ -441,44 +497,45 @@
     gains = gate_gains[0]
     margins = margin[0]
 
-    kv_parts, q_parts, w_self, w_rest = pack_video(
-        place, video_k[0], video_v[0], video_q[0], out_weight
-    )
+    parts, w_self, w_rest = pack_video(place, video_k[0], video_v[0], video_q[0], out_weight)
     w_rest = lax.all_gather(w_rest, "batch", axis=0, tiled=False)
     w_self = lax.all_gather(w_self, ("batch", "tower"), axis=0, tiled=False)
-    own = exchange_towers(kv_parts)
+    query = exchange_towers(parts)
+    own = query[:, :2]
     sibling = swap_core(own)
     near, far = hop(own), hop(sibling)
     third = far
 
-    query = exchange_towers(q_parts).reshape(TOWERS * VBLK, GW)
     audio = exchange_towers(pack_audio(place, audio_q[0], audio_k[0], audio_v[0]))
-    state = flash(query, [own, sibling], None, False)
-    started = state[2]
-
+    acc, stat, token = flash(query, [own, sibling], None, False)
+    audio = gate(audio, token)
+    crossed = cross(place, margins, query, audio, own, sibling, third)
+    rest, up, down, up_later, down_later = project_cross(place, crossed, swap_core(crossed), w_rest)
+    acc = gate(acc, rest)
+    up, down = shift_tower(up, 1), shift_tower(down, -1)
+    up_later = add(up_later, up[:BOTH])
+    down_later = add(down_later, down[BOTH:])
+
+    tokens = [token]
     for step in range(1, 4):
+        if step == 3:
+            acc = gate(acc, up_later, down_later)
+            up_later, down_later = shift_tower(up_later, 1), shift_tower(down_later, -1)
         now = [near, far, swap_core(near), swap_core(far)]
         near, far = hop(near), (hop(far) if step < 3 else None)
-        state = flash(query, now, state, False)
-        if step == 1:
-            near = gate(near, started)
-            audio = gate(audio, state[2])
-        if step == 2:
-            crossed = cross(place, margins, query, audio, own, sibling, third)
-            parts = project_cross(place, crossed, swap_core(crossed), w_rest)
-            base = [parts[0]] + [shift_tower(parts[i], i) for i in (1, 2, 3)]
-            near = gate(near, state[2], parts[0])
-    video_self = flash(query, [near, swap_core(near)], state, True)
+        acc, stat, token = flash(query, now, (acc, stat), False)
+        tokens.append(token)
+        if step < 3:
+            near, far = gate(near, tokens[step - 1]), gate(far, tokens[step - 1])
+        else:
+            near = gate(near, tokens[step - 1], up_later, down_later)
+    video_self = flash(query, [near, swap_core(near)], (acc, stat), True)
+    base = (rest, up, down, up_later, down_later)
+
     self_all = exchange_towers(video_self.reshape(TOWERS, VBLK, GW))
     mine, theirs = project_self(place, self_all, swap_core(self_all), w_self, base, gains)
-    theirs = swap_core(theirs)
-    outs = []
-    for first, count in ((0, VBLK), (VBLK, ABLK)):
-        a, b = mine[first : first + count], theirs[first : first + count]
-        outs.append(
-            jnp.where(core == 0, jnp.concatenate([a, b], axis=1), jnp.concatenate([b, a], axis=1))[None]
-        )
-    return tuple(outs)
+    video_out, audio_out = assemble(place, mine, swap_core(theirs))
+    return (video_out[None], audio_out[None])
 
 
 def solution(mesh):

time: 201 us -> 206 us (1.025)
  waiting for transfers between devices: 21.1 us -> 41.8 us
  blocking collectives: 42.2 us -> 30.9 us
  starting transfers between devices: 38.7 us -> 32.3 us
  other arithmetic: 1.76 us -> 4.15 us
    ppermute x3 -> x4, waiting for transfers between devices: 0.01 us -> 29.8 us  [shift_tower(): lax.ppermute(value, 'tower', [(i, (i + step) % TOWERS) for i in range(TOW...]
    all_to_all x2, blocking collectives: 42.2 us -> 30.9 us  [exchange_towers(): lax.all_to_all(value, 'tower', split_axis=0, concat_axis=0, tiled=True)]
    ppermute x7, waiting for transfers between devices: 16.2 us -> 8.21 us  [hop(): lax.ppermute(value, 'ctx', [(i, (i + 2 - 4 * (i % 2)) % total) for i in r...]
    pallas_call x5, Pallas kernels: 46.2 us -> 41.2 us  [flash(): pl.pallas_call(functools.partial(flash_kernel, len(kvs), state is None, l...]
    convert_element_type x0 -> x2, other arithmetic: none -> 4.15 us  [add(): return (a.astype(jnp.float32) + b.astype(jnp.float32)).astype(jnp.bfloat16)]
    all_to_all x2 -> x1, starting transfers between devices: 7.04 us -> 3.6 us  [exchange_towers(): lax.all_to_all(value, 'tower', split_axis=0, concat_axis=0, tiled=True)]
    pallas_call x1 -> x2, Pallas kernels: 6.51 us -> 9.31 us  [the longest x1 6.47 us: project_cross(): pl.pallas_call(project_cross_kernel, out_shape=[jax.ShapeDtypeStruct((n *...]
    ppermute x11, starting transfers between devices: 10.4 us -> 7.59 us  [swap_core(): return lax.ppermute(value, 'ctx', [(i, i ^ 1) for i in range(2 * CHIPS)])]
  transfers between devices with their start and end apart: 25 -> 25, of which waited for: 5 -> 6; matrix products, arithmetic and copies ran while one was open for 1% -> 2% of each run, Pallas kernels for 31% -> 28%
where the time goes in v2:
time: 206 us; the launch traced here: 205 us
  Pallas kernels  71.8 us (35%)
  waiting for transfers between devices  41.8 us (20%)
  starting transfers between devices  32.3 us (16%)
  blocking collectives  30.9 us (15%)
  between operations  14.2 us (7%)
  local copies, waits for them, and re-layouts  9.57 us (5%)
  other arithmetic  4.15 us (2%)
    pallas_call x5, Pallas kernels, flash(): pl.pallas_call(functools.partial(flash_kernel, len(kvs), state is None, l...  41.2 us
    all_to_all x2, blocking collectives, exchange_towers(): lax.all_to_all(value, 'tower', split_axis=0, concat_axis=0, tiled=True)  30.9 us
    ppermute x4, waiting for transfers between devices, shift_tower(): lax.ppermute(value, 'tower', [(i, (i + step) % TOWERS) for i in range(TOW...  29.8 us
    ppermute x7, starting transfers between devices, hop(): lax.ppermute(value, 'ctx', [(i, (i + 2 - 4 * (i % 2)) % total) for i in r...  18.1 us
    unnamed x43, local copies, waits for them, and re-layouts  8.88 us
    ppermute x7, waiting for transfers between devices, hop(): lax.ppermute(value, 'ctx', [(i, (i + 2 - 4 * (i % 2)) % total) for i in r...  8.21 us
    pallas_call x1, Pallas kernels, project_self(): pl.pallas_call(project_self_kernel, out_shape=[jax.ShapeDtypeStruct((BOTH...  7.83 us
    ppermute x11, starting transfers between devices, swap_core(): return lax.ppermute(value, 'ctx', [(i, i ^ 1) for i in range(2 * CHIPS)])  7.59 us
  transfers between devices with their start and end apart: 25, of which 6 were waited for; matrix products, arithmetic and copies ran while one was open for 2% of the time, Pallas kernels for 28%

profile of v2, /device:TPU:1, one launch (start us, length us, event | category | flops | bytes accessed | tf_op | source)
XLA Modules:
  0.0 204.7 jit_solution(15895974602797336418)
XLA Ops:
  7.9 3.5 %pack_video.1 = (bf16[4,3,3,128,128]{4,3,2,1,0:T(8,128)(2,1)}, bf16[3,32,1536]{2,1,0:T(8,128)(2,1)}, bf16[2,3,32,1536]{3,2,1,0:T(8,128)(2,1)}) custom-call(s32[5]{0:T(128)} %stack.23.place, bf16[128,1536]{1,0:T(8,128)(2,1)} %bitcast.24, bf16[128,1536]{1,0:T(8,128)(2,1)} %bitcast.25, bf16[128,1536]{1,0:T(8,128)(2,1)} %bitcast.26, bf16[3,3,32,3072]{3,2,1,0:T(8,128)(2,1)} %w_ref.1), custom_call_target="tpu_custom_call" | custom-call | tf_op jit(solution)/shard_map/pack_video/pallas_call | solution.py:74
  12.1 19.5 %all_to_all.15.refs_0_.q_ref = bf16[4,3,3,128,128]{4,3,2,1,0:T(8,128)(2,1)S(1)} all-to-all(bf16[4,3,3,128,128]{4,3,2,1,0:T(8,128)(2,1)} %get-tuple-element.25), channel_id=1, replica_groups=mesh['batch'=4,'ctx'=16,'tower'=4] {'tower'}, dimensions={0} | all-to-all | bytes 2359296 | tf_op jit(solution)/shard_map/all_to_all | solution.py:472
  31.7 2.9 %collective-permute-start.2 = (bf16[4,2,3,128,128]{4,3,2,1,0:T(8,128)(2,1)S(1)}, bf16[4,2,3,128,128]{4,3,2,1,0:T(8,128)(2,1)S(1)}, u32[]{:S(2)}, u32[]{:S(2)}) collective-permute-start(bf16[4,2,3,128,128]{4,3,2,1,0:T(8,128)(2,1)S(1)} %slice.12.refs_1_.own), channel_id=1, source_target_pairs={{0,4},{4,0},{8,12},{12,8},{16,20},{20,16},{24,28},{28,24},{32,36},... | collective-permute-start | bytes 2359304 | tf_op jit(solution)/shard_map/ppermute | solution.py:489
  34.6 3.5 %pack_audio.1 = bf16[4,576,384]{2,1,0:T(8,128)(2,1)} custom-call(s32[5]{0:T(128)} %stack.23.place, bf16[384,1536]{1,0:T(8,128)(2,1)} %bitcast.21, bf16[384,1536]{1,0:T(8,128)(2,1)} %bitcast.22, bf16[384,1536]{1,0:T(8,128)(2,1)} %bitcast.23), custom_call_target="tpu_custom_call" | custom-call | tf_op jit(solution)/shard_map/pack_audio/pallas_call | solution.py:137
  38.1 3.6 %all-to-all-start.1 = ((bf16[4,576,384]{2,1,0:T(8,128)(2,1)}), bf16[4,576,384]{2,1,0:T(8,128)(2,1)S(1)}, u32[]{:S(2)}, u32[]{:S(2)}) async-start(bf16[4,576,384]{2,1,0:T(8,128)(2,1)} %pack_audio.1), calls=%async_computation.1 | async-start | bytes 3538944 | tf_op jit(solution)/shard_map/all_to_all | solution.py:472
  41.7 5.6 %collective-permute-start = (bf16[4,2,3,128,128]{4,3,2,1,0:T(8,128)(2,1)S(1)}, bf16[4,2,3,128,128]{4,3,2,1,0:T(8,128)(2,1)}, u32[]{:S(2)}, u32[]{:S(2)}) collective-permute-start(bf16[4,2,3,128,128]{4,3,2,1,0:T(8,128)(2,1)S(1)} %slice.12.refs_1_.own), channel_id=1, source_target_pairs={{0,8},{4,60},{8,16},{12,4},{16,24},{20,12},{24,32},{28,20},{32,40}... | collective-permute-start | bytes 2359304 | tf_op jit(solution)/shard_map/ppermute | solution.py:485
  48.1 8.2 %collective-permute-done.refs_1_ = bf16[4,2,3,128,128]{4,3,2,1,0:T(8,128)(2,1)} collective-permute-done((bf16[4,2,3,128,128]{4,3,2,1,0:T(8,128)(2,1)S(1)}, bf16[4,2,3,128,128]{4,3,2,1,0:T(8,128)(2,1)}, u32[]{:S(2)}, u32[]{:S(2)}) %collective-permute-start) | collective-permute-done | bytes 786464 | tf_op jit(solution)/shard_map/ppermute | solution.py:485
  56.3 3.4 %collective-permute-start.1 = (bf16[4,2,3,128,128]{4,3,2,1,0:T(8,128)(2,1)}, bf16[4,2,3,128,128]{4,3,2,1,0:T(8,128)(2,1)S(1)}, u32[]{:S(2)}, u32[]{:S(2)}) collective-permute-start(bf16[4,2,3,128,128]{4,3,2,1,0:T(8,128)(2,1)} %collective-permute-done.refs_1_), channel_id=1, source_target_pairs={{0,8},{4,60},{8,16},{12,4},{16,24},{20,12},{24,32},{28,20},{32,40}... | collective-permute-start | bytes 2359304 | tf_op jit(solution)/shard_map/ppermute | solution.py:485
  60.4 5.5 %flash.5 = (f32[512,384]{1,0:T(8,128)}, f32[512,384]{1,0:T(8,128)}, f32[8,128]{1,0:T(8,128)}) custom-call(bf16[4,3,3,128,128]{4,3,2,1,0:T(8,128)(2,1)} %copy-done, bf16[4,2,3,128,128]{4,3,2,1,0:T(8,128)(2,1)} %copy-done.2, bf16[4,2,3,128,128]{4,3,2,1,0:T(8,128)(2,1)} %copy-done.4), custom_call_target="tpu_custom_call" | custom-call | flops 1 | bytes 1 | tf_op jit(solution)/shard_map/flash/pallas_call | solution.py:218
  67.1 6.4 %cross.1.own = bf16[4,160,384]{2,1,0:T(8,128)(2,1)} custom-call(s32[5]{0:T(128)} %stack.23.place, s32[64,3]{1,0:T(8,128)} %bitcast.27, bf16[4,3,3,128,128]{4,3,2,1,0:T(8,128)(2,1)} %copy-done, bf16[4,576,384]{2,1,0:T(8,128)(2,1)} %gate.9.main.edge, bf16[4,576,384]{2,1,0:T(8,128)(2,1)} %gate.9.main.edge, bf16[4,2,3,128,128]{4,3,2,1,0:T(8,128)(2,1)} %copy-done.2, ...), custom_call_target="tpu_custom_call" | custom-call | flops 1 | bytes 1 | tf_op jit(solution)/shard_map/cross/pallas_call | solution.py:297
  73.6 5.1 %collective-permute-start.9 = (bf16[4,2,3,128,128]{4,3,2,1,0:T(8,128)(2,1)}, bf16[4,2,3,128,128]{4,3,2,1,0:T(8,128)(2,1)S(1)}, u32[]{:S(2)}, u32[]{:S(2)}) collective-permute-start(bf16[4,2,3,128,128]{4,3,2,1,0:T(8,128)(2,1)} %collective-permute-done.4.third.refs_2_), channel_id=1, source_target_pairs={{0,8},{4,60},{8,16},{12,4},{16,24},{20,12},{24,32},{28,20},{32,40}... | collective-permute-start | bytes 2359304 | tf_op jit(solution)/shard_map/ppermute | solution.py:485
  79.5 6.5 %project_cross.1 = (bf16[320,1536]{1,0:T(8,128)(2,1)}, bf16[320,1536]{1,0:T(8,128)(2,1)}, bf16[320,1536]{1,0:T(8,128)(2,1)}, bf16[160,1536]{1,0:T(8,128)(2,1)}, bf16[160,1536]{1,0:T(8,128)(2,1)}) custom-call(s32[5]{0:T(128)} %stack.23.place, bf16[4,160,384]{2,1,0:T(8,128)(2,1)} %cross.1.own, bf16[4,160,384]{2,1,0:T(8,128)(2,1)} %copy-done.18, ...), custom_call_target="tpu_custom_call" | custom-call | flops 1 | bytes 1 | tf_op jit(solution)/shard_map/project_cross/pallas_call | solution.py:347
  88.2 1.8 collective-permute-start.3
  92.3 9.3 %flash.6 = (f32[512,384]{1,0:T(8,128)}, f32[512,384]{1,0:T(8,128)}, f32[8,128]{1,0:T(8,128)}) custom-call(bf16[4,3,3,128,128]{4,3,2,1,0:T(8,128)(2,1)} %copy-done, bf16[4,2,3,128,128]{4,3,2,1,0:T(8,128)(2,1)} %collective-permute-done.refs_1_, bf16[4,2,3,128,128]{4,3,2,1,0:T(8,128)(2,1)} %collective-permute-done.4.third.refs_2_, ...), custom_call_target="tpu_custom_call" | custom-call | flops 1 | bytes 1 | tf_op jit(solution)/shard_map/flash/pallas_call | solution.py:218
  102.7 23.5 %collective-permute-done.14.refs_2_ = bf16[320,1536]{1,0:T(8,128)(2,1)} collective-permute-done((bf16[320,1536]{1,0:T(8,128)(2,1)}, bf16[320,1536]{1,0:T(8,128)(2,1)}, u32[]{:S(2)}, u32[]{:S(2)}) %collective-permute-start.14) | collective-permute-done | bytes 983072 | tf_op jit(solution)/shard_map/ppermute | solution.py:480
  126.6 2.1 %add_convert_fusion.refs_2_ = bf16[160,1536]{1,0:T(8,128)(2,1)} fusion(bf16[160,1536]{1,0:T(8,128)(2,1)} %get-tuple-element.37, bf16[320,1536]{1,0:T(8,128)(2,1)} %collective-permute-done.14.refs_2_), kind=kLoop, calls=%fused_computation | loop fusion | flops 983040 | bytes 1474560 | tf_op jit(solution)/shard_map/convert_element_type | solution.py:476
  128.7 4.5 %collective-permute-done.12.refs_1_ = bf16[320,1536]{1,0:T(8,128)(2,1)} collective-permute-done((bf16[320,1536]{1,0:T(8,128)(2,1)}, bf16[320,1536]{1,0:T(8,128)(2,1)}, u32[]{:S(2)}, u32[]{:S(2)}) %collective-permute-start.12) | collective-permute-done | bytes 983072 | tf_op jit(solution)/shard_map/ppermute | solution.py:480
  133.2 2.1 %add_convert_fusion.1.refs_1_ = bf16[160,1536]{1,0:T(8,128)(2,1)} fusion(bf16[160,1536]{1,0:T(8,128)(2,1)} %get-tuple-element.35, bf16[320,1536]{1,0:T(8,128)(2,1)} %collective-permute-done.12.refs_1_), kind=kLoop, calls=%fused_computation.1 | loop fusion | flops 983040 | bytes 1474560 | tf_op jit(solution)/shard_map/convert_element_type | solution.py:476
  137.9 9.3 %flash.7 = (f32[512,384]{1,0:T(8,128)}, f32[512,384]{1,0:T(8,128)}, f32[8,128]{1,0:T(8,128)}) custom-call(bf16[4,3,3,128,128]{4,3,2,1,0:T(8,128)(2,1)} %copy-done, bf16[4,2,3,128,128]{4,3,2,1,0:T(8,128)(2,1)} %gate.8.refs_1_, bf16[4,2,3,128,128]{4,3,2,1,0:T(8,128)(2,1)} %gate.12.refs_2_, bf16[4,2,3,128,128]{4,3,2,1,0:T(8,128)(2,1)} %collective-permute-done.10.refs_3_, ...), custom_call_target="tpu_custom_call" | custom-call | flops 1 | bytes 1 | tf_op jit(solution)/shard_map/flash/pallas_call | solution.py:218
  151.6 9.3 %flash.8 = (f32[512,384]{1,0:T(8,128)}, f32[512,384]{1,0:T(8,128)}, f32[8,128]{1,0:T(8,128)}) custom-call(bf16[4,3,3,128,128]{4,3,2,1,0:T(8,128)(2,1)} %copy-done, bf16[4,2,3,128,128]{4,3,2,1,0:T(8,128)(2,1)} %gate.11.refs_1_, bf16[4,2,3,128,128]{4,3,2,1,0:T(8,128)(2,1)} %gate.14.refs_2_, bf16[4,2,3,128,128]{4,3,2,1,0:T(8,128)(2,1)} %copy-done.14, ...), custom_call_target="tpu_custom_call" | custom-call | flops 1 | bytes 1 | tf_op jit(solution)/shard_map/flash/pallas_call | solution.py:218
  161.8 7.9 %flash.9 = bf16[512,384]{1,0:T(8,128)(2,1)} custom-call(bf16[4,3,3,128,128]{4,3,2,1,0:T(8,128)(2,1)} %copy-done, bf16[4,2,3,128,128]{4,3,2,1,0:T(8,128)(2,1)} %gate.13.refs_1_, bf16[4,2,3,128,128]{4,3,2,1,0:T(8,128)(2,1)} %copy-done.13, f32[512,384]{1,0:T(8,128)} %get-tuple-element.41.refs_3_, f32[512,384]{1,0:T(8,128)} %get-tuple-element.42.refs_4_), custom_call_target="tpu_custom_call" | custom-call | flops 1 | bytes 1 | tf_op jit(solution)/shard_map/flash/pallas_call | solution.py:218
  169.7 11.4 %all_to_all.16.own = bf16[4,128,384]{2,1,0:T(8,128)(2,1)S(1)} all-to-all(bf16[4,128,384]{2,1,0:T(8,128)(2,1)} %bitcast.20), channel_id=1, replica_groups=mesh['batch'=4,'ctx'=16,'tower'=4] {'tower'}, dimensions={0} | all-to-all | bytes 786432 | tf_op jit(solution)/shard_map/all_to_all | solution.py:472
  184.2 7.8 %project_self.1 = (bf16[160,1536]{1,0:T(8,128)(2,1)}, bf16[160,1536]{1,0:T(8,128)(2,1)}) custom-call(s32[5]{0:T(128)} %stack.23.place, bf16[4,128,384]{2,1,0:T(8,128)(2,1)} %copy-done.12, bf16[4,128,384]{2,1,0:T(8,128)(2,1)} %copy-done.19, bf16[16,3,32,1536]{3,2,1,0:T(8,128)(2,1)} %bitcast.18, bf16[320,1536]{1,0:T(8,128)(2,1)} %get-tuple-element.29.refs_1_.refs_0_, ...), custom_call_target="tpu_custom_call" | custom-call | flops 1 | bytes 1 | tf_op jit(solution)/shard_map/project_self/pallas_call | solution.py:397
  195.0 2.8 %assemble.1 = (bf16[128,3072]{1,0:T(8,128)(2,1)}, bf16[24,3072]{1,0:T(8,128)(2,1)}) custom-call(s32[5]{0:T(128)} %stack.23.place, bf16[160,1536]{1,0:T(8,128)(2,1)} %get-tuple-element.44.mine, bf16[160,1536]{1,0:T(8,128)(2,1)} %copy-done.17), custom_call_target="tpu_custom_call" | custom-call | tf_op jit(solution)/shard_map/assemble/pallas_call | solution.py:438
  (96 shorter events, 25.0 us)
Async XLA Ops:
  7.2 71.5 %all-gather.5.cloned.1.call-start = ((), (), s32[]{:S(2)}) async-start(), calls=%async_computation.3 | async-start | bytes 2949120 | tf_op jit(solution)/shard_map/all_gather | solution.py:501
  11.4 172.1 %all-gather.7.cloned.1.call-start = ((), (), s32[]{:S(2)}) async-start(), calls=%async_computation.4 | async-start | bytes 5013504 | tf_op jit(solution)/shard_map/all_gather | solution.py:502
  31.7 15.7 %collective-permute-start.2 = (bf16[4,2,3,128,128]{4,3,2,1,0:T(8,128)(2,1)S(1)}, bf16[4,2,3,128,128]{4,3,2,1,0:T(8,128)(2,1)S(1)}, u32[]{:S(2)}, u32[]{:S(2)}) collective-permute-start(bf16[4,2,3,128,128]{4,3,2,1,0:T(8,128)(2,1)S(1)} %slice.12.refs_1_.own), channel_id=1, source_target_pairs={{0,4},{4,0},{8,12},{12,8},{16,20},{20,16},{24,28},{28,24},{32,36},... | collective-permute-start | bytes 2359304 | tf_op jit(solution)/shard_map/ppermute | solution.py:489
  38.1 27.7 %all-to-all-start.1 = ((bf16[4,576,384]{2,1,0:T(8,128)(2,1)}), bf16[4,576,384]{2,1,0:T(8,128)(2,1)S(1)}, u32[]{:S(2)}, u32[]{:S(2)}) async-start(bf16[4,576,384]{2,1,0:T(8,128)(2,1)} %pack_audio.1), calls=%async_computation.1 | async-start | bytes 3538944 | tf_op jit(solution)/shard_map/all_to_all | solution.py:472
  41.7 14.5 %collective-permute-start = (bf16[4,2,3,128,128]{4,3,2,1,0:T(8,128)(2,1)S(1)}, bf16[4,2,3,128,128]{4,3,2,1,0:T(8,128)(2,1)}, u32[]{:S(2)}, u32[]{:S(2)}) collective-permute-start(bf16[4,2,3,128,128]{4,3,2,1,0:T(8,128)(2,1)S(1)} %slice.12.refs_1_.own), channel_id=1, source_target_pairs={{0,8},{4,60},{8,16},{12,4},{16,24},{20,12},{24,32},{28,20},{32,40}... | collective-permute-start | bytes 2359304 | tf_op jit(solution)/shard_map/ppermute | solution.py:485
  47.4 19.7 %collective-permute-start.4 = (bf16[4,2,3,128,128]{4,3,2,1,0:T(8,128)(2,1)S(1)}, bf16[4,2,3,128,128]{4,3,2,1,0:T(8,128)(2,1)}, u32[]{:S(2)}, u32[]{:S(2)}) collective-permute-start(bf16[4,2,3,128,128]{4,3,2,1,0:T(8,128)(2,1)S(1)} %collective-permute-done.2.refs_2_.sibling), channel_id=1, source_target_pairs={{0,8},{4,60},{8,16},{12,4},{16,24},{20,12},{24,32},{28,20},{32,40}... | collective-permute-start | bytes 2359304 | tf_op jit(solution)/shard_map/ppermute | solution.py:485
  56.3 31.0 %collective-permute-start.1 = (bf16[4,2,3,128,128]{4,3,2,1,0:T(8,128)(2,1)}, bf16[4,2,3,128,128]{4,3,2,1,0:T(8,128)(2,1)S(1)}, u32[]{:S(2)}, u32[]{:S(2)}) collective-permute-start(bf16[4,2,3,128,128]{4,3,2,1,0:T(8,128)(2,1)} %collective-permute-done.refs_1_), channel_id=1, source_target_pairs={{0,8},{4,60},{8,16},{12,4},{16,24},{20,12},{24,32},{28,20},{32,40}... | collective-permute-start | bytes 2359304 | tf_op jit(solution)/shard_map/ppermute | solution.py:485
  73.5 5.1 %collective-permute-start.7 = (bf16[4,160,384]{2,1,0:T(8,128)(2,1)}, bf16[4,160,384]{2,1,0:T(8,128)(2,1)S(1)}, u32[]{:S(2)}, u32[]{:S(2)}) collective-permute-start(bf16[4,160,384]{2,1,0:T(8,128)(2,1)} %cross.1.own), channel_id=1, source_target_pairs={{0,4},{4,0},{8,12},{12,8},{16,20},{20,16},{24,28},{28,24},{32,36},... | collective-permute-start | bytes 1474568 | tf_op jit(solution)/shard_map/ppermute | solution.py:489
  73.6 16.5 %collective-permute-start.9 = (bf16[4,2,3,128,128]{4,3,2,1,0:T(8,128)(2,1)}, bf16[4,2,3,128,128]{4,3,2,1,0:T(8,128)(2,1)S(1)}, u32[]{:S(2)}, u32[]{:S(2)}) collective-permute-start(bf16[4,2,3,128,128]{4,3,2,1,0:T(8,128)(2,1)} %collective-permute-done.4.third.refs_2_), channel_id=1, source_target_pairs={{0,8},{4,60},{8,16},{12,4},{16,24},{20,12},{24,32},{28,20},{32,40}... | collective-permute-start | bytes 2359304 | tf_op jit(solution)/shard_map/ppermute | solution.py:485
  85.9 40.3 %collective-permute-start.14 = (bf16[320,1536]{1,0:T(8,128)(2,1)}, bf16[320,1536]{1,0:T(8,128)(2,1)}, u32[]{:S(2)}, u32[]{:S(2)}) collective-permute-start(bf16[320,1536]{1,0:T(8,128)(2,1)} %get-tuple-element.38), channel_id=1, source_target_pairs={{0,3},{1,0},{2,1},{3,2},{4,7},{5,4},{6,5},{7,6},{8,11},{9,8},{10,9... | collective-permute-start | bytes 2949128 | tf_op jit(solution)/shard_map/ppermute | solution.py:480
  86.8 4.2 %collective-permute-start.5 = (bf16[4,2,3,128,128]{4,3,2,1,0:T(8,128)(2,1)}, bf16[4,2,3,128,128]{4,3,2,1,0:T(8,128)(2,1)S(1)}, u32[]{:S(2)}, u32[]{:S(2)}) collective-permute-start(bf16[4,2,3,128,128]{4,3,2,1,0:T(8,128)(2,1)} %collective-permute-done.refs_1_), channel_id=1, source_target_pairs={{0,4},{4,0},{8,12},{12,8},{16,20},{20,16},{24,28},{28,24},{32,36},... | collective-permute-start | bytes 2359304 | tf_op jit(solution)/shard_map/ppermute | solution.py:489
  86.8 4.7 %collective-permute-start.6 = (bf16[4,2,3,128,128]{4,3,2,1,0:T(8,128)(2,1)}, bf16[4,2,3,128,128]{4,3,2,1,0:T(8,128)(2,1)}, u32[]{:S(2)}, u32[]{:S(2)}) collective-permute-start(bf16[4,2,3,128,128]{4,3,2,1,0:T(8,128)(2,1)} %collective-permute-done.4.third.refs_2_), channel_id=1, source_target_pairs={{0,4},{4,0},{8,12},{12,8},{16,20},{20,16},{24,28},{28,24},{32,36},... | collective-permute-start | bytes 2359304 | tf_op jit(solution)/shard_map/ppermute | solution.py:489
  88.2 13.5 %collective-permute-start.3 = (bf16[4,2,3,128,128]{4,3,2,1,0:T(8,128)(2,1)}, bf16[4,2,3,128,128]{4,3,2,1,0:T(8,128)(2,1)S(1)}, u32[]{:S(2)}, u32[]{:S(2)}) collective-permute-start(bf16[4,2,3,128,128]{4,3,2,1,0:T(8,128)(2,1)} %gate.8.refs_1_), channel_id=1, source_target_pairs={{0,8},{4,60},{8,16},{12,4},{16,24},{20,12},{24,32},{28,20},{32,40}... | collective-permute-start | bytes 2359304 | tf_op jit(solution)/shard_map/ppermute | solution.py:485
  90.0 43.1 %collective-permute-start.12 = (bf16[320,1536]{1,0:T(8,128)(2,1)}, bf16[320,1536]{1,0:T(8,128)(2,1)}, u32[]{:S(2)}, u32[]{:S(2)}) collective-permute-start(bf16[320,1536]{1,0:T(8,128)(2,1)} %get-tuple-element.36), channel_id=1, source_target_pairs={{0,1},{1,2},{2,3},{3,0},{4,5},{5,6},{6,7},{7,4},{8,9},{9,10},{10,1... | collective-permute-start | bytes 2949128 | tf_op jit(solution)/shard_map/ppermute | solution.py:480
  91.5 45.3 %collective-permute-start.10 = (bf16[4,2,3,128,128]{4,3,2,1,0:T(8,128)(2,1)S(1)}, bf16[4,2,3,128,128]{4,3,2,1,0:T(8,128)(2,1)}, u32[]{:S(2)}, u32[]{:S(2)}) collective-permute-start(bf16[4,2,3,128,128]{4,3,2,1,0:T(8,128)(2,1)S(1)} %copy-done.6), channel_id=1, source_target_pairs={{0,4},{4,0},{8,12},{12,8},{16,20},{20,16},{24,28},{28,24},{32,36},... | collective-permute-start | bytes 2359304 | tf_op jit(solution)/shard_map/ppermute | solution.py:489
  92.2 45.6 %collective-permute-start.11 = (bf16[4,2,3,128,128]{4,3,2,1,0:T(8,128)(2,1)S(1)}, bf16[4,2,3,128,128]{4,3,2,1,0:T(8,128)(2,1)}, u32[]{:S(2)}, u32[]{:S(2)}) collective-permute-start(bf16[4,2,3,128,128]{4,3,2,1,0:T(8,128)(2,1)S(1)} %copy-done.8), channel_id=1, source_target_pairs={{0,4},{4,0},{8,12},{12,8},{16,20},{20,16},{24,28},{28,24},{32,36},... | collective-permute-start | bytes 2359304 | tf_op jit(solution)/shard_map/ppermute | solution.py:489
  101.7 33.6 %collective-permute-start.17 = (bf16[4,2,3,128,128]{4,3,2,1,0:T(8,128)(2,1)S(1)}, bf16[4,2,3,128,128]{4,3,2,1,0:T(8,128)(2,1)S(1)}, u32[]{:S(2)}, u32[]{:S(2)}) collective-permute-start(bf16[4,2,3,128,128]{4,3,2,1,0:T(8,128)(2,1)S(1)} %copy-done.8), channel_id=1, source_target_pairs={{0,8},{4,60},{8,16},{12,4},{16,24},{20,12},{24,32},{28,20},{32,40}... | collective-permute-start | bytes 2359304 | tf_op jit(solution)/shard_map/ppermute | solution.py:485
  126.3 20.9 %collective-permute-start.8 = (bf16[4,2,3,128,128]{4,3,2,1,0:T(8,128)(2,1)}, bf16[4,2,3,128,128]{4,3,2,1,0:T(8,128)(2,1)S(1)}, u32[]{:S(2)}, u32[]{:S(2)}) collective-permute-start(bf16[4,2,3,128,128]{4,3,2,1,0:T(8,128)(2,1)} %gate.11.refs_1_), channel_id=1, source_target_pairs={{0,8},{4,60},{8,16},{12,4},{16,24},{20,12},{24,32},{28,20},{32,40}... | collective-permute-start | bytes 2359304 | tf_op jit(solution)/shard_map/ppermute | solution.py:485
  133.2 14.0 %collective-permute-start.15 = (bf16[160,1536]{1,0:T(8,128)(2,1)}, bf16[160,1536]{1,0:T(8,128)(2,1)}, u32[]{:S(2)}, u32[]{:S(2)}) collective-permute-start(bf16[160,1536]{1,0:T(8,128)(2,1)} %add_convert_fusion.refs_2_), channel_id=1, source_target_pairs={{0,3},{1,0},{2,1},{3,2},{4,7},{5,4},{6,5},{7,6},{8,11},{9,8},{10,9... | collective-permute-start | bytes 1474568 | tf_op jit(solution)/shard_map/ppermute | solution.py:480
  135.3 13.7 %collective-permute-start.13 = (bf16[160,1536]{1,0:T(8,128)(2,1)}, bf16[160,1536]{1,0:T(8,128)(2,1)}, u32[]{:S(2)}, u32[]{:S(2)}) collective-permute-start(bf16[160,1536]{1,0:T(8,128)(2,1)} %add_convert_fusion.1.refs_1_), channel_id=1, source_target_pairs={{0,1},{1,2},{2,3},{3,0},{4,5},{5,6},{6,7},{7,4},{8,9},{9,10},{10,1... | collective-permute-start | bytes 1474568 | tf_op jit(solution)/shard_map/ppermute | solution.py:480
  136.7 13.7 %collective-permute-start.18 = (bf16[4,2,3,128,128]{4,3,2,1,0:T(8,128)(2,1)S(1)}, bf16[4,2,3,128,128]{4,3,2,1,0:T(8,128)(2,1)S(1)}, u32[]{:S(2)}, u32[]{:S(2)}) collective-permute-start(bf16[4,2,3,128,128]{4,3,2,1,0:T(8,128)(2,1)S(1)} %copy-done.10), channel_id=1, source_target_pairs={{0,4},{4,0},{8,12},{12,8},{16,20},{20,16},{24,28},{28,24},{32,36},... | collective-permute-start | bytes 2359304 | tf_op jit(solution)/shard_map/ppermute | solution.py:489
  137.8 12.7 %collective-permute-start.19 = (bf16[4,2,3,128,128]{4,3,2,1,0:T(8,128)(2,1)}, bf16[4,2,3,128,128]{4,3,2,1,0:T(8,128)(2,1)S(1)}, u32[]{:S(2)}, u32[]{:S(2)}) collective-permute-start(bf16[4,2,3,128,128]{4,3,2,1,0:T(8,128)(2,1)} %gate.14.refs_2_), channel_id=1, source_target_pairs={{0,4},{4,0},{8,12},{12,8},{16,20},{20,16},{24,28},{28,24},{32,36},... | collective-permute-start | bytes 2359304 | tf_op jit(solution)/shard_map/ppermute | solution.py:489
  148.9 12.0 %collective-permute-start.16 = (bf16[4,2,3,128,128]{4,3,2,1,0:T(8,128)(2,1)}, bf16[4,2,3,128,128]{4,3,2,1,0:T(8,128)(2,1)S(1)}, u32[]{:S(2)}, u32[]{:S(2)}) collective-permute-start(bf16[4,2,3,128,128]{4,3,2,1,0:T(8,128)(2,1)} %gate.13.refs_1_), channel_id=1, source_target_pairs={{0,4},{4,0},{8,12},{12,8},{16,20},{20,16},{24,28},{28,24},{32,36},... | collective-permute-start | bytes 2359304 | tf_op jit(solution)/shard_map/ppermute | solution.py:489
  181.0 2.4 %collective-permute-start.20 = (bf16[4,128,384]{2,1,0:T(8,128)(2,1)S(1)}, bf16[4,128,384]{2,1,0:T(8,128)(2,1)S(1)}, u32[]{:S(2)}, u32[]{:S(2)}) collective-permute-start(bf16[4,128,384]{2,1,0:T(8,128)(2,1)S(1)} %all_to_all.16.own), channel_id=1, source_target_pairs={{0,4},{4,0},{8,12},{12,8},{16,20},{20,16},{24,28},{28,24},{32,36},... | collective-permute-start | bytes 1179656 | tf_op jit(solution)/shard_map/ppermute | solution.py:489
  (22 other events, 79.9 us)
Sparse Core Ops, SparseCore 0:
  11.5 39.3 all-gather.4
  53.3 77.3 all-gather.6

commit v3 on v2

--- a/solution.py
+++ b/solution.py
@@ -160,6 +160,10 @@
     return jnp.concatenate([kv_ref[r, which, 0] for r in range(TOWERS)], axis=0)
 
 
+def lane_tiles(x):
+    return [x[:, i : i + HD] for i in range(0, x.shape[1], HD)]
+
+
 def flash_kernel(kv_count, first, last, *refs):
     q_ref = refs[0]
     kv_refs = refs[1 : 1 + kv_count]
@@ -167,37 +171,34 @@
     if first:
         outs = rest
     else:
-        acc_in, stat_in = rest[:2]
-        outs = rest[2:]
-    size = TOWERS * VBLK
+        acc_in, top_in, total_in = rest[:3]
+        outs = rest[3:]
     query = rows_of(q_ref, 0)
     scores = [nn_dot(query, keys_of(kv)) for kv in kv_refs]
-    top = functools.reduce(
-        jnp.maximum, [jnp.max(s, axis=1, keepdims=True) for s in scores]
-    ) * SCALE2
-    if not first:
-        stat = stat_in[...]
-        old_top, old_total = stat[:, 0:1], stat[:, 64:65]
-        top = jnp.maximum(top, old_top)
-        factor = jnp.exp2(old_top - top)
-    total = None
-    acc = None
+    top = functools.reduce(jnp.maximum, [t for s in scores for t in lane_tiles(s)])
+    top = jnp.max(top, axis=1, keepdims=True) * SCALE2
+    if first:
+        top = jnp.broadcast_to(top, (TOWERS * VBLK, HD))
+        acc = total = None
+    else:
+        top = jnp.maximum(top, top_in[...])
+        factor = jnp.exp2(top_in[...] - top)
+        acc = acc_in[...] * factor
+        total = total_in[...] * factor
+    wide = jnp.concatenate([top] * TOWERS, axis=1)
     for s, kv in zip(scores, kv_refs):
-        weights = jnp.exp2(s * SCALE2 - top)
-        part = jnp.sum(weights, axis=1, keepdims=True)
+        weights = jnp.exp2(s * SCALE2 - wide)
+        part = functools.reduce(jnp.add, lane_tiles(weights))
         total = part if total is None else total + part
         part = nn_dot(weights.astype(jnp.bfloat16), rows_of(kv, 1))
         acc = part if acc is None else acc + part
-    if not first:
-        total = total + old_total * factor
-        acc = acc + acc_in[...] * factor
     if last:
-        outs[0][...] = (acc / total).astype(jnp.bfloat16)
+        outs[0][...] = (acc / jnp.sum(total, axis=1, keepdims=True)).astype(jnp.bfloat16)
     else:
         outs[0][...] = acc
-        lane = lax.broadcasted_iota(jnp.int32, (size, HD), 1)
-        outs[1][...] = jnp.where(lane < 64, top, total)
-        outs[2][...] = total[:8] + jnp.zeros((8, HD), jnp.float32)
+        outs[1][...] = top
+        outs[2][...] = total
+        outs[3][...] = total[:8]
 
 
 QUERY = pl.BlockSpec((TOWERS, 1, 1, VBLK, HD), lambda h, *_: (0, 2, h, 0, 0))
@@ -213,22 +214,28 @@
         out_shape = jax.ShapeDtypeStruct((rows, GW), jnp.bfloat16)
         out_specs = head
     else:
-        out_shape = [wide, wide, jax.ShapeDtypeStruct((8, HD), jnp.float32)]
-        out_specs = [head, head, pl.BlockSpec((8, HD), lambda h: (0, 0))]
+        out_shape = [wide, wide, wide, jax.ShapeDtypeStruct((8, HD), jnp.float32)]
+        out_specs = [head, head, head, pl.BlockSpec((8, HD), lambda h: (0, 0))]
     return pl.pallas_call(
         functools.partial(flash_kernel, len(kvs), state is None, last),
         out_shape=out_shape,
         grid=(LOCAL,),
-        in_specs=[QUERY] + [SHARD] * len(kvs) + ([] if state is None else [head, head]),
+        in_specs=[QUERY] + [SHARD] * len(kvs) + ([] if state is None else [head] * 3),
         out_specs=out_specs,
         compiler_params=pltpu.CompilerParams(vmem_limit_bytes=60 * MIB),
         cost_estimate=BRIEF,
         name="flash",
-    )(query, *kvs, *(() if state is None else state[:2]))
+    )(query, *kvs, *(() if state is None else state))
 
 
 AUDIO_ROWS = 32
 BOTH = VBLK + AUDIO_ROWS
+
+
+def weighted(scores, values):
+    weights = jnp.exp2(scores - jnp.max(scores, axis=1, keepdims=True)).astype(jnp.bfloat16)
+    result = nn_dot(weights, jnp.concatenate([values, jnp.ones_like(values)], axis=1))
+    return result[:, :HD] / result[:, HD:]
 
 
 def audio_rows(place, margin, audio, own, sibling, third):
@@ -254,9 +261,7 @@
         )
         scores.append(jnp.where(hit, raw[:, i * VBLK : (i + 1) * VBLK], NEG))
     scores = jnp.concatenate(scores, axis=1)
-    weights = jnp.exp2(scores - jnp.max(scores, axis=1, keepdims=True))
-    total = jnp.sum(weights, axis=1, keepdims=True)
-    return nn_dot(weights.astype(jnp.bfloat16), values) / total
+    return weighted(scores, values)
 
 
 def cross_kernel(place, margin, q_ref, main, edge, own, sibling, third, out):
@@ -280,9 +285,7 @@
         hit = (ids == margin[block, 0]) | (ids == margin[block, 1]) | (ids == margin[block, 2])
         parts.append(jnp.where(hit, scores[r * VBLK : (r + 1) * VBLK], NEG))
     scores = jnp.concatenate(parts, axis=0)
-    weights = jnp.exp2(scores - jnp.max(scores, axis=1, keepdims=True))
-    total = jnp.sum(weights, axis=1, keepdims=True)
-    result = (nn_dot(weights.astype(jnp.bfloat16), values) / total).astype(jnp.bfloat16)
+    result = weighted(scores, values).astype(jnp.bfloat16)
     mixed = audio_rows(place, margin, main, own, sibling, third)
     for r in range(TOWERS):
         out[r, pl.ds(0, VBLK), :] = result[r * VBLK : (r + 1) * VBLK]
@@ -366,13 +369,13 @@
 
 
 def project_self_kernel(place, own, sibling, w_ref, *refs):
-    mine, up, down, up_later, down_later, gain, own_out, sibling_out = refs
+    mine, up, down, up_later, down_later, gain, video_out, audio_out, sibling_out = refs
     a = jnp.concatenate(
         [jnp.concatenate([ref[t] for t in range(TOWERS)], axis=1) for ref in (own, sibling)], axis=0
     )
     w = jnp.concatenate(
         [
-            weight_rows([functools.partial(lambda b, h: w_ref[b * TOWERS + t, h], b) for b in range(4)])
+            weight_rows([functools.partial(lambda b, h: w_ref[t * 4 + b, h], b) for b in range(4)])
             for t in range(TOWERS)
         ],
         axis=0,
@@ -383,73 +386,69 @@
     base = jnp.concatenate(
         [functools.reduce(jnp.add, [x.astype(jnp.float32) for x in xs]) for xs in (top, bottom)], axis=0
     )
-    for i, out in enumerate((own_out, sibling_out)):
-        video = acc[i * VBLK : (i + 1) * VBLK] + base[i * BOTH : i * BOTH + VBLK]
-        audio = base[i * BOTH + VBLK : (i + 1) * BOTH]
-        out[pl.ds(0, VBLK), :] = (gain[0:1] * video).astype(jnp.bfloat16)
-        out[pl.ds(VBLK, AUDIO_ROWS), :] = (gain[1:2] * audio).astype(jnp.bfloat16)
+    video, audio = [], []
+    for i in range(2):
+        video.append(gain[0:1] * (acc[i * VBLK : (i + 1) * VBLK] + base[i * BOTH : i * BOTH + VBLK]))
+        audio.append(gain[1:2] * base[i * BOTH + VBLK : (i + 1) * BOTH])
+    video_out[...] = video[0].astype(jnp.bfloat16)
+    audio_out[...] = audio[0][:ABLK].astype(jnp.bfloat16)
+    sibling_out[pl.ds(0, VBLK), :] = video[1].astype(jnp.bfloat16)
+    sibling_out[pl.ds(VBLK, AUDIO_ROWS), :] = audio[1].astype(jnp.bfloat16)
 
 
 def project_self(place, own, sibling, w, base, gains):
     width = w.shape[-1]
-    tile = width // 6
-    rows = pl.BlockSpec((BOTH, tile), lambda i, place: (0, i))
+    tile = width // 3
+    out = lambda rows: pl.BlockSpec((rows, tile), lambda i, place: (0, place[4] * 3 + i))
     return pl.pallas_call(
         project_self_kernel,
-        out_shape=[jax.ShapeDtypeStruct((BOTH, width), jnp.bfloat16)] * 2,
+        out_shape=[
+            jax.ShapeDtypeStruct((VBLK, 2 * width), jnp.bfloat16),
+            jax.ShapeDtypeStruct((ABLK, 2 * width), jnp.bfloat16),
+            jax.ShapeDtypeStruct((BOTH, width), jnp.bfloat16),
+        ],
         grid_spec=pltpu.PrefetchScalarGridSpec(
             num_scalar_prefetch=1,
-            grid=(6,),
+            grid=(3,),
             in_specs=[
                 full(own.shape),
                 full(own.shape),
                 pl.BlockSpec(w.shape[:-1] + (tile,), lambda i, place: (0, 0, 0, i)),
             ]
             + [pl.BlockSpec((n * BOTH, tile), lambda i, place: (0, i)) for n in (2, 2, 2, 1, 1)]
-            + [pl.BlockSpec((2, tile), lambda i, place: (0, place[4] * 6 + i))],
-            out_specs=[rows] * 2,
-        ),
-        compiler_params=pltpu.CompilerParams(vmem_limit_bytes=60 * MIB),
+            + [pl.BlockSpec((2, tile), lambda i, place: (0, place[4] * 3 + i))],
+            out_specs=[out(VBLK), out(ABLK), pl.BlockSpec((BOTH, tile), lambda i, place: (0, i))],
+        ),
+        compiler_params=pltpu.CompilerParams(vmem_limit_bytes=24 * MIB),
         cost_estimate=BRIEF,
         name="project_self",
     )(place, own, sibling, w, *base, gains)
 
 
-def assemble_kernel(place, mine, theirs, video, audio):
-    def put(ref):
-        video[...] = ref[pl.ds(0, VBLK), :]
-        audio[...] = ref[pl.ds(VBLK, AUDIO_ROWS), :].astype(jnp.float32)[:ABLK].astype(jnp.bfloat16)
-
-    @pl.when(pl.program_id(0) == 0)
-    def _():
-        put(mine)
-
-    @pl.when(pl.program_id(0) == 1)
-    def _():
-        put(theirs)
-
-
-def assemble(place, mine, theirs):
-    width = mine.shape[1]
+def assemble_kernel(place, video_in, audio_in, theirs, video, audio):
+    video[...] = theirs[pl.ds(0, VBLK), :]
+    audio[...] = theirs[pl.ds(VBLK, AUDIO_ROWS), :].astype(jnp.float32)[:ABLK].astype(jnp.bfloat16)
+
+
+def assemble(place, video, audio, theirs):
+    width = theirs.shape[1]
 
     def column(i, place):
-        return (0, jnp.where(i == 0, place[4], 1 - place[4]))
+        return (0, 1 - place[4])
 
     return pl.pallas_call(
         assemble_kernel,
-        out_shape=[
-            jax.ShapeDtypeStruct((VBLK, 2 * width), jnp.bfloat16),
-            jax.ShapeDtypeStruct((ABLK, 2 * width), jnp.bfloat16),
-        ],
+        out_shape=[jax.ShapeDtypeStruct(x.shape, x.dtype) for x in (video, audio)],
         grid_spec=pltpu.PrefetchScalarGridSpec(
             num_scalar_prefetch=1,
-            grid=(2,),
-            in_specs=[full(mine.shape)] * 2,
+            grid=(1,),
+            in_specs=[ANY, ANY, full(theirs.shape)],
             out_specs=[pl.BlockSpec((VBLK, width), column), pl.BlockSpec((ABLK, width), column)],
         ),
-        compiler_params=pltpu.CompilerParams(vmem_limit_bytes=60 * MIB),
+        input_output_aliases={1: 0, 2: 1},
+        compiler_params=pltpu.CompilerParams(vmem_limit_bytes=16 * MIB),
         name="assemble",
-    )(place, mine, theirs)
+    )(place, video, audio, theirs)
 
 
 def gate_kernel(*refs):
@@ -499,15 +498,16 @@
 
     parts, w_self, w_rest = pack_video(place, video_k[0], video_v[0], video_q[0], out_weight)
     w_rest = lax.all_gather(w_rest, "batch", axis=0, tiled=False)
-    w_self = lax.all_gather(w_self, ("batch", "tower"), axis=0, tiled=False)
+    w_self = lax.all_gather(w_self, ("tower", "batch"), axis=0, tiled=False)
     query = exchange_towers(parts)
     own = query[:, :2]
     sibling = swap_core(own)
     near, far = hop(own), hop(sibling)
+
+    audio = exchange_towers(pack_audio(place, audio_q[0], audio_k[0], audio_v[0]))
+    acc, top, total, token = flash(query, [own, sibling], None, False)
+    near, far = gate(near, token), gate(far, token)
     third = far
-
-    audio = exchange_towers(pack_audio(place, audio_q[0], audio_k[0], audio_v[0]))
-    acc, stat, token = flash(query, [own, sibling], None, False)
     audio = gate(audio, token)
     crossed = cross(place, margins, query, audio, own, sibling, third)
     rest, up, down, up_later, down_later = project_cross(place, crossed, swap_core(crossed), w_rest)
@@ -518,23 +518,21 @@
 
     tokens = [token]
     for step in range(1, 4):
-        if step == 3:
-            acc = gate(acc, up_later, down_later)
-            up_later, down_later = shift_tower(up_later, 1), shift_tower(down_later, -1)
         now = [near, far, swap_core(near), swap_core(far)]
         near, far = hop(near), (hop(far) if step < 3 else None)
-        acc, stat, token = flash(query, now, (acc, stat), False)
+        acc, top, total, token = flash(query, now, (acc, top, total), False)
         tokens.append(token)
+        near = gate(near, tokens[step - 1])
         if step < 3:
-            near, far = gate(near, tokens[step - 1]), gate(far, tokens[step - 1])
-        else:
-            near = gate(near, tokens[step - 1], up_later, down_later)
-    video_self = flash(query, [near, swap_core(near)], (acc, stat), True)
+            far = gate(far, tokens[step - 1])
+    acc = gate(acc, up_later, down_later)
+    up_later, down_later = shift_tower(up_later, 1), shift_tower(down_later, -1)
+    video_self = flash(query, [near, swap_core(near)], (acc, top, total), True)
     base = (rest, up, down, up_later, down_later)
 
     self_all = exchange_towers(video_self.reshape(TOWERS, VBLK, GW))
-    mine, theirs = project_self(place, self_all, swap_core(self_all), w_self, base, gains)
-    video_out, audio_out = assemble(place, mine, swap_core(theirs))
+    video_out, audio_out, theirs = project_self(place, self_all, swap_core(self_all), w_self, base, gains)
+    video_out, audio_out = assemble(place, video_out, audio_out, swap_core(theirs))
     return (video_out[None], audio_out[None])
 
 

time: 206 us -> 193 us (0.937)
  blocking collectives: 30.9 us -> 19.5 us
  Pallas kernels: 71.8 us -> 65 us
  starting transfers between devices: 32.3 us -> 38.6 us
    all_to_all x2 -> x1, blocking collectives: 30.9 us -> 19.5 us  [exchange_towers(): lax.all_to_all(value, 'tower', split_axis=0, concat_axis=0, tiled=True)]
    all_to_all x1 -> x2, waiting for transfers between devices: 0.01 us -> 5.32 us  [exchange_towers(): lax.all_to_all(value, 'tower', split_axis=0, concat_axis=0, tiled=True)]
    pallas_call x2, Pallas kernels: 10.7 us -> 6.1 us  [the longest x1 4.77 us: project_self(): pl.pallas_call(project_self_kernel, out_shape=[jax.ShapeDtypeStruct((VBLK...]
    all_to_all x1 -> x2, starting transfers between devices: 3.6 us -> 7.05 us  [exchange_towers(): lax.all_to_all(value, 'tower', split_axis=0, concat_axis=0, tiled=True)]
    ppermute x4, waiting for transfers between devices: 29.8 us -> 26.4 us  [shift_tower(): lax.ppermute(value, 'tower', [(i, (i + step) % TOWERS) for i in range(TOW...]
    pallas_call x5, Pallas kernels: 41.2 us -> 39 us  [flash(): pl.pallas_call(functools.partial(flash_kernel, len(kvs), state is None, l...]
    ppermute x7, starting transfers between devices: 18.1 us -> 20.2 us  [hop(): lax.ppermute(value, 'ctx', [(i, (i + 2 - 4 * (i % 2)) % total) for i in r...]
    unnamed x43 -> x37, local copies, waits for them, and re-layouts: 8.88 us -> 10.7 us
  transfers between devices with their start and end apart: 25 -> 26, of which waited for: 6 -> 7; matrix products, arithmetic and copies ran while one was open for 2% -> 2% of each run, Pallas kernels for 28% -> 29%
where the time goes in v3:
time: 193 us; the launch traced here: 192 us
  Pallas kernels  65 us (34%)
  waiting for transfers between devices  40.8 us (21%)
  starting transfers between devices  38.6 us (20%)
  blocking collectives  19.5 us (10%)
  between operations  14.3 us (7%)
  local copies, waits for them, and re-layouts  11.4 us (6%)
  other arithmetic  2.86 us (1%)
    pallas_call x5, Pallas kernels, flash(): pl.pallas_call(functools.partial(flash_kernel, len(kvs), state is None, l...  39 us
    ppermute x4, waiting for transfers between devices, shift_tower(): lax.ppermute(value, 'tower', [(i, (i + step) % TOWERS) for i in range(TOW...  26.4 us
    ppermute x7, starting transfers between devices, hop(): lax.ppermute(value, 'ctx', [(i, (i + 2 - 4 * (i % 2)) % total) for i in r...  20.2 us
    all_to_all x1, blocking collectives, exchange_towers(): lax.all_to_all(value, 'tower', split_axis=0, concat_axis=0, tiled=True)  19.5 us
    unnamed x37, local copies, waits for them, and re-layouts  10.7 us
    ppermute x11, starting transfers between devices, swap_core(): return lax.ppermute(value, 'ctx', [(i, i ^ 1) for i in range(2 * CHIPS)])  7.5 us
    all_to_all x2, starting transfers between devices, exchange_towers(): lax.all_to_all(value, 'tower', split_axis=0, concat_axis=0, tiled=True)  7.05 us
    ppermute x7, waiting for transfers between devices, hop(): lax.ppermute(value, 'ctx', [(i, (i + 2 - 4 * (i % 2)) % total) for i in r...  6.83 us
  transfers between devices with their start and end apart: 26, of which 7 were waited for; matrix products, arithmetic and copies ran while one was open for 2% of the time, Pallas kernels for 29%

profile of v3, /device:TPU:1, one launch (start us, length us, event | category | flops | bytes accessed | tf_op | source)
XLA Modules:
  0.0 192.5 jit_solution(1386973625772747428)
XLA Ops:
  7.9 3.4 %pack_video.1 = (bf16[4,3,3,128,128]{4,3,2,1,0:T(8,128)(2,1)}, bf16[3,32,1536]{2,1,0:T(8,128)(2,1)}, bf16[2,3,32,1536]{3,2,1,0:T(8,128)(2,1)}) custom-call(s32[5]{0:T(128)} %stack.23.place, bf16[128,1536]{1,0:T(8,128)(2,1)} %bitcast.26, bf16[128,1536]{1,0:T(8,128)(2,1)} %bitcast.27, bf16[128,1536]{1,0:T(8,128)(2,1)} %bitcast.28, bf16[3,3,32,3072]{3,2,1,0:T(8,128)(2,1)} %w_ref.1), custom_call_target="tpu_custom_call" | custom-call | tf_op jit(solution)/shard_map/pack_video/pallas_call | solution.py:74
  12.1 19.5 %all_to_all.15.refs_0_.q_ref = bf16[4,3,3,128,128]{4,3,2,1,0:T(8,128)(2,1)S(1)} all-to-all(bf16[4,3,3,128,128]{4,3,2,1,0:T(8,128)(2,1)} %get-tuple-element.30), channel_id=1, replica_groups=mesh['batch'=4,'ctx'=16,'tower'=4] {'tower'}, dimensions={0} | all-to-all | bytes 2359296 | tf_op jit(solution)/shard_map/all_to_all | solution.py:471
  31.7 2.9 %collective-permute-start.1 = (bf16[4,2,3,128,128]{4,3,2,1,0:T(8,128)(2,1)S(1)}, bf16[4,2,3,128,128]{4,3,2,1,0:T(8,128)(2,1)}, u32[]{:S(2)}, u32[]{:S(2)}) collective-permute-start(bf16[4,2,3,128,128]{4,3,2,1,0:T(8,128)(2,1)S(1)} %slice.12.refs_1_.own), channel_id=1, source_target_pairs={{0,4},{4,0},{8,12},{12,8},{16,20},{20,16},{24,28},{28,24},{32,36},... | collective-permute-start | bytes 2359304 | tf_op jit(solution)/shard_map/ppermute | solution.py:488
  34.6 5.6 %collective-permute-start = (bf16[4,2,3,128,128]{4,3,2,1,0:T(8,128)(2,1)S(1)}, bf16[4,2,3,128,128]{4,3,2,1,0:T(8,128)(2,1)}, u32[]{:S(2)}, u32[]{:S(2)}) collective-permute-start(bf16[4,2,3,128,128]{4,3,2,1,0:T(8,128)(2,1)S(1)} %slice.12.refs_1_.own), channel_id=1, source_target_pairs={{0,8},{4,60},{8,16},{12,4},{16,24},{20,12},{24,32},{28,20},{32,40}... | collective-permute-start | bytes 2359304 | tf_op jit(solution)/shard_map/ppermute | solution.py:484
  42.2 3.5 %pack_audio.1 = bf16[4,576,384]{2,1,0:T(8,128)(2,1)} custom-call(s32[5]{0:T(128)} %stack.23.place, bf16[384,1536]{1,0:T(8,128)(2,1)} %bitcast.22, bf16[384,1536]{1,0:T(8,128)(2,1)} %bitcast.23, bf16[384,1536]{1,0:T(8,128)(2,1)} %bitcast.24), custom_call_target="tpu_custom_call" | custom-call | tf_op jit(solution)/shard_map/pack_audio/pallas_call | solution.py:137
  45.7 3.6 %all-to-all-start.1 = ((bf16[4,576,384]{2,1,0:T(8,128)(2,1)}), bf16[4,576,384]{2,1,0:T(8,128)(2,1)S(1)}, u32[]{:S(2)}, u32[]{:S(2)}) async-start(bf16[4,576,384]{2,1,0:T(8,128)(2,1)} %pack_audio.1), calls=%async_computation.1 | async-start | bytes 3538944 | tf_op jit(solution)/shard_map/all_to_all | solution.py:471
  49.3 5.3 %flash.5 = (f32[512,384]{1,0:T(8,128)}, f32[512,384]{1,0:T(8,128)}, f32[512,384]{1,0:T(8,128)}, f32[8,128]{1,0:T(8,128)}) custom-call(bf16[4,3,3,128,128]{4,3,2,1,0:T(8,128)(2,1)} %copy-done.6, bf16[4,2,3,128,128]{4,3,2,1,0:T(8,128)(2,1)} %copy-done.8, bf16[4,2,3,128,128]{4,3,2,1,0:T(8,128)(2,1)} %collective-permute-done.1.refs_2_.sibling), custom_call_target="tpu_custom_call" | custom-call | flops 1 | bytes 1 | tf_op jit(solution)/shard_map/flash/pallas_call | solution.py:219
  57.7 3.3 %collective-permute-start.9 = (bf16[4,2,3,128,128]{4,3,2,1,0:T(8,128)(2,1)}, bf16[4,2,3,128,128]{4,3,2,1,0:T(8,128)(2,1)}, u32[]{:S(2)}, u32[]{:S(2)}) collective-permute-start(bf16[4,2,3,128,128]{4,3,2,1,0:T(8,128)(2,1)} %gate.12.third.refs_2_), channel_id=1, source_target_pairs={{0,8},{4,60},{8,16},{12,4},{16,24},{20,12},{24,32},{28,20},{32,40}... | collective-permute-start | bytes 2359304 | tf_op jit(solution)/shard_map/ppermute | solution.py:484
  61.5 4.6 %collective-permute-done.2.refs_0_ = bf16[4,2,3,128,128]{4,3,2,1,0:T(8,128)(2,1)S(1)} collective-permute-done((bf16[4,2,3,128,128]{4,3,2,1,0:T(8,128)(2,1)}, bf16[4,2,3,128,128]{4,3,2,1,0:T(8,128)(2,1)S(1)}, u32[]{:S(2)}, u32[]{:S(2)}) %collective-permute-start.2) | collective-permute-done | bytes 786464 | tf_op jit(solution)/shard_map/ppermute | solution.py:484
  67.0 3.3 %collective-permute-start.3 = (bf16[4,2,3,128,128]{4,3,2,1,0:T(8,128)(2,1)}, bf16[4,2,3,128,128]{4,3,2,1,0:T(8,128)(2,1)S(1)}, u32[]{:S(2)}, u32[]{:S(2)}) collective-permute-start(bf16[4,2,3,128,128]{4,3,2,1,0:T(8,128)(2,1)} %gate.11.refs_1_), channel_id=1, source_target_pairs={{0,8},{4,60},{8,16},{12,4},{16,24},{20,12},{24,32},{28,20},{32,40}... | collective-permute-start | bytes 2359304 | tf_op jit(solution)/shard_map/ppermute | solution.py:484
  72.3 6.5 %cross.1.own = bf16[4,160,384]{2,1,0:T(8,128)(2,1)} custom-call(s32[5]{0:T(128)} %stack.23.place, s32[64,3]{1,0:T(8,128)} %bitcast.30, bf16[4,3,3,128,128]{4,3,2,1,0:T(8,128)(2,1)} %copy-done.6, bf16[4,576,384]{2,1,0:T(8,128)(2,1)} %gate.13.main.edge, bf16[4,576,384]{2,1,0:T(8,128)(2,1)} %gate.13.main.edge, bf16[4,2,3,128,128]{4,3,2,1,0:T(8,128)(2,1)} %copy-done.8, ...), custom_call_target="tpu_custom_call" | custom-call | flops 1 | bytes 1 | tf_op jit(solution)/shard_map/cross/pallas_call | solution.py:300
  78.8 2.8 %collective-permute-start.13 = (bf16[4,2,3,128,128]{4,3,2,1,0:T(8,128)(2,1)}, bf16[4,2,3,128,128]{4,3,2,1,0:T(8,128)(2,1)S(1)}, u32[]{:S(2)}, u32[]{:S(2)}) collective-permute-start(bf16[4,2,3,128,128]{4,3,2,1,0:T(8,128)(2,1)} %gate.16.refs_2_), channel_id=1, source_target_pairs={{0,8},{4,60},{8,16},{12,4},{16,24},{20,12},{24,32},{28,20},{32,40}... | collective-permute-start | bytes 2359304 | tf_op jit(solution)/shard_map/ppermute | solution.py:484
  82.4 6.4 %project_cross.1 = (bf16[320,1536]{1,0:T(8,128)(2,1)}, bf16[320,1536]{1,0:T(8,128)(2,1)}, bf16[320,1536]{1,0:T(8,128)(2,1)}, bf16[160,1536]{1,0:T(8,128)(2,1)}, bf16[160,1536]{1,0:T(8,128)(2,1)}) custom-call(s32[5]{0:T(128)} %stack.23.place, bf16[4,160,384]{2,1,0:T(8,128)(2,1)} %cross.1.own, bf16[4,160,384]{2,1,0:T(8,128)(2,1)} %copy-done.16, ...), custom_call_target="tpu_custom_call" | custom-call | flops 1 | bytes 1 | tf_op jit(solution)/shard_map/project_cross/pallas_call | solution.py:350
  90.5 9.2 %flash.6 = (f32[512,384]{1,0:T(8,128)}, f32[512,384]{1,0:T(8,128)}, f32[512,384]{1,0:T(8,128)}, f32[8,128]{1,0:T(8,128)}) custom-call(bf16[4,3,3,128,128]{4,3,2,1,0:T(8,128)(2,1)} %copy-done.6, bf16[4,2,3,128,128]{4,3,2,1,0:T(8,128)(2,1)} %gate.10.refs_1_, bf16[4,2,3,128,128]{4,3,2,1,0:T(8,128)(2,1)} %gate.12.third.refs_2_, ...), custom_call_target="tpu_custom_call" | custom-call | flops 1 | bytes 1 | tf_op jit(solution)/shard_map/flash/pallas_call | solution.py:219
  100.6 2.4 %collective-permute-start.8 = (bf16[4,2,3,128,128]{4,3,2,1,0:T(8,128)(2,1)}, bf16[4,2,3,128,128]{4,3,2,1,0:T(8,128)(2,1)}, u32[]{:S(2)}, u32[]{:S(2)}) collective-permute-start(bf16[4,2,3,128,128]{4,3,2,1,0:T(8,128)(2,1)} %gate.15.refs_1_), channel_id=1, source_target_pairs={{0,8},{4,60},{8,16},{12,4},{16,24},{20,12},{24,32},{28,20},{32,40}... | collective-permute-start | bytes 2359304 | tf_op jit(solution)/shard_map/ppermute | solution.py:484
  104.4 9.2 %flash.7 = (f32[512,384]{1,0:T(8,128)}, f32[512,384]{1,0:T(8,128)}, f32[512,384]{1,0:T(8,128)}, f32[8,128]{1,0:T(8,128)}) custom-call(bf16[4,3,3,128,128]{4,3,2,1,0:T(8,128)(2,1)} %copy-done.6, bf16[4,2,3,128,128]{4,3,2,1,0:T(8,128)(2,1)} %gate.11.refs_1_, bf16[4,2,3,128,128]{4,3,2,1,0:T(8,128)(2,1)} %gate.16.refs_2_, ...), custom_call_target="tpu_custom_call" | custom-call | flops 1 | bytes 1 | tf_op jit(solution)/shard_map/flash/pallas_call | solution.py:219
  114.5 17.2 %collective-permute-done.17.refs_2_ = bf16[320,1536]{1,0:T(8,128)(2,1)S(1)} collective-permute-done((bf16[320,1536]{1,0:T(8,128)(2,1)}, bf16[320,1536]{1,0:T(8,128)(2,1)S(1)}, u32[]{:S(2)}, u32[]{:S(2)}) %collective-permute-start.17) | collective-permute-done | bytes 983072 | tf_op jit(solution)/shard_map/ppermute | solution.py:479
  135.7 9.2 %flash.8 = (f32[512,384]{1,0:T(8,128)}, f32[512,384]{1,0:T(8,128)}, f32[512,384]{1,0:T(8,128)}, f32[8,128]{1,0:T(8,128)}) custom-call(bf16[4,3,3,128,128]{4,3,2,1,0:T(8,128)(2,1)} %copy-done.6, bf16[4,2,3,128,128]{4,3,2,1,0:T(8,128)(2,1)} %gate.15.refs_1_, bf16[4,2,3,128,128]{4,3,2,1,0:T(8,128)(2,1)} %gate.18.refs_2_, ...), custom_call_target="tpu_custom_call" | custom-call | flops 1 | bytes 1 | tf_op jit(solution)/shard_map/flash/pallas_call | solution.py:219
  145.0 6.0 %flash.9 = bf16[512,384]{1,0:T(8,128)(2,1)} custom-call(bf16[4,3,3,128,128]{4,3,2,1,0:T(8,128)(2,1)} %copy-done.6, bf16[4,2,3,128,128]{4,3,2,1,0:T(8,128)(2,1)} %gate.17.refs_1_, bf16[4,2,3,128,128]{4,3,2,1,0:T(8,128)(2,1)} %collective-permute-done.12.refs_2_, f32[512,384]{1,0:T(8,128)} %gate.19.refs_3_, f32[512,384]{1,0:T(8,128)} %get-tuple-element.50.refs_4_, ...), custom_call_target="tpu_custom_call" | custom-call | flops 1 | bytes 1 | tf_op jit(solution)/shard_map/flash/pallas_call | solution.py:219
  151.0 3.5 %all-to-all-start.2 = ((bf16[4,128,384]{2,1,0:T(8,128)(2,1)}), bf16[4,128,384]{2,1,0:T(8,128)(2,1)S(1)}, u32[]{:S(2)}, u32[]{:S(2)}) async-start(bf16[4,128,384]{2,1,0:T(8,128)(2,1)} %bitcast.21), calls=%async_computation.2 | async-start | bytes 786432 | tf_op jit(solution)/shard_map/all_to_all | solution.py:471
  154.5 2.6 %collective-permute-start.20 = (bf16[160,1536]{1,0:T(8,128)(2,1)}, bf16[160,1536]{1,0:T(8,128)(2,1)}, u32[]{:S(2)}, u32[]{:S(2)}) collective-permute-start(bf16[160,1536]{1,0:T(8,128)(2,1)} %add_convert_fusion.refs_2_), channel_id=1, source_target_pairs={{0,3},{1,0},{2,1},{3,2},{4,7},{5,4},{6,5},{7,6},{8,11},{9,8},{10,9... | collective-permute-start | bytes 1474568 | tf_op jit(solution)/shard_map/ppermute | solution.py:479
  157.1 5.3 %all-to-all-done.2.own = bf16[4,128,384]{2,1,0:T(8,128)(2,1)S(1)} async-done(((bf16[4,128,384]{2,1,0:T(8,128)(2,1)}), bf16[4,128,384]{2,1,0:T(8,128)(2,1)S(1)}, u32[]{:S(2)}, u32[]{:S(2)}) %all-to-all-start.2) | async-done | bytes 393248 | tf_op jit(solution)/shard_map/all_to_all | solution.py:471
  164.1 7.5 %collective-permute-done.20.refs_4_ = bf16[160,1536]{1,0:T(8,128)(2,1)} collective-permute-done((bf16[160,1536]{1,0:T(8,128)(2,1)}, bf16[160,1536]{1,0:T(8,128)(2,1)}, u32[]{:S(2)}, u32[]{:S(2)}) %collective-permute-start.20) | collective-permute-done | bytes 491552 | tf_op jit(solution)/shard_map/ppermute | solution.py:479
  177.4 4.8 %project_self.1 = (bf16[128,3072]{1,0:T(8,128)(2,1)}, bf16[24,3072]{1,0:T(8,128)(2,1)}, bf16[160,1536]{1,0:T(8,128)(2,1)S(1)}) custom-call(s32[5]{0:T(128)S(1)} %copy-done.4, bf16[4,128,384]{2,1,0:T(8,128)(2,1)S(1)} %all-to-all-done.2.own, bf16[4,128,384]{2,1,0:T(8,128)(2,1)S(1)} %copy-done.3, bf16[16,3,32,1536]{3,2,1,0:T(8,128)(2,1)S(1)} %bitcast.18, ...), custom_call_target="tpu_custom_call" | custom-call | flops 1 | bytes 1 | tf_op jit(solution)/shard_map/project_self/pallas_call | solution.py:403
  (93 shorter events, 30.4 us)
Async XLA Ops:
  7.2 74.5 %all-gather.5.cloned.1.call-start = ((), (), s32[]{:S(2)}) async-start(), calls=%async_computation.3 | async-start | bytes 2949120 | tf_op jit(solution)/shard_map/all_gather | solution.py:500
  11.4 162.6 %all-gather.7.cloned.1.call-start = ((), (), s32[]{:S(2)}) async-start(), calls=%async_computation.4 | async-start | bytes 5013504 | tf_op jit(solution)/shard_map/all_gather | solution.py:501
  31.7 8.5 %collective-permute-start.1 = (bf16[4,2,3,128,128]{4,3,2,1,0:T(8,128)(2,1)S(1)}, bf16[4,2,3,128,128]{4,3,2,1,0:T(8,128)(2,1)}, u32[]{:S(2)}, u32[]{:S(2)}) collective-permute-start(bf16[4,2,3,128,128]{4,3,2,1,0:T(8,128)(2,1)S(1)} %slice.12.refs_1_.own), channel_id=1, source_target_pairs={{0,4},{4,0},{8,12},{12,8},{16,20},{20,16},{24,28},{28,24},{32,36},... | collective-permute-start | bytes 2359304 | tf_op jit(solution)/shard_map/ppermute | solution.py:488
  34.6 20.1 %collective-permute-start = (bf16[4,2,3,128,128]{4,3,2,1,0:T(8,128)(2,1)S(1)}, bf16[4,2,3,128,128]{4,3,2,1,0:T(8,128)(2,1)}, u32[]{:S(2)}, u32[]{:S(2)}) collective-permute-start(bf16[4,2,3,128,128]{4,3,2,1,0:T(8,128)(2,1)S(1)} %slice.12.refs_1_.own), channel_id=1, source_target_pairs={{0,8},{4,60},{8,16},{12,4},{16,24},{20,12},{24,32},{28,20},{32,40}... | collective-permute-start | bytes 2359304 | tf_op jit(solution)/shard_map/ppermute | solution.py:484
  40.2 17.5 %collective-permute-start.4 = (bf16[4,2,3,128,128]{4,3,2,1,0:T(8,128)(2,1)}, bf16[4,2,3,128,128]{4,3,2,1,0:T(8,128)(2,1)}, u32[]{:S(2)}, u32[]{:S(2)}) collective-permute-start(bf16[4,2,3,128,128]{4,3,2,1,0:T(8,128)(2,1)} %collective-permute-done.1.refs_2_.sibling), channel_id=1, source_target_pairs={{0,8},{4,60},{8,16},{12,4},{16,24},{20,12},{24,32},{28,20},{32,40}... | collective-permute-start | bytes 2359304 | tf_op jit(solution)/shard_map/ppermute | solution.py:484
  45.7 25.2 %all-to-all-start.1 = ((bf16[4,576,384]{2,1,0:T(8,128)(2,1)}), bf16[4,576,384]{2,1,0:T(8,128)(2,1)S(1)}, u32[]{:S(2)}, u32[]{:S(2)}) async-start(bf16[4,576,384]{2,1,0:T(8,128)(2,1)} %pack_audio.1), calls=%async_computation.1 | async-start | bytes 3538944 | tf_op jit(solution)/shard_map/all_to_all | solution.py:471
  54.7 11.4 %collective-permute-start.2 = (bf16[4,2,3,128,128]{4,3,2,1,0:T(8,128)(2,1)}, bf16[4,2,3,128,128]{4,3,2,1,0:T(8,128)(2,1)S(1)}, u32[]{:S(2)}, u32[]{:S(2)}) collective-permute-start(bf16[4,2,3,128,128]{4,3,2,1,0:T(8,128)(2,1)} %gate.10.refs_1_), channel_id=1, source_target_pairs={{0,8},{4,60},{8,16},{12,4},{16,24},{20,12},{24,32},{28,20},{32,40}... | collective-permute-start | bytes 2359304 | tf_op jit(solution)/shard_map/ppermute | solution.py:484
  57.7 21.2 %collective-permute-start.9 = (bf16[4,2,3,128,128]{4,3,2,1,0:T(8,128)(2,1)}, bf16[4,2,3,128,128]{4,3,2,1,0:T(8,128)(2,1)}, u32[]{:S(2)}, u32[]{:S(2)}) collective-permute-start(bf16[4,2,3,128,128]{4,3,2,1,0:T(8,128)(2,1)} %gate.12.third.refs_2_), channel_id=1, source_target_pairs={{0,8},{4,60},{8,16},{12,4},{16,24},{20,12},{24,32},{28,20},{32,40}... | collective-permute-start | bytes 2359304 | tf_op jit(solution)/shard_map/ppermute | solution.py:484
  61.0 28.9 %collective-permute-start.5 = (bf16[4,2,3,128,128]{4,3,2,1,0:T(8,128)(2,1)}, bf16[4,2,3,128,128]{4,3,2,1,0:T(8,128)(2,1)}, u32[]{:S(2)}, u32[]{:S(2)}) collective-permute-start(bf16[4,2,3,128,128]{4,3,2,1,0:T(8,128)(2,1)} %gate.10.refs_1_), channel_id=1, source_target_pairs={{0,4},{4,0},{8,12},{12,8},{16,20},{20,16},{24,28},{28,24},{32,36},... | collective-permute-start | bytes 2359304 | tf_op jit(solution)/shard_map/ppermute | solution.py:488
  61.0 29.0 %collective-permute-start.6 = (bf16[4,2,3,128,128]{4,3,2,1,0:T(8,128)(2,1)}, bf16[4,2,3,128,128]{4,3,2,1,0:T(8,128)(2,1)}, u32[]{:S(2)}, u32[]{:S(2)}) collective-permute-start(bf16[4,2,3,128,128]{4,3,2,1,0:T(8,128)(2,1)} %gate.12.third.refs_2_), channel_id=1, source_target_pairs={{0,4},{4,0},{8,12},{12,8},{16,20},{20,16},{24,28},{28,24},{32,36},... | collective-permute-start | bytes 2359304 | tf_op jit(solution)/shard_map/ppermute | solution.py:488
  67.0 32.7 %collective-permute-start.3 = (bf16[4,2,3,128,128]{4,3,2,1,0:T(8,128)(2,1)}, bf16[4,2,3,128,128]{4,3,2,1,0:T(8,128)(2,1)S(1)}, u32[]{:S(2)}, u32[]{:S(2)}) collective-permute-start(bf16[4,2,3,128,128]{4,3,2,1,0:T(8,128)(2,1)} %gate.11.refs_1_), channel_id=1, source_target_pairs={{0,8},{4,60},{8,16},{12,4},{16,24},{20,12},{24,32},{28,20},{32,40}... | collective-permute-start | bytes 2359304 | tf_op jit(solution)/shard_map/ppermute | solution.py:484
  78.8 24.2 %collective-permute-start.13 = (bf16[4,2,3,128,128]{4,3,2,1,0:T(8,128)(2,1)}, bf16[4,2,3,128,128]{4,3,2,1,0:T(8,128)(2,1)S(1)}, u32[]{:S(2)}, u32[]{:S(2)}) collective-permute-start(bf16[4,2,3,128,128]{4,3,2,1,0:T(8,128)(2,1)} %gate.16.refs_2_), channel_id=1, source_target_pairs={{0,8},{4,60},{8,16},{12,4},{16,24},{20,12},{24,32},{28,20},{32,40}... | collective-permute-start | bytes 2359304 | tf_op jit(solution)/shard_map/ppermute | solution.py:484
  88.8 42.8 %collective-permute-start.17 = (bf16[320,1536]{1,0:T(8,128)(2,1)}, bf16[320,1536]{1,0:T(8,128)(2,1)S(1)}, u32[]{:S(2)}, u32[]{:S(2)}) collective-permute-start(bf16[320,1536]{1,0:T(8,128)(2,1)} %get-tuple-element.49), channel_id=1, source_target_pairs={{0,3},{1,0},{2,1},{3,2},{4,7},{5,4},{6,5},{7,6},{8,11},{9,8},{10,9... | collective-permute-start | bytes 2949128 | tf_op jit(solution)/shard_map/ppermute | solution.py:479
  90.0 14.0 %collective-permute-start.10 = (bf16[4,2,3,128,128]{4,3,2,1,0:T(8,128)(2,1)S(1)}, bf16[4,2,3,128,128]{4,3,2,1,0:T(8,128)(2,1)}, u32[]{:S(2)}, u32[]{:S(2)}) collective-permute-start(bf16[4,2,3,128,128]{4,3,2,1,0:T(8,128)(2,1)S(1)} %copy-done.12), channel_id=1, source_target_pairs={{0,4},{4,0},{8,12},{12,8},{16,20},{20,16},{24,28},{28,24},{32,36},... | collective-permute-start | bytes 2359304 | tf_op jit(solution)/shard_map/ppermute | solution.py:488
  90.0 14.0 %collective-permute-start.11 = (bf16[4,2,3,128,128]{4,3,2,1,0:T(8,128)(2,1)}, bf16[4,2,3,128,128]{4,3,2,1,0:T(8,128)(2,1)}, u32[]{:S(2)}, u32[]{:S(2)}) collective-permute-start(bf16[4,2,3,128,128]{4,3,2,1,0:T(8,128)(2,1)} %gate.16.refs_2_), channel_id=1, source_target_pairs={{0,4},{4,0},{8,12},{12,8},{16,20},{20,16},{24,28},{28,24},{32,36},... | collective-permute-start | bytes 2359304 | tf_op jit(solution)/shard_map/ppermute | solution.py:488
  100.6 13.1 %collective-permute-start.8 = (bf16[4,2,3,128,128]{4,3,2,1,0:T(8,128)(2,1)}, bf16[4,2,3,128,128]{4,3,2,1,0:T(8,128)(2,1)}, u32[]{:S(2)}, u32[]{:S(2)}) collective-permute-start(bf16[4,2,3,128,128]{4,3,2,1,0:T(8,128)(2,1)} %gate.15.refs_1_), channel_id=1, source_target_pairs={{0,8},{4,60},{8,16},{12,4},{16,24},{20,12},{24,32},{28,20},{32,40}... | collective-permute-start | bytes 2359304 | tf_op jit(solution)/shard_map/ppermute | solution.py:484
  103.0 30.6 %collective-permute-start.16 = (bf16[320,1536]{1,0:T(8,128)(2,1)}, bf16[320,1536]{1,0:T(8,128)(2,1)S(1)}, u32[]{:S(2)}, u32[]{:S(2)}) collective-permute-start(bf16[320,1536]{1,0:T(8,128)(2,1)} %get-tuple-element.47), channel_id=1, source_target_pairs={{0,1},{1,2},{2,3},{3,0},{4,5},{5,6},{6,7},{7,4},{8,9},{9,10},{10,1... | collective-permute-start | bytes 2949128 | tf_op jit(solution)/shard_map/ppermute | solution.py:479
  103.9 30.6 %collective-permute-start.14 = (bf16[4,2,3,128,128]{4,3,2,1,0:T(8,128)(2,1)}, bf16[4,2,3,128,128]{4,3,2,1,0:T(8,128)(2,1)S(1)}, u32[]{:S(2)}, u32[]{:S(2)}) collective-permute-start(bf16[4,2,3,128,128]{4,3,2,1,0:T(8,128)(2,1)} %gate.15.refs_1_), channel_id=1, source_target_pairs={{0,4},{4,0},{8,12},{12,8},{16,20},{20,16},{24,28},{28,24},{32,36},... | collective-permute-start | bytes 2359304 | tf_op jit(solution)/shard_map/ppermute | solution.py:488
  103.9 30.6 %collective-permute-start.15 = (bf16[4,2,3,128,128]{4,3,2,1,0:T(8,128)(2,1)}, bf16[4,2,3,128,128]{4,3,2,1,0:T(8,128)(2,1)S(1)}, u32[]{:S(2)}, u32[]{:S(2)}) collective-permute-start(bf16[4,2,3,128,128]{4,3,2,1,0:T(8,128)(2,1)} %gate.18.refs_2_), channel_id=1, source_target_pairs={{0,4},{4,0},{8,12},{12,8},{16,20},{20,16},{24,28},{28,24},{32,36},... | collective-permute-start | bytes 2359304 | tf_op jit(solution)/shard_map/ppermute | solution.py:488
  113.7 31.3 %collective-permute-start.12 = (bf16[4,2,3,128,128]{4,3,2,1,0:T(8,128)(2,1)}, bf16[4,2,3,128,128]{4,3,2,1,0:T(8,128)(2,1)}, u32[]{:S(2)}, u32[]{:S(2)}) collective-permute-start(bf16[4,2,3,128,128]{4,3,2,1,0:T(8,128)(2,1)} %gate.17.refs_1_), channel_id=1, source_target_pairs={{0,4},{4,0},{8,12},{12,8},{16,20},{20,16},{24,28},{28,24},{32,36},... | collective-permute-start | bytes 2359304 | tf_op jit(solution)/shard_map/ppermute | solution.py:488
  151.0 11.4 %all-to-all-start.2 = ((bf16[4,128,384]{2,1,0:T(8,128)(2,1)}), bf16[4,128,384]{2,1,0:T(8,128)(2,1)S(1)}, u32[]{:S(2)}, u32[]{:S(2)}) async-start(bf16[4,128,384]{2,1,0:T(8,128)(2,1)} %bitcast.21), calls=%async_computation.2 | async-start | bytes 786432 | tf_op jit(solution)/shard_map/all_to_all | solution.py:471
  154.5 17.1 %collective-permute-start.20 = (bf16[160,1536]{1,0:T(8,128)(2,1)}, bf16[160,1536]{1,0:T(8,128)(2,1)}, u32[]{:S(2)}, u32[]{:S(2)}) collective-permute-start(bf16[160,1536]{1,0:T(8,128)(2,1)} %add_convert_fusion.refs_2_), channel_id=1, source_target_pairs={{0,3},{1,0},{2,1},{3,2},{4,7},{5,4},{6,5},{7,6},{8,11},{9,8},{10,9... | collective-permute-start | bytes 1474568 | tf_op jit(solution)/shard_map/ppermute | solution.py:479
  157.1 16.1 %collective-permute-start.19 = (bf16[160,1536]{1,0:T(8,128)(2,1)}, bf16[160,1536]{1,0:T(8,128)(2,1)}, u32[]{:S(2)}, u32[]{:S(2)}) collective-permute-start(bf16[160,1536]{1,0:T(8,128)(2,1)} %add_convert_fusion.1.refs_1_), channel_id=1, source_target_pairs={{0,1},{1,2},{2,3},{3,0},{4,5},{5,6},{6,7},{7,4},{8,9},{9,10},{10,1... | collective-permute-start | bytes 1474568 | tf_op jit(solution)/shard_map/ppermute | solution.py:479
  162.4 10.8 %collective-permute-start.18 = (bf16[4,128,384]{2,1,0:T(8,128)(2,1)S(1)}, bf16[4,128,384]{2,1,0:T(8,128)(2,1)S(1)}, u32[]{:S(2)}, u32[]{:S(2)}) collective-permute-start(bf16[4,128,384]{2,1,0:T(8,128)(2,1)S(1)} %all-to-all-done.2.own), channel_id=1, source_target_pairs={{0,4},{4,0},{8,12},{12,8},{16,20},{20,16},{24,28},{28,24},{32,36},... | collective-permute-start | bytes 1179656 | tf_op jit(solution)/shard_map/ppermute | solution.py:488
  (20 other events, 167.8 us)
Sparse Core Ops, SparseCore 0:
  11.5 39.3 all-gather.4
  53.4 76.8 all-gather.6

commit v4 on v3

--- a/solution.py
+++ b/solution.py
@@ -173,32 +173,36 @@
     else:
         acc_in, top_in, total_in = rest[:3]
         outs = rest[3:]
+    size = 2 * VBLK
+    tiles = [slice(i * size, (i + 1) * size) for i in range(2)]
     query = rows_of(q_ref, 0)
-    scores = [nn_dot(query, keys_of(kv)) for kv in kv_refs]
-    top = functools.reduce(jnp.maximum, [t for s in scores for t in lane_tiles(s)])
-    top = jnp.max(top, axis=1, keepdims=True) * SCALE2
-    if first:
-        top = jnp.broadcast_to(top, (TOWERS * VBLK, HD))
-        acc = total = None
-    else:
-        top = jnp.maximum(top, top_in[...])
-        factor = jnp.exp2(top_in[...] - top)
-        acc = acc_in[...] * factor
-        total = total_in[...] * factor
-    wide = jnp.concatenate([top] * TOWERS, axis=1)
-    for s, kv in zip(scores, kv_refs):
-        weights = jnp.exp2(s * SCALE2 - wide)
-        part = functools.reduce(jnp.add, lane_tiles(weights))
-        total = part if total is None else total + part
-        part = nn_dot(weights.astype(jnp.bfloat16), rows_of(kv, 1))
-        acc = part if acc is None else acc + part
-    if last:
-        outs[0][...] = (acc / jnp.sum(total, axis=1, keepdims=True)).astype(jnp.bfloat16)
-    else:
-        outs[0][...] = acc
-        outs[1][...] = top
-        outs[2][...] = total
-        outs[3][...] = total[:8]
+    keys = [keys_of(kv) for kv in kv_refs]
+    all_scores = [[nn_dot(query[rows], k) for k in keys] for rows in tiles]
+    for rows, scores in zip(tiles, all_scores):
+        top = functools.reduce(jnp.maximum, [t for s in scores for t in lane_tiles(s)])
+        top = jnp.max(top, axis=1, keepdims=True) * SCALE2
+        if first:
+            top = jnp.broadcast_to(top, (size, HD))
+            acc = total = None
+        else:
+            top = jnp.maximum(top, top_in[rows])
+            factor = jnp.exp2(top_in[rows] - top)
+            acc = acc_in[rows] * factor
+            total = total_in[rows] * factor
+        wide = jnp.concatenate([top] * TOWERS, axis=1)
+        for s, kv in zip(scores, kv_refs):
+            weights = jnp.exp2(s * SCALE2 - wide)
+            part = functools.reduce(jnp.add, lane_tiles(weights))
+            total = part if total is None else total + part
+            part = nn_dot(weights.astype(jnp.bfloat16), rows_of(kv, 1))
+            acc = part if acc is None else acc + part
+        if last:
+            outs[0][rows] = (acc / jnp.sum(total, axis=1, keepdims=True)).astype(jnp.bfloat16)
+        else:
+            outs[0][rows] = acc
+            outs[1][rows] = top
+            outs[2][rows] = total
+            outs[3][...] = total[:8]
 
 
 QUERY = pl.BlockSpec((TOWERS, 1, 1, VBLK, HD), lambda h, *_: (0, 2, h, 0, 0))
@@ -375,7 +379,7 @@
     )
     w = jnp.concatenate(
         [
-            weight_rows([functools.partial(lambda b, h: w_ref[t * 4 + b, h], b) for b in range(4)])
+            weight_rows([functools.partial(lambda b, h: w_ref[b * TOWERS + t, h], b) for b in range(4)])
             for t in range(TOWERS)
         ],
         axis=0,
@@ -498,7 +502,7 @@
 
     parts, w_self, w_rest = pack_video(place, video_k[0], video_v[0], video_q[0], out_weight)
     w_rest = lax.all_gather(w_rest, "batch", axis=0, tiled=False)
-    w_self = lax.all_gather(w_self, ("tower", "batch"), axis=0, tiled=False)
+    w_self = lax.all_gather(w_self, "tower", axis=0, tiled=False)
     query = exchange_towers(parts)
     own = query[:, :2]
     sibling = swap_core(own)
@@ -508,20 +512,23 @@
     acc, top, total, token = flash(query, [own, sibling], None, False)
     near, far = gate(near, token), gate(far, token)
     third = far
-    audio = gate(audio, token)
-    crossed = cross(place, margins, query, audio, own, sibling, third)
-    rest, up, down, up_later, down_later = project_cross(place, crossed, swap_core(crossed), w_rest)
-    acc = gate(acc, rest)
-    up, down = shift_tower(up, 1), shift_tower(down, -1)
-    up_later = add(up_later, up[:BOTH])
-    down_later = add(down_later, down[BOTH:])
-
     tokens = [token]
     for step in range(1, 4):
         now = [near, far, swap_core(near), swap_core(far)]
         near, far = hop(near), (hop(far) if step < 3 else None)
         acc, top, total, token = flash(query, now, (acc, top, total), False)
         tokens.append(token)
+        if step == 1:
+            crossed = cross(place, margins, query, gate(audio, token), own, sibling, third)
+            rest, up, down, up_later, down_later = project_cross(
+                place, crossed, swap_core(crossed), w_rest
+            )
+            acc = gate(acc, rest)
+            w_self = lax.all_gather(gate(w_self, token), "batch", axis=0, tiled=False)
+            w_self = w_self.reshape((16,) + w_self.shape[2:])
+            up, down = shift_tower(up, 1), shift_tower(down, -1)
+            up_later = add(up_later, up[:BOTH])
+            down_later = add(down_later, down[BOTH:])
         near = gate(near, tokens[step - 1])
         if step < 3:
             far = gate(far, tokens[step - 1])

time: 193 us -> 209 us (1.083)
  starting transfers between devices: 38.6 us -> 51.7 us
  waiting for transfers between devices: 40.8 us -> 49.6 us
  Pallas kernels: 65 us -> 56.9 us
    ppermute x11, starting transfers between devices: 7.5 us -> 21.7 us  [swap_core(): return lax.ppermute(value, 'ctx', [(i, i ^ 1) for i in range(2 * CHIPS)])]
    ppermute x7, waiting for transfers between devices: 6.83 us -> 18.5 us  [hop(): lax.ppermute(value, 'ctx', [(i, (i + 2 - 4 * (i % 2)) % total) for i in r...]
    ppermute x4, waiting for transfers between devices: 26.4 us -> 15.7 us  [shift_tower(): lax.ppermute(value, 'tower', [(i, (i + step) % TOWERS) for i in range(TOW...]
    pallas_call x5, Pallas kernels: 39 us -> 30.8 us  [flash(): pl.pallas_call(functools.partial(flash_kernel, len(kvs), state is None, l...]
    all_to_all x2, waiting for transfers between devices: 5.32 us -> 11 us  [exchange_towers(): lax.all_to_all(value, 'tower', split_axis=0, concat_axis=0, tiled=True)]
    ppermute x11, waiting for transfers between devices: 1.52 us -> 3.63 us  [swap_core(): return lax.ppermute(value, 'ctx', [(i, i ^ 1) for i in range(2 * CHIPS)])]
    unnamed x37 -> x45, local copies, waits for them, and re-layouts: 10.7 us -> 12.6 us
  transfers between devices with their start and end apart: 26 -> 27, of which waited for: 7 -> 12; matrix products, arithmetic and copies ran while one was open for 2% -> 2% of each run, Pallas kernels for 29% -> 23%
where the time goes in v4:
time: 209 us; the launch traced here: 208 us
  Pallas kernels  56.9 us (27%)
  starting transfers between devices  51.7 us (25%)
  waiting for transfers between devices  49.6 us (24%)
  blocking collectives  19.5 us (9%)
  between operations  14 us (7%)
  local copies, waits for them, and re-layouts  13.3 us (6%)
  other arithmetic  2.82 us (1%)
    pallas_call x5, Pallas kernels, flash(): pl.pallas_call(functools.partial(flash_kernel, len(kvs), state is None, l...  30.8 us
    ppermute x11, starting transfers between devices, swap_core(): return lax.ppermute(value, 'ctx', [(i, i ^ 1) for i in range(2 * CHIPS)])  21.7 us
    all_to_all x1, blocking collectives, exchange_towers(): lax.all_to_all(value, 'tower', split_axis=0, concat_axis=0, tiled=True)  19.5 us
    ppermute x7, starting transfers between devices, hop(): lax.ppermute(value, 'ctx', [(i, (i + 2 - 4 * (i % 2)) % total) for i in r...  18.5 us
    ppermute x7, waiting for transfers between devices, hop(): lax.ppermute(value, 'ctx', [(i, (i + 2 - 4 * (i % 2)) % total) for i in r...  18.5 us
    ppermute x4, waiting for transfers between devices, shift_tower(): lax.ppermute(value, 'tower', [(i, (i + step) % TOWERS) for i in range(TOW...  15.7 us
    unnamed x45, local copies, waits for them, and re-layouts  12.6 us
    all_to_all x2, waiting for transfers between devices, exchange_towers(): lax.all_to_all(value, 'tower', split_axis=0, concat_axis=0, tiled=True)  11 us
  transfers between devices with their start and end apart: 27, of which 12 were waited for; matrix products, arithmetic and copies ran while one was open for 2% of the time, Pallas kernels for 23%

profile of v4, /device:TPU:1, one launch (start us, length us, event | category | flops | bytes accessed | tf_op | source)
XLA Modules:
  0.0 207.8 jit_solution(2843624073158009272)
XLA Ops:
  7.9 3.4 %pack_video.1 = (bf16[4,3,3,128,128]{4,3,2,1,0:T(8,128)(2,1)}, bf16[3,32,1536]{2,1,0:T(8,128)(2,1)}, bf16[2,3,32,1536]{3,2,1,0:T(8,128)(2,1)}) custom-call(s32[5]{0:T(128)} %stack.23.place, bf16[128,1536]{1,0:T(8,128)(2,1)} %bitcast.26, bf16[128,1536]{1,0:T(8,128)(2,1)} %bitcast.27, bf16[128,1536]{1,0:T(8,128)(2,1)} %bitcast.28, bf16[3,3,32,3072]{3,2,1,0:T(8,128)(2,1)} %w_ref.1), custom_call_target="tpu_custom_call" | custom-call | tf_op jit(solution)/shard_map/pack_video/pallas_call | solution.py:74
  12.1 19.5 %all_to_all.15.refs_0_.q_ref = bf16[4,3,3,128,128]{4,3,2,1,0:T(8,128)(2,1)S(1)} all-to-all(bf16[4,3,3,128,128]{4,3,2,1,0:T(8,128)(2,1)} %get-tuple-element.30), channel_id=1, replica_groups=mesh['batch'=4,'ctx'=16,'tower'=4] {'tower'}, dimensions={0} | all-to-all | bytes 2359296 | tf_op jit(solution)/shard_map/all_to_all | solution.py:475
  31.7 7.3 %collective-permute-start.1 = (bf16[4,2,3,128,128]{4,3,2,1,0:T(8,128)(2,1)S(1)}, bf16[4,2,3,128,128]{4,3,2,1,0:T(8,128)(2,1)}, u32[]{:S(2)}, u32[]{:S(2)}) collective-permute-start(bf16[4,2,3,128,128]{4,3,2,1,0:T(8,128)(2,1)S(1)} %slice.12.refs_1_.own), channel_id=1, source_target_pairs={{0,4},{4,0},{8,12},{12,8},{16,20},{20,16},{24,28},{28,24},{32,36},... | collective-permute-start | bytes 2359304 | tf_op jit(solution)/shard_map/ppermute | solution.py:492
  39.0 7.4 %collective-permute-start = (bf16[4,2,3,128,128]{4,3,2,1,0:T(8,128)(2,1)S(1)}, bf16[4,2,3,128,128]{4,3,2,1,0:T(8,128)(2,1)S(1)}, u32[]{:S(2)}, u32[]{:S(2)}) collective-permute-start(bf16[4,2,3,128,128]{4,3,2,1,0:T(8,128)(2,1)S(1)} %slice.12.refs_1_.own), channel_id=1, source_target_pairs={{0,8},{4,60},{8,16},{12,4},{16,24},{20,12},{24,32},{28,20},{32,40}... | collective-permute-start | bytes 2359304 | tf_op jit(solution)/shard_map/ppermute | solution.py:488
  48.4 4.8 %flash.5 = (f32[512,384]{1,0:T(8,128)}, f32[512,384]{1,0:T(8,128)}, f32[512,384]{1,0:T(8,128)}, f32[8,128]{1,0:T(8,128)}) custom-call(bf16[4,3,3,128,128]{4,3,2,1,0:T(8,128)(2,1)} %copy-done.6, bf16[4,2,3,128,128]{4,3,2,1,0:T(8,128)(2,1)} %copy-done.10, bf16[4,2,3,128,128]{4,3,2,1,0:T(8,128)(2,1)} %collective-permute-done.1.refs_2_.sibling), custom_call_target="tpu_custom_call" | custom-call | flops 1 | bytes 1 | tf_op jit(solution)/shard_map/flash/pallas_call | solution.py:223
  57.5 6.2 %collective-permute-done.4.refs_0_ = bf16[4,2,3,128,128]{4,3,2,1,0:T(8,128)(2,1)S(1)} collective-permute-done((bf16[4,2,3,128,128]{4,3,2,1,0:T(8,128)(2,1)}, bf16[4,2,3,128,128]{4,3,2,1,0:T(8,128)(2,1)S(1)}, u32[]{:S(2)}, u32[]{:S(2)}) %collective-permute-start.4) | collective-permute-done | bytes 786464 | tf_op jit(solution)/shard_map/ppermute | solution.py:488
  69.0 6.9 %flash.6 = (f32[512,384]{1,0:T(8,128)}, f32[512,384]{1,0:T(8,128)}, f32[512,384]{1,0:T(8,128)}, f32[8,128]{1,0:T(8,128)}) custom-call(bf16[4,3,3,128,128]{4,3,2,1,0:T(8,128)(2,1)} %copy-done.6, bf16[4,2,3,128,128]{4,3,2,1,0:T(8,128)(2,1)} %gate.11.refs_1_, bf16[4,2,3,128,128]{4,3,2,1,0:T(8,128)(2,1)} %gate.13.refs_2_.third, ...), custom_call_target="tpu_custom_call" | custom-call | flops 1 | bytes 1 | tf_op jit(solution)/shard_map/flash/pallas_call | solution.py:223
  76.0 3.5 %pack_audio.1 = bf16[4,576,384]{2,1,0:T(8,128)(2,1)} custom-call(s32[5]{0:T(128)} %stack.23.place, bf16[384,1536]{1,0:T(8,128)(2,1)} %bitcast.22, bf16[384,1536]{1,0:T(8,128)(2,1)} %bitcast.23, bf16[384,1536]{1,0:T(8,128)(2,1)} %bitcast.24), custom_call_target="tpu_custom_call" | custom-call | tf_op jit(solution)/shard_map/pack_audio/pallas_call | solution.py:137
  79.5 3.7 %all-to-all-start.1 = ((bf16[4,576,384]{2,1,0:T(8,128)(2,1)}), bf16[4,576,384]{2,1,0:T(8,128)(2,1)S(1)}, u32[]{:S(2)}, u32[]{:S(2)}) async-start(bf16[4,576,384]{2,1,0:T(8,128)(2,1)} %pack_audio.1), calls=%async_computation.1 | async-start | bytes 3538944 | tf_op jit(solution)/shard_map/all_to_all | solution.py:475
  85.4 9.1 %collective-permute-done.2.refs_0_ = bf16[4,2,3,128,128]{4,3,2,1,0:T(8,128)(2,1)} collective-permute-done((bf16[4,2,3,128,128]{4,3,2,1,0:T(8,128)(2,1)S(1)}, bf16[4,2,3,128,128]{4,3,2,1,0:T(8,128)(2,1)}, u32[]{:S(2)}, u32[]{:S(2)}) %collective-permute-start.2) | collective-permute-done | bytes 786464 | tf_op jit(solution)/shard_map/ppermute | solution.py:488
  94.6 3.1 %collective-permute-start.3 = (bf16[4,2,3,128,128]{4,3,2,1,0:T(8,128)(2,1)}, bf16[4,2,3,128,128]{4,3,2,1,0:T(8,128)(2,1)}, u32[]{:S(2)}, u32[]{:S(2)}) collective-permute-start(bf16[4,2,3,128,128]{4,3,2,1,0:T(8,128)(2,1)} %gate.12.refs_1_), channel_id=1, source_target_pairs={{0,8},{4,60},{8,16},{12,4},{16,24},{20,12},{24,32},{28,20},{32,40}... | collective-permute-start | bytes 2359304 | tf_op jit(solution)/shard_map/ppermute | solution.py:488
  98.4 7.5 %all-to-all-done.1.refs_0_ = bf16[4,576,384]{2,1,0:T(8,128)(2,1)S(1)} async-done(((bf16[4,576,384]{2,1,0:T(8,128)(2,1)}), bf16[4,576,384]{2,1,0:T(8,128)(2,1)S(1)}, u32[]{:S(2)}, u32[]{:S(2)}) %all-to-all-start.1) | async-done | bytes 1769504 | tf_op jit(solution)/shard_map/all_to_all | solution.py:475
  107.1 6.5 %cross.1.own = bf16[4,160,384]{2,1,0:T(8,128)(2,1)} custom-call(s32[5]{0:T(128)} %stack.23.place, s32[64,3]{1,0:T(8,128)} %bitcast.30, bf16[4,3,3,128,128]{4,3,2,1,0:T(8,128)(2,1)} %copy-done.6, bf16[4,576,384]{2,1,0:T(8,128)(2,1)} %gate.16.main.edge, bf16[4,576,384]{2,1,0:T(8,128)(2,1)} %gate.16.main.edge, bf16[4,2,3,128,128]{4,3,2,1,0:T(8,128)(2,1)} %copy-done.10, ...), custom_call_target="tpu_custom_call" | custom-call | flops 1 | bytes 1 | tf_op jit(solution)/shard_map/cross/pallas_call | solution.py:304
  117.6 6.6 %project_cross.1 = (bf16[320,1536]{1,0:T(8,128)(2,1)}, bf16[320,1536]{1,0:T(8,128)(2,1)}, bf16[320,1536]{1,0:T(8,128)(2,1)}, bf16[160,1536]{1,0:T(8,128)(2,1)}, bf16[160,1536]{1,0:T(8,128)(2,1)}) custom-call(s32[5]{0:T(128)} %stack.23.place, bf16[4,160,384]{2,1,0:T(8,128)(2,1)} %cross.1.own, bf16[4,160,384]{2,1,0:T(8,128)(2,1)} %copy-done.20, ...), custom_call_target="tpu_custom_call" | custom-call | flops 1 | bytes 1 | tf_op jit(solution)/shard_map/project_cross/pallas_call | solution.py:354
  129.3 6.9 %flash.7 = (f32[512,384]{1,0:T(8,128)}, f32[512,384]{1,0:T(8,128)}, f32[512,384]{1,0:T(8,128)}, f32[8,128]{1,0:T(8,128)}) custom-call(bf16[4,3,3,128,128]{4,3,2,1,0:T(8,128)(2,1)} %copy-done.6, bf16[4,2,3,128,128]{4,3,2,1,0:T(8,128)(2,1)} %gate.12.refs_1_, bf16[4,2,3,128,128]{4,3,2,1,0:T(8,128)(2,1)} %gate.15.refs_2_, ...), custom_call_target="tpu_custom_call" | custom-call | flops 1 | bytes 1 | tf_op jit(solution)/shard_map/flash/pallas_call | solution.py:223
  140.3 7.5 %collective-permute-done.17.refs_2_ = bf16[320,1536]{1,0:T(8,128)(2,1)S(1)} collective-permute-done((bf16[320,1536]{1,0:T(8,128)(2,1)}, bf16[320,1536]{1,0:T(8,128)(2,1)S(1)}, u32[]{:S(2)}, u32[]{:S(2)}) %collective-permute-start.17) | collective-permute-done | bytes 983072 | tf_op jit(solution)/shard_map/ppermute | solution.py:483
  153.2 6.9 %flash.8 = (f32[512,384]{1,0:T(8,128)}, f32[512,384]{1,0:T(8,128)}, f32[512,384]{1,0:T(8,128)}, f32[8,128]{1,0:T(8,128)}) custom-call(bf16[4,3,3,128,128]{4,3,2,1,0:T(8,128)(2,1)} %copy-done.6, bf16[4,2,3,128,128]{4,3,2,1,0:T(8,128)(2,1)} %gate.14.refs_1_, bf16[4,2,3,128,128]{4,3,2,1,0:T(8,128)(2,1)} %gate.19.refs_2_, ...), custom_call_target="tpu_custom_call" | custom-call | flops 1 | bytes 1 | tf_op jit(solution)/shard_map/flash/pallas_call | solution.py:223
  161.0 5.4 %flash.9 = bf16[512,384]{1,0:T(8,128)(2,1)} custom-call(bf16[4,3,3,128,128]{4,3,2,1,0:T(8,128)(2,1)} %copy-done.6, bf16[4,2,3,128,128]{4,3,2,1,0:T(8,128)(2,1)} %gate.18.refs_1_, bf16[4,2,3,128,128]{4,3,2,1,0:T(8,128)(2,1)} %copy-done.18, f32[512,384]{1,0:T(8,128)} %gate.20.refs_3_, f32[512,384]{1,0:T(8,128)} %get-tuple-element.50.refs_4_, ...), custom_call_target="tpu_custom_call" | custom-call | flops 1 | bytes 1 | tf_op jit(solution)/shard_map/flash/pallas_call | solution.py:223
  166.4 3.5 %all-to-all-start.2 = ((bf16[4,128,384]{2,1,0:T(8,128)(2,1)}), bf16[4,128,384]{2,1,0:T(8,128)(2,1)S(1)}, u32[]{:S(2)}, u32[]{:S(2)}) async-start(bf16[4,128,384]{2,1,0:T(8,128)(2,1)} %bitcast.21), calls=%async_computation.2 | async-start | bytes 786432 | tf_op jit(solution)/shard_map/all_to_all | solution.py:475
  169.9 2.6 %collective-permute-start.20 = (bf16[160,1536]{1,0:T(8,128)(2,1)}, bf16[160,1536]{1,0:T(8,128)(2,1)}, u32[]{:S(2)}, u32[]{:S(2)}) collective-permute-start(bf16[160,1536]{1,0:T(8,128)(2,1)} %add_convert_fusion.refs_2_), channel_id=1, source_target_pairs={{0,3},{1,0},{2,1},{3,2},{4,7},{5,4},{6,5},{7,6},{8,11},{9,8},{10,9... | collective-permute-start | bytes 1474568 | tf_op jit(solution)/shard_map/ppermute | solution.py:483
  172.6 3.6 %all-to-all-done.2.own = bf16[4,128,384]{2,1,0:T(8,128)(2,1)S(1)} async-done(((bf16[4,128,384]{2,1,0:T(8,128)(2,1)}), bf16[4,128,384]{2,1,0:T(8,128)(2,1)S(1)}, u32[]{:S(2)}, u32[]{:S(2)}) %all-to-all-start.2) | async-done | bytes 393248 | tf_op jit(solution)/shard_map/all_to_all | solution.py:475
  176.1 5.0 %collective-permute-start.18 = (bf16[4,128,384]{2,1,0:T(8,128)(2,1)S(1)}, bf16[4,128,384]{2,1,0:T(8,128)(2,1)S(1)}, u32[]{:S(2)}, u32[]{:S(2)}) collective-permute-start(bf16[4,128,384]{2,1,0:T(8,128)(2,1)S(1)} %all-to-all-done.2.own), channel_id=1, source_target_pairs={{0,4},{4,0},{8,12},{12,8},{16,20},{20,16},{24,28},{28,24},{32,36},... | collective-permute-start | bytes 1179656 | tf_op jit(solution)/shard_map/ppermute | solution.py:492
  181.1 4.5 %collective-permute-done.20.refs_4_ = bf16[160,1536]{1,0:T(8,128)(2,1)} collective-permute-done((bf16[160,1536]{1,0:T(8,128)(2,1)}, bf16[160,1536]{1,0:T(8,128)(2,1)}, u32[]{:S(2)}, u32[]{:S(2)}) %collective-permute-start.20) | collective-permute-done | bytes 491552 | tf_op jit(solution)/shard_map/ppermute | solution.py:483
  191.6 4.8 %project_self.1 = (bf16[128,3072]{1,0:T(8,128)(2,1)}, bf16[24,3072]{1,0:T(8,128)(2,1)}, bf16[160,1536]{1,0:T(8,128)(2,1)S(1)}) custom-call(s32[5]{0:T(128)S(1)} %copy-done.4, bf16[4,128,384]{2,1,0:T(8,128)(2,1)S(1)} %all-to-all-done.2.own, bf16[4,128,384]{2,1,0:T(8,128)(2,1)S(1)} %copy-done.3, bf16[16,3,32,1536]{3,2,1,0:T(8,128)(2,1)S(1)} %copy-done, ...), custom_call_target="tpu_custom_call" | custom-call | flops 1 | bytes 1 | tf_op jit(solution)/shard_map/project_self/pallas_call | solution.py:407
  (105 shorter events, 47.9 us)
Async XLA Ops:
  7.2 68.8 %all-gather.9.cloned.1.call-start = ((), (), s32[]{:S(2)}) async-start(), calls=%async_computation.4 | async-start | bytes 1474560 | tf_op jit(solution)/shard_map/all_gather | solution.py:505
  11.3 105.4 %all-gather.7.cloned.1.call-start = ((), (), s32[]{:S(2)}) async-start(), calls=%async_computation.3 | async-start | bytes 2949120 | tf_op jit(solution)/shard_map/all_gather | solution.py:504
  12.1 176.2 %all-gather.11.cloned.1.call-start = ((), (), s32[]{:S(2)}) async-start(), calls=%async_computation.5 | async-start | bytes 5898240 | tf_op jit(solution)/shard_map/all_gather | solution.py:527
  31.7 14.6 %collective-permute-start.1 = (bf16[4,2,3,128,128]{4,3,2,1,0:T(8,128)(2,1)S(1)}, bf16[4,2,3,128,128]{4,3,2,1,0:T(8,128)(2,1)}, u32[]{:S(2)}, u32[]{:S(2)}) collective-permute-start(bf16[4,2,3,128,128]{4,3,2,1,0:T(8,128)(2,1)S(1)} %slice.12.refs_1_.own), channel_id=1, source_target_pairs={{0,4},{4,0},{8,12},{12,8},{16,20},{20,16},{24,28},{28,24},{32,36},... | collective-permute-start | bytes 2359304 | tf_op jit(solution)/shard_map/ppermute | solution.py:492
  39.0 16.3 %collective-permute-start = (bf16[4,2,3,128,128]{4,3,2,1,0:T(8,128)(2,1)S(1)}, bf16[4,2,3,128,128]{4,3,2,1,0:T(8,128)(2,1)S(1)}, u32[]{:S(2)}, u32[]{:S(2)}) collective-permute-start(bf16[4,2,3,128,128]{4,3,2,1,0:T(8,128)(2,1)S(1)} %slice.12.refs_1_.own), channel_id=1, source_target_pairs={{0,8},{4,60},{8,16},{12,4},{16,24},{20,12},{24,32},{28,20},{32,40}... | collective-permute-start | bytes 2359304 | tf_op jit(solution)/shard_map/ppermute | solution.py:488
  46.3 17.5 %collective-permute-start.4 = (bf16[4,2,3,128,128]{4,3,2,1,0:T(8,128)(2,1)}, bf16[4,2,3,128,128]{4,3,2,1,0:T(8,128)(2,1)S(1)}, u32[]{:S(2)}, u32[]{:S(2)}) collective-permute-start(bf16[4,2,3,128,128]{4,3,2,1,0:T(8,128)(2,1)} %collective-permute-done.1.refs_2_.sibling), channel_id=1, source_target_pairs={{0,8},{4,60},{8,16},{12,4},{16,24},{20,12},{24,32},{28,20},{32,40}... | collective-permute-start | bytes 2359304 | tf_op jit(solution)/shard_map/ppermute | solution.py:488
  56.1 9.8 %collective-permute-start.5 = (bf16[4,2,3,128,128]{4,3,2,1,0:T(8,128)(2,1)}, bf16[4,2,3,128,128]{4,3,2,1,0:T(8,128)(2,1)S(1)}, u32[]{:S(2)}, u32[]{:S(2)}) collective-permute-start(bf16[4,2,3,128,128]{4,3,2,1,0:T(8,128)(2,1)} %gate.11.refs_1_), channel_id=1, source_target_pairs={{0,4},{4,0},{8,12},{12,8},{16,20},{20,16},{24,28},{28,24},{32,36},... | collective-permute-start | bytes 2359304 | tf_op jit(solution)/shard_map/ppermute | solution.py:492
  79.5 26.4 %all-to-all-start.1 = ((bf16[4,576,384]{2,1,0:T(8,128)(2,1)}), bf16[4,576,384]{2,1,0:T(8,128)(2,1)S(1)}, u32[]{:S(2)}, u32[]{:S(2)}) async-start(bf16[4,576,384]{2,1,0:T(8,128)(2,1)} %pack_audio.1), calls=%async_computation.1 | async-start | bytes 3538944 | tf_op jit(solution)/shard_map/all_to_all | solution.py:475
  83.2 11.3 %collective-permute-start.2 = (bf16[4,2,3,128,128]{4,3,2,1,0:T(8,128)(2,1)S(1)}, bf16[4,2,3,128,128]{4,3,2,1,0:T(8,128)(2,1)}, u32[]{:S(2)}, u32[]{:S(2)}) collective-permute-start(bf16[4,2,3,128,128]{4,3,2,1,0:T(8,128)(2,1)S(1)} %copy-done.13), channel_id=1, source_target_pairs={{0,8},{4,60},{8,16},{12,4},{16,24},{20,12},{24,32},{28,20},{32,40}... | collective-permute-start | bytes 2359304 | tf_op jit(solution)/shard_map/ppermute | solution.py:488
  85.3 29.5 %collective-permute-start.8 = (bf16[4,2,3,128,128]{4,3,2,1,0:T(8,128)(2,1)S(1)}, bf16[4,2,3,128,128]{4,3,2,1,0:T(8,128)(2,1)}, u32[]{:S(2)}, u32[]{:S(2)}) collective-permute-start(bf16[4,2,3,128,128]{4,3,2,1,0:T(8,128)(2,1)S(1)} %copy-done.9), channel_id=1, source_target_pairs={{0,8},{4,60},{8,16},{12,4},{16,24},{20,12},{24,32},{28,20},{32,40}... | collective-permute-start | bytes 2359304 | tf_op jit(solution)/shard_map/ppermute | solution.py:488
  94.6 31.1 %collective-permute-start.3 = (bf16[4,2,3,128,128]{4,3,2,1,0:T(8,128)(2,1)}, bf16[4,2,3,128,128]{4,3,2,1,0:T(8,128)(2,1)}, u32[]{:S(2)}, u32[]{:S(2)}) collective-permute-start(bf16[4,2,3,128,128]{4,3,2,1,0:T(8,128)(2,1)} %gate.12.refs_1_), channel_id=1, source_target_pairs={{0,8},{4,60},{8,16},{12,4},{16,24},{20,12},{24,32},{28,20},{32,40}... | collective-permute-start | bytes 2359304 | tf_op jit(solution)/shard_map/ppermute | solution.py:488
  114.8 12.7 %collective-permute-start.13 = (bf16[4,2,3,128,128]{4,3,2,1,0:T(8,128)(2,1)}, bf16[4,2,3,128,128]{4,3,2,1,0:T(8,128)(2,1)S(1)}, u32[]{:S(2)}, u32[]{:S(2)}) collective-permute-start(bf16[4,2,3,128,128]{4,3,2,1,0:T(8,128)(2,1)} %gate.15.refs_2_), channel_id=1, source_target_pairs={{0,8},{4,60},{8,16},{12,4},{16,24},{20,12},{24,32},{28,20},{32,40}... | collective-permute-start | bytes 2359304 | tf_op jit(solution)/shard_map/ppermute | solution.py:488
  124.2 23.6 %collective-permute-start.17 = (bf16[320,1536]{1,0:T(8,128)(2,1)}, bf16[320,1536]{1,0:T(8,128)(2,1)S(1)}, u32[]{:S(2)}, u32[]{:S(2)}) collective-permute-start(bf16[320,1536]{1,0:T(8,128)(2,1)} %get-tuple-element.49), channel_id=1, source_target_pairs={{0,3},{1,0},{2,1},{3,2},{4,7},{5,4},{6,5},{7,6},{8,11},{9,8},{10,9... | collective-permute-start | bytes 2949128 | tf_op jit(solution)/shard_map/ppermute | solution.py:483
  125.5 3.7 %collective-permute-start.10 = (bf16[4,2,3,128,128]{4,3,2,1,0:T(8,128)(2,1)}, bf16[4,2,3,128,128]{4,3,2,1,0:T(8,128)(2,1)}, u32[]{:S(2)}, u32[]{:S(2)}) collective-permute-start(bf16[4,2,3,128,128]{4,3,2,1,0:T(8,128)(2,1)} %gate.15.refs_2_), channel_id=1, source_target_pairs={{0,4},{4,0},{8,12},{12,8},{16,20},{20,16},{24,28},{28,24},{32,36},... | collective-permute-start | bytes 2359304 | tf_op jit(solution)/shard_map/ppermute | solution.py:492
  125.7 11.5 %collective-permute-start.7 = (bf16[4,2,3,128,128]{4,3,2,1,0:T(8,128)(2,1)}, bf16[4,2,3,128,128]{4,3,2,1,0:T(8,128)(2,1)S(1)}, u32[]{:S(2)}, u32[]{:S(2)}) collective-permute-start(bf16[4,2,3,128,128]{4,3,2,1,0:T(8,128)(2,1)} %gate.14.refs_1_), channel_id=1, source_target_pairs={{0,8},{4,60},{8,16},{12,4},{16,24},{20,12},{24,32},{28,20},{32,40}... | collective-permute-start | bytes 2359304 | tf_op jit(solution)/shard_map/ppermute | solution.py:488
  127.5 23.9 %collective-permute-start.16 = (bf16[320,1536]{1,0:T(8,128)(2,1)}, bf16[320,1536]{1,0:T(8,128)(2,1)S(1)}, u32[]{:S(2)}, u32[]{:S(2)}) collective-permute-start(bf16[320,1536]{1,0:T(8,128)(2,1)} %get-tuple-element.47), channel_id=1, source_target_pairs={{0,1},{1,2},{2,3},{3,0},{4,5},{5,6},{6,7},{7,4},{8,9},{9,10},{10,1... | collective-permute-start | bytes 2949128 | tf_op jit(solution)/shard_map/ppermute | solution.py:483
  128.4 23.9 %collective-permute-start.14 = (bf16[4,2,3,128,128]{4,3,2,1,0:T(8,128)(2,1)}, bf16[4,2,3,128,128]{4,3,2,1,0:T(8,128)(2,1)S(1)}, u32[]{:S(2)}, u32[]{:S(2)}) collective-permute-start(bf16[4,2,3,128,128]{4,3,2,1,0:T(8,128)(2,1)} %gate.14.refs_1_), channel_id=1, source_target_pairs={{0,4},{4,0},{8,12},{12,8},{16,20},{20,16},{24,28},{28,24},{32,36},... | collective-permute-start | bytes 2359304 | tf_op jit(solution)/shard_map/ppermute | solution.py:492
  129.2 23.2 %collective-permute-start.15 = (bf16[4,2,3,128,128]{4,3,2,1,0:T(8,128)(2,1)}, bf16[4,2,3,128,128]{4,3,2,1,0:T(8,128)(2,1)}, u32[]{:S(2)}, u32[]{:S(2)}) collective-permute-start(bf16[4,2,3,128,128]{4,3,2,1,0:T(8,128)(2,1)} %gate.19.refs_2_), channel_id=1, source_target_pairs={{0,4},{4,0},{8,12},{12,8},{16,20},{20,16},{24,28},{28,24},{32,36},... | collective-permute-start | bytes 2359304 | tf_op jit(solution)/shard_map/ppermute | solution.py:492
  138.0 22.1 %collective-permute-start.12 = (bf16[4,2,3,128,128]{4,3,2,1,0:T(8,128)(2,1)}, bf16[4,2,3,128,128]{4,3,2,1,0:T(8,128)(2,1)S(1)}, u32[]{:S(2)}, u32[]{:S(2)}) collective-permute-start(bf16[4,2,3,128,128]{4,3,2,1,0:T(8,128)(2,1)} %gate.18.refs_1_), channel_id=1, source_target_pairs={{0,4},{4,0},{8,12},{12,8},{16,20},{20,16},{24,28},{28,24},{32,36},... | collective-permute-start | bytes 2359304 | tf_op jit(solution)/shard_map/ppermute | solution.py:492
  166.4 9.7 %all-to-all-start.2 = ((bf16[4,128,384]{2,1,0:T(8,128)(2,1)}), bf16[4,128,384]{2,1,0:T(8,128)(2,1)S(1)}, u32[]{:S(2)}, u32[]{:S(2)}) async-start(bf16[4,128,384]{2,1,0:T(8,128)(2,1)} %bitcast.21), calls=%async_computation.2 | async-start | bytes 786432 | tf_op jit(solution)/shard_map/all_to_all | solution.py:475
  169.9 15.6 %collective-permute-start.20 = (bf16[160,1536]{1,0:T(8,128)(2,1)}, bf16[160,1536]{1,0:T(8,128)(2,1)}, u32[]{:S(2)}, u32[]{:S(2)}) collective-permute-start(bf16[160,1536]{1,0:T(8,128)(2,1)} %add_convert_fusion.refs_2_), channel_id=1, source_target_pairs={{0,3},{1,0},{2,1},{3,2},{4,7},{5,4},{6,5},{7,6},{8,11},{9,8},{10,9... | collective-permute-start | bytes 1474568 | tf_op jit(solution)/shard_map/ppermute | solution.py:483
  172.6 15.0 %collective-permute-start.19 = (bf16[160,1536]{1,0:T(8,128)(2,1)}, bf16[160,1536]{1,0:T(8,128)(2,1)}, u32[]{:S(2)}, u32[]{:S(2)}) collective-permute-start(bf16[160,1536]{1,0:T(8,128)(2,1)} %add_convert_fusion.1.refs_1_), channel_id=1, source_target_pairs={{0,1},{1,2},{2,3},{3,0},{4,5},{5,6},{6,7},{7,4},{8,9},{9,10},{10,1... | collective-permute-start | bytes 1474568 | tf_op jit(solution)/shard_map/ppermute | solution.py:483
  176.1 11.4 %collective-permute-start.18 = (bf16[4,128,384]{2,1,0:T(8,128)(2,1)S(1)}, bf16[4,128,384]{2,1,0:T(8,128)(2,1)S(1)}, u32[]{:S(2)}, u32[]{:S(2)}) collective-permute-start(bf16[4,128,384]{2,1,0:T(8,128)(2,1)S(1)} %all-to-all-done.2.own), channel_id=1, source_target_pairs={{0,4},{4,0},{8,12},{12,8},{16,20},{20,16},{24,28},{28,24},{32,36},... | collective-permute-start | bytes 1179656 | tf_op jit(solution)/shard_map/ppermute | solution.py:492
  196.4 3.5 %collective-permute-start.21 = (bf16[160,1536]{1,0:T(8,128)(2,1)S(1)}, bf16[160,1536]{1,0:T(8,128)(2,1)S(1)}, u32[]{:S(2)}, u32[]{:S(2)}) collective-permute-start(bf16[160,1536]{1,0:T(8,128)(2,1)S(1)} %get-tuple-element.55), channel_id=1, source_target_pairs={{0,4},{4,0},{8,12},{12,8},{16,20},{20,16},{24,28},{28,24},{32,36},... | collective-permute-start | bytes 1474568 | tf_op jit(solution)/shard_map/ppermute | solution.py:492
  (25 other events, 177.1 us)
Sparse Core Ops, SparseCore 0:
  11.5 31.8 all-gather.8
  45.2 37.8 all-gather.6
  84.9 55.2 all-gather.10

commit v5 on v4

--- a/solution.py
+++ b/solution.py
@@ -43,11 +43,49 @@
     return copies
 
 
-def pack_video_kernel(place, k_ref, v_ref, q_ref, w_ref, out, self_out, rest_out, rows, turned, w_rows, sem):
+WIN = 192
+HALO = 48
+QROWS = 96
+QAT = 2 * WIN
+HAT = QAT + QROWS
+AROWS = HAT + 2 * HALO
+
+
+def main_first(ctx):
+    return jnp.clip(lax.rem(ctx, 4) * QROWS - HALO, 0, 384 - WIN)
+
+
+def edge_tower(ctx):
+    phase = lax.rem(ctx, 4)
+    edge = jnp.where(phase == 0, ctx // 4 - 1, ctx // 4 + 1)
+    return jnp.where(((phase == 0) | (phase == 3)) & (edge >= 0) & (edge < TOWERS), edge, -1)
+
+
+def pack_kernel(
+    place, k_ref, v_ref, q_ref, ak_ref, av_ref, aq_ref, w_ref,
+    out, self_out, rest_out, main0, main1, main2, main3, halo0, halo1, halo2, halo3,
+    rows, turned, audio, w_rows, sem,
+):
+    ctx, tower = place[0], place[1]
+    phase = lax.rem(ctx, 4)
+    main = pl.ds(pl.multiple_of(main_first(ctx), 16), WIN)
+    mine = pl.ds(pl.multiple_of(phase * QROWS, 16), QROWS)
+    halo = pl.ds(pl.multiple_of(jnp.where(phase == 0, 384 - HALO, 0), 16), HALO)
     half = w_ref.shape[3] // 2
     columns = pl.ds(pl.multiple_of(place[4] * half, 128), half)
     coming = start_copies([(ref, rows.at[i]) for i, ref in enumerate((k_ref, v_ref, q_ref))], sem, 0)
-    coming += start_copies([(w_ref.at[:, :, :, columns], w_rows)], sem, 3)
+    coming_w = start_copies([(w_ref.at[:, :, :, columns], w_rows)], sem, 3)
+    coming_audio = start_copies(
+        [
+            (ak_ref.at[main], audio.at[pl.ds(0, WIN)]),
+            (av_ref.at[main], audio.at[pl.ds(WIN, WIN)]),
+            (aq_ref.at[mine], audio.at[pl.ds(QAT, QROWS)]),
+            (ak_ref.at[halo], audio.at[pl.ds(HAT, HALO)]),
+            (av_ref.at[halo], audio.at[pl.ds(HAT + HALO, HALO)]),
+        ],
+        sem,
+        4,
+    )
     heads = [(g, h) for g in range(TOWERS) for h in range(LOCAL)]
     going = []
     for i in (1, 2):
@@ -55,101 +93,70 @@
         pairs = [
             (rows.at[i, :, pl.ds((g * LOCAL + h) * HD, HD)], out.at[g, i, h]) for g, h in heads
         ]
-        going += start_copies(pairs, sem, 4 + (i - 1) * H)
+        going += start_copies(pairs, sem, 9 + (i - 1) * H)
     coming[0].wait()
     for g, h in heads:
         block = rows[0, :, pl.ds((g * LOCAL + h) * HD, HD)]
         turned[g, h] = block.astype(jnp.float32).T.astype(jnp.bfloat16)
-    going += start_copies([(turned.at[g], out.at[g, 0]) for g in range(TOWERS)], sem, 28)
-    coming[3].wait()
-    going += start_copies([(w_rows.at[0], self_out), (w_rows.at[pl.ds(1, 2)], rest_out)], sem, 32)
+    going += start_copies([(turned.at[g], out.at[g, 0]) for g in range(TOWERS)], sem, 33)
+    coming_w[0].wait()
+    going += start_copies([(w_rows.at[0], self_out), (w_rows.at[pl.ds(1, 2)], rest_out)], sem, 37)
+    for copy in coming_audio:
+        copy.wait()
+    pairs = []
+    for step, (main_out, halo_out) in enumerate(
+        ((main0, halo0), (main1, halo1), (main2, halo2), (main3, halo3))
+    ):
+        group = pl.ds(pl.multiple_of(lax.rem(tower + step, TOWERS) * GW, 128), GW)
+        pairs.append((audio.at[pl.ds(0, HAT), group], main_out))
+        pairs.append((audio.at[pl.ds(HAT, 2 * HALO), group], halo_out))
+    going += start_copies(pairs, sem, 39)
     for copy in going:
         copy.wait()
 
 
-def pack_video(place, k, v, q, w):
+def pack(place, k, v, q, ak, av, aq, w):
     rows = k.shape[0]
     narrow = (LOCAL, w.shape[2], w.shape[3] // 2)
     shapes = [(TOWERS, 3, LOCAL, rows, HD), narrow, (2,) + narrow]
-    return pl.pallas_call(
-        pack_video_kernel,
+    shapes += [(HAT, GW)] * TOWERS + [(2 * HALO, GW)] * TOWERS
+    return pl.pallas_call(
+        pack_kernel,
         out_shape=[jax.ShapeDtypeStruct(shape, jnp.bfloat16) for shape in shapes],
         grid_spec=pltpu.PrefetchScalarGridSpec(
             num_scalar_prefetch=1,
             grid=(1,),
-            in_specs=[ANY] * 4,
-            out_specs=[ANY] * 3,
+            in_specs=[ANY] * 7,
+            out_specs=[ANY] * len(shapes),
             scratch_shapes=[
                 pltpu.VMEM((3,) + k.shape, jnp.bfloat16),
                 pltpu.VMEM((TOWERS, LOCAL, HD, rows), jnp.bfloat16),
+                pltpu.VMEM((AROWS, aq.shape[1]), jnp.bfloat16),
                 pltpu.VMEM((3,) + narrow, jnp.bfloat16),
-                pltpu.SemaphoreType.DMA((34,)),
+                pltpu.SemaphoreType.DMA((47,)),
             ],
         ),
         compiler_params=pltpu.CompilerParams(vmem_limit_bytes=60 * MIB),
-        name="pack_video",
-    )(place, k, v, q, w)
-
-
-WIN = 192
-HALO = 48
-QROWS = 96
-QAT = 2 * WIN
-HAT = QAT + QROWS
-AROWS = HAT + 2 * HALO
-
-
-def main_first(ctx):
-    return jnp.clip(lax.rem(ctx, 4) * QROWS - HALO, 0, 384 - WIN)
-
-
-def edge_tower(ctx):
-    return jnp.clip(jnp.where(lax.rem(ctx, 4) == 0, ctx // 4 - 1, ctx // 4 + 1), 0, TOWERS - 1)
-
-
-def pack_audio_kernel(place, q_ref, k_ref, v_ref, out, rows, sem):
-    ctx = place[0]
-    phase = lax.rem(ctx, 4)
-    main = pl.ds(pl.multiple_of(main_first(ctx), 16), WIN)
-    mine = pl.ds(pl.multiple_of(phase * QROWS, 16), QROWS)
-    halo = pl.ds(pl.multiple_of(jnp.where(phase == 0, 384 - HALO, 0), 16), HALO)
-    coming = start_copies(
-        [
-            (k_ref.at[main], rows.at[pl.ds(0, WIN)]),
-            (v_ref.at[main], rows.at[pl.ds(WIN, WIN)]),
-            (q_ref.at[mine], rows.at[pl.ds(QAT, QROWS)]),
-            (k_ref.at[halo], rows.at[pl.ds(HAT, HALO)]),
-            (v_ref.at[halo], rows.at[pl.ds(HAT + HALO, HALO)]),
-        ],
-        sem,
-        0,
-    )
-    for copy in coming:
-        copy.wait()
-    going = start_copies(
-        [(rows.at[:, pl.ds(g * GW, GW)], out.at[g]) for g in range(TOWERS)], sem, 5
-    )
-    for copy in going:
-        copy.wait()
-
-
-def pack_audio(place, q, k, v):
-    return pl.pallas_call(
-        pack_audio_kernel,
-        out_shape=jax.ShapeDtypeStruct((TOWERS, AROWS, GW), jnp.bfloat16),
-        grid_spec=pltpu.PrefetchScalarGridSpec(
-            num_scalar_prefetch=1,
-            grid=(1,),
-            in_specs=[ANY] * 3,
-            out_specs=ANY,
-            scratch_shapes=[
-                pltpu.VMEM((AROWS, q.shape[1]), jnp.bfloat16),
-                pltpu.SemaphoreType.DMA((9,)),
-            ],
-        ),
-        compiler_params=pltpu.CompilerParams(vmem_limit_bytes=60 * MIB),
-        name="pack_audio",
-    )(place, q, k, v)
+        name="pack",
+    )(place, k, v, q, ak, av, aq, w)
+
+
+def ctx_towers(pairs):
+    return [(c * TOWERS + s, c * TOWERS + d) for c, s, d in pairs]
+
+
+def send_main(value, step):
+    pairs = [(c, c // 4, (c // 4 + step) % TOWERS) for c in range(16)]
+    return lax.ppermute(value, ("ctx", "tower"), ctx_towers(pairs))
+
+
+def send_halo(value, step):
+    pairs = []
+    for c in range(16):
+        source = c // 4 - 1 if c % 4 == 0 else c // 4 + 1
+        if c % 4 in (0, 3) and 0 <= source < TOWERS:
+            pairs.append((c, source, (source + step) % TOWERS))
+    return lax.ppermute(value, ("ctx", "tower"), ctx_towers(pairs))
 
 
 def keys_of(kv_ref):
@@ -164,10 +171,11 @@
     return [x[:, i : i + HD] for i in range(0, x.shape[1], HD)]
 
 
-def flash_kernel(kv_count, first, last, *refs):
+def flash_kernel(kv_count, first, last, after, *refs):
     q_ref = refs[0]
     kv_refs = refs[1 : 1 + kv_count]
     rest = refs[1 + kv_count :]
+    rest = rest[: len(rest) - (1 if last else 4) - after] + rest[len(rest) - (1 if last else 4) :]
     if first:
         outs = rest
     else:
@@ -209,7 +217,7 @@
 SHARD = pl.BlockSpec((TOWERS, 2, 1, VBLK, HD), lambda h, *_: (0, 0, h, 0, 0))
 
 
-def flash(query, kvs, state, last):
+def flash(query, kvs, state, last, after=()):
     rows = TOWERS * VBLK
     keys = rows * len(kvs)
     wide = jax.ShapeDtypeStruct((rows, GW), jnp.float32)
@@ -221,15 +229,15 @@
         out_shape = [wide, wide, wide, jax.ShapeDtypeStruct((8, HD), jnp.float32)]
         out_specs = [head, head, head, pl.BlockSpec((8, HD), lambda h: (0, 0))]
     return pl.pallas_call(
-        functools.partial(flash_kernel, len(kvs), state is None, last),
+        functools.partial(flash_kernel, len(kvs), state is None, last, len(after)),
         out_shape=out_shape,
         grid=(LOCAL,),
-        in_specs=[QUERY] + [SHARD] * len(kvs) + ([] if state is None else [head] * 3),
+        in_specs=[QUERY] + [SHARD] * len(kvs) + ([] if state is None else [head] * 3) + [ANY] * len(after),
         out_specs=out_specs,
         compiler_params=pltpu.CompilerParams(vmem_limit_bytes=60 * MIB),
         cost_estimate=BRIEF,
         name="flash",
-    )(query, *kvs, *(() if state is None else state))
+    )(query, *kvs, *(() if state is None else state), *after)
 
 
 AUDIO_ROWS = 32
@@ -242,11 +250,11 @@
     return result[:, :HD] / result[:, HD:]
 
 
-def audio_rows(place, margin, audio, own, sibling, third):
+def audio_rows(place, margin, main, own, sibling, third):
     ctx = place[0]
     core = lax.rem(ctx, 2)
     row_block = lax.broadcasted_iota(jnp.int32, (QROWS, 1), 0) // ABLK + ctx * 4
-    query = audio[0, pl.ds(QAT, QROWS), :]
+    query = main[QAT:]
     pieces = [(own, r, ctx * 4 + r) for r in range(TOWERS)]
     after = lax.rem(ctx + 1, 16) * 4
     before = lax.rem(ctx + 15, 16) * 4 + 2
@@ -268,7 +276,14 @@
     return weighted(scores, values)
 
 
-def cross_kernel(place, margin, q_ref, main, edge, own, sibling, third, out):
+def cross_kernel(place, margin, q_ref, *refs):
+    mains, halos, (own, sibling, third, out) = refs[:4], refs[4:8], refs[8:]
+    main = functools.reduce(
+        jnp.add, [ref[...] for ref in mains[1:]], jnp.where(place[1] == place[2], mains[0][...], 0)
+    )
+    halo = functools.reduce(
+        jnp.add, [ref[...] for ref in halos[1:]], jnp.where(place[1] == place[3], halos[0][...], 0)
+    )
     ctx = place[0]
     phase = lax.rem(ctx, 4)
     base = (ctx - phase) * 4
@@ -278,9 +293,9 @@
     ids = jnp.where(lane < WIN, lane // ABLK + main_base, lane // ABLK - WIN // ABLK + halo_base)
     ids = jnp.where(lane < WIN + HALO, ids, -100)
     spare = jnp.zeros((256 - WIN - HALO, HD), jnp.bfloat16)
-    keys = jnp.concatenate([main[0, pl.ds(0, WIN), :], edge[0, pl.ds(HAT, HALO), :], spare], axis=0)
+    keys = jnp.concatenate([main[:WIN], halo[:HALO], spare], axis=0)
     values = jnp.concatenate(
-        [main[0, pl.ds(WIN, WIN), :], edge[0, pl.ds(HAT + HALO, HALO), :], spare], axis=0
+        [main[WIN:QAT], halo[HALO:], spare], axis=0
     )
     scores = nt_dot(rows_of(q_ref, 0), keys) * SCALE2
     parts = []
@@ -299,7 +314,7 @@
         out[r, pl.ds(VBLK, AUDIO_ROWS), :] = padded.astype(jnp.bfloat16)
 
 
-def cross(place, margin, query, audio, own, sibling, third):
+def cross(place, margin, query, mains, halos, own, sibling, third):
     rows = TOWERS * VBLK
     return pl.pallas_call(
         cross_kernel,
@@ -309,27 +324,24 @@
             grid=(LOCAL,),
             in_specs=[
                 QUERY,
-                pl.BlockSpec((1, AROWS, HD), lambda h, place, margin: (place[2], 0, h)),
-                pl.BlockSpec((1, AROWS, HD), lambda h, place, margin: (place[3], 0, h)),
-                SHARD,
-                SHARD,
-                SHARD,
-            ],
+            ]
+            + [pl.BlockSpec((HAT, HD), lambda h, *_: (0, h))] * TOWERS
+            + [pl.BlockSpec((2 * HALO, HD), lambda h, *_: (0, h))] * TOWERS
+            + [SHARD] * 3,
             out_specs=pl.BlockSpec((TOWERS, BOTH, HD), lambda h, *_: (0, 0, h)),
         ),
         compiler_params=pltpu.CompilerParams(vmem_limit_bytes=60 * MIB),
         cost_estimate=BRIEF,
         name="cross",
-    )(place, margin, query, audio, audio, own, sibling, third)
+    )(place, margin, query, *mains, *halos, own, sibling, third)
 
 
 def weight_rows(pieces):
     return jnp.concatenate([piece(h) for h in range(LOCAL) for piece in pieces], axis=0)
 
 
-def project_cross_kernel(place, own, sibling, w_ref, mine, up, down, up_later, down_later):
+def project_cross_kernel(place, own, sibling, w_ref, _, __, mine, up, down, up_later, down_later):
     towers = [lax.rem(place[1] + step, TOWERS) for step in range(TOWERS)]
-    pairs = [(step, ref) for step in range(TOWERS) for ref in (own, sibling)]
     targets = (
         (mine, 0),
         (mine, BOTH),
@@ -340,15 +352,20 @@
         (down, 0),
         (down_later, 0),
     )
-    for kind, (first, count) in enumerate(((0, VBLK), (VBLK, AUDIO_ROWS))):
-        w = weight_rows([functools.partial(lambda b, h: w_ref[b, kind, h], b) for b in range(4)])
-        a = jnp.concatenate([ref[towers[step], pl.ds(first, count), :] for step, ref in pairs], axis=0)
-        y = nn_dot(a, w).astype(jnp.bfloat16)
-        for i, (out, at) in enumerate(targets):
-            out[pl.ds(at + first, count), :] = y[i * count : (i + 1) * count]
-
-
-def project_cross(place, own, sibling, w):
+    ws = [
+        weight_rows([functools.partial(lambda b, h: w_ref[b, kind, h], b) for b in range(4)])
+        for kind in range(2)
+    ]
+    for step in range(TOWERS):
+        for w, (first, count) in zip(ws, ((0, VBLK), (VBLK, AUDIO_ROWS))):
+            both = [ref[towers[step], pl.ds(first, count), :] for ref in (own, sibling)]
+            y = nn_dot(jnp.concatenate(both, axis=0), w).astype(jnp.bfloat16)
+            for i in range(2):
+                out, at = targets[2 * step + i]
+                out[pl.ds(at + first, count), :] = y[i * count : (i + 1) * count]
+
+
+def project_cross(place, own, sibling, w, after):
     width = w.shape[-1]
     tile = width // 3
     return pl.pallas_call(
@@ -361,6 +378,8 @@
                 full(own.shape),
                 full(own.shape),
                 pl.BlockSpec(w.shape[:-1] + (tile,), lambda i, place: (0, 0, 0, 0, i)),
+                ANY,
+                ANY,
             ],
             out_specs=[
                 pl.BlockSpec((n * BOTH, tile), lambda i, place: (0, i)) for n in (2, 2, 2, 1, 1)
@@ -369,7 +388,7 @@
         compiler_params=pltpu.CompilerParams(vmem_limit_bytes=60 * MIB),
         cost_estimate=BRIEF,
         name="project_cross",
-    )(place, own, sibling, w)
+    )(place, own, sibling, w, *after)
 
 
 def project_self_kernel(place, own, sibling, w_ref, *refs):
@@ -379,7 +398,7 @@
     )
     w = jnp.concatenate(
         [
-            weight_rows([functools.partial(lambda b, h: w_ref[b * TOWERS + t, h], b) for b in range(4)])
+            weight_rows([functools.partial(lambda b, h: w_ref[b * TOWERS + lax.rem(place[1] - t + TOWERS, TOWERS), h], b) for b in range(4)])
             for t in range(TOWERS)
         ],
         axis=0,
@@ -500,41 +519,47 @@
     gains = gate_gains[0]
     margins = margin[0]
 
-    parts, w_self, w_rest = pack_video(place, video_k[0], video_v[0], video_q[0], out_weight)
+    parts, w_self, w_rest, *audio = pack(
+        place, video_k[0], video_v[0], video_q[0], audio_k[0], audio_v[0], audio_q[0], out_weight
+    )
     w_rest = lax.all_gather(w_rest, "batch", axis=0, tiled=False)
-    w_self = lax.all_gather(w_self, "tower", axis=0, tiled=False)
     query = exchange_towers(parts)
     own = query[:, :2]
     sibling = swap_core(own)
     near, far = hop(own), hop(sibling)
-
-    audio = exchange_towers(pack_audio(place, audio_q[0], audio_k[0], audio_v[0]))
+    mains = [audio[0]] + [send_main(audio[step], step) for step in (1, 2, 3)]
+    halos = [audio[4]] + [send_halo(audio[4 + step], step) for step in (1, 2, 3)]
+    w_self = gate(w_self, *mains[1:])
+    w_parts = jnp.stack([w_self] + [shift_tower(w_self, step) for step in (1, 2, 3)])
+    w_self = lax.all_gather(w_parts, "batch", axis=0, tiled=False)
+    w_self = w_self.reshape((16,) + w_self.shape[2:])
+
     acc, top, total, token = flash(query, [own, sibling], None, False)
-    near, far = gate(near, token), gate(far, token)
-    third = far
+    near, far = gate(near, token, *mains[1:], *halos[1:]), gate(far, token)
+    crossed = cross(place, margins, query, mains, halos, own, sibling, far)
+
     tokens = [token]
+    after = (crossed,)
     for step in range(1, 4):
         now = [near, far, swap_core(near), swap_core(far)]
         near, far = hop(near), (hop(far) if step < 3 else None)
-        acc, top, total, token = flash(query, now, (acc, top, total), False)
+        acc, top, total, token = flash(query, now, (acc, top, total), False, after)
         tokens.append(token)
+        after = ()
         if step == 1:
-            crossed = cross(place, margins, query, gate(audio, token), own, sibling, third)
             rest, up, down, up_later, down_later = project_cross(
-                place, crossed, swap_core(crossed), w_rest
+                place, crossed, swap_core(crossed), w_rest, (token, w_parts)
             )
-            acc = gate(acc, rest)
-            w_self = lax.all_gather(gate(w_self, token), "batch", axis=0, tiled=False)
-            w_self = w_self.reshape((16,) + w_self.shape[2:])
+            after = (rest,)
             up, down = shift_tower(up, 1), shift_tower(down, -1)
             up_later = add(up_later, up[:BOTH])
             down_later = add(down_later, down[BOTH:])
         near = gate(near, tokens[step - 1])
         if step < 3:
             far = gate(far, tokens[step - 1])
-    acc = gate(acc, up_later, down_later)
+    after = (up_later, down_later)
     up_later, down_later = shift_tower(up_later, 1), shift_tower(down_later, -1)
-    video_self = flash(query, [near, swap_core(near)], (acc, top, total), True)
+    video_self = flash(query, [near, swap_core(near)], (acc, top, total), True, after)
     base = (rest, up, down, up_later, down_later)
 
     self_all = exchange_towers(video_self.reshape(TOWERS, VBLK, GW))

time: 209 us -> 219 us (1.048)
  waiting for transfers between devices: 49.6 us -> 58.5 us
  starting transfers between devices: 51.7 us -> 54.9 us
  Pallas kernels: 56.9 us -> 54.3 us
    ppermute x4 -> x7, waiting for transfers between devices: 15.7 us -> 30.5 us  [shift_tower(): lax.ppermute(value, 'tower', [(i, (i + step) % TOWERS) for i in range(TOW...]
    ppermute x0 -> x6, waiting for transfers between devices: none -> 11.9 us  [the longest x3 11.9 us: send_main(): return lax.ppermute(value, ('ctx', 'tower'), ctx_towers(pairs))]
    ppermute x11, starting transfers between devices: 21.7 us -> 10 us  [swap_core(): return lax.ppermute(value, 'ctx', [(i, i ^ 1) for i in range(2 * CHIPS)])]
    ppermute x0 -> x6, starting transfers between devices: none -> 9.48 us  [the longest x3 7.5 us: send_main(): return lax.ppermute(value, ('ctx', 'tower'), ctx_towers(pairs))]
    ppermute x7, waiting for transfers between devices: 18.5 us -> 9.49 us  [hop(): lax.ppermute(value, 'ctx', [(i, (i + 2 - 4 * (i % 2)) % total) for i in r...]
    all_to_all x2 -> x1, waiting for transfers between devices: 11 us -> 5.12 us  [exchange_towers(): lax.all_to_all(value, 'tower', split_axis=0, concat_axis=0, tiled=True)]
    ppermute x4 -> x7, starting transfers between devices: 4.17 us -> 9.78 us  [shift_tower(): lax.ppermute(value, 'tower', [(i, (i + step) % TOWERS) for i in range(TOW...]
    all_to_all x2 -> x1, starting transfers between devices: 7.18 us -> 3.46 us  [exchange_towers(): lax.all_to_all(value, 'tower', split_axis=0, concat_axis=0, tiled=True)]
  transfers between devices with their start and end apart: 27 -> 34, of which waited for: 12 -> 14; matrix products, arithmetic and copies ran while one was open for 2% -> 3% of each run, Pallas kernels for 23% -> 20%
where the time goes in v5:
time: 219 us; the launch traced here: 218 us
  waiting for transfers between devices  58.5 us (27%)
  starting transfers between devices  54.9 us (25%)
  Pallas kernels  54.3 us (25%)
  blocking collectives  18.5 us (8%)
  between operations  14.4 us (7%)
  local copies, waits for them, and re-layouts  12.3 us (6%)
  other arithmetic  4.98 us (2%)
    pallas_call x5, Pallas kernels, flash(): pl.pallas_call(functools.partial(flash_kernel, len(kvs), state is None, l...  30.7 us
    ppermute x7, waiting for transfers between devices, shift_tower(): lax.ppermute(value, 'tower', [(i, (i + step) % TOWERS) for i in range(TOW...  30.5 us
    ppermute x7, starting transfers between devices, hop(): lax.ppermute(value, 'ctx', [(i, (i + 2 - 4 * (i % 2)) % total) for i in r...  22.1 us
    all_to_all x1, blocking collectives, exchange_towers(): lax.all_to_all(value, 'tower', split_axis=0, concat_axis=0, tiled=True)  18.5 us
    ppermute x3, waiting for transfers between devices, send_main(): return lax.ppermute(value, ('ctx', 'tower'), ctx_towers(pairs))  11.9 us
    unnamed x57, local copies, waits for them, and re-layouts  11.6 us
    ppermute x11, starting transfers between devices, swap_core(): return lax.ppermute(value, 'ctx', [(i, i ^ 1) for i in range(2 * CHIPS)])  10 us
    ppermute x7, starting transfers between devices, shift_tower(): lax.ppermute(value, 'tower', [(i, (i + step) % TOWERS) for i in range(TOW...  9.78 us
  transfers between devices with their start and end apart: 34, of which 14 were waited for; matrix products, arithmetic and copies ran while one was open for 3% of the time, Pallas kernels for 20%

profile of v5, /device:TPU:1, one launch (start us, length us, event | category | flops | bytes accessed | tf_op | source)
XLA Modules:
  0.0 218.0 jit_solution(150727836459869505)
XLA Ops:
  7.9 4.3 %pack.1 = (bf16[4,3,3,128,128]{4,3,2,1,0:T(8,128)(2,1)}, bf16[3,32,1536]{2,1,0:T(8,128)(2,1)}, bf16[2,3,32,1536]{3,2,1,0:T(8,128)(2,1)}, bf16[480,384]{1,0:T(8,1...) custom-call(s32[5]{0:T(128)} %stack.38.place, ...), custom_call_target="tpu_custom_call" | custom-call | tf_op jit(solution)/shard_map/pack/pallas_call | solution.py:123
  12.3 4.0 %collective-permute-start.2 = (bf16[480,384]{1,0:T(8,128)(2,1)}, bf16[480,384]{1,0:T(8,128)(2,1)S(1)}, u32[]{:S(2)}, u32[]{:S(2)}) collective-permute-start(bf16[480,384]{1,0:T(8,128)(2,1)} %get-tuple-element.40), channel_id=1, source_target_pairs={{0,1},{4,5},{8,9},{12,13},{17,18},{21,22},{25,26},{29,30},{34,35},... | collective-permute-start | bytes 1105928 | tf_op jit(solution)/shard_map/ppermute | solution.py:150
  19.8 4.0 %collective-permute-done.2.refs_2_.refs_1_ = bf16[480,384]{1,0:T(8,128)(2,1)S(1)} collective-permute-done((bf16[480,384]{1,0:T(8,128)(2,1)}, bf16[480,384]{1,0:T(8,128)(2,1)S(1)}, u32[]{:S(2)}, u32[]{:S(2)}) %collective-permute-start.2) | collective-permute-done | bytes 368672 | tf_op jit(solution)/shard_map/ppermute | solution.py:150
  23.8 7.9 %collective-permute-done.3.refs_3_.refs_2_ = bf16[480,384]{1,0:T(8,128)(2,1)S(1)} collective-permute-done((bf16[480,384]{1,0:T(8,128)(2,1)}, bf16[480,384]{1,0:T(8,128)(2,1)S(1)}, u32[]{:S(2)}, u32[]{:S(2)}) %collective-permute-start.3) | collective-permute-done | bytes 368672 | tf_op jit(solution)/shard_map/ppermute | solution.py:150
  32.6 3.6 %collective-permute-start.19 = (bf16[3,32,1536]{2,1,0:T(8,128)(2,1)}, bf16[3,32,1536]{2,1,0:T(8,128)(2,1)S(1)}, u32[]{:S(2)}, u32[]{:S(2)}) collective-permute-start(bf16[3,32,1536]{2,1,0:T(8,128)(2,1)} %gate.13), channel_id=1, source_target_pairs={{0,2},{1,3},{2,0},{3,1},{4,6},{5,7},{6,4},{7,5},{8,10},{9,11},{10,... | collective-permute-start | bytes 884744 | tf_op jit(solution)/shard_map/ppermute | solution.py:502
  41.1 7.4 %collective-permute-done.19 = bf16[3,32,1536]{2,1,0:T(8,128)(2,1)S(1)} collective-permute-done((bf16[3,32,1536]{2,1,0:T(8,128)(2,1)}, bf16[3,32,1536]{2,1,0:T(8,128)(2,1)S(1)}, u32[]{:S(2)}, u32[]{:S(2)}) %collective-permute-start.19) | collective-permute-done | bytes 294944 | tf_op jit(solution)/shard_map/ppermute | solution.py:502
  51.9 18.5 %all_to_all.10.refs_0_.q_ref = bf16[4,3,3,128,128]{4,3,2,1,0:T(8,128)(2,1)S(1)} all-to-all(bf16[4,3,3,128,128]{4,3,2,1,0:T(8,128)(2,1)S(1)} %copy-done.16), channel_id=1, replica_groups=mesh['batch'=4,'ctx'=16,'tower'=4] {'tower'}, dimensions={0} | all-to-all | bytes 2359296 | tf_op jit(solution)/shard_map/all_to_all | solution.py:494
  73.9 6.9 %collective-permute-start = (bf16[4,2,3,128,128]{4,3,2,1,0:T(8,128)(2,1)S(1)}, bf16[4,2,3,128,128]{4,3,2,1,0:T(8,128)(2,1)}, u32[]{:S(2)}, u32[]{:S(2)}) collective-permute-start(bf16[4,2,3,128,128]{4,3,2,1,0:T(8,128)(2,1)S(1)} %slice.12.refs_1_.refs_8_), channel_id=1, source_target_pairs={{0,8},{4,60},{8,16},{12,4},{16,24},{20,12},{24,32},{28,20},{32,40}... | collective-permute-start | bytes 2359304 | tf_op jit(solution)/shard_map/ppermute | solution.py:507
  84.8 4.8 %flash.5 = (f32[512,384]{1,0:T(8,128)}, f32[512,384]{1,0:T(8,128)}, f32[512,384]{1,0:T(8,128)}, f32[8,128]{1,0:T(8,128)}) custom-call(bf16[4,3,3,128,128]{4,3,2,1,0:T(8,128)(2,1)} %copy-done.6, bf16[4,2,3,128,128]{4,3,2,1,0:T(8,128)(2,1)} %copy-done.8, bf16[4,2,3,128,128]{4,3,2,1,0:T(8,128)(2,1)} %copy-done.15), custom_call_target="tpu_custom_call" | custom-call | flops 1 | bytes 1 | tf_op jit(solution)/shard_map/flash/pallas_call | solution.py:231
  93.4 4.8 %collective-permute-done.10.refs_0_ = bf16[4,2,3,128,128]{4,3,2,1,0:T(8,128)(2,1)S(1)} collective-permute-done((bf16[4,2,3,128,128]{4,3,2,1,0:T(8,128)(2,1)S(1)}, bf16[4,2,3,128,128]{4,3,2,1,0:T(8,128)(2,1)S(1)}, u32[]{:S(2)}, u32[]{:S(2)}) %collective-permute-start.10) | collective-permute-done | bytes 786464 | tf_op jit(solution)/shard_map/ppermute | solution.py:507
  99.1 3.5 %collective-permute-start.14 = (bf16[4,2,3,128,128]{4,3,2,1,0:T(8,128)(2,1)}, bf16[4,2,3,128,128]{4,3,2,1,0:T(8,128)(2,1)}, u32[]{:S(2)}, u32[]{:S(2)}) collective-permute-start(bf16[4,2,3,128,128]{4,3,2,1,0:T(8,128)(2,1)} %gate.10.refs_10_.refs_2_), channel_id=1, source_target_pairs={{0,8},{4,60},{8,16},{12,4},{16,24},{20,12},{24,32},{28,20},{32,40}... | collective-permute-start | bytes 2359304 | tf_op jit(solution)/shard_map/ppermute | solution.py:507
  103.2 3.6 %collective-permute-done.8.refs_0_ = bf16[4,2,3,128,128]{4,3,2,1,0:T(8,128)(2,1)} collective-permute-done((bf16[4,2,3,128,128]{4,3,2,1,0:T(8,128)(2,1)}, bf16[4,2,3,128,128]{4,3,2,1,0:T(8,128)(2,1)}, u32[]{:S(2)}, u32[]{:S(2)}) %collective-permute-start.8) | collective-permute-done | bytes 786464 | tf_op jit(solution)/shard_map/ppermute | solution.py:507
  110.9 6.8 %cross.1.refs_8_.own = bf16[4,160,384]{2,1,0:T(8,128)(2,1)} custom-call(s32[5]{0:T(128)} %stack.38.place, s32[64,3]{1,0:T(8,128)} %bitcast.36, bf16[4,3,3,128,128]{4,3,2,1,0:T(8,128)(2,1)} %copy-done.6, bf16[480,384]{1,0:T(8,128)(2,1)} %get-tuple-element.49.refs_0_, bf16[480,384]{1,0:T(8,128)(2,1)} %copy-done.9, bf16[480,384]{1,0:T(8,128)(2,1)} %copy-done.10, ...), custom_call_target="tpu_custom_call" | custom-call | flops 1 | bytes 1 | tf_op jit(solution)/shard_map/cross/pallas_call | solution.py:319
  119.9 6.8 %flash.6 = (f32[512,384]{1,0:T(8,128)}, f32[512,384]{1,0:T(8,128)}, f32[512,384]{1,0:T(8,128)}, f32[8,128]{1,0:T(8,128)}) custom-call(bf16[4,3,3,128,128]{4,3,2,1,0:T(8,128)(2,1)} %copy-done.6, bf16[4,2,3,128,128]{4,3,2,1,0:T(8,128)(2,1)} %gate.8.refs_1_, bf16[4,2,3,128,128]{4,3,2,1,0:T(8,128)(2,1)} %gate.10.refs_10_.refs_2_, ...), custom_call_target="tpu_custom_call" | custom-call | flops 1 | bytes 1 | tf_op jit(solution)/shard_map/flash/pallas_call | solution.py:231
  126.8 6.4 %project_cross.1 = (bf16[320,1536]{1,0:T(8,128)(2,1)}, bf16[320,1536]{1,0:T(8,128)(2,1)}, bf16[320,1536]{1,0:T(8,128)(2,1)}, bf16[160,1536]{1,0:T(8,128)(2,1)}, bf16[160,1536]{1,0:T(8,128)(2,1)}) custom-call(s32[5]{0:T(128)} %stack.38.place, bf16[4,160,384]{2,1,0:T(8,128)(2,1)} %cross.1.refs_8_.own, bf16[4,160,384]{2,1,0:T(8,128)(2,1)} %collective-permute-done.17.sibling, ...), custom_call_target="tpu_custom_call" | custom-call | flops 1 | bytes 1 | tf_op jit(solution)/shard_map/project_cross/pallas_call | solution.py:371
  139.2 6.9 %flash.7 = (f32[512,384]{1,0:T(8,128)}, f32[512,384]{1,0:T(8,128)}, f32[512,384]{1,0:T(8,128)}, f32[8,128]{1,0:T(8,128)}) custom-call(bf16[4,3,3,128,128]{4,3,2,1,0:T(8,128)(2,1)} %copy-done.6, bf16[4,2,3,128,128]{4,3,2,1,0:T(8,128)(2,1)} %gate.9.refs_1_, bf16[4,2,3,128,128]{4,3,2,1,0:T(8,128)(2,1)} %gate.12.refs_2_, ...), custom_call_target="tpu_custom_call" | custom-call | flops 1 | bytes 1 | tf_op jit(solution)/shard_map/flash/pallas_call | solution.py:231
  148.9 8.1 %collective-permute-done.26.refs_2_ = bf16[320,1536]{1,0:T(8,128)(2,1)S(1)} collective-permute-done((bf16[320,1536]{1,0:T(8,128)(2,1)}, bf16[320,1536]{1,0:T(8,128)(2,1)S(1)}, u32[]{:S(2)}, u32[]{:S(2)}) %collective-permute-start.26) | collective-permute-done | bytes 983072 | tf_op jit(solution)/shard_map/ppermute | solution.py:502
  159.0 3.5 %collective-permute-done.25.refs_1_ = bf16[320,1536]{1,0:T(8,128)(2,1)S(1)} collective-permute-done((bf16[320,1536]{1,0:T(8,128)(2,1)}, bf16[320,1536]{1,0:T(8,128)(2,1)S(1)}, u32[]{:S(2)}, u32[]{:S(2)}) %collective-permute-start.25) | collective-permute-done | bytes 983072 | tf_op jit(solution)/shard_map/ppermute | solution.py:502
  164.3 6.8 %flash.8 = (f32[512,384]{1,0:T(8,128)}, f32[512,384]{1,0:T(8,128)}, f32[512,384]{1,0:T(8,128)}, f32[8,128]{1,0:T(8,128)}) custom-call(bf16[4,3,3,128,128]{4,3,2,1,0:T(8,128)(2,1)} %copy-done.6, bf16[4,2,3,128,128]{4,3,2,1,0:T(8,128)(2,1)} %gate.11.refs_1_, bf16[4,2,3,128,128]{4,3,2,1,0:T(8,128)(2,1)} %gate.15.refs_2_, ...), custom_call_target="tpu_custom_call" | custom-call | flops 1 | bytes 1 | tf_op jit(solution)/shard_map/flash/pallas_call | solution.py:231
  171.2 5.4 %flash.9 = bf16[512,384]{1,0:T(8,128)(2,1)} custom-call(bf16[4,3,3,128,128]{4,3,2,1,0:T(8,128)(2,1)} %copy-done.6, bf16[4,2,3,128,128]{4,3,2,1,0:T(8,128)(2,1)} %gate.14.refs_1_, bf16[4,2,3,128,128]{4,3,2,1,0:T(8,128)(2,1)} %collective-permute-done.21.refs_2_, f32[512,384]{1,0:T(8,128)} %get-tuple-element.62.refs_3_, f32[512,384]{1,0:T(8,128)} %get-tuple-element.63.refs_4_, ...), custom_call_target="tpu_custom_call" | custom-call | flops 1 | bytes 1 | tf_op jit(solution)/shard_map/flash/pallas_call | solution.py:231
  176.7 3.5 %all-to-all-start.1 = ((bf16[4,128,384]{2,1,0:T(8,128)(2,1)}), bf16[4,128,384]{2,1,0:T(8,128)(2,1)S(1)}, u32[]{:S(2)}, u32[]{:S(2)}) async-start(bf16[4,128,384]{2,1,0:T(8,128)(2,1)} %bitcast.23), calls=%async_computation.1 | async-start | bytes 786432 | tf_op jit(solution)/shard_map/all_to_all | solution.py:494
  182.8 5.1 %all-to-all-done.1.own = bf16[4,128,384]{2,1,0:T(8,128)(2,1)S(1)} async-done(((bf16[4,128,384]{2,1,0:T(8,128)(2,1)}), bf16[4,128,384]{2,1,0:T(8,128)(2,1)S(1)}, u32[]{:S(2)}, u32[]{:S(2)}) %all-to-all-start.1) | async-done | bytes 393248 | tf_op jit(solution)/shard_map/all_to_all | solution.py:494
  189.9 7.1 %collective-permute-done.29.refs_4_ = bf16[160,1536]{1,0:T(8,128)(2,1)} collective-permute-done((bf16[160,1536]{1,0:T(8,128)(2,1)}, bf16[160,1536]{1,0:T(8,128)(2,1)}, u32[]{:S(2)}, u32[]{:S(2)}) %collective-permute-start.29) | collective-permute-done | bytes 491552 | tf_op jit(solution)/shard_map/ppermute | solution.py:502
  202.6 4.8 %project_self.1 = (bf16[128,3072]{1,0:T(8,128)(2,1)}, bf16[24,3072]{1,0:T(8,128)(2,1)}, bf16[160,1536]{1,0:T(8,128)(2,1)S(1)}) custom-call(s32[5]{0:T(128)S(1)} %copy-done.5, bf16[4,128,384]{2,1,0:T(8,128)(2,1)S(1)} %all-to-all-done.1.own, bf16[4,128,384]{2,1,0:T(8,128)(2,1)S(1)} %copy-done.3, bf16[16,3,32,1536]{3,2,1,0:T(8,128)(2,1)S(1)} %copy-done, ...), custom_call_target="tpu_custom_call" | custom-call | flops 1 | bytes 1 | tf_op jit(solution)/shard_map/project_self/pallas_call | solution.py:426
  (127 shorter events, 59.1 us)
Async XLA Ops:
  7.2 119.6 %all-gather.5.cloned.1.call-start = ((), (), s32[]{:S(2)}) async-start(), calls=%async_computation.2 | async-start | bytes 2949120 | tf_op jit(solution)/shard_map/all_gather | solution.py:525
  12.2 187.1 %all-gather.7.cloned.1.call-start = ((), (), s32[]{:S(2)}) async-start(), calls=%async_computation.3 | async-start | bytes 5898240 | tf_op jit(solution)/shard_map/all_gather | solution.py:534
  12.3 11.5 %collective-permute-start.2 = (bf16[480,384]{1,0:T(8,128)(2,1)}, bf16[480,384]{1,0:T(8,128)(2,1)S(1)}, u32[]{:S(2)}, u32[]{:S(2)}) collective-permute-start(bf16[480,384]{1,0:T(8,128)(2,1)} %get-tuple-element.40), channel_id=1, source_target_pairs={{0,1},{4,5},{8,9},{12,13},{17,18},{21,22},{25,26},{29,30},{34,35},... | collective-permute-start | bytes 1105928 | tf_op jit(solution)/shard_map/ppermute | solution.py:150
  16.2 15.4 %collective-permute-start.3 = (bf16[480,384]{1,0:T(8,128)(2,1)}, bf16[480,384]{1,0:T(8,128)(2,1)S(1)}, u32[]{:S(2)}, u32[]{:S(2)}) collective-permute-start(bf16[480,384]{1,0:T(8,128)(2,1)} %get-tuple-element.41), channel_id=1, source_target_pairs={{0,2},{4,6},{8,10},{12,14},{17,19},{21,23},{25,27},{29,31},{34,32}... | collective-permute-start | bytes 1105928 | tf_op jit(solution)/shard_map/ppermute | solution.py:150
  18.5 13.2 %collective-permute-start.4 = (bf16[480,384]{1,0:T(8,128)(2,1)}, bf16[480,384]{1,0:T(8,128)(2,1)S(1)}, u32[]{:S(2)}, u32[]{:S(2)}) collective-permute-start(bf16[480,384]{1,0:T(8,128)(2,1)} %get-tuple-element.42), channel_id=1, source_target_pairs={{0,3},{4,7},{8,11},{12,15},{17,16},{21,20},{25,24},{29,28},{34,33}... | collective-permute-start | bytes 1105928 | tf_op jit(solution)/shard_map/ppermute | solution.py:150
  32.6 15.9 %collective-permute-start.19 = (bf16[3,32,1536]{2,1,0:T(8,128)(2,1)}, bf16[3,32,1536]{2,1,0:T(8,128)(2,1)S(1)}, u32[]{:S(2)}, u32[]{:S(2)}) collective-permute-start(bf16[3,32,1536]{2,1,0:T(8,128)(2,1)} %gate.13), channel_id=1, source_target_pairs={{0,2},{1,3},{2,0},{3,1},{4,6},{5,7},{6,4},{7,5},{8,10},{9,11},{10,... | collective-permute-start | bytes 884744 | tf_op jit(solution)/shard_map/ppermute | solution.py:502
  36.2 12.3 %collective-permute-start.20 = (bf16[3,32,1536]{2,1,0:T(8,128)(2,1)}, bf16[3,32,1536]{2,1,0:T(8,128)(2,1)S(1)}, u32[]{:S(2)}, u32[]{:S(2)}) collective-permute-start(bf16[3,32,1536]{2,1,0:T(8,128)(2,1)} %gate.13), channel_id=1, source_target_pairs={{0,3},{1,0},{2,1},{3,2},{4,7},{5,4},{6,5},{7,6},{8,11},{9,8},{10,9... | collective-permute-start | bytes 884744 | tf_op jit(solution)/shard_map/ppermute | solution.py:502
  73.9 15.9 %collective-permute-start = (bf16[4,2,3,128,128]{4,3,2,1,0:T(8,128)(2,1)S(1)}, bf16[4,2,3,128,128]{4,3,2,1,0:T(8,128)(2,1)}, u32[]{:S(2)}, u32[]{:S(2)}) collective-permute-start(bf16[4,2,3,128,128]{4,3,2,1,0:T(8,128)(2,1)S(1)} %slice.12.refs_1_.refs_8_), channel_id=1, source_target_pairs={{0,8},{4,60},{8,16},{12,4},{16,24},{20,12},{24,32},{28,20},{32,40}... | collective-permute-start | bytes 2359304 | tf_op jit(solution)/shard_map/ppermute | solution.py:507
  80.9 17.4 %collective-permute-start.10 = (bf16[4,2,3,128,128]{4,3,2,1,0:T(8,128)(2,1)S(1)}, bf16[4,2,3,128,128]{4,3,2,1,0:T(8,128)(2,1)S(1)}, u32[]{:S(2)}, u32[]{:S(2)}) collective-permute-start(bf16[4,2,3,128,128]{4,3,2,1,0:T(8,128)(2,1)S(1)} %collective-permute-done.1.refs_2_.refs_9_), channel_id=1, source_target_pairs={{0,8},{4,60},{8,16},{12,4},{16,24},{20,12},{24,32},{28,20},{32,40}... | collective-permute-start | bytes 2359304 | tf_op jit(solution)/shard_map/ppermute | solution.py:507
  90.3 16.5 %collective-permute-start.8 = (bf16[4,2,3,128,128]{4,3,2,1,0:T(8,128)(2,1)}, bf16[4,2,3,128,128]{4,3,2,1,0:T(8,128)(2,1)}, u32[]{:S(2)}, u32[]{:S(2)}) collective-permute-start(bf16[4,2,3,128,128]{4,3,2,1,0:T(8,128)(2,1)} %gate.8.refs_1_), channel_id=1, source_target_pairs={{0,8},{4,60},{8,16},{12,4},{16,24},{20,12},{24,32},{28,20},{32,40}... | collective-permute-start | bytes 2359304 | tf_op jit(solution)/shard_map/ppermute | solution.py:507
  99.1 18.6 %collective-permute-start.14 = (bf16[4,2,3,128,128]{4,3,2,1,0:T(8,128)(2,1)}, bf16[4,2,3,128,128]{4,3,2,1,0:T(8,128)(2,1)}, u32[]{:S(2)}, u32[]{:S(2)}) collective-permute-start(bf16[4,2,3,128,128]{4,3,2,1,0:T(8,128)(2,1)} %gate.10.refs_10_.refs_2_), channel_id=1, source_target_pairs={{0,8},{4,60},{8,16},{12,4},{16,24},{20,12},{24,32},{28,20},{32,40}... | collective-permute-start | bytes 2359304 | tf_op jit(solution)/shard_map/ppermute | solution.py:507
  102.6 16.1 %collective-permute-start.11 = (bf16[4,2,3,128,128]{4,3,2,1,0:T(8,128)(2,1)}, bf16[4,2,3,128,128]{4,3,2,1,0:T(8,128)(2,1)S(1)}, u32[]{:S(2)}, u32[]{:S(2)}) collective-permute-start(bf16[4,2,3,128,128]{4,3,2,1,0:T(8,128)(2,1)} %gate.8.refs_1_), channel_id=1, source_target_pairs={{0,4},{4,0},{8,12},{12,8},{16,20},{20,16},{24,28},{28,24},{32,36},... | collective-permute-start | bytes 2359304 | tf_op jit(solution)/shard_map/ppermute | solution.py:511
  102.6 16.1 %collective-permute-start.12 = (bf16[4,2,3,128,128]{4,3,2,1,0:T(8,128)(2,1)}, bf16[4,2,3,128,128]{4,3,2,1,0:T(8,128)(2,1)S(1)}, u32[]{:S(2)}, u32[]{:S(2)}) collective-permute-start(bf16[4,2,3,128,128]{4,3,2,1,0:T(8,128)(2,1)} %gate.10.refs_10_.refs_2_), channel_id=1, source_target_pairs={{0,4},{4,0},{8,12},{12,8},{16,20},{20,16},{24,28},{28,24},{32,36},... | collective-permute-start | bytes 2359304 | tf_op jit(solution)/shard_map/ppermute | solution.py:511
  106.8 27.8 %collective-permute-start.9 = (bf16[4,2,3,128,128]{4,3,2,1,0:T(8,128)(2,1)}, bf16[4,2,3,128,128]{4,3,2,1,0:T(8,128)(2,1)S(1)}, u32[]{:S(2)}, u32[]{:S(2)}) collective-permute-start(bf16[4,2,3,128,128]{4,3,2,1,0:T(8,128)(2,1)} %gate.9.refs_1_), channel_id=1, source_target_pairs={{0,8},{4,60},{8,16},{12,4},{16,24},{20,12},{24,32},{28,20},{32,40}... | collective-permute-start | bytes 2359304 | tf_op jit(solution)/shard_map/ppermute | solution.py:507
  117.8 19.9 %collective-permute-start.22 = (bf16[4,2,3,128,128]{4,3,2,1,0:T(8,128)(2,1)}, bf16[4,2,3,128,128]{4,3,2,1,0:T(8,128)(2,1)S(1)}, u32[]{:S(2)}, u32[]{:S(2)}) collective-permute-start(bf16[4,2,3,128,128]{4,3,2,1,0:T(8,128)(2,1)} %gate.12.refs_2_), channel_id=1, source_target_pairs={{0,8},{4,60},{8,16},{12,4},{16,24},{20,12},{24,32},{28,20},{32,40}... | collective-permute-start | bytes 2359304 | tf_op jit(solution)/shard_map/ppermute | solution.py:507
  133.1 24.0 %collective-permute-start.26 = (bf16[320,1536]{1,0:T(8,128)(2,1)}, bf16[320,1536]{1,0:T(8,128)(2,1)S(1)}, u32[]{:S(2)}, u32[]{:S(2)}) collective-permute-start(bf16[320,1536]{1,0:T(8,128)(2,1)} %get-tuple-element.68), channel_id=1, source_target_pairs={{0,3},{1,0},{2,1},{3,2},{4,7},{5,4},{6,5},{7,6},{8,11},{9,8},{10,9... | collective-permute-start | bytes 2949128 | tf_op jit(solution)/shard_map/ppermute | solution.py:502
  135.4 11.5 %collective-permute-start.13 = (bf16[4,2,3,128,128]{4,3,2,1,0:T(8,128)(2,1)}, bf16[4,2,3,128,128]{4,3,2,1,0:T(8,128)(2,1)}, u32[]{:S(2)}, u32[]{:S(2)}) collective-permute-start(bf16[4,2,3,128,128]{4,3,2,1,0:T(8,128)(2,1)} %gate.11.refs_1_), channel_id=1, source_target_pairs={{0,8},{4,60},{8,16},{12,4},{16,24},{20,12},{24,32},{28,20},{32,40}... | collective-permute-start | bytes 2359304 | tf_op jit(solution)/shard_map/ppermute | solution.py:507
  137.7 24.8 %collective-permute-start.25 = (bf16[320,1536]{1,0:T(8,128)(2,1)}, bf16[320,1536]{1,0:T(8,128)(2,1)S(1)}, u32[]{:S(2)}, u32[]{:S(2)}) collective-permute-start(bf16[320,1536]{1,0:T(8,128)(2,1)} %get-tuple-element.66), channel_id=1, source_target_pairs={{0,1},{1,2},{2,3},{3,0},{4,5},{5,6},{6,7},{7,4},{8,9},{9,10},{10,1... | collective-permute-start | bytes 2949128 | tf_op jit(solution)/shard_map/ppermute | solution.py:502
  138.6 24.8 %collective-permute-start.23 = (bf16[4,2,3,128,128]{4,3,2,1,0:T(8,128)(2,1)S(1)}, bf16[4,2,3,128,128]{4,3,2,1,0:T(8,128)(2,1)S(1)}, u32[]{:S(2)}, u32[]{:S(2)}) collective-permute-start(bf16[4,2,3,128,128]{4,3,2,1,0:T(8,128)(2,1)S(1)} %copy-done.13), channel_id=1, source_target_pairs={{0,4},{4,0},{8,12},{12,8},{16,20},{20,16},{24,28},{28,24},{32,36},... | collective-permute-start | bytes 2359304 | tf_op jit(solution)/shard_map/ppermute | solution.py:511
  138.7 24.8 %collective-permute-start.24 = (bf16[4,2,3,128,128]{4,3,2,1,0:T(8,128)(2,1)}, bf16[4,2,3,128,128]{4,3,2,1,0:T(8,128)(2,1)}, u32[]{:S(2)}, u32[]{:S(2)}) collective-permute-start(bf16[4,2,3,128,128]{4,3,2,1,0:T(8,128)(2,1)} %gate.15.refs_2_), channel_id=1, source_target_pairs={{0,4},{4,0},{8,12},{12,8},{16,20},{20,16},{24,28},{28,24},{32,36},... | collective-permute-start | bytes 2359304 | tf_op jit(solution)/shard_map/ppermute | solution.py:511
  147.0 24.2 %collective-permute-start.21 = (bf16[4,2,3,128,128]{4,3,2,1,0:T(8,128)(2,1)}, bf16[4,2,3,128,128]{4,3,2,1,0:T(8,128)(2,1)}, u32[]{:S(2)}, u32[]{:S(2)}) collective-permute-start(bf16[4,2,3,128,128]{4,3,2,1,0:T(8,128)(2,1)} %gate.14.refs_1_), channel_id=1, source_target_pairs={{0,4},{4,0},{8,12},{12,8},{16,20},{20,16},{24,28},{28,24},{32,36},... | collective-permute-start | bytes 2359304 | tf_op jit(solution)/shard_map/ppermute | solution.py:511
  176.7 11.2 %all-to-all-start.1 = ((bf16[4,128,384]{2,1,0:T(8,128)(2,1)}), bf16[4,128,384]{2,1,0:T(8,128)(2,1)S(1)}, u32[]{:S(2)}, u32[]{:S(2)}) async-start(bf16[4,128,384]{2,1,0:T(8,128)(2,1)} %bitcast.23), calls=%async_computation.1 | async-start | bytes 786432 | tf_op jit(solution)/shard_map/all_to_all | solution.py:494
  180.1 16.9 %collective-permute-start.29 = (bf16[160,1536]{1,0:T(8,128)(2,1)}, bf16[160,1536]{1,0:T(8,128)(2,1)}, u32[]{:S(2)}, u32[]{:S(2)}) collective-permute-start(bf16[160,1536]{1,0:T(8,128)(2,1)} %add_convert_fusion.refs_7_), channel_id=1, source_target_pairs={{0,3},{1,0},{2,1},{3,2},{4,7},{5,4},{6,5},{7,6},{8,11},{9,8},{10,9... | collective-permute-start | bytes 1474568 | tf_op jit(solution)/shard_map/ppermute | solution.py:502
  182.8 15.8 %collective-permute-start.28 = (bf16[160,1536]{1,0:T(8,128)(2,1)}, bf16[160,1536]{1,0:T(8,128)(2,1)}, u32[]{:S(2)}, u32[]{:S(2)}) collective-permute-start(bf16[160,1536]{1,0:T(8,128)(2,1)} %add_convert_fusion.1.refs_6_), channel_id=1, source_target_pairs={{0,1},{1,2},{2,3},{3,0},{4,5},{5,6},{6,7},{7,4},{8,9},{9,10},{10,1... | collective-permute-start | bytes 1474568 | tf_op jit(solution)/shard_map/ppermute | solution.py:502
  (38 other events, 277.2 us)
Sparse Core Ops, SparseCore 0:
  12.3 39.3 all-gather.4
  53.6 58.9 all-gather.6

commit v6 on v5

--- a/solution.py
+++ b/solution.py
@@ -527,16 +527,17 @@
     own = query[:, :2]
     sibling = swap_core(own)
     near, far = hop(own), hop(sibling)
+    audio = [gate(rows, own) for rows in audio]
     mains = [audio[0]] + [send_main(audio[step], step) for step in (1, 2, 3)]
     halos = [audio[4]] + [send_halo(audio[4 + step], step) for step in (1, 2, 3)]
-    w_self = gate(w_self, *mains[1:])
+
+    acc, top, total, token = flash(query, [own, sibling], None, False)
+    near, far = gate(near, token, *mains[1:], *halos[1:]), gate(far, token)
+    crossed = cross(place, margins, query, mains, halos, own, sibling, far)
+    w_self = gate(w_self, token, *mains[1:])
     w_parts = jnp.stack([w_self] + [shift_tower(w_self, step) for step in (1, 2, 3)])
     w_self = lax.all_gather(w_parts, "batch", axis=0, tiled=False)
     w_self = w_self.reshape((16,) + w_self.shape[2:])
-
-    acc, top, total, token = flash(query, [own, sibling], None, False)
-    near, far = gate(near, token, *mains[1:], *halos[1:]), gate(far, token)
-    crossed = cross(place, margins, query, mains, halos, own, sibling, far)
 
     tokens = [token]
     after = (crossed,)
@@ -552,11 +553,11 @@
             )
             after = (rest,)
             up, down = shift_tower(up, 1), shift_tower(down, -1)
-            up_later = add(up_later, up[:BOTH])
-            down_later = add(down_later, down[BOTH:])
         near = gate(near, tokens[step - 1])
         if step < 3:
             far = gate(far, tokens[step - 1])
+    up_later = add(gate(up_later, token), up[:BOTH])
+    down_later = add(gate(down_later, token), down[BOTH:])
     after = (up_later, down_later)
     up_later, down_later = shift_tower(up_later, 1), shift_tower(down_later, -1)
     video_self = flash(query, [near, swap_core(near)], (acc, top, total), True, after)

time: 219 us -> 221 us (level)
  waiting for transfers between devices: 58.5 us -> 52.9 us
  local copies, waits for them, and re-layouts: 12.3 us -> 16.4 us
  starting transfers between devices: 54.9 us -> 58.5 us
    ppermute x7, waiting for transfers between devices: 9.49 us -> 20.4 us  [hop(): lax.ppermute(value, 'ctx', [(i, (i + 2 - 4 * (i % 2)) % total) for i in r...]
    ppermute x7, waiting for transfers between devices: 30.5 us -> 20.6 us  [shift_tower(): lax.ppermute(value, 'tower', [(i, (i + step) % TOWERS) for i in range(TOW...]
    ppermute x3, waiting for transfers between devices: 11.9 us -> 6.49 us  [send_main(): return lax.ppermute(value, ('ctx', 'tower'), ctx_towers(pairs))]
    unnamed x57 -> x61, local copies, waits for them, and re-layouts: 11.6 us -> 15.7 us
    ppermute x11, starting transfers between devices: 10 us -> 13.2 us  [swap_core(): return lax.ppermute(value, 'ctx', [(i, i ^ 1) for i in range(2 * CHIPS)])]
    ppermute x3, starting transfers between devices: 7.5 us -> 4.82 us  [send_main(): return lax.ppermute(value, ('ctx', 'tower'), ctx_towers(pairs))]
  transfers between devices with their start and end apart: 34 -> 34, of which waited for: 14 -> 13; matrix products, arithmetic and copies ran while one was open for 3% -> 2% of each run, Pallas kernels for 20% -> 20%
where the time goes in v6:
time: 221 us; the launch traced here: 220 us
  starting transfers between devices  58.5 us (26%)
  Pallas kernels  54.6 us (25%)
  waiting for transfers between devices  52.9 us (24%)
  blocking collectives  19.5 us (9%)
  local copies, waits for them, and re-layouts  16.4 us (7%)
  between operations  14.4 us (7%)
  other arithmetic  4.04 us (2%)
    pallas_call x5, Pallas kernels, flash(): pl.pallas_call(functools.partial(flash_kernel, len(kvs), state is None, l...  30.7 us
    ppermute x7, starting transfers between devices, hop(): lax.ppermute(value, 'ctx', [(i, (i + 2 - 4 * (i % 2)) % total) for i in r...  23.7 us
    ppermute x7, waiting for transfers between devices, shift_tower(): lax.ppermute(value, 'tower', [(i, (i + step) % TOWERS) for i in range(TOW...  20.6 us
    ppermute x7, waiting for transfers between devices, hop(): lax.ppermute(value, 'ctx', [(i, (i + 2 - 4 * (i % 2)) % total) for i in r...  20.4 us
    all_to_all x1, blocking collectives, exchange_towers(): lax.all_to_all(value, 'tower', split_axis=0, concat_axis=0, tiled=True)  19.5 us
    unnamed x61, local copies, waits for them, and re-layouts  15.7 us
    ppermute x11, starting transfers between devices, swap_core(): return lax.ppermute(value, 'ctx', [(i, i ^ 1) for i in range(2 * CHIPS)])  13.2 us
    ppermute x7, starting transfers between devices, shift_tower(): lax.ppermute(value, 'tower', [(i, (i + step) % TOWERS) for i in range(TOW...  11.3 us
  transfers between devices with their start and end apart: 34, of which 13 were waited for; matrix products, arithmetic and copies ran while one was open for 2% of the time, Pallas kernels for 20%

profile of v6, /device:TPU:1, one launch (start us, length us, event | category | flops | bytes accessed | tf_op | source)
XLA Modules:
  0.0 220.4 jit_solution(3664862769367558994)
XLA Ops:
  7.8 4.3 %pack.1 = (bf16[4,3,3,128,128]{4,3,2,1,0:T(8,128)(2,1)}, bf16[3,32,1536]{2,1,0:T(8,128)(2,1)}, bf16[2,3,32,1536]{3,2,1,0:T(8,128)(2,1)}, bf16[480,384]{1,0:T(8,1...) custom-call(s32[5]{0:T(128)} %stack.38.place, ...), custom_call_target="tpu_custom_call" | custom-call | tf_op jit(solution)/shard_map/pack/pallas_call | solution.py:123
  12.3 19.5 %all_to_all.10.refs_0_.q_ref = bf16[4,3,3,128,128]{4,3,2,1,0:T(8,128)(2,1)S(1)} all-to-all(bf16[4,3,3,128,128]{4,3,2,1,0:T(8,128)(2,1)} %get-tuple-element.39), channel_id=1, replica_groups=mesh['batch'=4,'ctx'=16,'tower'=4] {'tower'}, dimensions={0} | all-to-all | bytes 2359296 | tf_op jit(solution)/shard_map/all_to_all | solution.py:494
  40.6 4.7 %flash.5 = (f32[512,384]{1,0:T(8,128)}, f32[512,384]{1,0:T(8,128)}, f32[512,384]{1,0:T(8,128)}, f32[8,128]{1,0:T(8,128)}) custom-call(bf16[4,3,3,128,128]{4,3,2,1,0:T(8,128)(2,1)} %copy-done.8, bf16[4,2,3,128,128]{4,3,2,1,0:T(8,128)(2,1)} %copy-done.6, bf16[4,2,3,128,128]{4,3,2,1,0:T(8,128)(2,1)} %copy-done.18), custom_call_target="tpu_custom_call" | custom-call | flops 1 | bytes 1 | tf_op jit(solution)/shard_map/flash/pallas_call | solution.py:231
  45.4 6.5 %collective-permute-done.3.refs_3_.refs_2_ = bf16[480,384]{1,0:T(8,128)(2,1)S(1)} collective-permute-done((bf16[480,384]{1,0:T(8,128)(2,1)}, bf16[480,384]{1,0:T(8,128)(2,1)S(1)}, u32[]{:S(2)}, u32[]{:S(2)}) %collective-permute-start.3) | collective-permute-done | bytes 368672 | tf_op jit(solution)/shard_map/ppermute | solution.py:150
  52.7 3.6 %collective-permute-start.19 = (bf16[3,32,1536]{2,1,0:T(8,128)(2,1)}, bf16[3,32,1536]{2,1,0:T(8,128)(2,1)S(1)}, u32[]{:S(2)}, u32[]{:S(2)}) collective-permute-start(bf16[3,32,1536]{2,1,0:T(8,128)(2,1)} %gate.31), channel_id=1, source_target_pairs={{0,2},{1,3},{2,0},{3,1},{4,6},{5,7},{6,4},{7,5},{8,10},{9,11},{10,... | collective-permute-start | bytes 884744 | tf_op jit(solution)/shard_map/ppermute | solution.py:502
  60.5 7.5 %collective-permute-done.19 = bf16[3,32,1536]{2,1,0:T(8,128)(2,1)S(1)} collective-permute-done((bf16[3,32,1536]{2,1,0:T(8,128)(2,1)}, bf16[3,32,1536]{2,1,0:T(8,128)(2,1)S(1)}, u32[]{:S(2)}, u32[]{:S(2)}) %collective-permute-start.19) | collective-permute-done | bytes 294944 | tf_op jit(solution)/shard_map/ppermute | solution.py:502
  71.4 7.4 %collective-permute-start = (bf16[4,2,3,128,128]{4,3,2,1,0:T(8,128)(2,1)S(1)}, bf16[4,2,3,128,128]{4,3,2,1,0:T(8,128)(2,1)S(1)}, u32[]{:S(2)}, u32[]{:S(2)}) collective-permute-start(bf16[4,2,3,128,128]{4,3,2,1,0:T(8,128)(2,1)S(1)} %copy-done.7), channel_id=1, source_target_pairs={{0,8},{4,60},{8,16},{12,4},{16,24},{20,12},{24,32},{28,20},{32,40}... | collective-permute-start | bytes 2359304 | tf_op jit(solution)/shard_map/ppermute | solution.py:507
  81.6 6.1 %collective-permute-done.refs_0_ = bf16[4,2,3,128,128]{4,3,2,1,0:T(8,128)(2,1)S(1)} collective-permute-done((bf16[4,2,3,128,128]{4,3,2,1,0:T(8,128)(2,1)S(1)}, bf16[4,2,3,128,128]{4,3,2,1,0:T(8,128)(2,1)S(1)}, u32[]{:S(2)}, u32[]{:S(2)}) %collective-permute-start) | collective-permute-done | bytes 786464 | tf_op jit(solution)/shard_map/ppermute | solution.py:507
  91.8 4.4 %collective-permute-done.10.refs_0_ = bf16[4,2,3,128,128]{4,3,2,1,0:T(8,128)(2,1)S(1)} collective-permute-done((bf16[4,2,3,128,128]{4,3,2,1,0:T(8,128)(2,1)S(1)}, bf16[4,2,3,128,128]{4,3,2,1,0:T(8,128)(2,1)S(1)}, u32[]{:S(2)}, u32[]{:S(2)}) %collective-permute-start.10) | collective-permute-done | bytes 786464 | tf_op jit(solution)/shard_map/ppermute | solution.py:507
  97.1 3.5 %collective-permute-start.14 = (bf16[4,2,3,128,128]{4,3,2,1,0:T(8,128)(2,1)}, bf16[4,2,3,128,128]{4,3,2,1,0:T(8,128)(2,1)S(1)}, u32[]{:S(2)}, u32[]{:S(2)}) collective-permute-start(bf16[4,2,3,128,128]{4,3,2,1,0:T(8,128)(2,1)} %gate.26.refs_10_.refs_2_), channel_id=1, source_target_pairs={{0,8},{4,60},{8,16},{12,4},{16,24},{20,12},{24,32},{28,20},{32,40}... | collective-permute-start | bytes 2359304 | tf_op jit(solution)/shard_map/ppermute | solution.py:507
  101.2 3.5 %collective-permute-done.8.refs_0_ = bf16[4,2,3,128,128]{4,3,2,1,0:T(8,128)(2,1)} collective-permute-done((bf16[4,2,3,128,128]{4,3,2,1,0:T(8,128)(2,1)}, bf16[4,2,3,128,128]{4,3,2,1,0:T(8,128)(2,1)}, u32[]{:S(2)}, u32[]{:S(2)}) %collective-permute-start.8) | collective-permute-done | bytes 786464 | tf_op jit(solution)/shard_map/ppermute | solution.py:507
  108.1 5.0 %collective-permute-done.14.refs_0_ = bf16[4,2,3,128,128]{4,3,2,1,0:T(8,128)(2,1)S(1)} collective-permute-done((bf16[4,2,3,128,128]{4,3,2,1,0:T(8,128)(2,1)}, bf16[4,2,3,128,128]{4,3,2,1,0:T(8,128)(2,1)S(1)}, u32[]{:S(2)}, u32[]{:S(2)}) %collective-permute-start.14) | collective-permute-done | bytes 786464 | tf_op jit(solution)/shard_map/ppermute | solution.py:507
  118.7 6.9 %cross.1.refs_8_.own = bf16[4,160,384]{2,1,0:T(8,128)(2,1)} custom-call(s32[5]{0:T(128)} %stack.38.place, s32[64,3]{1,0:T(8,128)} %bitcast.36, bf16[4,3,3,128,128]{4,3,2,1,0:T(8,128)(2,1)} %copy-done.8, bf16[480,384]{1,0:T(8,128)(2,1)} %gate.27.refs_0_, bf16[480,384]{1,0:T(8,128)(2,1)} %copy-done.10, bf16[480,384]{1,0:T(8,128)(2,1)} %copy-done.11, ...), custom_call_target="tpu_custom_call" | custom-call | flops 1 | bytes 1 | tf_op jit(solution)/shard_map/cross/pallas_call | solution.py:319
  126.2 6.8 %flash.6 = (f32[512,384]{1,0:T(8,128)}, f32[512,384]{1,0:T(8,128)}, f32[512,384]{1,0:T(8,128)}, f32[8,128]{1,0:T(8,128)}) custom-call(bf16[4,3,3,128,128]{4,3,2,1,0:T(8,128)(2,1)} %copy-done.8, bf16[4,2,3,128,128]{4,3,2,1,0:T(8,128)(2,1)} %gate.24.refs_1_, bf16[4,2,3,128,128]{4,3,2,1,0:T(8,128)(2,1)} %gate.26.refs_10_.refs_2_, ...), custom_call_target="tpu_custom_call" | custom-call | flops 1 | bytes 1 | tf_op jit(solution)/shard_map/flash/pallas_call | solution.py:231
  133.8 6.4 %project_cross.1 = (bf16[320,1536]{1,0:T(8,128)(2,1)}, bf16[320,1536]{1,0:T(8,128)(2,1)}, bf16[320,1536]{1,0:T(8,128)(2,1)}, bf16[160,1536]{1,0:T(8,128)(2,1)}, bf16[160,1536]{1,0:T(8,128)(2,1)}) custom-call(s32[5]{0:T(128)} %stack.38.place, bf16[4,160,384]{2,1,0:T(8,128)(2,1)} %cross.1.refs_8_.own, bf16[4,160,384]{2,1,0:T(8,128)(2,1)} %copy-done.25, ...), custom_call_target="tpu_custom_call" | custom-call | flops 1 | bytes 1 | tf_op jit(solution)/shard_map/project_cross/pallas_call | solution.py:371
  147.2 6.9 %flash.7 = (f32[512,384]{1,0:T(8,128)}, f32[512,384]{1,0:T(8,128)}, f32[512,384]{1,0:T(8,128)}, f32[8,128]{1,0:T(8,128)}) custom-call(bf16[4,3,3,128,128]{4,3,2,1,0:T(8,128)(2,1)} %copy-done.8, bf16[4,2,3,128,128]{4,3,2,1,0:T(8,128)(2,1)} %gate.25.refs_1_, bf16[4,2,3,128,128]{4,3,2,1,0:T(8,128)(2,1)} %gate.30.refs_2_, ...), custom_call_target="tpu_custom_call" | custom-call | flops 1 | bytes 1 | tf_op jit(solution)/shard_map/flash/pallas_call | solution.py:231
  159.0 6.9 %flash.8 = (f32[512,384]{1,0:T(8,128)}, f32[512,384]{1,0:T(8,128)}, f32[512,384]{1,0:T(8,128)}, f32[8,128]{1,0:T(8,128)}) custom-call(bf16[4,3,3,128,128]{4,3,2,1,0:T(8,128)(2,1)} %copy-done.8, bf16[4,2,3,128,128]{4,3,2,1,0:T(8,128)(2,1)} %gate.29.refs_1_, bf16[4,2,3,128,128]{4,3,2,1,0:T(8,128)(2,1)} %gate.33.refs_2_, ...), custom_call_target="tpu_custom_call" | custom-call | flops 1 | bytes 1 | tf_op jit(solution)/shard_map/flash/pallas_call | solution.py:231
  167.9 3.7 %collective-permute-done.25.refs_1_ = bf16[320,1536]{1,0:T(8,128)(2,1)S(1)} collective-permute-done((bf16[320,1536]{1,0:T(8,128)(2,1)}, bf16[320,1536]{1,0:T(8,128)(2,1)S(1)}, u32[]{:S(2)}, u32[]{:S(2)}) %collective-permute-start.25) | collective-permute-done | bytes 983072 | tf_op jit(solution)/shard_map/ppermute | solution.py:502
  173.3 5.4 %flash.9 = bf16[512,384]{1,0:T(8,128)(2,1)} custom-call(bf16[4,3,3,128,128]{4,3,2,1,0:T(8,128)(2,1)} %copy-done.8, bf16[4,2,3,128,128]{4,3,2,1,0:T(8,128)(2,1)} %gate.32.refs_1_, bf16[4,2,3,128,128]{4,3,2,1,0:T(8,128)(2,1)} %copy-done.24, f32[512,384]{1,0:T(8,128)} %get-tuple-element.63.refs_3_, f32[512,384]{1,0:T(8,128)} %get-tuple-element.64.refs_4_, ...), custom_call_target="tpu_custom_call" | custom-call | flops 1 | bytes 1 | tf_op jit(solution)/shard_map/flash/pallas_call | solution.py:231
  178.8 3.5 %all-to-all-start.1 = ((bf16[4,128,384]{2,1,0:T(8,128)(2,1)}), bf16[4,128,384]{2,1,0:T(8,128)(2,1)S(1)}, u32[]{:S(2)}, u32[]{:S(2)}) async-start(bf16[4,128,384]{2,1,0:T(8,128)(2,1)} %bitcast.23), calls=%async_computation.1 | async-start | bytes 786432 | tf_op jit(solution)/shard_map/all_to_all | solution.py:494
  184.9 3.9 %all-to-all-done.1.own = bf16[4,128,384]{2,1,0:T(8,128)(2,1)S(1)} async-done(((bf16[4,128,384]{2,1,0:T(8,128)(2,1)}), bf16[4,128,384]{2,1,0:T(8,128)(2,1)S(1)}, u32[]{:S(2)}, u32[]{:S(2)}) %all-to-all-start.1) | async-done | bytes 393248 | tf_op jit(solution)/shard_map/all_to_all | solution.py:494
  188.8 4.3 %collective-permute-start.27 = (bf16[4,128,384]{2,1,0:T(8,128)(2,1)S(1)}, bf16[4,128,384]{2,1,0:T(8,128)(2,1)S(1)}, u32[]{:S(2)}, u32[]{:S(2)}) collective-permute-start(bf16[4,128,384]{2,1,0:T(8,128)(2,1)S(1)} %all-to-all-done.1.own), channel_id=1, source_target_pairs={{0,4},{4,0},{8,12},{12,8},{16,20},{20,16},{24,28},{28,24},{32,36},... | collective-permute-start | bytes 1179656 | tf_op jit(solution)/shard_map/ppermute | solution.py:511
  193.0 5.2 %collective-permute-done.29.refs_4_ = bf16[160,1536]{1,0:T(8,128)(2,1)} collective-permute-done((bf16[160,1536]{1,0:T(8,128)(2,1)}, bf16[160,1536]{1,0:T(8,128)(2,1)}, u32[]{:S(2)}, u32[]{:S(2)}) %collective-permute-start.29) | collective-permute-done | bytes 491552 | tf_op jit(solution)/shard_map/ppermute | solution.py:502
  204.4 4.8 %project_self.1 = (bf16[128,3072]{1,0:T(8,128)(2,1)}, bf16[24,3072]{1,0:T(8,128)(2,1)}, bf16[160,1536]{1,0:T(8,128)(2,1)S(1)}) custom-call(s32[5]{0:T(128)S(1)} %copy-done.5, bf16[4,128,384]{2,1,0:T(8,128)(2,1)S(1)} %all-to-all-done.1.own, bf16[4,128,384]{2,1,0:T(8,128)(2,1)S(1)} %copy-done.3, bf16[16,3,32,1536]{3,2,1,0:T(8,128)(2,1)S(1)} %copy-done, ...), custom_call_target="tpu_custom_call" | custom-call | flops 1 | bytes 1 | tf_op jit(solution)/shard_map/project_self/pallas_call | solution.py:426
  (141 shorter events, 65.3 us)
Async XLA Ops:
  7.2 125.9 %all-gather.5.cloned.1.call-start = ((), (), s32[]{:S(2)}) async-start(), calls=%async_computation.2 | async-start | bytes 2949120 | tf_op jit(solution)/shard_map/all_gather | solution.py:525
  12.2 188.8 %all-gather.7.cloned.1.call-start = ((), (), s32[]{:S(2)}) async-start(), calls=%async_computation.3 | async-start | bytes 5898240 | tf_op jit(solution)/shard_map/all_gather | solution.py:539
  37.0 14.9 %collective-permute-start.3 = (bf16[480,384]{1,0:T(8,128)(2,1)}, bf16[480,384]{1,0:T(8,128)(2,1)S(1)}, u32[]{:S(2)}, u32[]{:S(2)}) collective-permute-start(bf16[480,384]{1,0:T(8,128)(2,1)} %gate.19), channel_id=1, source_target_pairs={{0,2},{4,6},{8,10},{12,14},{17,19},{21,23},{25,27},{29,31},{34,32}... | collective-permute-start | bytes 1105928 | tf_op jit(solution)/shard_map/ppermute | solution.py:150
  38.3 13.5 %collective-permute-start.4 = (bf16[480,384]{1,0:T(8,128)(2,1)}, bf16[480,384]{1,0:T(8,128)(2,1)S(1)}, u32[]{:S(2)}, u32[]{:S(2)}) collective-permute-start(bf16[480,384]{1,0:T(8,128)(2,1)} %gate.20), channel_id=1, source_target_pairs={{0,3},{4,7},{8,11},{12,15},{17,16},{21,20},{25,24},{29,28},{34,33}... | collective-permute-start | bytes 1105928 | tf_op jit(solution)/shard_map/ppermute | solution.py:150
  52.7 15.3 %collective-permute-start.19 = (bf16[3,32,1536]{2,1,0:T(8,128)(2,1)}, bf16[3,32,1536]{2,1,0:T(8,128)(2,1)S(1)}, u32[]{:S(2)}, u32[]{:S(2)}) collective-permute-start(bf16[3,32,1536]{2,1,0:T(8,128)(2,1)} %gate.31), channel_id=1, source_target_pairs={{0,2},{1,3},{2,0},{3,1},{4,6},{5,7},{6,4},{7,5},{8,10},{9,11},{10,... | collective-permute-start | bytes 884744 | tf_op jit(solution)/shard_map/ppermute | solution.py:502
  56.3 11.7 %collective-permute-start.20 = (bf16[3,32,1536]{2,1,0:T(8,128)(2,1)}, bf16[3,32,1536]{2,1,0:T(8,128)(2,1)S(1)}, u32[]{:S(2)}, u32[]{:S(2)}) collective-permute-start(bf16[3,32,1536]{2,1,0:T(8,128)(2,1)} %gate.31), channel_id=1, source_target_pairs={{0,3},{1,0},{2,1},{3,2},{4,7},{5,4},{6,5},{7,6},{8,11},{9,8},{10,9... | collective-permute-start | bytes 884744 | tf_op jit(solution)/shard_map/ppermute | solution.py:502
  71.4 16.3 %collective-permute-start = (bf16[4,2,3,128,128]{4,3,2,1,0:T(8,128)(2,1)S(1)}, bf16[4,2,3,128,128]{4,3,2,1,0:T(8,128)(2,1)S(1)}, u32[]{:S(2)}, u32[]{:S(2)}) collective-permute-start(bf16[4,2,3,128,128]{4,3,2,1,0:T(8,128)(2,1)S(1)} %copy-done.7), channel_id=1, source_target_pairs={{0,8},{4,60},{8,16},{12,4},{16,24},{20,12},{24,32},{28,20},{32,40}... | collective-permute-start | bytes 2359304 | tf_op jit(solution)/shard_map/ppermute | solution.py:507
  78.8 17.4 %collective-permute-start.10 = (bf16[4,2,3,128,128]{4,3,2,1,0:T(8,128)(2,1)S(1)}, bf16[4,2,3,128,128]{4,3,2,1,0:T(8,128)(2,1)S(1)}, u32[]{:S(2)}, u32[]{:S(2)}) collective-permute-start(bf16[4,2,3,128,128]{4,3,2,1,0:T(8,128)(2,1)S(1)} %copy-done.19), channel_id=1, source_target_pairs={{0,8},{4,60},{8,16},{12,4},{16,24},{20,12},{24,32},{28,20},{32,40}... | collective-permute-start | bytes 2359304 | tf_op jit(solution)/shard_map/ppermute | solution.py:507
  88.7 16.1 %collective-permute-start.8 = (bf16[4,2,3,128,128]{4,3,2,1,0:T(8,128)(2,1)}, bf16[4,2,3,128,128]{4,3,2,1,0:T(8,128)(2,1)}, u32[]{:S(2)}, u32[]{:S(2)}) collective-permute-start(bf16[4,2,3,128,128]{4,3,2,1,0:T(8,128)(2,1)} %gate.24.refs_1_), channel_id=1, source_target_pairs={{0,8},{4,60},{8,16},{12,4},{16,24},{20,12},{24,32},{28,20},{32,40}... | collective-permute-start | bytes 2359304 | tf_op jit(solution)/shard_map/ppermute | solution.py:507
  97.1 16.1 %collective-permute-start.14 = (bf16[4,2,3,128,128]{4,3,2,1,0:T(8,128)(2,1)}, bf16[4,2,3,128,128]{4,3,2,1,0:T(8,128)(2,1)S(1)}, u32[]{:S(2)}, u32[]{:S(2)}) collective-permute-start(bf16[4,2,3,128,128]{4,3,2,1,0:T(8,128)(2,1)} %gate.26.refs_10_.refs_2_), channel_id=1, source_target_pairs={{0,8},{4,60},{8,16},{12,4},{16,24},{20,12},{24,32},{28,20},{32,40}... | collective-permute-start | bytes 2359304 | tf_op jit(solution)/shard_map/ppermute | solution.py:507
  100.6 25.0 %collective-permute-start.11 = (bf16[4,2,3,128,128]{4,3,2,1,0:T(8,128)(2,1)S(1)}, bf16[4,2,3,128,128]{4,3,2,1,0:T(8,128)(2,1)}, u32[]{:S(2)}, u32[]{:S(2)}) collective-permute-start(bf16[4,2,3,128,128]{4,3,2,1,0:T(8,128)(2,1)S(1)} %copy-done.21), channel_id=1, source_target_pairs={{0,4},{4,0},{8,12},{12,8},{16,20},{20,16},{24,28},{28,24},{32,36},... | collective-permute-start | bytes 2359304 | tf_op jit(solution)/shard_map/ppermute | solution.py:511
  101.1 24.6 %collective-permute-start.12 = (bf16[4,2,3,128,128]{4,3,2,1,0:T(8,128)(2,1)}, bf16[4,2,3,128,128]{4,3,2,1,0:T(8,128)(2,1)}, u32[]{:S(2)}, u32[]{:S(2)}) collective-permute-start(bf16[4,2,3,128,128]{4,3,2,1,0:T(8,128)(2,1)} %gate.26.refs_10_.refs_2_), channel_id=1, source_target_pairs={{0,4},{4,0},{8,12},{12,8},{16,20},{20,16},{24,28},{28,24},{32,36},... | collective-permute-start | bytes 2359304 | tf_op jit(solution)/shard_map/ppermute | solution.py:511
  104.7 38.5 %collective-permute-start.9 = (bf16[4,2,3,128,128]{4,3,2,1,0:T(8,128)(2,1)}, bf16[4,2,3,128,128]{4,3,2,1,0:T(8,128)(2,1)S(1)}, u32[]{:S(2)}, u32[]{:S(2)}) collective-permute-start(bf16[4,2,3,128,128]{4,3,2,1,0:T(8,128)(2,1)} %gate.25.refs_1_), channel_id=1, source_target_pairs={{0,8},{4,60},{8,16},{12,4},{16,24},{20,12},{24,32},{28,20},{32,40}... | collective-permute-start | bytes 2359304 | tf_op jit(solution)/shard_map/ppermute | solution.py:507
  114.0 32.2 %collective-permute-start.22 = (bf16[4,2,3,128,128]{4,3,2,1,0:T(8,128)(2,1)}, bf16[4,2,3,128,128]{4,3,2,1,0:T(8,128)(2,1)S(1)}, u32[]{:S(2)}, u32[]{:S(2)}) collective-permute-start(bf16[4,2,3,128,128]{4,3,2,1,0:T(8,128)(2,1)} %gate.30.refs_2_), channel_id=1, source_target_pairs={{0,8},{4,60},{8,16},{12,4},{16,24},{20,12},{24,32},{28,20},{32,40}... | collective-permute-start | bytes 2359304 | tf_op jit(solution)/shard_map/ppermute | solution.py:507
  117.4 29.7 %collective-permute-start.15 = (bf16[4,2,3,128,128]{4,3,2,1,0:T(8,128)(2,1)}, bf16[4,2,3,128,128]{4,3,2,1,0:T(8,128)(2,1)}, u32[]{:S(2)}, u32[]{:S(2)}) collective-permute-start(bf16[4,2,3,128,128]{4,3,2,1,0:T(8,128)(2,1)} %gate.25.refs_1_), channel_id=1, source_target_pairs={{0,4},{4,0},{8,12},{12,8},{16,20},{20,16},{24,28},{28,24},{32,36},... | collective-permute-start | bytes 2359304 | tf_op jit(solution)/shard_map/ppermute | solution.py:511
  125.7 21.4 %collective-permute-start.16 = (bf16[4,2,3,128,128]{4,3,2,1,0:T(8,128)(2,1)S(1)}, bf16[4,2,3,128,128]{4,3,2,1,0:T(8,128)(2,1)}, u32[]{:S(2)}, u32[]{:S(2)}) collective-permute-start(bf16[4,2,3,128,128]{4,3,2,1,0:T(8,128)(2,1)S(1)} %copy-done.17), channel_id=1, source_target_pairs={{0,4},{4,0},{8,12},{12,8},{16,20},{20,16},{24,28},{28,24},{32,36},... | collective-permute-start | bytes 2359304 | tf_op jit(solution)/shard_map/ppermute | solution.py:511
  140.3 25.7 %collective-permute-start.26 = (bf16[320,1536]{1,0:T(8,128)(2,1)}, bf16[320,1536]{1,0:T(8,128)(2,1)S(1)}, u32[]{:S(2)}, u32[]{:S(2)}) collective-permute-start(bf16[320,1536]{1,0:T(8,128)(2,1)} %get-tuple-element.70), channel_id=1, source_target_pairs={{0,3},{1,0},{2,1},{3,2},{4,7},{5,4},{6,5},{7,6},{8,11},{9,8},{10,9... | collective-permute-start | bytes 2949128 | tf_op jit(solution)/shard_map/ppermute | solution.py:502
  146.2 12.8 %collective-permute-start.23 = (bf16[4,2,3,128,128]{4,3,2,1,0:T(8,128)(2,1)}, bf16[4,2,3,128,128]{4,3,2,1,0:T(8,128)(2,1)}, u32[]{:S(2)}, u32[]{:S(2)}) collective-permute-start(bf16[4,2,3,128,128]{4,3,2,1,0:T(8,128)(2,1)} %gate.29.refs_1_), channel_id=1, source_target_pairs={{0,4},{4,0},{8,12},{12,8},{16,20},{20,16},{24,28},{28,24},{32,36},... | collective-permute-start | bytes 2359304 | tf_op jit(solution)/shard_map/ppermute | solution.py:511
  147.1 11.9 %collective-permute-start.24 = (bf16[4,2,3,128,128]{4,3,2,1,0:T(8,128)(2,1)}, bf16[4,2,3,128,128]{4,3,2,1,0:T(8,128)(2,1)}, u32[]{:S(2)}, u32[]{:S(2)}) collective-permute-start(bf16[4,2,3,128,128]{4,3,2,1,0:T(8,128)(2,1)} %gate.33.refs_2_), channel_id=1, source_target_pairs={{0,4},{4,0},{8,12},{12,8},{16,20},{20,16},{24,28},{28,24},{32,36},... | collective-permute-start | bytes 2359304 | tf_op jit(solution)/shard_map/ppermute | solution.py:511
  147.1 24.4 %collective-permute-start.25 = (bf16[320,1536]{1,0:T(8,128)(2,1)}, bf16[320,1536]{1,0:T(8,128)(2,1)S(1)}, u32[]{:S(2)}, u32[]{:S(2)}) collective-permute-start(bf16[320,1536]{1,0:T(8,128)(2,1)} %get-tuple-element.68), channel_id=1, source_target_pairs={{0,1},{1,2},{2,3},{3,0},{4,5},{5,6},{6,7},{7,4},{8,9},{9,10},{10,1... | collective-permute-start | bytes 2949128 | tf_op jit(solution)/shard_map/ppermute | solution.py:502
  156.3 16.1 %collective-permute-start.21 = (bf16[4,2,3,128,128]{4,3,2,1,0:T(8,128)(2,1)}, bf16[4,2,3,128,128]{4,3,2,1,0:T(8,128)(2,1)S(1)}, u32[]{:S(2)}, u32[]{:S(2)}) collective-permute-start(bf16[4,2,3,128,128]{4,3,2,1,0:T(8,128)(2,1)} %gate.32.refs_1_), channel_id=1, source_target_pairs={{0,4},{4,0},{8,12},{12,8},{16,20},{20,16},{24,28},{28,24},{32,36},... | collective-permute-start | bytes 2359304 | tf_op jit(solution)/shard_map/ppermute | solution.py:511
  182.3 15.9 %collective-permute-start.29 = (bf16[160,1536]{1,0:T(8,128)(2,1)}, bf16[160,1536]{1,0:T(8,128)(2,1)}, u32[]{:S(2)}, u32[]{:S(2)}) collective-permute-start(bf16[160,1536]{1,0:T(8,128)(2,1)} %add_convert_fusion.refs_7_), channel_id=1, source_target_pairs={{0,3},{1,0},{2,1},{3,2},{4,7},{5,4},{6,5},{7,6},{8,11},{9,8},{10,9... | collective-permute-start | bytes 1474568 | tf_op jit(solution)/shard_map/ppermute | solution.py:502
  184.9 15.4 %collective-permute-start.28 = (bf16[160,1536]{1,0:T(8,128)(2,1)}, bf16[160,1536]{1,0:T(8,128)(2,1)}, u32[]{:S(2)}, u32[]{:S(2)}) collective-permute-start(bf16[160,1536]{1,0:T(8,128)(2,1)} %add_convert_fusion.1.refs_6_), channel_id=1, source_target_pairs={{0,1},{1,2},{2,3},{3,0},{4,5},{5,6},{6,7},{7,4},{8,9},{9,10},{10,1... | collective-permute-start | bytes 1474568 | tf_op jit(solution)/shard_map/ppermute | solution.py:502
  188.8 11.5 %collective-permute-start.27 = (bf16[4,128,384]{2,1,0:T(8,128)(2,1)S(1)}, bf16[4,128,384]{2,1,0:T(8,128)(2,1)S(1)}, u32[]{:S(2)}, u32[]{:S(2)}) collective-permute-start(bf16[4,128,384]{2,1,0:T(8,128)(2,1)S(1)} %all-to-all-done.1.own), channel_id=1, source_target_pairs={{0,4},{4,0},{8,12},{12,8},{16,20},{20,16},{24,28},{28,24},{32,36},... | collective-permute-start | bytes 1179656 | tf_op jit(solution)/shard_map/ppermute | solution.py:511
  (40 other events, 240.6 us)
Sparse Core Ops, SparseCore 0:
  12.3 39.3 all-gather.4
  70.4 61.6 all-gather.6

commit v7 on v6

--- a/solution.py
+++ b/solution.py
@@ -398,7 +398,7 @@
     )
     w = jnp.concatenate(
         [
-            weight_rows([functools.partial(lambda b, h: w_ref[b * TOWERS + lax.rem(place[1] - t + TOWERS, TOWERS), h], b) for b in range(4)])
+            weight_rows([functools.partial(lambda b, h: w_ref[b * TOWERS + t, h], b) for b in range(4)])
             for t in range(TOWERS)
         ],
         axis=0,
@@ -523,6 +523,7 @@
         place, video_k[0], video_v[0], video_q[0], audio_k[0], audio_v[0], audio_q[0], out_weight
     )
     w_rest = lax.all_gather(w_rest, "batch", axis=0, tiled=False)
+    w_self = lax.all_gather(w_self, ("batch", "tower"), axis=0, tiled=False)
     query = exchange_towers(parts)
     own = query[:, :2]
     sibling = swap_core(own)
@@ -534,10 +535,6 @@
     acc, top, total, token = flash(query, [own, sibling], None, False)
     near, far = gate(near, token, *mains[1:], *halos[1:]), gate(far, token)
     crossed = cross(place, margins, query, mains, halos, own, sibling, far)
-    w_self = gate(w_self, token, *mains[1:])
-    w_parts = jnp.stack([w_self] + [shift_tower(w_self, step) for step in (1, 2, 3)])
-    w_self = lax.all_gather(w_parts, "batch", axis=0, tiled=False)
-    w_self = w_self.reshape((16,) + w_self.shape[2:])
 
     tokens = [token]
     after = (crossed,)
@@ -549,18 +546,17 @@
         after = ()
         if step == 1:
             rest, up, down, up_later, down_later = project_cross(
-                place, crossed, swap_core(crossed), w_rest, (token, w_parts)
+                place, crossed, swap_core(crossed), w_rest, (token, token)
             )
             after = (rest,)
             up, down = shift_tower(up, 1), shift_tower(down, -1)
         near = gate(near, tokens[step - 1])
         if step < 3:
             far = gate(far, tokens[step - 1])
-    up_later = add(gate(up_later, token), up[:BOTH])
-    down_later = add(gate(down_later, token), down[BOTH:])
-    after = (up_later, down_later)
+    video_self = flash(query, [near, swap_core(near)], (acc, top, total), True)
+    up_later = add(gate(up_later, video_self), up[:BOTH])
+    down_later = add(gate(down_later, video_self), down[BOTH:])
     up_later, down_later = shift_tower(up_later, 1), shift_tower(down_later, -1)
-    video_self = flash(query, [near, swap_core(near)], (acc, top, total), True, after)
     base = (rest, up, down, up_later, down_later)
 
     self_all = exchange_towers(video_self.reshape(TOWERS, VBLK, GW))

time: 221 us -> 179 us (0.81)
  waiting for transfers between devices: 52.9 us -> 29.9 us
  starting transfers between devices: 58.5 us -> 42.7 us
  local copies, waits for them, and re-layouts: 16.4 us -> 12.7 us
    ppermute x7, waiting for transfers between devices: 20.4 us -> 6.5 us  [hop(): lax.ppermute(value, 'ctx', [(i, (i + 2 - 4 * (i % 2)) % total) for i in r...]
    ppermute x7 -> x4, waiting for transfers between devices: 20.6 us -> 9.05 us  [shift_tower(): lax.ppermute(value, 'tower', [(i, (i + step) % TOWERS) for i in range(TOW...]
    ppermute x7, starting transfers between devices: 23.7 us -> 12.9 us  [hop(): lax.ppermute(value, 'ctx', [(i, (i + 2 - 4 * (i % 2)) % total) for i in r...]
    ppermute x7 -> x4, starting transfers between devices: 11.3 us -> 3.14 us  [shift_tower(): lax.ppermute(value, 'tower', [(i, (i + step) % TOWERS) for i in range(TOW...]
    unnamed x61 -> x55, local copies, waits for them, and re-layouts: 15.7 us -> 12 us
    ppermute x11, starting transfers between devices: 13.2 us -> 16 us  [swap_core(): return lax.ppermute(value, 'ctx', [(i, i ^ 1) for i in range(2 * CHIPS)])]
  transfers between devices with their start and end apart: 34 -> 31, of which waited for: 13 -> 9; matrix products, arithmetic and copies ran while one was open for 2% -> 3% of each run, Pallas kernels for 20% -> 25%
where the time goes in v7:
time: 179 us; the launch traced here: 178 us
  Pallas kernels  54.5 us (30%)
  starting transfers between devices  42.7 us (24%)
  waiting for transfers between devices  29.9 us (17%)
  blocking collectives  19.5 us (11%)
  between operations  14.5 us (8%)
  local copies, waits for them, and re-layouts  12.7 us (7%)
  other arithmetic  3.86 us (2%)
    pallas_call x5, Pallas kernels, flash(): pl.pallas_call(functools.partial(flash_kernel, len(kvs), state is None, l...  30.7 us
    all_to_all x1, blocking collectives, exchange_towers(): lax.all_to_all(value, 'tower', split_axis=0, concat_axis=0, tiled=True)  19.5 us
    ppermute x11, starting transfers between devices, swap_core(): return lax.ppermute(value, 'ctx', [(i, i ^ 1) for i in range(2 * CHIPS)])  16 us
    ppermute x7, starting transfers between devices, hop(): lax.ppermute(value, 'ctx', [(i, (i + 2 - 4 * (i % 2)) % total) for i in r...  12.9 us
    unnamed x55, local copies, waits for them, and re-layouts  12 us
    ppermute x4, waiting for transfers between devices, shift_tower(): lax.ppermute(value, 'tower', [(i, (i + step) % TOWERS) for i in range(TOW...  9.05 us
    pallas_call x1, Pallas kernels, cross(): pl.pallas_call(cross_kernel, out_shape=jax.ShapeDtypeStruct((TOWERS, BOTH...  6.82 us
    pallas_call x1, Pallas kernels, project_cross(): pl.pallas_call(project_cross_kernel, out_shape=[jax.ShapeDtypeStruct((n *...  6.59 us
  transfers between devices with their start and end apart: 31, of which 9 were waited for; matrix products, arithmetic and copies ran while one was open for 3% of the time, Pallas kernels for 25%

profile of v7, /device:TPU:1, one launch (start us, length us, event | category | flops | bytes accessed | tf_op | source)
XLA Modules:
  0.0 177.6 jit_solution(3774710275229214815)
XLA Ops:
  7.9 4.3 %pack.1 = (bf16[4,3,3,128,128]{4,3,2,1,0:T(8,128)(2,1)}, bf16[3,32,1536]{2,1,0:T(8,128)(2,1)}, bf16[2,3,32,1536]{3,2,1,0:T(8,128)(2,1)}, bf16[480,384]{1,0:T(8,1...) custom-call(s32[5]{0:T(128)} %stack.23.place, ...), custom_call_target="tpu_custom_call" | custom-call | tf_op jit(solution)/shard_map/pack/pallas_call | solution.py:123
  13.0 19.5 %all_to_all.10.refs_0_.q_ref = bf16[4,3,3,128,128]{4,3,2,1,0:T(8,128)(2,1)S(1)} all-to-all(bf16[4,3,3,128,128]{4,3,2,1,0:T(8,128)(2,1)} %get-tuple-element.38), channel_id=1, replica_groups=mesh['batch'=4,'ctx'=16,'tower'=4] {'tower'}, dimensions={0} | all-to-all | bytes 2359296 | tf_op jit(solution)/shard_map/all_to_all | solution.py:494
  32.6 2.9 %collective-permute-start.1 = (bf16[4,2,3,128,128]{4,3,2,1,0:T(8,128)(2,1)S(1)}, bf16[4,2,3,128,128]{4,3,2,1,0:T(8,128)(2,1)S(1)}, u32[]{:S(2)}, u32[]{:S(2)}) collective-permute-start(bf16[4,2,3,128,128]{4,3,2,1,0:T(8,128)(2,1)S(1)} %slice.12.refs_1_.refs_8_), channel_id=1, source_target_pairs={{0,4},{4,0},{8,12},{12,8},{16,20},{20,16},{24,28},{28,24},{32,36},... | collective-permute-start | bytes 2359304 | tf_op jit(solution)/shard_map/ppermute | solution.py:511
  35.5 5.6 %collective-permute-start = (bf16[4,2,3,128,128]{4,3,2,1,0:T(8,128)(2,1)S(1)}, bf16[4,2,3,128,128]{4,3,2,1,0:T(8,128)(2,1)}, u32[]{:S(2)}, u32[]{:S(2)}) collective-permute-start(bf16[4,2,3,128,128]{4,3,2,1,0:T(8,128)(2,1)S(1)} %slice.12.refs_1_.refs_8_), channel_id=1, source_target_pairs={{0,8},{4,60},{8,16},{12,4},{16,24},{20,12},{24,32},{28,20},{32,40}... | collective-permute-start | bytes 2359304 | tf_op jit(solution)/shard_map/ppermute | solution.py:507
  43.2 2.3 %collective-permute-start.2 = (bf16[480,384]{1,0:T(8,128)(2,1)}, bf16[480,384]{1,0:T(8,128)(2,1)S(1)}, u32[]{:S(2)}, u32[]{:S(2)}) collective-permute-start(bf16[480,384]{1,0:T(8,128)(2,1)} %gate.17), channel_id=1, source_target_pairs={{0,1},{4,5},{8,9},{12,13},{17,18},{21,22},{25,26},{29,30},{34,35},... | collective-permute-start | bytes 1105928 | tf_op jit(solution)/shard_map/ppermute | solution.py:150
  49.1 4.7 %flash.5 = (f32[512,384]{1,0:T(8,128)}, f32[512,384]{1,0:T(8,128)}, f32[512,384]{1,0:T(8,128)}, f32[8,128]{1,0:T(8,128)}) custom-call(bf16[4,3,3,128,128]{4,3,2,1,0:T(8,128)(2,1)} %copy-done.7, bf16[4,2,3,128,128]{4,3,2,1,0:T(8,128)(2,1)} %copy-done.6, bf16[4,2,3,128,128]{4,3,2,1,0:T(8,128)(2,1)} %copy-done.14), custom_call_target="tpu_custom_call" | custom-call | flops 1 | bytes 1 | tf_op jit(solution)/shard_map/flash/pallas_call | solution.py:231
  54.3 4.6 %collective-permute-done.3.refs_3_.refs_2_ = bf16[480,384]{1,0:T(8,128)(2,1)S(1)} collective-permute-done((bf16[480,384]{1,0:T(8,128)(2,1)S(1)}, bf16[480,384]{1,0:T(8,128)(2,1)S(1)}, u32[]{:S(2)}, u32[]{:S(2)}) %collective-permute-start.3) | collective-permute-done | bytes 368672 | tf_op jit(solution)/shard_map/ppermute | solution.py:150
  62.4 2.5 %collective-permute-start.11 = (bf16[4,2,3,128,128]{4,3,2,1,0:T(8,128)(2,1)}, bf16[4,2,3,128,128]{4,3,2,1,0:T(8,128)(2,1)S(1)}, u32[]{:S(2)}, u32[]{:S(2)}) collective-permute-start(bf16[4,2,3,128,128]{4,3,2,1,0:T(8,128)(2,1)} %gate.23.refs_1_), channel_id=1, source_target_pairs={{0,4},{4,0},{8,12},{12,8},{16,20},{20,16},{24,28},{28,24},{32,36},... | collective-permute-start | bytes 2359304 | tf_op jit(solution)/shard_map/ppermute | solution.py:511
  64.9 6.5 %collective-permute-done.8.refs_0_ = bf16[4,2,3,128,128]{4,3,2,1,0:T(8,128)(2,1)} collective-permute-done((bf16[4,2,3,128,128]{4,3,2,1,0:T(8,128)(2,1)}, bf16[4,2,3,128,128]{4,3,2,1,0:T(8,128)(2,1)}, u32[]{:S(2)}, u32[]{:S(2)}) %collective-permute-start.8) | collective-permute-done | bytes 786464 | tf_op jit(solution)/shard_map/ppermute | solution.py:507
  74.6 6.8 %cross.1.refs_8_.own = bf16[4,160,384]{2,1,0:T(8,128)(2,1)} custom-call(s32[5]{0:T(128)} %stack.23.place, s32[64,3]{1,0:T(8,128)} %bitcast.30, bf16[4,3,3,128,128]{4,3,2,1,0:T(8,128)(2,1)} %copy-done.7, bf16[480,384]{1,0:T(8,128)(2,1)} %gate.26.refs_0_, bf16[480,384]{1,0:T(8,128)(2,1)} %copy-done.16, bf16[480,384]{1,0:T(8,128)(2,1)} %copy-done.17, ...), custom_call_target="tpu_custom_call" | custom-call | flops 1 | bytes 1 | tf_op jit(solution)/shard_map/cross/pallas_call | solution.py:319
  82.3 3.6 %collective-permute-start.19 = (bf16[4,2,3,128,128]{4,3,2,1,0:T(8,128)(2,1)}, bf16[4,2,3,128,128]{4,3,2,1,0:T(8,128)(2,1)S(1)}, u32[]{:S(2)}, u32[]{:S(2)}) collective-permute-start(bf16[4,2,3,128,128]{4,3,2,1,0:T(8,128)(2,1)} %gate.29.refs_2_), channel_id=1, source_target_pairs={{0,8},{4,60},{8,16},{12,4},{16,24},{20,12},{24,32},{28,20},{32,40}... | collective-permute-start | bytes 2359304 | tf_op jit(solution)/shard_map/ppermute | solution.py:507
  87.7 6.9 %flash.6 = (f32[512,384]{1,0:T(8,128)}, f32[512,384]{1,0:T(8,128)}, f32[512,384]{1,0:T(8,128)}, f32[8,128]{1,0:T(8,128)}) custom-call(bf16[4,3,3,128,128]{4,3,2,1,0:T(8,128)(2,1)} %copy-done.7, bf16[4,2,3,128,128]{4,3,2,1,0:T(8,128)(2,1)} %gate.23.refs_1_, bf16[4,2,3,128,128]{4,3,2,1,0:T(8,128)(2,1)} %gate.25.refs_10_.refs_2_, ...), custom_call_target="tpu_custom_call" | custom-call | flops 1 | bytes 1 | tf_op jit(solution)/shard_map/flash/pallas_call | solution.py:231
  96.7 2.1 %collective-permute-start.17 = (bf16[4,160,384]{2,1,0:T(8,128)(2,1)S(1)}, bf16[4,160,384]{2,1,0:T(8,128)(2,1)S(1)}, u32[]{:S(2)}, u32[]{:S(2)}) collective-permute-start(bf16[4,160,384]{2,1,0:T(8,128)(2,1)S(1)} %copy-done.9), channel_id=1, source_target_pairs={{0,4},{4,0},{8,12},{12,8},{16,20},{20,16},{24,28},{28,24},{32,36},... | collective-permute-start | bytes 1474568 | tf_op jit(solution)/shard_map/ppermute | solution.py:511
  101.1 6.6 %project_cross.1 = (bf16[320,1536]{1,0:T(8,128)(2,1)}, bf16[320,1536]{1,0:T(8,128)(2,1)}, bf16[320,1536]{1,0:T(8,128)(2,1)}, bf16[160,1536]{1,0:T(8,128)(2,1)}, bf16[160,1536]{1,0:T(8,128)(2,1)}) custom-call(s32[5]{0:T(128)} %stack.23.place, bf16[4,160,384]{2,1,0:T(8,128)(2,1)} %cross.1.refs_8_.own, bf16[4,160,384]{2,1,0:T(8,128)(2,1)} %copy-done.21, ...), custom_call_target="tpu_custom_call" | custom-call | flops 1 | bytes 1 | tf_op jit(solution)/shard_map/project_cross/pallas_call | solution.py:371
  109.2 6.9 %flash.7 = (f32[512,384]{1,0:T(8,128)}, f32[512,384]{1,0:T(8,128)}, f32[512,384]{1,0:T(8,128)}, f32[8,128]{1,0:T(8,128)}) custom-call(bf16[4,3,3,128,128]{4,3,2,1,0:T(8,128)(2,1)} %copy-done.7, bf16[4,2,3,128,128]{4,3,2,1,0:T(8,128)(2,1)} %gate.24.refs_1_, bf16[4,2,3,128,128]{4,3,2,1,0:T(8,128)(2,1)} %gate.29.refs_2_, ...), custom_call_target="tpu_custom_call" | custom-call | flops 1 | bytes 1 | tf_op jit(solution)/shard_map/flash/pallas_call | solution.py:231
  118.4 6.8 %flash.8 = (f32[512,384]{1,0:T(8,128)}, f32[512,384]{1,0:T(8,128)}, f32[512,384]{1,0:T(8,128)}, f32[8,128]{1,0:T(8,128)}) custom-call(bf16[4,3,3,128,128]{4,3,2,1,0:T(8,128)(2,1)} %copy-done.7, bf16[4,2,3,128,128]{4,3,2,1,0:T(8,128)(2,1)} %gate.28.refs_1_, bf16[4,2,3,128,128]{4,3,2,1,0:T(8,128)(2,1)} %gate.31.refs_2_, ...), custom_call_target="tpu_custom_call" | custom-call | flops 1 | bytes 1 | tf_op jit(solution)/shard_map/flash/pallas_call | solution.py:231
  126.2 5.3 %flash.9.refs_1_ = bf16[512,384]{1,0:T(8,128)(2,1)} custom-call(bf16[4,3,3,128,128]{4,3,2,1,0:T(8,128)(2,1)} %copy-done.7, bf16[4,2,3,128,128]{4,3,2,1,0:T(8,128)(2,1)} %gate.30.refs_1_, bf16[4,2,3,128,128]{4,3,2,1,0:T(8,128)(2,1)} %copy-done.20, f32[512,384]{1,0:T(8,128)} %get-tuple-element.61.refs_3_, f32[512,384]{1,0:T(8,128)} %get-tuple-element.62.refs_4_, ...), custom_call_target="tpu_custom_call" | custom-call | flops 1 | bytes 1 | tf_op jit(solution)/shard_map/flash/pallas_call | solution.py:231
  132.6 1.9 %add_convert_fusion = bf16[160,1536]{1,0:T(8,128)(2,1)} fusion(bf16[160,1536]{1,0:T(8,128)(2,1)} %gate.33, bf16[320,1536]{1,0:T(8,128)(2,1)S(1)} %collective-permute-done.24.refs_2_), kind=kLoop, calls=%fused_computation | loop fusion | flops 983040 | bytes 1474560 | tf_op jit(solution)/shard_map/convert_element_type | solution.py:498
  135.8 3.6 %all-to-all-start.1 = ((bf16[4,128,384]{2,1,0:T(8,128)(2,1)}), bf16[4,128,384]{2,1,0:T(8,128)(2,1)S(1)}, u32[]{:S(2)}, u32[]{:S(2)}) async-start(bf16[4,128,384]{2,1,0:T(8,128)(2,1)} %bitcast.20), calls=%async_computation.1 | async-start | bytes 786432 | tf_op jit(solution)/shard_map/all_to_all | solution.py:494
  143.5 5.6 %all-to-all-done.1.own = bf16[4,128,384]{2,1,0:T(8,128)(2,1)S(1)} async-done(((bf16[4,128,384]{2,1,0:T(8,128)(2,1)}), bf16[4,128,384]{2,1,0:T(8,128)(2,1)S(1)}, u32[]{:S(2)}, u32[]{:S(2)}) %all-to-all-start.1) | async-done | bytes 393248 | tf_op jit(solution)/shard_map/all_to_all | solution.py:494
  149.1 2.5 %collective-permute-start.22 = (bf16[4,128,384]{2,1,0:T(8,128)(2,1)S(1)}, bf16[4,128,384]{2,1,0:T(8,128)(2,1)S(1)}, u32[]{:S(2)}, u32[]{:S(2)}) collective-permute-start(bf16[4,128,384]{2,1,0:T(8,128)(2,1)S(1)} %all-to-all-done.1.own), channel_id=1, source_target_pairs={{0,4},{4,0},{8,12},{12,8},{16,20},{20,16},{24,28},{28,24},{32,36},... | collective-permute-start | bytes 1179656 | tf_op jit(solution)/shard_map/ppermute | solution.py:511
  151.6 6.1 %collective-permute-done.25.refs_3_ = bf16[160,1536]{1,0:T(8,128)(2,1)} collective-permute-done((bf16[160,1536]{1,0:T(8,128)(2,1)}, bf16[160,1536]{1,0:T(8,128)(2,1)}, u32[]{:S(2)}, u32[]{:S(2)}) %collective-permute-start.25) | collective-permute-done | bytes 491552 | tf_op jit(solution)/shard_map/ppermute | solution.py:502
  158.4 2.3 %copy-done = bf16[48,32,1536]{2,1,0:T(8,128)(2,1)S(1)} copy-done((bf16[48,32,1536]{2,1,0:T(8,128)(2,1)S(1)}, bf16[48,32,1536]{2,1,0:T(8,128)(2,1)}, u32[]{:S(2)}) %copy-start) | copy-done | bytes 4718616
  161.7 4.8 %project_self.1 = (bf16[128,3072]{1,0:T(8,128)(2,1)}, bf16[24,3072]{1,0:T(8,128)(2,1)}, bf16[160,1536]{1,0:T(8,128)(2,1)S(1)}) custom-call(s32[5]{0:T(128)S(1)} %copy-done.5, bf16[4,128,384]{2,1,0:T(8,128)(2,1)S(1)} %all-to-all-done.1.own, bf16[4,128,384]{2,1,0:T(8,128)(2,1)S(1)} %copy-done.3, bf16[16,3,32,1536]{3,2,1,0:T(8,128)(2,1)S(1)} %bitcast.18, ...), custom_call_target="tpu_custom_call" | custom-call | flops 1 | bytes 1 | tf_op jit(solution)/shard_map/project_self/pallas_call | solution.py:426
  (127 shorter events, 38.5 us)
Async XLA Ops:
  7.2 93.1 %all-gather.5.cloned.1.call-start = ((), (), s32[]{:S(2)}) async-start(), calls=%async_computation.2 | async-start | bytes 2949120 | tf_op jit(solution)/shard_map/all_gather | solution.py:525
  12.3 146.1 %all-gather.7.cloned.1.call-start = ((), (), s32[]{:S(2)}) async-start(), calls=%async_computation.3 | async-start | bytes 5013504 | tf_op jit(solution)/shard_map/all_gather | solution.py:526
  32.6 15.6 %collective-permute-start.1 = (bf16[4,2,3,128,128]{4,3,2,1,0:T(8,128)(2,1)S(1)}, bf16[4,2,3,128,128]{4,3,2,1,0:T(8,128)(2,1)S(1)}, u32[]{:S(2)}, u32[]{:S(2)}) collective-permute-start(bf16[4,2,3,128,128]{4,3,2,1,0:T(8,128)(2,1)S(1)} %slice.12.refs_1_.refs_8_), channel_id=1, source_target_pairs={{0,4},{4,0},{8,12},{12,8},{16,20},{20,16},{24,28},{28,24},{32,36},... | collective-permute-start | bytes 2359304 | tf_op jit(solution)/shard_map/ppermute | solution.py:511
  35.5 23.4 %collective-permute-start = (bf16[4,2,3,128,128]{4,3,2,1,0:T(8,128)(2,1)S(1)}, bf16[4,2,3,128,128]{4,3,2,1,0:T(8,128)(2,1)}, u32[]{:S(2)}, u32[]{:S(2)}) collective-permute-start(bf16[4,2,3,128,128]{4,3,2,1,0:T(8,128)(2,1)S(1)} %slice.12.refs_1_.refs_8_), channel_id=1, source_target_pairs={{0,8},{4,60},{8,16},{12,4},{16,24},{20,12},{24,32},{28,20},{32,40}... | collective-permute-start | bytes 2359304 | tf_op jit(solution)/shard_map/ppermute | solution.py:507
  43.2 11.1 %collective-permute-start.2 = (bf16[480,384]{1,0:T(8,128)(2,1)}, bf16[480,384]{1,0:T(8,128)(2,1)S(1)}, u32[]{:S(2)}, u32[]{:S(2)}) collective-permute-start(bf16[480,384]{1,0:T(8,128)(2,1)} %gate.17), channel_id=1, source_target_pairs={{0,1},{4,5},{8,9},{12,13},{17,18},{21,22},{25,26},{29,30},{34,35},... | collective-permute-start | bytes 1105928 | tf_op jit(solution)/shard_map/ppermute | solution.py:150
  45.6 13.3 %collective-permute-start.3 = (bf16[480,384]{1,0:T(8,128)(2,1)S(1)}, bf16[480,384]{1,0:T(8,128)(2,1)S(1)}, u32[]{:S(2)}, u32[]{:S(2)}) collective-permute-start(bf16[480,384]{1,0:T(8,128)(2,1)S(1)} %copy-done.22), channel_id=1, source_target_pairs={{0,2},{4,6},{8,10},{12,14},{17,19},{21,23},{25,27},{29,31},{34,32}... | collective-permute-start | bytes 1105928 | tf_op jit(solution)/shard_map/ppermute | solution.py:150
  46.9 12.0 %collective-permute-start.4 = (bf16[480,384]{1,0:T(8,128)(2,1)}, bf16[480,384]{1,0:T(8,128)(2,1)S(1)}, u32[]{:S(2)}, u32[]{:S(2)}) collective-permute-start(bf16[480,384]{1,0:T(8,128)(2,1)} %gate.19), channel_id=1, source_target_pairs={{0,3},{4,7},{8,11},{12,15},{17,16},{21,20},{25,24},{29,28},{34,33}... | collective-permute-start | bytes 1105928 | tf_op jit(solution)/shard_map/ppermute | solution.py:150
  48.2 11.5 %collective-permute-start.10 = (bf16[4,2,3,128,128]{4,3,2,1,0:T(8,128)(2,1)S(1)}, bf16[4,2,3,128,128]{4,3,2,1,0:T(8,128)(2,1)S(1)}, u32[]{:S(2)}, u32[]{:S(2)}) collective-permute-start(bf16[4,2,3,128,128]{4,3,2,1,0:T(8,128)(2,1)S(1)} %collective-permute-done.1.refs_2_.refs_9_), channel_id=1, source_target_pairs={{0,8},{4,60},{8,16},{12,4},{16,24},{20,12},{24,32},{28,20},{32,40}... | collective-permute-start | bytes 2359304 | tf_op jit(solution)/shard_map/ppermute | solution.py:507
  59.8 11.6 %collective-permute-start.8 = (bf16[4,2,3,128,128]{4,3,2,1,0:T(8,128)(2,1)}, bf16[4,2,3,128,128]{4,3,2,1,0:T(8,128)(2,1)}, u32[]{:S(2)}, u32[]{:S(2)}) collective-permute-start(bf16[4,2,3,128,128]{4,3,2,1,0:T(8,128)(2,1)} %gate.23.refs_1_), channel_id=1, source_target_pairs={{0,8},{4,60},{8,16},{12,4},{16,24},{20,12},{24,32},{28,20},{32,40}... | collective-permute-start | bytes 2359304 | tf_op jit(solution)/shard_map/ppermute | solution.py:507
  60.7 20.7 %collective-permute-start.14 = (bf16[4,2,3,128,128]{4,3,2,1,0:T(8,128)(2,1)}, bf16[4,2,3,128,128]{4,3,2,1,0:T(8,128)(2,1)S(1)}, u32[]{:S(2)}, u32[]{:S(2)}) collective-permute-start(bf16[4,2,3,128,128]{4,3,2,1,0:T(8,128)(2,1)} %gate.25.refs_10_.refs_2_), channel_id=1, source_target_pairs={{0,8},{4,60},{8,16},{12,4},{16,24},{20,12},{24,32},{28,20},{32,40}... | collective-permute-start | bytes 2359304 | tf_op jit(solution)/shard_map/ppermute | solution.py:507
  62.4 23.4 %collective-permute-start.11 = (bf16[4,2,3,128,128]{4,3,2,1,0:T(8,128)(2,1)}, bf16[4,2,3,128,128]{4,3,2,1,0:T(8,128)(2,1)S(1)}, u32[]{:S(2)}, u32[]{:S(2)}) collective-permute-start(bf16[4,2,3,128,128]{4,3,2,1,0:T(8,128)(2,1)} %gate.23.refs_1_), channel_id=1, source_target_pairs={{0,4},{4,0},{8,12},{12,8},{16,20},{20,16},{24,28},{28,24},{32,36},... | collective-permute-start | bytes 2359304 | tf_op jit(solution)/shard_map/ppermute | solution.py:511
  64.9 22.8 %collective-permute-start.12 = (bf16[4,2,3,128,128]{4,3,2,1,0:T(8,128)(2,1)}, bf16[4,2,3,128,128]{4,3,2,1,0:T(8,128)(2,1)}, u32[]{:S(2)}, u32[]{:S(2)}) collective-permute-start(bf16[4,2,3,128,128]{4,3,2,1,0:T(8,128)(2,1)} %gate.25.refs_10_.refs_2_), channel_id=1, source_target_pairs={{0,4},{4,0},{8,12},{12,8},{16,20},{20,16},{24,28},{28,24},{32,36},... | collective-permute-start | bytes 2359304 | tf_op jit(solution)/shard_map/ppermute | solution.py:511
  71.4 23.2 %collective-permute-start.9 = (bf16[4,2,3,128,128]{4,3,2,1,0:T(8,128)(2,1)}, bf16[4,2,3,128,128]{4,3,2,1,0:T(8,128)(2,1)S(1)}, u32[]{:S(2)}, u32[]{:S(2)}) collective-permute-start(bf16[4,2,3,128,128]{4,3,2,1,0:T(8,128)(2,1)} %gate.24.refs_1_), channel_id=1, source_target_pairs={{0,8},{4,60},{8,16},{12,4},{16,24},{20,12},{24,32},{28,20},{32,40}... | collective-permute-start | bytes 2359304 | tf_op jit(solution)/shard_map/ppermute | solution.py:507
  72.9 35.9 %collective-permute-start.15 = (bf16[4,2,3,128,128]{4,3,2,1,0:T(8,128)(2,1)}, bf16[4,2,3,128,128]{4,3,2,1,0:T(8,128)(2,1)}, u32[]{:S(2)}, u32[]{:S(2)}) collective-permute-start(bf16[4,2,3,128,128]{4,3,2,1,0:T(8,128)(2,1)} %gate.24.refs_1_), channel_id=1, source_target_pairs={{0,4},{4,0},{8,12},{12,8},{16,20},{20,16},{24,28},{28,24},{32,36},... | collective-permute-start | bytes 2359304 | tf_op jit(solution)/shard_map/ppermute | solution.py:511
  82.3 25.6 %collective-permute-start.19 = (bf16[4,2,3,128,128]{4,3,2,1,0:T(8,128)(2,1)}, bf16[4,2,3,128,128]{4,3,2,1,0:T(8,128)(2,1)S(1)}, u32[]{:S(2)}, u32[]{:S(2)}) collective-permute-start(bf16[4,2,3,128,128]{4,3,2,1,0:T(8,128)(2,1)} %gate.29.refs_2_), channel_id=1, source_target_pairs={{0,8},{4,60},{8,16},{12,4},{16,24},{20,12},{24,32},{28,20},{32,40}... | collective-permute-start | bytes 2359304 | tf_op jit(solution)/shard_map/ppermute | solution.py:507
  85.9 23.3 %collective-permute-start.16 = (bf16[4,2,3,128,128]{4,3,2,1,0:T(8,128)(2,1)}, bf16[4,2,3,128,128]{4,3,2,1,0:T(8,128)(2,1)}, u32[]{:S(2)}, u32[]{:S(2)}) collective-permute-start(bf16[4,2,3,128,128]{4,3,2,1,0:T(8,128)(2,1)} %gate.29.refs_2_), channel_id=1, source_target_pairs={{0,4},{4,0},{8,12},{12,8},{16,20},{20,16},{24,28},{28,24},{32,36},... | collective-permute-start | bytes 2359304 | tf_op jit(solution)/shard_map/ppermute | solution.py:511
  95.5 20.5 %collective-permute-start.13 = (bf16[4,2,3,128,128]{4,3,2,1,0:T(8,128)(2,1)}, bf16[4,2,3,128,128]{4,3,2,1,0:T(8,128)(2,1)S(1)}, u32[]{:S(2)}, u32[]{:S(2)}) collective-permute-start(bf16[4,2,3,128,128]{4,3,2,1,0:T(8,128)(2,1)} %gate.28.refs_1_), channel_id=1, source_target_pairs={{0,8},{4,60},{8,16},{12,4},{16,24},{20,12},{24,32},{28,20},{32,40}... | collective-permute-start | bytes 2359304 | tf_op jit(solution)/shard_map/ppermute | solution.py:507
  107.7 24.9 %collective-permute-start.24 = (bf16[320,1536]{1,0:T(8,128)(2,1)}, bf16[320,1536]{1,0:T(8,128)(2,1)S(1)}, u32[]{:S(2)}, u32[]{:S(2)}) collective-permute-start(bf16[320,1536]{1,0:T(8,128)(2,1)} %get-tuple-element.66), channel_id=1, source_target_pairs={{0,3},{1,0},{2,1},{3,2},{4,7},{5,4},{6,5},{7,6},{8,11},{9,8},{10,9... | collective-permute-start | bytes 2949128 | tf_op jit(solution)/shard_map/ppermute | solution.py:502
  107.8 10.6 %collective-permute-start.20 = (bf16[4,2,3,128,128]{4,3,2,1,0:T(8,128)(2,1)S(1)}, bf16[4,2,3,128,128]{4,3,2,1,0:T(8,128)(2,1)}, u32[]{:S(2)}, u32[]{:S(2)}) collective-permute-start(bf16[4,2,3,128,128]{4,3,2,1,0:T(8,128)(2,1)S(1)} %copy-done.12), channel_id=1, source_target_pairs={{0,4},{4,0},{8,12},{12,8},{16,20},{20,16},{24,28},{28,24},{32,36},... | collective-permute-start | bytes 2359304 | tf_op jit(solution)/shard_map/ppermute | solution.py:511
  108.7 9.7 %collective-permute-start.21 = (bf16[4,2,3,128,128]{4,3,2,1,0:T(8,128)(2,1)}, bf16[4,2,3,128,128]{4,3,2,1,0:T(8,128)(2,1)}, u32[]{:S(2)}, u32[]{:S(2)}) collective-permute-start(bf16[4,2,3,128,128]{4,3,2,1,0:T(8,128)(2,1)} %gate.31.refs_2_), channel_id=1, source_target_pairs={{0,4},{4,0},{8,12},{12,8},{16,20},{20,16},{24,28},{28,24},{32,36},... | collective-permute-start | bytes 2359304 | tf_op jit(solution)/shard_map/ppermute | solution.py:511
  117.0 24.3 %collective-permute-start.23 = (bf16[320,1536]{1,0:T(8,128)(2,1)}, bf16[320,1536]{1,0:T(8,128)(2,1)S(1)}, u32[]{:S(2)}, u32[]{:S(2)}) collective-permute-start(bf16[320,1536]{1,0:T(8,128)(2,1)} %get-tuple-element.65), channel_id=1, source_target_pairs={{0,1},{1,2},{2,3},{3,0},{4,5},{5,6},{6,7},{7,4},{8,9},{9,10},{10,1... | collective-permute-start | bytes 2949128 | tf_op jit(solution)/shard_map/ppermute | solution.py:502
  134.5 17.0 %collective-permute-start.26 = (bf16[160,1536]{1,0:T(8,128)(2,1)}, bf16[160,1536]{1,0:T(8,128)(2,1)}, u32[]{:S(2)}, u32[]{:S(2)}) collective-permute-start(bf16[160,1536]{1,0:T(8,128)(2,1)} %add_convert_fusion), channel_id=1, source_target_pairs={{0,3},{1,0},{2,1},{3,2},{4,7},{5,4},{6,5},{7,6},{8,11},{9,8},{10,9... | collective-permute-start | bytes 1474568 | tf_op jit(solution)/shard_map/ppermute | solution.py:502
  135.8 13.3 %all-to-all-start.1 = ((bf16[4,128,384]{2,1,0:T(8,128)(2,1)}), bf16[4,128,384]{2,1,0:T(8,128)(2,1)S(1)}, u32[]{:S(2)}, u32[]{:S(2)}) async-start(bf16[4,128,384]{2,1,0:T(8,128)(2,1)} %bitcast.20), calls=%async_computation.1 | async-start | bytes 786432 | tf_op jit(solution)/shard_map/all_to_all | solution.py:494
  143.2 14.4 %collective-permute-start.25 = (bf16[160,1536]{1,0:T(8,128)(2,1)}, bf16[160,1536]{1,0:T(8,128)(2,1)}, u32[]{:S(2)}, u32[]{:S(2)}) collective-permute-start(bf16[160,1536]{1,0:T(8,128)(2,1)} %add_convert_fusion.1), channel_id=1, source_target_pairs={{0,1},{1,2},{2,3},{3,0},{4,5},{5,6},{6,7},{7,4},{8,9},{9,10},{10,1... | collective-permute-start | bytes 1474568 | tf_op jit(solution)/shard_map/ppermute | solution.py:502
  (34 other events, 201.7 us)
Sparse Core Ops, SparseCore 0:
  12.4 39.3 all-gather.4
  54.2 58.9 all-gather.6

commit v8 on v7

--- a/solution.py
+++ b/solution.py
@@ -234,7 +234,7 @@
         grid=(LOCAL,),
         in_specs=[QUERY] + [SHARD] * len(kvs) + ([] if state is None else [head] * 3) + [ANY] * len(after),
         out_specs=out_specs,
-        compiler_params=pltpu.CompilerParams(vmem_limit_bytes=60 * MIB),
+        compiler_params=pltpu.CompilerParams(vmem_limit_bytes=(32 if last else 60) * MIB),
         cost_estimate=BRIEF,
         name="flash",
     )(query, *kvs, *(() if state is None else state), *after)
@@ -494,8 +494,26 @@
     return lax.all_to_all(value, "tower", split_axis=0, concat_axis=0, tiled=True)
 
 
-def add(a, b):
-    return (a.astype(jnp.float32) + b.astype(jnp.float32)).astype(jnp.bfloat16)
+def add_later_kernel(up, down, up_later, down_later, _, up_out, down_out):
+    for a, b, out in ((up, up_later, up_out), (down, down_later, down_out)):
+        out[...] = (a[...].astype(jnp.float32) + b[...].astype(jnp.float32)).astype(jnp.bfloat16)
+
+
+def add_later(up, down, up_later, down_later, after):
+    rows, width = up_later.shape
+    tile = width // 3
+    first = pl.BlockSpec((rows, tile), lambda i: (0, i))
+    second = pl.BlockSpec((rows, tile), lambda i: (1, i))
+    return pl.pallas_call(
+        add_later_kernel,
+        out_shape=[jax.ShapeDtypeStruct(up_later.shape, up_later.dtype)] * 2,
+        grid=(3,),
+        in_specs=[first, second, first, first, ANY],
+        out_specs=[first, first],
+        compiler_params=pltpu.CompilerParams(vmem_limit_bytes=24 * MIB),
+        cost_estimate=BRIEF,
+        name="add_later",
+    )(up, down, up_later, down_later, after)
 
 
 def shift_tower(value, step):
@@ -528,7 +546,7 @@
     own = query[:, :2]
     sibling = swap_core(own)
     near, far = hop(own), hop(sibling)
-    audio = [gate(rows, own) for rows in audio]
+    audio = [gate(rows, sibling) for rows in audio]
     mains = [audio[0]] + [send_main(audio[step], step) for step in (1, 2, 3)]
     halos = [audio[4]] + [send_halo(audio[4 + step], step) for step in (1, 2, 3)]
 
@@ -550,12 +568,12 @@
             )
             after = (rest,)
             up, down = shift_tower(up, 1), shift_tower(down, -1)
-        near = gate(near, tokens[step - 1])
+        behind = crossed if step == 1 else tokens[step - 1]
+        near = gate(near, behind)
         if step < 3:
-            far = gate(far, tokens[step - 1])
-    video_self = flash(query, [near, swap_core(near)], (acc, top, total), True)
-    up_later = add(gate(up_later, video_self), up[:BOTH])
-    down_later = add(gate(down_later, video_self), down[BOTH:])
+            far = gate(far, behind)
+    video_self = flash(query, [near, swap_core(near)], (acc, top, total), True, (w_self,))
+    up_later, down_later = add_later(up, down, up_later, down_later, video_self)
     up_later, down_later = shift_tower(up_later, 1), shift_tower(down_later, -1)
     base = (rest, up, down, up_later, down_later)
 

time: 179 us -> 179 us (level)
  waiting for transfers between devices: 29.9 us -> 18.2 us
  local copies, waits for them, and re-layouts: 12.7 us -> 21.3 us
  starting transfers between devices: 42.7 us -> 48.5 us
  other arithmetic: 3.86 us -> 0 us
    ppermute x7, starting transfers between devices: 12.9 us -> 25.9 us  [hop(): lax.ppermute(value, 'ctx', [(i, (i + 2 - 4 * (i % 2)) % total) for i in r...]
    ppermute x11, starting transfers between devices: 16 us -> 6.59 us  [swap_core(): return lax.ppermute(value, 'ctx', [(i, i ^ 1) for i in range(2 * CHIPS)])]
    unnamed x55 -> x65, local copies, waits for them, and re-layouts: 12 us -> 20.7 us
    ppermute x3, waiting for transfers between devices: 5.05 us -> 0.01 us  [send_main(): return lax.ppermute(value, ('ctx', 'tower'), ctx_towers(pairs))]
    all_to_all x1, waiting for transfers between devices: 5.56 us -> 0.6 us  [exchange_towers(): lax.all_to_all(value, 'tower', split_axis=0, concat_axis=0, tiled=True)]
    convert_element_type x2 -> x0, other arithmetic: 3.86 us -> none  [add(): return (a.astype(jnp.float32) + b.astype(jnp.float32)).astype(jnp.bfloat16)]
    ppermute x7, waiting for transfers between devices: 6.5 us -> 3.83 us  [hop(): lax.ppermute(value, 'ctx', [(i, (i + 2 - 4 * (i % 2)) % total) for i in r...]
    ppermute x4, starting transfers between devices: 3.14 us -> 5.34 us  [shift_tower(): lax.ppermute(value, 'tower', [(i, (i + step) % TOWERS) for i in range(TOW...]
  transfers between devices with their start and end apart: 31 -> 31, of which waited for: 9 -> 6; matrix products, arithmetic and copies ran while one was open for 3% -> 0% of each run, Pallas kernels for 25% -> 25%
where the time goes in v8:
time: 179 us; the launch traced here: 178 us
  Pallas kernels  55.6 us (31%)
  starting transfers between devices  48.5 us (27%)
  local copies, waits for them, and re-layouts  21.3 us (12%)
  blocking collectives  19.5 us (11%)
  waiting for transfers between devices  18.2 us (10%)
  between operations  14.5 us (8%)
    pallas_call x5, Pallas kernels, flash(): pl.pallas_call(functools.partial(flash_kernel, len(kvs), state is None, l...  30.1 us
    ppermute x7, starting transfers between devices, hop(): lax.ppermute(value, 'ctx', [(i, (i + 2 - 4 * (i % 2)) % total) for i in r...  25.9 us
    unnamed x65, local copies, waits for them, and re-layouts  20.7 us
    all_to_all x1, blocking collectives, exchange_towers(): lax.all_to_all(value, 'tower', split_axis=0, concat_axis=0, tiled=True)  19.5 us
    ppermute x4, waiting for transfers between devices, shift_tower(): lax.ppermute(value, 'tower', [(i, (i + step) % TOWERS) for i in range(TOW...  9.64 us
    pallas_call x1, Pallas kernels, cross(): pl.pallas_call(cross_kernel, out_shape=jax.ShapeDtypeStruct((TOWERS, BOTH...  6.77 us
    ppermute x11, starting transfers between devices, swap_core(): return lax.ppermute(value, 'ctx', [(i, i ^ 1) for i in range(2 * CHIPS)])  6.59 us
    pallas_call x1, Pallas kernels, project_cross(): pl.pallas_call(project_cross_kernel, out_shape=[jax.ShapeDtypeStruct((n *...  6.57 us
  transfers between devices with their start and end apart: 31, of which 6 were waited for; matrix products, arithmetic and copies ran while one was open for 0% of the time, Pallas kernels for 25%

profile of v8, /device:TPU:1, one launch (start us, length us, event | category | flops | bytes accessed | tf_op | source)
XLA Modules:
  0.0 177.7 jit_solution(7841022056324857199)
XLA Ops:
  7.8 4.3 %pack.1 = (bf16[4,3,3,128,128]{4,3,2,1,0:T(8,128)(2,1)}, bf16[3,32,1536]{2,1,0:T(8,128)(2,1)}, bf16[2,3,32,1536]{3,2,1,0:T(8,128)(2,1)}, bf16[480,384]{1,0:T(8,1...) custom-call(s32[5]{0:T(128)} %stack.23.place, ...), custom_call_target="tpu_custom_call" | custom-call | tf_op jit(solution)/shard_map/pack/pallas_call | solution.py:123
  12.9 19.5 %all_to_all.10.refs_0_.q_ref = bf16[4,3,3,128,128]{4,3,2,1,0:T(8,128)(2,1)S(1)} all-to-all(bf16[4,3,3,128,128]{4,3,2,1,0:T(8,128)(2,1)} %get-tuple-element.40), channel_id=1, replica_groups=mesh['batch'=4,'ctx'=16,'tower'=4] {'tower'}, dimensions={0} | all-to-all | bytes 2359296 | tf_op jit(solution)/shard_map/all_to_all | solution.py:494
  32.5 2.9 %collective-permute-start.1 = (bf16[4,2,3,128,128]{4,3,2,1,0:T(8,128)(2,1)S(1)}, bf16[4,2,3,128,128]{4,3,2,1,0:T(8,128)(2,1)S(1)}, u32[]{:S(2)}, u32[]{:S(2)}) collective-permute-start(bf16[4,2,3,128,128]{4,3,2,1,0:T(8,128)(2,1)S(1)} %slice.4.refs_1_.refs_8_), channel_id=1, source_target_pairs={{0,4},{4,0},{8,12},{12,8},{16,20},{20,16},{24,28},{28,24},{32,36},... | collective-permute-start | bytes 2359304 | tf_op jit(solution)/shard_map/ppermute | solution.py:529
  35.4 5.6 %collective-permute-start = (bf16[4,2,3,128,128]{4,3,2,1,0:T(8,128)(2,1)S(1)}, bf16[4,2,3,128,128]{4,3,2,1,0:T(8,128)(2,1)}, u32[]{:S(2)}, u32[]{:S(2)}) collective-permute-start(bf16[4,2,3,128,128]{4,3,2,1,0:T(8,128)(2,1)S(1)} %slice.4.refs_1_.refs_8_), channel_id=1, source_target_pairs={{0,8},{4,60},{8,16},{12,4},{16,24},{20,12},{24,32},{28,20},{32,40}... | collective-permute-start | bytes 2359304 | tf_op jit(solution)/shard_map/ppermute | solution.py:525
  41.9 2.5 %collective-permute-start.3 = (bf16[480,384]{1,0:T(8,128)(2,1)}, bf16[480,384]{1,0:T(8,128)(2,1)S(1)}, u32[]{:S(2)}, u32[]{:S(2)}) collective-permute-start(bf16[480,384]{1,0:T(8,128)(2,1)} %gate.16), channel_id=1, source_target_pairs={{0,2},{4,6},{8,10},{12,14},{17,19},{21,23},{25,27},{29,31},{34,32}... | collective-permute-start | bytes 1105928 | tf_op jit(solution)/shard_map/ppermute | solution.py:150
  47.9 2.1 %collective-permute-done.refs_0_ = bf16[4,2,3,128,128]{4,3,2,1,0:T(8,128)(2,1)} collective-permute-done((bf16[4,2,3,128,128]{4,3,2,1,0:T(8,128)(2,1)S(1)}, bf16[4,2,3,128,128]{4,3,2,1,0:T(8,128)(2,1)}, u32[]{:S(2)}, u32[]{:S(2)}) %collective-permute-start) | collective-permute-done | bytes 786464 | tf_op jit(solution)/shard_map/ppermute | solution.py:525
  51.4 3.6 %collective-permute-start.9 = (bf16[4,2,3,128,128]{4,3,2,1,0:T(8,128)(2,1)S(1)}, bf16[4,2,3,128,128]{4,3,2,1,0:T(8,128)(2,1)S(1)}, u32[]{:S(2)}, u32[]{:S(2)}) collective-permute-start(bf16[4,2,3,128,128]{4,3,2,1,0:T(8,128)(2,1)S(1)} %copy-done.15), channel_id=1, source_target_pairs={{0,8},{4,60},{8,16},{12,4},{16,24},{20,12},{24,32},{28,20},{32,40}... | collective-permute-start | bytes 2359304 | tf_op jit(solution)/shard_map/ppermute | solution.py:525
  54.9 4.7 %flash.5 = (f32[512,384]{1,0:T(8,128)}, f32[512,384]{1,0:T(8,128)}, f32[512,384]{1,0:T(8,128)}, f32[8,128]{1,0:T(8,128)}) custom-call(bf16[4,3,3,128,128]{4,3,2,1,0:T(8,128)(2,1)} %copy-done, bf16[4,2,3,128,128]{4,3,2,1,0:T(8,128)(2,1)} %copy-done.19, bf16[4,2,3,128,128]{4,3,2,1,0:T(8,128)(2,1)} %copy-done.14), custom_call_target="tpu_custom_call" | custom-call | flops 1 | bytes 1 | tf_op jit(solution)/shard_map/flash/pallas_call | solution.py:231
  64.8 3.6 %collective-permute-start.14 = (bf16[4,2,3,128,128]{4,3,2,1,0:T(8,128)(2,1)}, bf16[4,2,3,128,128]{4,3,2,1,0:T(8,128)(2,1)S(1)}, u32[]{:S(2)}, u32[]{:S(2)}) collective-permute-start(bf16[4,2,3,128,128]{4,3,2,1,0:T(8,128)(2,1)} %gate.24.refs_10_.refs_2_), channel_id=1, source_target_pairs={{0,8},{4,60},{8,16},{12,4},{16,24},{20,12},{24,32},{28,20},{32,40}... | collective-permute-start | bytes 2359304 | tf_op jit(solution)/shard_map/ppermute | solution.py:525
  69.6 6.8 %cross.1.refs_1_.refs_8_.own = bf16[4,160,384]{2,1,0:T(8,128)(2,1)} custom-call(s32[5]{0:T(128)} %stack.23.place, s32[64,3]{1,0:T(8,128)} %bitcast.30, bf16[4,3,3,128,128]{4,3,2,1,0:T(8,128)(2,1)} %copy-done, bf16[480,384]{1,0:T(8,128)(2,1)} %gate.22.refs_0_, bf16[480,384]{1,0:T(8,128)(2,1)} %copy-done.26, bf16[480,384]{1,0:T(8,128)(2,1)} %copy-done.24, ...), custom_call_target="tpu_custom_call" | custom-call | flops 1 | bytes 1 | tf_op jit(solution)/shard_map/cross/pallas_call | solution.py:319
  76.4 4.9 %collective-permute-start.10 = (bf16[4,2,3,128,128]{4,3,2,1,0:T(8,128)(2,1)}, bf16[4,2,3,128,128]{4,3,2,1,0:T(8,128)(2,1)S(1)}, u32[]{:S(2)}, u32[]{:S(2)}) collective-permute-start(bf16[4,2,3,128,128]{4,3,2,1,0:T(8,128)(2,1)} %gate.25.refs_1_), channel_id=1, source_target_pairs={{0,8},{4,60},{8,16},{12,4},{16,24},{20,12},{24,32},{28,20},{32,40}... | collective-permute-start | bytes 2359304 | tf_op jit(solution)/shard_map/ppermute | solution.py:525
  82.1 3.2 %collective-permute-start.19 = (bf16[4,2,3,128,128]{4,3,2,1,0:T(8,128)(2,1)}, bf16[4,2,3,128,128]{4,3,2,1,0:T(8,128)(2,1)S(1)}, u32[]{:S(2)}, u32[]{:S(2)}) collective-permute-start(bf16[4,2,3,128,128]{4,3,2,1,0:T(8,128)(2,1)} %gate.27.refs_2_), channel_id=1, source_target_pairs={{0,8},{4,60},{8,16},{12,4},{16,24},{20,12},{24,32},{28,20},{32,40}... | collective-permute-start | bytes 2359304 | tf_op jit(solution)/shard_map/ppermute | solution.py:525
  85.4 6.9 %flash.6 = (f32[512,384]{1,0:T(8,128)}, f32[512,384]{1,0:T(8,128)}, f32[512,384]{1,0:T(8,128)}, f32[8,128]{1,0:T(8,128)}) custom-call(bf16[4,3,3,128,128]{4,3,2,1,0:T(8,128)(2,1)} %copy-done, bf16[4,2,3,128,128]{4,3,2,1,0:T(8,128)(2,1)} %gate.21.refs_1_, bf16[4,2,3,128,128]{4,3,2,1,0:T(8,128)(2,1)} %gate.24.refs_10_.refs_2_, ...), custom_call_target="tpu_custom_call" | custom-call | flops 1 | bytes 1 | tf_op jit(solution)/shard_map/flash/pallas_call | solution.py:231
  93.2 4.9 %collective-permute-start.13 = (bf16[4,2,3,128,128]{4,3,2,1,0:T(8,128)(2,1)}, bf16[4,2,3,128,128]{4,3,2,1,0:T(8,128)(2,1)S(1)}, u32[]{:S(2)}, u32[]{:S(2)}) collective-permute-start(bf16[4,2,3,128,128]{4,3,2,1,0:T(8,128)(2,1)} %gate.26.refs_1_), channel_id=1, source_target_pairs={{0,8},{4,60},{8,16},{12,4},{16,24},{20,12},{24,32},{28,20},{32,40}... | collective-permute-start | bytes 2359304 | tf_op jit(solution)/shard_map/ppermute | solution.py:525
  100.8 6.6 %project_cross.1 = (bf16[320,1536]{1,0:T(8,128)(2,1)}, bf16[320,1536]{1,0:T(8,128)(2,1)}, bf16[320,1536]{1,0:T(8,128)(2,1)}, bf16[160,1536]{1,0:T(8,128)(2,1)}, bf16[160,1536]{1,0:T(8,128)(2,1)}) custom-call(s32[5]{0:T(128)} %stack.23.place, bf16[4,160,384]{2,1,0:T(8,128)(2,1)} %cross.1.refs_1_.refs_8_.own, bf16[4,160,384]{2,1,0:T(8,128)(2,1)} %copy-done.27, ...), custom_call_target="tpu_custom_call" | custom-call | flops 1 | bytes 1 | tf_op jit(solution)/shard_map/project_cross/pallas_call | solution.py:371
  108.5 6.8 %flash.7 = (f32[512,384]{1,0:T(8,128)}, f32[512,384]{1,0:T(8,128)}, f32[512,384]{1,0:T(8,128)}, f32[8,128]{1,0:T(8,128)}) custom-call(bf16[4,3,3,128,128]{4,3,2,1,0:T(8,128)(2,1)} %copy-done, bf16[4,2,3,128,128]{4,3,2,1,0:T(8,128)(2,1)} %gate.25.refs_1_, bf16[4,2,3,128,128]{4,3,2,1,0:T(8,128)(2,1)} %gate.27.refs_2_, ...), custom_call_target="tpu_custom_call" | custom-call | flops 1 | bytes 1 | tf_op jit(solution)/shard_map/flash/pallas_call | solution.py:231
  116.5 2.7 %collective-permute-start.24 = (bf16[320,1536]{1,0:T(8,128)(2,1)}, bf16[320,1536]{1,0:T(8,128)(2,1)S(1)}, u32[]{:S(2)}, u32[]{:S(2)}) collective-permute-start(bf16[320,1536]{1,0:T(8,128)(2,1)} %get-tuple-element.68), channel_id=1, source_target_pairs={{0,3},{1,0},{2,1},{3,2},{4,7},{5,4},{6,5},{7,6},{8,11},{9,8},{10,9... | collective-permute-start | bytes 2949128 | tf_op jit(solution)/shard_map/ppermute | solution.py:520
  119.2 7.0 %flash.8 = (f32[512,384]{1,0:T(8,128)}, f32[512,384]{1,0:T(8,128)}, f32[512,384]{1,0:T(8,128)}, f32[8,128]{1,0:T(8,128)}) custom-call(bf16[4,3,3,128,128]{4,3,2,1,0:T(8,128)(2,1)} %copy-done, bf16[4,2,3,128,128]{4,3,2,1,0:T(8,128)(2,1)} %gate.26.refs_1_, bf16[4,2,3,128,128]{4,3,2,1,0:T(8,128)(2,1)} %gate.29.refs_2_, ...), custom_call_target="tpu_custom_call" | custom-call | flops 1 | bytes 1 | tf_op jit(solution)/shard_map/flash/pallas_call | solution.py:231
  126.2 2.3 %copy-done.2 = bf16[48,32,1536]{2,1,0:T(8,128)(2,1)S(1)} copy-done((bf16[48,32,1536]{2,1,0:T(8,128)(2,1)S(1)}, bf16[48,32,1536]{2,1,0:T(8,128)(2,1)}, u32[]{:S(2)}) %copy-start.2) | copy-done | bytes 4718616
  133.1 4.6 %flash.9._ = bf16[512,384]{1,0:T(8,128)(2,1)} custom-call(bf16[4,3,3,128,128]{4,3,2,1,0:T(8,128)(2,1)S(1)} %copy-done.1, bf16[4,2,3,128,128]{4,3,2,1,0:T(8,128)(2,1)S(1)} %copy-done.6, bf16[4,2,3,128,128]{4,3,2,1,0:T(8,128)(2,1)} %collective-permute-done.18.refs_2_, f32[512,384]{1,0:T(8,128)S(1)} %copy-done.7, f32[512,384]{1,0:T(8,128)S(1)} %copy-done.8, ...), custom_call_target="tpu_custom_call" | custom-call | flops 1 | bytes 1 | tf_op jit(solution)/shard_map/flash/pallas_call | solution.py:231
  137.8 3.5 %all-to-all-start.1 = ((bf16[4,128,384]{2,1,0:T(8,128)(2,1)}), bf16[4,128,384]{2,1,0:T(8,128)(2,1)S(1)}, u32[]{:S(2)}, u32[]{:S(2)}) async-start(bf16[4,128,384]{2,1,0:T(8,128)(2,1)} %bitcast.14), calls=%async_computation.1 | async-start | bytes 786432 | tf_op jit(solution)/shard_map/all_to_all | solution.py:494
  150.3 9.6 %collective-permute-done.25.refs_3_ = bf16[160,1536]{1,0:T(8,128)(2,1)} collective-permute-done((bf16[160,1536]{1,0:T(8,128)(2,1)}, bf16[160,1536]{1,0:T(8,128)(2,1)}, u32[]{:S(2)}, u32[]{:S(2)}) %collective-permute-start.25) | collective-permute-done | bytes 491552 | tf_op jit(solution)/shard_map/ppermute | solution.py:520
  159.9 2.3 %copy-done.3 = bf16[48,32,1536]{2,1,0:T(8,128)(2,1)S(1)} copy-done((bf16[48,32,1536]{2,1,0:T(8,128)(2,1)S(1)}, bf16[48,32,1536]{2,1,0:T(8,128)(2,1)}, u32[]{:S(2)}) %copy-start.3) | copy-done | bytes 4718616
  162.3 4.8 %project_self.1 = (bf16[128,3072]{1,0:T(8,128)(2,1)}, bf16[24,3072]{1,0:T(8,128)(2,1)}, bf16[160,1536]{1,0:T(8,128)(2,1)S(1)}) custom-call(s32[5]{0:T(128)S(1)} %copy-done.13, bf16[4,128,384]{2,1,0:T(8,128)(2,1)S(1)} %all-to-all-done.1.own, bf16[4,128,384]{2,1,0:T(8,128)(2,1)S(1)} %collective-permute-done.22.sibling, bf16[16,3,32,1536]{3,2,1,0:T(8,128)(2,1)S(1)} %bitcast.19, ...), custom_call_target="tpu_custom_call" | custom-call | flops 1 | bytes 1 | tf_op jit(solution)/shard_map/project_self/pallas_call | solution.py:426
  (134 shorter events, 37.5 us)
Async XLA Ops:
  7.2 92.8 %all-gather.5.cloned.1.call-start = ((), (), s32[]{:S(2)}) async-start(), calls=%async_computation.2 | async-start | bytes 2949120 | tf_op jit(solution)/shard_map/all_gather | solution.py:543
  12.2 114.0 %all-gather.7.cloned.1.call-start = ((), (), s32[]{:S(2)}) async-start(), calls=%async_computation.3 | async-start | bytes 5013504 | tf_op jit(solution)/shard_map/all_gather | solution.py:544
  35.4 14.5 %collective-permute-start = (bf16[4,2,3,128,128]{4,3,2,1,0:T(8,128)(2,1)S(1)}, bf16[4,2,3,128,128]{4,3,2,1,0:T(8,128)(2,1)}, u32[]{:S(2)}, u32[]{:S(2)}) collective-permute-start(bf16[4,2,3,128,128]{4,3,2,1,0:T(8,128)(2,1)S(1)} %slice.4.refs_1_.refs_8_), channel_id=1, source_target_pairs={{0,8},{4,60},{8,16},{12,4},{16,24},{20,12},{24,32},{28,20},{32,40}... | collective-permute-start | bytes 2359304 | tf_op jit(solution)/shard_map/ppermute | solution.py:525
  41.9 17.8 %collective-permute-start.3 = (bf16[480,384]{1,0:T(8,128)(2,1)}, bf16[480,384]{1,0:T(8,128)(2,1)S(1)}, u32[]{:S(2)}, u32[]{:S(2)}) collective-permute-start(bf16[480,384]{1,0:T(8,128)(2,1)} %gate.16), channel_id=1, source_target_pairs={{0,2},{4,6},{8,10},{12,14},{17,19},{21,23},{25,27},{29,31},{34,32}... | collective-permute-start | bytes 1105928 | tf_op jit(solution)/shard_map/ppermute | solution.py:150
  44.4 15.3 %collective-permute-start.4 = (bf16[480,384]{1,0:T(8,128)(2,1)}, bf16[480,384]{1,0:T(8,128)(2,1)S(1)}, u32[]{:S(2)}, u32[]{:S(2)}) collective-permute-start(bf16[480,384]{1,0:T(8,128)(2,1)} %gate.17), channel_id=1, source_target_pairs={{0,3},{4,7},{8,11},{12,15},{17,16},{21,20},{25,24},{29,28},{34,33}... | collective-permute-start | bytes 1105928 | tf_op jit(solution)/shard_map/ppermute | solution.py:150
  45.7 14.0 %collective-permute-start.2 = (bf16[480,384]{1,0:T(8,128)(2,1)}, bf16[480,384]{1,0:T(8,128)(2,1)S(1)}, u32[]{:S(2)}, u32[]{:S(2)}) collective-permute-start(bf16[480,384]{1,0:T(8,128)(2,1)} %gate.15), channel_id=1, source_target_pairs={{0,1},{4,5},{8,9},{12,13},{17,18},{21,22},{25,26},{29,30},{34,35},... | collective-permute-start | bytes 1105928 | tf_op jit(solution)/shard_map/ppermute | solution.py:150
  51.4 12.5 %collective-permute-start.9 = (bf16[4,2,3,128,128]{4,3,2,1,0:T(8,128)(2,1)S(1)}, bf16[4,2,3,128,128]{4,3,2,1,0:T(8,128)(2,1)S(1)}, u32[]{:S(2)}, u32[]{:S(2)}) collective-permute-start(bf16[4,2,3,128,128]{4,3,2,1,0:T(8,128)(2,1)S(1)} %copy-done.15), channel_id=1, source_target_pairs={{0,8},{4,60},{8,16},{12,4},{16,24},{20,12},{24,32},{28,20},{32,40}... | collective-permute-start | bytes 2359304 | tf_op jit(solution)/shard_map/ppermute | solution.py:525
  60.8 15.6 %collective-permute-start.8 = (bf16[4,2,3,128,128]{4,3,2,1,0:T(8,128)(2,1)}, bf16[4,2,3,128,128]{4,3,2,1,0:T(8,128)(2,1)}, u32[]{:S(2)}, u32[]{:S(2)}) collective-permute-start(bf16[4,2,3,128,128]{4,3,2,1,0:T(8,128)(2,1)} %gate.21.refs_1_), channel_id=1, source_target_pairs={{0,8},{4,60},{8,16},{12,4},{16,24},{20,12},{24,32},{28,20},{32,40}... | collective-permute-start | bytes 2359304 | tf_op jit(solution)/shard_map/ppermute | solution.py:525
  64.8 16.5 %collective-permute-start.14 = (bf16[4,2,3,128,128]{4,3,2,1,0:T(8,128)(2,1)}, bf16[4,2,3,128,128]{4,3,2,1,0:T(8,128)(2,1)S(1)}, u32[]{:S(2)}, u32[]{:S(2)}) collective-permute-start(bf16[4,2,3,128,128]{4,3,2,1,0:T(8,128)(2,1)} %gate.24.refs_10_.refs_2_), channel_id=1, source_target_pairs={{0,8},{4,60},{8,16},{12,4},{16,24},{20,12},{24,32},{28,20},{32,40}... | collective-permute-start | bytes 2359304 | tf_op jit(solution)/shard_map/ppermute | solution.py:525
  68.4 17.0 %collective-permute-start.11 = (bf16[4,2,3,128,128]{4,3,2,1,0:T(8,128)(2,1)}, bf16[4,2,3,128,128]{4,3,2,1,0:T(8,128)(2,1)}, u32[]{:S(2)}, u32[]{:S(2)}) collective-permute-start(bf16[4,2,3,128,128]{4,3,2,1,0:T(8,128)(2,1)} %gate.21.refs_1_), channel_id=1, source_target_pairs={{0,4},{4,0},{8,12},{12,8},{16,20},{20,16},{24,28},{28,24},{32,36},... | collective-permute-start | bytes 2359304 | tf_op jit(solution)/shard_map/ppermute | solution.py:529
  69.6 15.8 %collective-permute-start.12 = (bf16[4,2,3,128,128]{4,3,2,1,0:T(8,128)(2,1)S(1)}, bf16[4,2,3,128,128]{4,3,2,1,0:T(8,128)(2,1)}, u32[]{:S(2)}, u32[]{:S(2)}) collective-permute-start(bf16[4,2,3,128,128]{4,3,2,1,0:T(8,128)(2,1)S(1)} %copy-done.18), channel_id=1, source_target_pairs={{0,4},{4,0},{8,12},{12,8},{16,20},{20,16},{24,28},{28,24},{32,36},... | collective-permute-start | bytes 2359304 | tf_op jit(solution)/shard_map/ppermute | solution.py:529
  76.4 15.9 %collective-permute-start.10 = (bf16[4,2,3,128,128]{4,3,2,1,0:T(8,128)(2,1)}, bf16[4,2,3,128,128]{4,3,2,1,0:T(8,128)(2,1)S(1)}, u32[]{:S(2)}, u32[]{:S(2)}) collective-permute-start(bf16[4,2,3,128,128]{4,3,2,1,0:T(8,128)(2,1)} %gate.25.refs_1_), channel_id=1, source_target_pairs={{0,8},{4,60},{8,16},{12,4},{16,24},{20,12},{24,32},{28,20},{32,40}... | collective-permute-start | bytes 2359304 | tf_op jit(solution)/shard_map/ppermute | solution.py:525
  81.2 27.0 %collective-permute-start.15 = (bf16[4,2,3,128,128]{4,3,2,1,0:T(8,128)(2,1)}, bf16[4,2,3,128,128]{4,3,2,1,0:T(8,128)(2,1)}, u32[]{:S(2)}, u32[]{:S(2)}) collective-permute-start(bf16[4,2,3,128,128]{4,3,2,1,0:T(8,128)(2,1)} %gate.25.refs_1_), channel_id=1, source_target_pairs={{0,4},{4,0},{8,12},{12,8},{16,20},{20,16},{24,28},{28,24},{32,36},... | collective-permute-start | bytes 2359304 | tf_op jit(solution)/shard_map/ppermute | solution.py:529
  82.1 25.2 %collective-permute-start.19 = (bf16[4,2,3,128,128]{4,3,2,1,0:T(8,128)(2,1)}, bf16[4,2,3,128,128]{4,3,2,1,0:T(8,128)(2,1)S(1)}, u32[]{:S(2)}, u32[]{:S(2)}) collective-permute-start(bf16[4,2,3,128,128]{4,3,2,1,0:T(8,128)(2,1)} %gate.27.refs_2_), channel_id=1, source_target_pairs={{0,8},{4,60},{8,16},{12,4},{16,24},{20,12},{24,32},{28,20},{32,40}... | collective-permute-start | bytes 2359304 | tf_op jit(solution)/shard_map/ppermute | solution.py:525
  85.4 23.1 %collective-permute-start.16 = (bf16[4,2,3,128,128]{4,3,2,1,0:T(8,128)(2,1)}, bf16[4,2,3,128,128]{4,3,2,1,0:T(8,128)(2,1)}, u32[]{:S(2)}, u32[]{:S(2)}) collective-permute-start(bf16[4,2,3,128,128]{4,3,2,1,0:T(8,128)(2,1)} %gate.27.refs_2_), channel_id=1, source_target_pairs={{0,4},{4,0},{8,12},{12,8},{16,20},{20,16},{24,28},{28,24},{32,36},... | collective-permute-start | bytes 2359304 | tf_op jit(solution)/shard_map/ppermute | solution.py:529
  93.2 22.1 %collective-permute-start.13 = (bf16[4,2,3,128,128]{4,3,2,1,0:T(8,128)(2,1)}, bf16[4,2,3,128,128]{4,3,2,1,0:T(8,128)(2,1)S(1)}, u32[]{:S(2)}, u32[]{:S(2)}) collective-permute-start(bf16[4,2,3,128,128]{4,3,2,1,0:T(8,128)(2,1)} %gate.26.refs_1_), channel_id=1, source_target_pairs={{0,8},{4,60},{8,16},{12,4},{16,24},{20,12},{24,32},{28,20},{32,40}... | collective-permute-start | bytes 2359304 | tf_op jit(solution)/shard_map/ppermute | solution.py:525
  107.3 33.9 %collective-permute-start.23 = (bf16[320,1536]{1,0:T(8,128)(2,1)}, bf16[320,1536]{1,0:T(8,128)(2,1)S(1)}, u32[]{:S(2)}, u32[]{:S(2)}) collective-permute-start(bf16[320,1536]{1,0:T(8,128)(2,1)} %get-tuple-element.67), channel_id=1, source_target_pairs={{0,1},{1,2},{2,3},{3,0},{4,5},{5,6},{6,7},{7,4},{8,9},{9,10},{10,1... | collective-permute-start | bytes 2949128 | tf_op jit(solution)/shard_map/ppermute | solution.py:520
  107.4 11.8 %collective-permute-start.20 = (bf16[4,2,3,128,128]{4,3,2,1,0:T(8,128)(2,1)S(1)}, bf16[4,2,3,128,128]{4,3,2,1,0:T(8,128)(2,1)}, u32[]{:S(2)}, u32[]{:S(2)}) collective-permute-start(bf16[4,2,3,128,128]{4,3,2,1,0:T(8,128)(2,1)S(1)} %copy-done.22), channel_id=1, source_target_pairs={{0,4},{4,0},{8,12},{12,8},{16,20},{20,16},{24,28},{28,24},{32,36},... | collective-permute-start | bytes 2359304 | tf_op jit(solution)/shard_map/ppermute | solution.py:529
  108.3 10.9 %collective-permute-start.21 = (bf16[4,2,3,128,128]{4,3,2,1,0:T(8,128)(2,1)}, bf16[4,2,3,128,128]{4,3,2,1,0:T(8,128)(2,1)}, u32[]{:S(2)}, u32[]{:S(2)}) collective-permute-start(bf16[4,2,3,128,128]{4,3,2,1,0:T(8,128)(2,1)} %gate.29.refs_2_), channel_id=1, source_target_pairs={{0,4},{4,0},{8,12},{12,8},{16,20},{20,16},{24,28},{28,24},{32,36},... | collective-permute-start | bytes 2359304 | tf_op jit(solution)/shard_map/ppermute | solution.py:529
  116.5 24.7 %collective-permute-start.24 = (bf16[320,1536]{1,0:T(8,128)(2,1)}, bf16[320,1536]{1,0:T(8,128)(2,1)S(1)}, u32[]{:S(2)}, u32[]{:S(2)}) collective-permute-start(bf16[320,1536]{1,0:T(8,128)(2,1)} %get-tuple-element.68), channel_id=1, source_target_pairs={{0,3},{1,0},{2,1},{3,2},{4,7},{5,4},{6,5},{7,6},{8,11},{9,8},{10,9... | collective-permute-start | bytes 2949128 | tf_op jit(solution)/shard_map/ppermute | solution.py:520
  137.8 10.6 %all-to-all-start.1 = ((bf16[4,128,384]{2,1,0:T(8,128)(2,1)}), bf16[4,128,384]{2,1,0:T(8,128)(2,1)S(1)}, u32[]{:S(2)}, u32[]{:S(2)}) async-start(bf16[4,128,384]{2,1,0:T(8,128)(2,1)} %bitcast.14), calls=%async_computation.1 | async-start | bytes 786432 | tf_op jit(solution)/shard_map/all_to_all | solution.py:494
  145.0 14.9 %collective-permute-start.25 = (bf16[160,1536]{1,0:T(8,128)(2,1)}, bf16[160,1536]{1,0:T(8,128)(2,1)}, u32[]{:S(2)}, u32[]{:S(2)}) collective-permute-start(bf16[160,1536]{1,0:T(8,128)(2,1)} %get-tuple-element.71), channel_id=1, source_target_pairs={{0,1},{1,2},{2,3},{3,0},{4,5},{5,6},{6,7},{7,4},{8,9},{9,10},{10,1... | collective-permute-start | bytes 1474568 | tf_op jit(solution)/shard_map/ppermute | solution.py:520
  146.4 13.5 %collective-permute-start.26 = (bf16[160,1536]{1,0:T(8,128)(2,1)}, bf16[160,1536]{1,0:T(8,128)(2,1)}, u32[]{:S(2)}, u32[]{:S(2)}) collective-permute-start(bf16[160,1536]{1,0:T(8,128)(2,1)} %get-tuple-element.72), channel_id=1, source_target_pairs={{0,3},{1,0},{2,1},{3,2},{4,7},{5,4},{6,5},{7,6},{8,11},{9,8},{10,9... | collective-permute-start | bytes 1474568 | tf_op jit(solution)/shard_map/ppermute | solution.py:520
  148.3 11.6 %collective-permute-start.22 = (bf16[4,128,384]{2,1,0:T(8,128)(2,1)S(1)}, bf16[4,128,384]{2,1,0:T(8,128)(2,1)S(1)}, u32[]{:S(2)}, u32[]{:S(2)}) collective-permute-start(bf16[4,128,384]{2,1,0:T(8,128)(2,1)S(1)} %all-to-all-done.1.own), channel_id=1, source_target_pairs={{0,4},{4,0},{8,12},{12,8},{16,20},{20,16},{24,28},{28,24},{32,36},... | collective-permute-start | bytes 1179656 | tf_op jit(solution)/shard_map/ppermute | solution.py:529
  (39 other events, 177.8 us)
Sparse Core Ops, SparseCore 0:
  12.3 39.3 all-gather.4
  54.2 60.0 all-gather.6

commit v9 on v8

--- a/solution.py
+++ b/solution.py
@@ -234,7 +234,7 @@
         grid=(LOCAL,),
         in_specs=[QUERY] + [SHARD] * len(kvs) + ([] if state is None else [head] * 3) + [ANY] * len(after),
         out_specs=out_specs,
-        compiler_params=pltpu.CompilerParams(vmem_limit_bytes=(32 if last else 60) * MIB),
+        compiler_params=pltpu.CompilerParams(vmem_limit_bytes=60 * MIB),
         cost_estimate=BRIEF,
         name="flash",
     )(query, *kvs, *(() if state is None else state), *after)
@@ -546,33 +546,30 @@
     own = query[:, :2]
     sibling = swap_core(own)
     near, far = hop(own), hop(sibling)
-    audio = [gate(rows, sibling) for rows in audio]
-    mains = [audio[0]] + [send_main(audio[step], step) for step in (1, 2, 3)]
-    halos = [audio[4]] + [send_halo(audio[4 + step], step) for step in (1, 2, 3)]
+    mains = [audio[0]] + [send_main(gate(audio[step], sibling), step) for step in (1, 2, 3)]
 
     acc, top, total, token = flash(query, [own, sibling], None, False)
+    halos = [audio[4]] + [send_halo(gate(audio[4 + step], token), step) for step in (1, 2, 3)]
     near, far = gate(near, token, *mains[1:], *halos[1:]), gate(far, token)
     crossed = cross(place, margins, query, mains, halos, own, sibling, far)
 
-    tokens = [token]
-    after = (crossed,)
+    rest, up, down, up_later, down_later = project_cross(
+        place, crossed, swap_core(crossed), w_rest, (token, token)
+    )
+    up, down = shift_tower(up, 1), shift_tower(down, -1)
+
+    behind = [crossed]
+    after = (rest,)
     for step in range(1, 4):
         now = [near, far, swap_core(near), swap_core(far)]
         near, far = hop(near), (hop(far) if step < 3 else None)
         acc, top, total, token = flash(query, now, (acc, top, total), False, after)
-        tokens.append(token)
+        behind.append(token)
         after = ()
-        if step == 1:
-            rest, up, down, up_later, down_later = project_cross(
-                place, crossed, swap_core(crossed), w_rest, (token, token)
-            )
-            after = (rest,)
-            up, down = shift_tower(up, 1), shift_tower(down, -1)
-        behind = crossed if step == 1 else tokens[step - 1]
-        near = gate(near, behind)
+        near = gate(near, behind[step - 1])
         if step < 3:
-            far = gate(far, behind)
-    video_self = flash(query, [near, swap_core(near)], (acc, top, total), True, (w_self,))
+            far = gate(far, behind[step - 1])
+    video_self = flash(query, [near, swap_core(near)], (acc, top, total), True)
     up_later, down_later = add_later(up, down, up_later, down_later, video_self)
     up_later, down_later = shift_tower(up_later, 1), shift_tower(down_later, -1)
     base = (rest, up, down, up_later, down_later)

time: 179 us -> 174 us (0.972)
  local copies, waits for them, and re-layouts: 21.3 us -> 13.8 us
  waiting for transfers between devices: 18.2 us -> 22.6 us
  starting transfers between devices: 48.5 us -> 46.4 us
    unnamed x65 -> x61, local copies, waits for them, and re-layouts: 20.7 us -> 13.1 us
    ppermute x7, starting transfers between devices: 25.9 us -> 21.1 us  [hop(): lax.ppermute(value, 'ctx', [(i, (i + 2 - 4 * (i % 2)) % total) for i in r...]
    ppermute x3, waiting for transfers between devices: 0.01 us -> 3.15 us  [send_main(): return lax.ppermute(value, ('ctx', 'tower'), ctx_towers(pairs))]
    ppermute x11, starting transfers between devices: 6.59 us -> 9.19 us  [swap_core(): return lax.ppermute(value, 'ctx', [(i, i ^ 1) for i in range(2 * CHIPS)])]
    ppermute x7, waiting for transfers between devices: 3.83 us -> 6.3 us  [hop(): lax.ppermute(value, 'ctx', [(i, (i + 2 - 4 * (i % 2)) % total) for i in r...]
    ppermute x11, waiting for transfers between devices: 3.37 us -> 1.52 us  [swap_core(): return lax.ppermute(value, 'ctx', [(i, i ^ 1) for i in range(2 * CHIPS)])]
  transfers between devices with their start and end apart: 31 -> 31, of which waited for: 6 -> 6; matrix products, arithmetic and copies ran while one was open for 0% -> 0% of each run, Pallas kernels for 25% -> 26%
where the time goes in v9:
time: 174 us; the launch traced here: 173 us
  Pallas kernels  56.3 us (32%)
  starting transfers between devices  46.4 us (27%)
  waiting for transfers between devices  22.6 us (13%)
  blocking collectives  19.5 us (11%)
  between operations  14.5 us (8%)
  local copies, waits for them, and re-layouts  13.8 us (8%)
    pallas_call x5, Pallas kernels, flash(): pl.pallas_call(functools.partial(flash_kernel, len(kvs), state is None, l...  30.8 us
    ppermute x7, starting transfers between devices, hop(): lax.ppermute(value, 'ctx', [(i, (i + 2 - 4 * (i % 2)) % total) for i in r...  21.1 us
    all_to_all x1, blocking collectives, exchange_towers(): lax.all_to_all(value, 'tower', split_axis=0, concat_axis=0, tiled=True)  19.5 us
    unnamed x61, local copies, waits for them, and re-layouts  13.1 us
    ppermute x4, waiting for transfers between devices, shift_tower(): lax.ppermute(value, 'tower', [(i, (i + step) % TOWERS) for i in range(TOW...  10.2 us
    ppermute x11, starting transfers between devices, swap_core(): return lax.ppermute(value, 'ctx', [(i, i ^ 1) for i in range(2 * CHIPS)])  9.19 us
    pallas_call x1, Pallas kernels, cross(): pl.pallas_call(cross_kernel, out_shape=jax.ShapeDtypeStruct((TOWERS, BOTH...  6.8 us
    pallas_call x1, Pallas kernels, project_cross(): pl.pallas_call(project_cross_kernel, out_shape=[jax.ShapeDtypeStruct((n *...  6.53 us
  transfers between devices with their start and end apart: 31, of which 6 were waited for; matrix products, arithmetic and copies ran while one was open for 0% of the time, Pallas kernels for 26%

profile of v9, /device:TPU:1, one launch (start us, length us, event | category | flops | bytes accessed | tf_op | source)
XLA Modules:
  0.0 173.1 jit_solution(8733092933601988700)
XLA Ops:
  7.9 4.3 %pack.1 = (bf16[4,3,3,128,128]{4,3,2,1,0:T(8,128)(2,1)}, bf16[3,32,1536]{2,1,0:T(8,128)(2,1)}, bf16[2,3,32,1536]{3,2,1,0:T(8,128)(2,1)}, bf16[480,384]{1,0:T(8,1...) custom-call(s32[5]{0:T(128)} %stack.23.place, ...), custom_call_target="tpu_custom_call" | custom-call | tf_op jit(solution)/shard_map/pack/pallas_call | solution.py:123
  13.0 19.5 %all_to_all.10.refs_0_.q_ref = bf16[4,3,3,128,128]{4,3,2,1,0:T(8,128)(2,1)S(1)} all-to-all(bf16[4,3,3,128,128]{4,3,2,1,0:T(8,128)(2,1)} %get-tuple-element.40), channel_id=1, replica_groups=mesh['batch'=4,'ctx'=16,'tower'=4] {'tower'}, dimensions={0} | all-to-all | bytes 2359296 | tf_op jit(solution)/shard_map/all_to_all | solution.py:494
  32.6 2.9 %collective-permute-start.1 = (bf16[4,2,3,128,128]{4,3,2,1,0:T(8,128)(2,1)S(1)}, bf16[4,2,3,128,128]{4,3,2,1,0:T(8,128)(2,1)S(1)}, u32[]{:S(2)}, u32[]{:S(2)}) collective-permute-start(bf16[4,2,3,128,128]{4,3,2,1,0:T(8,128)(2,1)S(1)} %slice.4.refs_1_.refs_8_), channel_id=1, source_target_pairs={{0,4},{4,0},{8,12},{12,8},{16,20},{20,16},{24,28},{28,24},{32,36},... | collective-permute-start | bytes 2359304 | tf_op jit(solution)/shard_map/ppermute | solution.py:529
  35.5 5.6 %collective-permute-start = (bf16[4,2,3,128,128]{4,3,2,1,0:T(8,128)(2,1)S(1)}, bf16[4,2,3,128,128]{4,3,2,1,0:T(8,128)(2,1)S(1)}, u32[]{:S(2)}, u32[]{:S(2)}) collective-permute-start(bf16[4,2,3,128,128]{4,3,2,1,0:T(8,128)(2,1)S(1)} %slice.4.refs_1_.refs_8_), channel_id=1, source_target_pairs={{0,8},{4,60},{8,16},{12,4},{16,24},{20,12},{24,32},{28,20},{32,40}... | collective-permute-start | bytes 2359304 | tf_op jit(solution)/shard_map/ppermute | solution.py:525
  41.9 2.5 %collective-permute-start.3 = (bf16[480,384]{1,0:T(8,128)(2,1)}, bf16[480,384]{1,0:T(8,128)(2,1)S(1)}, u32[]{:S(2)}, u32[]{:S(2)}) collective-permute-start(bf16[480,384]{1,0:T(8,128)(2,1)} %gate.14), channel_id=1, source_target_pairs={{0,2},{4,6},{8,10},{12,14},{17,19},{21,23},{25,27},{29,31},{34,32}... | collective-permute-start | bytes 1105928 | tf_op jit(solution)/shard_map/ppermute | solution.py:150
  47.2 4.7 %flash.5 = (f32[512,384]{1,0:T(8,128)}, f32[512,384]{1,0:T(8,128)}, f32[512,384]{1,0:T(8,128)}, f32[8,128]{1,0:T(8,128)}) custom-call(bf16[4,3,3,128,128]{4,3,2,1,0:T(8,128)(2,1)} %copy-done.9, bf16[4,2,3,128,128]{4,3,2,1,0:T(8,128)(2,1)} %copy-done.14, bf16[4,2,3,128,128]{4,3,2,1,0:T(8,128)(2,1)} %copy-done.10), custom_call_target="tpu_custom_call" | custom-call | flops 1 | bytes 1 | tf_op jit(solution)/shard_map/flash/pallas_call | solution.py:231
  55.0 3.1 %collective-permute-done.2.refs_2_.refs_1_ = bf16[480,384]{1,0:T(8,128)(2,1)S(1)} collective-permute-done((bf16[480,384]{1,0:T(8,128)(2,1)}, bf16[480,384]{1,0:T(8,128)(2,1)S(1)}, u32[]{:S(2)}, u32[]{:S(2)}) %collective-permute-start.2) | collective-permute-done | bytes 368672 | tf_op jit(solution)/shard_map/ppermute | solution.py:150
  59.0 1.6 collective-permute-start.8
  60.6 5.1 %collective-permute-done.9.refs_0_ = bf16[4,2,3,128,128]{4,3,2,1,0:T(8,128)(2,1)S(1)} collective-permute-done((bf16[4,2,3,128,128]{4,3,2,1,0:T(8,128)(2,1)S(1)}, bf16[4,2,3,128,128]{4,3,2,1,0:T(8,128)(2,1)S(1)}, u32[]{:S(2)}, u32[]{:S(2)}) %collective-permute-start.9) | collective-permute-done | bytes 786464 | tf_op jit(solution)/shard_map/ppermute | solution.py:525
  69.2 6.8 %cross.1.refs_1_.own = bf16[4,160,384]{2,1,0:T(8,128)(2,1)} custom-call(s32[5]{0:T(128)} %stack.23.place, s32[64,3]{1,0:T(8,128)} %bitcast.30, bf16[4,3,3,128,128]{4,3,2,1,0:T(8,128)(2,1)} %copy-done.9, bf16[480,384]{1,0:T(8,128)(2,1)} %get-tuple-element.48.refs_0_, bf16[480,384]{1,0:T(8,128)(2,1)} %copy-done.23, bf16[480,384]{1,0:T(8,128)(2,1)} %copy-done.21, ...), custom_call_target="tpu_custom_call" | custom-call | flops 1 | bytes 1 | tf_op jit(solution)/shard_map/cross/pallas_call | solution.py:319
  76.9 4.6 %collective-permute-start.10 = (bf16[4,2,3,128,128]{4,3,2,1,0:T(8,128)(2,1)}, bf16[4,2,3,128,128]{4,3,2,1,0:T(8,128)(2,1)S(1)}, u32[]{:S(2)}, u32[]{:S(2)}) collective-permute-start(bf16[4,2,3,128,128]{4,3,2,1,0:T(8,128)(2,1)} %gate.21.refs_1_), channel_id=1, source_target_pairs={{0,8},{4,60},{8,16},{12,4},{16,24},{20,12},{24,32},{28,20},{32,40}... | collective-permute-start | bytes 2359304 | tf_op jit(solution)/shard_map/ppermute | solution.py:525
  83.6 5.5 %collective-permute-start.19 = (bf16[4,2,3,128,128]{4,3,2,1,0:T(8,128)(2,1)}, bf16[4,2,3,128,128]{4,3,2,1,0:T(8,128)(2,1)S(1)}, u32[]{:S(2)}, u32[]{:S(2)}) collective-permute-start(bf16[4,2,3,128,128]{4,3,2,1,0:T(8,128)(2,1)} %gate.23.refs_2_), channel_id=1, source_target_pairs={{0,8},{4,60},{8,16},{12,4},{16,24},{20,12},{24,32},{28,20},{32,40}... | collective-permute-start | bytes 2359304 | tf_op jit(solution)/shard_map/ppermute | solution.py:525
  89.1 6.5 %project_cross.1 = (bf16[320,1536]{1,0:T(8,128)(2,1)}, bf16[320,1536]{1,0:T(8,128)(2,1)}, bf16[320,1536]{1,0:T(8,128)(2,1)}, bf16[160,1536]{1,0:T(8,128)(2,1)}, bf16[160,1536]{1,0:T(8,128)(2,1)}) custom-call(s32[5]{0:T(128)} %stack.23.place, bf16[4,160,384]{2,1,0:T(8,128)(2,1)} %cross.1.refs_1_.own, bf16[4,160,384]{2,1,0:T(8,128)(2,1)} %copy-done.25, ...), custom_call_target="tpu_custom_call" | custom-call | flops 1 | bytes 1 | tf_op jit(solution)/shard_map/project_cross/pallas_call | solution.py:371
  96.0 7.0 %flash.6 = (f32[512,384]{1,0:T(8,128)}, f32[512,384]{1,0:T(8,128)}, f32[512,384]{1,0:T(8,128)}, f32[8,128]{1,0:T(8,128)}) custom-call(bf16[4,3,3,128,128]{4,3,2,1,0:T(8,128)(2,1)} %copy-done.9, bf16[4,2,3,128,128]{4,3,2,1,0:T(8,128)(2,1)} %gate.19.refs_1_, bf16[4,2,3,128,128]{4,3,2,1,0:T(8,128)(2,1)} %gate.20.refs_10_.refs_2_, ...), custom_call_target="tpu_custom_call" | custom-call | flops 1 | bytes 1 | tf_op jit(solution)/shard_map/flash/pallas_call | solution.py:231
  105.5 2.7 %collective-permute-start.24 = (bf16[320,1536]{1,0:T(8,128)(2,1)}, bf16[320,1536]{1,0:T(8,128)(2,1)S(1)}, u32[]{:S(2)}, u32[]{:S(2)}) collective-permute-start(bf16[320,1536]{1,0:T(8,128)(2,1)} %get-tuple-element.68), channel_id=1, source_target_pairs={{0,3},{1,0},{2,1},{3,2},{4,7},{5,4},{6,5},{7,6},{8,11},{9,8},{10,9... | collective-permute-start | bytes 2949128 | tf_op jit(solution)/shard_map/ppermute | solution.py:520
  108.8 6.8 %flash.7 = (f32[512,384]{1,0:T(8,128)}, f32[512,384]{1,0:T(8,128)}, f32[512,384]{1,0:T(8,128)}, f32[8,128]{1,0:T(8,128)}) custom-call(bf16[4,3,3,128,128]{4,3,2,1,0:T(8,128)(2,1)} %copy-done.9, bf16[4,2,3,128,128]{4,3,2,1,0:T(8,128)(2,1)} %gate.21.refs_1_, bf16[4,2,3,128,128]{4,3,2,1,0:T(8,128)(2,1)} %gate.23.refs_2_, ...), custom_call_target="tpu_custom_call" | custom-call | flops 1 | bytes 1 | tf_op jit(solution)/shard_map/flash/pallas_call | solution.py:231
  115.6 2.2 %collective-permute-start.18 = (bf16[4,2,3,128,128]{4,3,2,1,0:T(8,128)(2,1)}, bf16[4,2,3,128,128]{4,3,2,1,0:T(8,128)(2,1)}, u32[]{:S(2)}, u32[]{:S(2)}) collective-permute-start(bf16[4,2,3,128,128]{4,3,2,1,0:T(8,128)(2,1)} %gate.24.refs_1_), channel_id=1, source_target_pairs={{0,4},{4,0},{8,12},{12,8},{16,20},{20,16},{24,28},{28,24},{32,36},... | collective-permute-start | bytes 2359304 | tf_op jit(solution)/shard_map/ppermute | solution.py:529
  118.7 6.9 %flash.8 = (f32[512,384]{1,0:T(8,128)}, f32[512,384]{1,0:T(8,128)}, f32[512,384]{1,0:T(8,128)}, f32[8,128]{1,0:T(8,128)}) custom-call(bf16[4,3,3,128,128]{4,3,2,1,0:T(8,128)(2,1)} %copy-done.9, bf16[4,2,3,128,128]{4,3,2,1,0:T(8,128)(2,1)} %gate.22.refs_1_, bf16[4,2,3,128,128]{4,3,2,1,0:T(8,128)(2,1)} %gate.25.refs_2_, ...), custom_call_target="tpu_custom_call" | custom-call | flops 1 | bytes 1 | tf_op jit(solution)/shard_map/flash/pallas_call | solution.py:231
  125.6 5.4 %flash.9._ = bf16[512,384]{1,0:T(8,128)(2,1)} custom-call(bf16[4,3,3,128,128]{4,3,2,1,0:T(8,128)(2,1)} %copy-done.9, bf16[4,2,3,128,128]{4,3,2,1,0:T(8,128)(2,1)} %gate.24.refs_1_, bf16[4,2,3,128,128]{4,3,2,1,0:T(8,128)(2,1)} %collective-permute-done.18.refs_2_, f32[512,384]{1,0:T(8,128)} %get-tuple-element.63.refs_3_, ...), custom_call_target="tpu_custom_call" | custom-call | flops 1 | bytes 1 | tf_op jit(solution)/shard_map/flash/pallas_call | solution.py:231
  131.0 3.5 %all-to-all-start.1 = ((bf16[4,128,384]{2,1,0:T(8,128)(2,1)}), bf16[4,128,384]{2,1,0:T(8,128)(2,1)S(1)}, u32[]{:S(2)}, u32[]{:S(2)}) async-start(bf16[4,128,384]{2,1,0:T(8,128)(2,1)} %bitcast.19), calls=%async_computation.1 | async-start | bytes 786432 | tf_op jit(solution)/shard_map/all_to_all | solution.py:494
  137.6 1.7 add_later.1
  143.4 10.2 %collective-permute-done.25.refs_3_ = bf16[160,1536]{1,0:T(8,128)(2,1)} collective-permute-done((bf16[160,1536]{1,0:T(8,128)(2,1)}, bf16[160,1536]{1,0:T(8,128)(2,1)}, u32[]{:S(2)}, u32[]{:S(2)}) %collective-permute-start.25) | collective-permute-done | bytes 491552 | tf_op jit(solution)/shard_map/ppermute | solution.py:520
  154.4 2.3 %copy-done = bf16[48,32,1536]{2,1,0:T(8,128)(2,1)S(1)} copy-done((bf16[48,32,1536]{2,1,0:T(8,128)(2,1)S(1)}, bf16[48,32,1536]{2,1,0:T(8,128)(2,1)}, u32[]{:S(2)}) %copy-start) | copy-done | bytes 4718616
  157.7 4.8 %project_self.1 = (bf16[128,3072]{1,0:T(8,128)(2,1)}, bf16[24,3072]{1,0:T(8,128)(2,1)}, bf16[160,1536]{1,0:T(8,128)(2,1)S(1)}) custom-call(s32[5]{0:T(128)S(1)} %copy-done.8, bf16[4,128,384]{2,1,0:T(8,128)(2,1)S(1)} %all-to-all-done.1.own, bf16[4,128,384]{2,1,0:T(8,128)(2,1)S(1)} %copy-done.6, bf16[16,3,32,1536]{3,2,1,0:T(8,128)(2,1)S(1)} %bitcast.18, ...), custom_call_target="tpu_custom_call" | custom-call | flops 1 | bytes 1 | tf_op jit(solution)/shard_map/project_self/pallas_call | solution.py:426
  (128 shorter events, 32.4 us)
Async XLA Ops:
  7.2 82.0 %all-gather.5.cloned.1.call-start = ((), (), s32[]{:S(2)}) async-start(), calls=%async_computation.2 | async-start | bytes 2949120 | tf_op jit(solution)/shard_map/all_gather | solution.py:543
  12.2 142.1 %all-gather.7.cloned.1.call-start = ((), (), s32[]{:S(2)}) async-start(), calls=%async_computation.3 | async-start | bytes 5013504 | tf_op jit(solution)/shard_map/all_gather | solution.py:544
  35.5 17.2 %collective-permute-start = (bf16[4,2,3,128,128]{4,3,2,1,0:T(8,128)(2,1)S(1)}, bf16[4,2,3,128,128]{4,3,2,1,0:T(8,128)(2,1)S(1)}, u32[]{:S(2)}, u32[]{:S(2)}) collective-permute-start(bf16[4,2,3,128,128]{4,3,2,1,0:T(8,128)(2,1)S(1)} %slice.4.refs_1_.refs_8_), channel_id=1, source_target_pairs={{0,8},{4,60},{8,16},{12,4},{16,24},{20,12},{24,32},{28,20},{32,40}... | collective-permute-start | bytes 2359304 | tf_op jit(solution)/shard_map/ppermute | solution.py:525
  41.9 13.0 %collective-permute-start.3 = (bf16[480,384]{1,0:T(8,128)(2,1)}, bf16[480,384]{1,0:T(8,128)(2,1)S(1)}, u32[]{:S(2)}, u32[]{:S(2)}) collective-permute-start(bf16[480,384]{1,0:T(8,128)(2,1)} %gate.14), channel_id=1, source_target_pairs={{0,2},{4,6},{8,10},{12,14},{17,19},{21,23},{25,27},{29,31},{34,32}... | collective-permute-start | bytes 1105928 | tf_op jit(solution)/shard_map/ppermute | solution.py:150
  44.4 10.6 %collective-permute-start.4 = (bf16[480,384]{1,0:T(8,128)(2,1)}, bf16[480,384]{1,0:T(8,128)(2,1)S(1)}, u32[]{:S(2)}, u32[]{:S(2)}) collective-permute-start(bf16[480,384]{1,0:T(8,128)(2,1)} %gate.15), channel_id=1, source_target_pairs={{0,3},{4,7},{8,11},{12,15},{17,16},{21,20},{25,24},{29,28},{34,33}... | collective-permute-start | bytes 1105928 | tf_op jit(solution)/shard_map/ppermute | solution.py:150
  45.8 12.4 %collective-permute-start.2 = (bf16[480,384]{1,0:T(8,128)(2,1)}, bf16[480,384]{1,0:T(8,128)(2,1)S(1)}, u32[]{:S(2)}, u32[]{:S(2)}) collective-permute-start(bf16[480,384]{1,0:T(8,128)(2,1)} %gate.13), channel_id=1, source_target_pairs={{0,1},{4,5},{8,9},{12,13},{17,18},{21,22},{25,26},{29,30},{34,35},... | collective-permute-start | bytes 1105928 | tf_op jit(solution)/shard_map/ppermute | solution.py:150
  54.1 11.6 %collective-permute-start.9 = (bf16[4,2,3,128,128]{4,3,2,1,0:T(8,128)(2,1)S(1)}, bf16[4,2,3,128,128]{4,3,2,1,0:T(8,128)(2,1)S(1)}, u32[]{:S(2)}, u32[]{:S(2)}) collective-permute-start(bf16[4,2,3,128,128]{4,3,2,1,0:T(8,128)(2,1)S(1)} %copy-done.11), channel_id=1, source_target_pairs={{0,8},{4,60},{8,16},{12,4},{16,24},{20,12},{24,32},{28,20},{32,40}... | collective-permute-start | bytes 2359304 | tf_op jit(solution)/shard_map/ppermute | solution.py:525
  59.0 17.0 %collective-permute-start.8 = (bf16[4,2,3,128,128]{4,3,2,1,0:T(8,128)(2,1)}, bf16[4,2,3,128,128]{4,3,2,1,0:T(8,128)(2,1)S(1)}, u32[]{:S(2)}, u32[]{:S(2)}) collective-permute-start(bf16[4,2,3,128,128]{4,3,2,1,0:T(8,128)(2,1)} %gate.19.refs_1_), channel_id=1, source_target_pairs={{0,8},{4,60},{8,16},{12,4},{16,24},{20,12},{24,32},{28,20},{32,40}... | collective-permute-start | bytes 2359304 | tf_op jit(solution)/shard_map/ppermute | solution.py:525
  66.6 16.0 %collective-permute-start.15 = (bf16[4,2,3,128,128]{4,3,2,1,0:T(8,128)(2,1)}, bf16[4,2,3,128,128]{4,3,2,1,0:T(8,128)(2,1)}, u32[]{:S(2)}, u32[]{:S(2)}) collective-permute-start(bf16[4,2,3,128,128]{4,3,2,1,0:T(8,128)(2,1)} %gate.20.refs_10_.refs_2_), channel_id=1, source_target_pairs={{0,8},{4,60},{8,16},{12,4},{16,24},{20,12},{24,32},{28,20},{32,40}... | collective-permute-start | bytes 2359304 | tf_op jit(solution)/shard_map/ppermute | solution.py:525
  68.7 27.0 %collective-permute-start.11 = (bf16[4,2,3,128,128]{4,3,2,1,0:T(8,128)(2,1)S(1)}, bf16[4,2,3,128,128]{4,3,2,1,0:T(8,128)(2,1)}, u32[]{:S(2)}, u32[]{:S(2)}) collective-permute-start(bf16[4,2,3,128,128]{4,3,2,1,0:T(8,128)(2,1)S(1)} %copy-done.19), channel_id=1, source_target_pairs={{0,4},{4,0},{8,12},{12,8},{16,20},{20,16},{24,28},{28,24},{32,36},... | collective-permute-start | bytes 2359304 | tf_op jit(solution)/shard_map/ppermute | solution.py:529
  68.7 27.3 %collective-permute-start.12 = (bf16[4,2,3,128,128]{4,3,2,1,0:T(8,128)(2,1)}, bf16[4,2,3,128,128]{4,3,2,1,0:T(8,128)(2,1)}, u32[]{:S(2)}, u32[]{:S(2)}) collective-permute-start(bf16[4,2,3,128,128]{4,3,2,1,0:T(8,128)(2,1)} %gate.20.refs_10_.refs_2_), channel_id=1, source_target_pairs={{0,4},{4,0},{8,12},{12,8},{16,20},{20,16},{24,28},{28,24},{32,36},... | collective-permute-start | bytes 2359304 | tf_op jit(solution)/shard_map/ppermute | solution.py:529
  76.9 26.1 %collective-permute-start.10 = (bf16[4,2,3,128,128]{4,3,2,1,0:T(8,128)(2,1)}, bf16[4,2,3,128,128]{4,3,2,1,0:T(8,128)(2,1)S(1)}, u32[]{:S(2)}, u32[]{:S(2)}) collective-permute-start(bf16[4,2,3,128,128]{4,3,2,1,0:T(8,128)(2,1)} %gate.21.refs_1_), channel_id=1, source_target_pairs={{0,8},{4,60},{8,16},{12,4},{16,24},{20,12},{24,32},{28,20},{32,40}... | collective-permute-start | bytes 2359304 | tf_op jit(solution)/shard_map/ppermute | solution.py:525
  82.7 25.5 %collective-permute-start.16 = (bf16[4,2,3,128,128]{4,3,2,1,0:T(8,128)(2,1)}, bf16[4,2,3,128,128]{4,3,2,1,0:T(8,128)(2,1)}, u32[]{:S(2)}, u32[]{:S(2)}) collective-permute-start(bf16[4,2,3,128,128]{4,3,2,1,0:T(8,128)(2,1)} %gate.21.refs_1_), channel_id=1, source_target_pairs={{0,4},{4,0},{8,12},{12,8},{16,20},{20,16},{24,28},{28,24},{32,36},... | collective-permute-start | bytes 2359304 | tf_op jit(solution)/shard_map/ppermute | solution.py:529
  83.6 21.8 %collective-permute-start.19 = (bf16[4,2,3,128,128]{4,3,2,1,0:T(8,128)(2,1)}, bf16[4,2,3,128,128]{4,3,2,1,0:T(8,128)(2,1)S(1)}, u32[]{:S(2)}, u32[]{:S(2)}) collective-permute-start(bf16[4,2,3,128,128]{4,3,2,1,0:T(8,128)(2,1)} %gate.23.refs_2_), channel_id=1, source_target_pairs={{0,8},{4,60},{8,16},{12,4},{16,24},{20,12},{24,32},{28,20},{32,40}... | collective-permute-start | bytes 2359304 | tf_op jit(solution)/shard_map/ppermute | solution.py:525
  95.7 12.6 %collective-permute-start.17 = (bf16[4,2,3,128,128]{4,3,2,1,0:T(8,128)(2,1)}, bf16[4,2,3,128,128]{4,3,2,1,0:T(8,128)(2,1)}, u32[]{:S(2)}, u32[]{:S(2)}) collective-permute-start(bf16[4,2,3,128,128]{4,3,2,1,0:T(8,128)(2,1)} %gate.23.refs_2_), channel_id=1, source_target_pairs={{0,4},{4,0},{8,12},{12,8},{16,20},{20,16},{24,28},{28,24},{32,36},... | collective-permute-start | bytes 2359304 | tf_op jit(solution)/shard_map/ppermute | solution.py:529
  103.9 11.7 %collective-permute-start.14 = (bf16[4,2,3,128,128]{4,3,2,1,0:T(8,128)(2,1)}, bf16[4,2,3,128,128]{4,3,2,1,0:T(8,128)(2,1)}, u32[]{:S(2)}, u32[]{:S(2)}) collective-permute-start(bf16[4,2,3,128,128]{4,3,2,1,0:T(8,128)(2,1)} %gate.22.refs_1_), channel_id=1, source_target_pairs={{0,8},{4,60},{8,16},{12,4},{16,24},{20,12},{24,32},{28,20},{32,40}... | collective-permute-start | bytes 2359304 | tf_op jit(solution)/shard_map/ppermute | solution.py:525
  105.5 29.0 %collective-permute-start.23 = (bf16[320,1536]{1,0:T(8,128)(2,1)}, bf16[320,1536]{1,0:T(8,128)(2,1)S(1)}, u32[]{:S(2)}, u32[]{:S(2)}) collective-permute-start(bf16[320,1536]{1,0:T(8,128)(2,1)} %get-tuple-element.67), channel_id=1, source_target_pairs={{0,1},{1,2},{2,3},{3,0},{4,5},{5,6},{6,7},{7,4},{8,9},{9,10},{10,1... | collective-permute-start | bytes 2949128 | tf_op jit(solution)/shard_map/ppermute | solution.py:520
  105.5 29.0 %collective-permute-start.24 = (bf16[320,1536]{1,0:T(8,128)(2,1)}, bf16[320,1536]{1,0:T(8,128)(2,1)S(1)}, u32[]{:S(2)}, u32[]{:S(2)}) collective-permute-start(bf16[320,1536]{1,0:T(8,128)(2,1)} %get-tuple-element.68), channel_id=1, source_target_pairs={{0,3},{1,0},{2,1},{3,2},{4,7},{5,4},{6,5},{7,6},{8,11},{9,8},{10,9... | collective-permute-start | bytes 2949128 | tf_op jit(solution)/shard_map/ppermute | solution.py:520
  108.2 9.7 %collective-permute-start.20 = (bf16[4,2,3,128,128]{4,3,2,1,0:T(8,128)(2,1)S(1)}, bf16[4,2,3,128,128]{4,3,2,1,0:T(8,128)(2,1)S(1)}, u32[]{:S(2)}, u32[]{:S(2)}) collective-permute-start(bf16[4,2,3,128,128]{4,3,2,1,0:T(8,128)(2,1)S(1)} %copy-done.16), channel_id=1, source_target_pairs={{0,4},{4,0},{8,12},{12,8},{16,20},{20,16},{24,28},{28,24},{32,36},... | collective-permute-start | bytes 2359304 | tf_op jit(solution)/shard_map/ppermute | solution.py:529
  115.6 9.9 %collective-permute-start.18 = (bf16[4,2,3,128,128]{4,3,2,1,0:T(8,128)(2,1)}, bf16[4,2,3,128,128]{4,3,2,1,0:T(8,128)(2,1)}, u32[]{:S(2)}, u32[]{:S(2)}) collective-permute-start(bf16[4,2,3,128,128]{4,3,2,1,0:T(8,128)(2,1)} %gate.24.refs_1_), channel_id=1, source_target_pairs={{0,4},{4,0},{8,12},{12,8},{16,20},{20,16},{24,28},{28,24},{32,36},... | collective-permute-start | bytes 2359304 | tf_op jit(solution)/shard_map/ppermute | solution.py:529
  131.0 11.7 %all-to-all-start.1 = ((bf16[4,128,384]{2,1,0:T(8,128)(2,1)}), bf16[4,128,384]{2,1,0:T(8,128)(2,1)S(1)}, u32[]{:S(2)}, u32[]{:S(2)}) async-start(bf16[4,128,384]{2,1,0:T(8,128)(2,1)} %bitcast.19), calls=%async_computation.1 | async-start | bytes 786432 | tf_op jit(solution)/shard_map/all_to_all | solution.py:494
  139.2 14.4 %collective-permute-start.25 = (bf16[160,1536]{1,0:T(8,128)(2,1)}, bf16[160,1536]{1,0:T(8,128)(2,1)}, u32[]{:S(2)}, u32[]{:S(2)}) collective-permute-start(bf16[160,1536]{1,0:T(8,128)(2,1)} %get-tuple-element.71), channel_id=1, source_target_pairs={{0,1},{1,2},{2,3},{3,0},{4,5},{5,6},{6,7},{7,4},{8,9},{9,10},{10,1... | collective-permute-start | bytes 1474568 | tf_op jit(solution)/shard_map/ppermute | solution.py:520
  140.6 13.0 %collective-permute-start.26 = (bf16[160,1536]{1,0:T(8,128)(2,1)}, bf16[160,1536]{1,0:T(8,128)(2,1)}, u32[]{:S(2)}, u32[]{:S(2)}) collective-permute-start(bf16[160,1536]{1,0:T(8,128)(2,1)} %get-tuple-element.72), channel_id=1, source_target_pairs={{0,3},{1,0},{2,1},{3,2},{4,7},{5,4},{6,5},{7,6},{8,11},{9,8},{10,9... | collective-permute-start | bytes 1474568 | tf_op jit(solution)/shard_map/ppermute | solution.py:520
  142.7 11.0 %collective-permute-start.22 = (bf16[4,128,384]{2,1,0:T(8,128)(2,1)S(1)}, bf16[4,128,384]{2,1,0:T(8,128)(2,1)S(1)}, u32[]{:S(2)}, u32[]{:S(2)}) collective-permute-start(bf16[4,128,384]{2,1,0:T(8,128)(2,1)S(1)} %all-to-all-done.1.own), channel_id=1, source_target_pairs={{0,4},{4,0},{8,12},{12,8},{16,20},{20,16},{24,28},{28,24},{32,36},... | collective-permute-start | bytes 1179656 | tf_op jit(solution)/shard_map/ppermute | solution.py:529
  (37 other events, 183.0 us)
Sparse Core Ops, SparseCore 0:
  12.4 39.3 all-gather.4
  54.2 62.6 all-gather.6

commit v10 on v9

--- a/solution.py
+++ b/solution.py
@@ -340,17 +340,17 @@
     return jnp.concatenate([piece(h) for h in range(LOCAL) for piece in pieces], axis=0)
 
 
-def project_cross_kernel(place, own, sibling, w_ref, _, __, mine, up, down, up_later, down_later):
+def project_cross_kernel(place, own, sibling, w_ref, _, __, mine, up, down, up_first, down_first):
     towers = [lax.rem(place[1] + step, TOWERS) for step in range(TOWERS)]
     targets = (
         (mine, 0),
         (mine, BOTH),
-        (up_later, 0),
+        (up, 0),
         (up, BOTH),
-        (up, 0),
+        (up_first, 0),
+        (down_first, 0),
+        (down, 0),
         (down, BOTH),
-        (down, 0),
-        (down_later, 0),
     )
     ws = [
         weight_rows([functools.partial(lambda b, h: w_ref[b, kind, h], b) for b in range(4)])
@@ -392,7 +392,7 @@
 
 
 def project_self_kernel(place, own, sibling, w_ref, *refs):
-    mine, up, down, up_later, down_later, gain, video_out, audio_out, sibling_out = refs
+    mine, up, down, gain, video_out, audio_out, sibling_out = refs
     a = jnp.concatenate(
         [jnp.concatenate([ref[t] for t in range(TOWERS)], axis=1) for ref in (own, sibling)], axis=0
     )
@@ -404,11 +404,7 @@
         axis=0,
     )
     acc = nn_dot(a, w)
-    top = [mine[pl.ds(0, BOTH), :], down[pl.ds(0, BOTH), :], up_later[...]]
-    bottom = [mine[pl.ds(BOTH, BOTH), :], up[pl.ds(BOTH, BOTH), :], down_later[...]]
-    base = jnp.concatenate(
-        [functools.reduce(jnp.add, [x.astype(jnp.float32) for x in xs]) for xs in (top, bottom)], axis=0
-    )
+    base = functools.reduce(jnp.add, [ref[...].astype(jnp.float32) for ref in (mine, up, down)])
     video, audio = [], []
     for i in range(2):
         video.append(gain[0:1] * (acc[i * VBLK : (i + 1) * VBLK] + base[i * BOTH : i * BOTH + VBLK]))
@@ -438,11 +434,11 @@
                 full(own.shape),
                 pl.BlockSpec(w.shape[:-1] + (tile,), lambda i, place: (0, 0, 0, i)),
             ]
-            + [pl.BlockSpec((n * BOTH, tile), lambda i, place: (0, i)) for n in (2, 2, 2, 1, 1)]
+            + [pl.BlockSpec((2 * BOTH, tile), lambda i, place: (0, i))] * 3
             + [pl.BlockSpec((2, tile), lambda i, place: (0, place[4] * 3 + i))],
             out_specs=[out(VBLK), out(ABLK), pl.BlockSpec((BOTH, tile), lambda i, place: (0, i))],
         ),
-        compiler_params=pltpu.CompilerParams(vmem_limit_bytes=24 * MIB),
+        compiler_params=pltpu.CompilerParams(vmem_limit_bytes=60 * MIB),
         cost_estimate=BRIEF,
         name="project_self",
     )(place, own, sibling, w, *base, gains)
@@ -494,26 +490,27 @@
     return lax.all_to_all(value, "tower", split_axis=0, concat_axis=0, tiled=True)
 
 
-def add_later_kernel(up, down, up_later, down_later, _, up_out, down_out):
-    for a, b, out in ((up, up_later, up_out), (down, down_later, down_out)):
+def add_kernel(up, down, up_first, down_first, up_out, down_out):
+    for a, b, out in ((up, up_first, up_out), (down, down_first, down_out)):
         out[...] = (a[...].astype(jnp.float32) + b[...].astype(jnp.float32)).astype(jnp.bfloat16)
 
 
-def add_later(up, down, up_later, down_later, after):
-    rows, width = up_later.shape
+def add_halves(up, down, up_first, down_first):
+    rows, width = up_first.shape
     tile = width // 3
     first = pl.BlockSpec((rows, tile), lambda i: (0, i))
     second = pl.BlockSpec((rows, tile), lambda i: (1, i))
     return pl.pallas_call(
-        add_later_kernel,
-        out_shape=[jax.ShapeDtypeStruct(up_later.shape, up_later.dtype)] * 2,
+        add_kernel,
+        out_shape=[jax.ShapeDtypeStruct(up.shape, up.dtype)] * 2,
         grid=(3,),
-        in_specs=[first, second, first, first, ANY],
-        out_specs=[first, first],
-        compiler_params=pltpu.CompilerParams(vmem_limit_bytes=24 * MIB),
+        in_specs=[first, second, first, first],
+        out_specs=[first, second],
+        input_output_aliases={0: 0, 1: 1},
+        compiler_params=pltpu.CompilerParams(vmem_limit_bytes=60 * MIB),
         cost_estimate=BRIEF,
-        name="add_later",
-    )(up, down, up_later, down_later, after)
+        name="add_halves",
+    )(up, down, up_first, down_first)
 
 
 def shift_tower(value, step):
@@ -553,14 +550,17 @@
     near, far = gate(near, token, *mains[1:], *halos[1:]), gate(far, token)
     crossed = cross(place, margins, query, mains, halos, own, sibling, far)
 
-    rest, up, down, up_later, down_later = project_cross(
+    rest, up, down, up_first, down_first = project_cross(
         place, crossed, swap_core(crossed), w_rest, (token, token)
     )
-    up, down = shift_tower(up, 1), shift_tower(down, -1)
+    up_first, down_first = shift_tower(up_first, 1), shift_tower(down_first, -1)
 
     behind = [crossed]
     after = (rest,)
     for step in range(1, 4):
+        if step == 3:
+            up, down = add_halves(up, down, up_first, down_first)
+            after = (up, down)
         now = [near, far, swap_core(near), swap_core(far)]
         near, far = hop(near), (hop(far) if step < 3 else None)
         acc, top, total, token = flash(query, now, (acc, top, total), False, after)
@@ -570,9 +570,7 @@
         if step < 3:
             far = gate(far, behind[step - 1])
     video_self = flash(query, [near, swap_core(near)], (acc, top, total), True)
-    up_later, down_later = add_later(up, down, up_later, down_later, video_self)
-    up_later, down_later = shift_tower(up_later, 1), shift_tower(down_later, -1)
-    base = (rest, up, down, up_later, down_later)
+    base = (rest, shift_tower(up, 1), shift_tower(down, -1))
 
     self_all = exchange_towers(video_self.reshape(TOWERS, VBLK, GW))
     video_out, audio_out, theirs = project_self(place, self_all, swap_core(self_all), w_self, base, gains)

time: 174 us -> 177 us (1.017)
  blocking collectives: 19.5 us -> 32.3 us
  local copies, waits for them, and re-layouts: 13.8 us -> 8.19 us
  waiting for transfers between devices: 22.6 us -> 18.7 us
  Pallas kernels: 56.3 us -> 60.1 us
  starting transfers between devices: 46.4 us -> 42.6 us
    all_to_all x1 -> x2, blocking collectives: 19.5 us -> 32.3 us  [exchange_towers(): lax.all_to_all(value, 'tower', split_axis=0, concat_axis=0, tiled=True)]
    unnamed x61 -> x57, local copies, waits for them, and re-layouts: 13.1 us -> 7.52 us
    ppermute x4, waiting for transfers between devices: 10.2 us -> 4.63 us  [shift_tower(): lax.ppermute(value, 'tower', [(i, (i + step) % TOWERS) for i in range(TOW...]
    all_to_all x1 -> x0, starting transfers between devices: 3.46 us -> none  [exchange_towers(): lax.all_to_all(value, 'tower', split_axis=0, concat_axis=0, tiled=True)]
    pallas_call x1, Pallas kernels: 4.77 us -> 6.73 us  [project_self(): pl.pallas_call(project_self_kernel, out_shape=[jax.ShapeDtypeStruct((VBLK...]
  transfers between devices with their start and end apart: 31 -> 30, of which waited for: 6 -> 6; matrix products, arithmetic and copies ran while one was open for 0% -> 0% of each run, Pallas kernels for 26% -> 27%
where the time goes in v10:
time: 177 us; the launch traced here: 176 us
  Pallas kernels  60.1 us (34%)
  starting transfers between devices  42.6 us (24%)
  blocking collectives  32.3 us (18%)
  waiting for transfers between devices  18.7 us (11%)
  between operations  14.5 us (8%)
  local copies, waits for them, and re-layouts  8.19 us (5%)
    all_to_all x2, blocking collectives, exchange_towers(): lax.all_to_all(value, 'tower', split_axis=0, concat_axis=0, tiled=True)  32.3 us
    pallas_call x5, Pallas kernels, flash(): pl.pallas_call(functools.partial(flash_kernel, len(kvs), state is None, l...  30.8 us
    ppermute x7, starting transfers between devices, hop(): lax.ppermute(value, 'ctx', [(i, (i + 2 - 4 * (i % 2)) % total) for i in r...  21 us
    ppermute x11, starting transfers between devices, swap_core(): return lax.ppermute(value, 'ctx', [(i, i ^ 1) for i in range(2 * CHIPS)])  8.94 us
    unnamed x57, local copies, waits for them, and re-layouts  7.52 us
    ppermute x7, waiting for transfers between devices, hop(): lax.ppermute(value, 'ctx', [(i, (i + 2 - 4 * (i % 2)) % total) for i in r...  7.18 us
    pallas_call x1, Pallas kernels, cross(): pl.pallas_call(cross_kernel, out_shape=jax.ShapeDtypeStruct((TOWERS, BOTH...  6.79 us
    pallas_call x1, Pallas kernels, project_self(): pl.pallas_call(project_self_kernel, out_shape=[jax.ShapeDtypeStruct((VBLK...  6.73 us
  transfers between devices with their start and end apart: 30, of which 6 were waited for; matrix products, arithmetic and copies ran while one was open for 0% of the time, Pallas kernels for 27%

profile of v10, /device:TPU:1, one launch (start us, length us, event | category | flops | bytes accessed | tf_op | source)
XLA Modules:
  0.0 176.3 jit_solution(13387112397516762440)
XLA Ops:
  7.9 4.3 %pack.1 = (bf16[4,3,3,128,128]{4,3,2,1,0:T(8,128)(2,1)}, bf16[3,32,1536]{2,1,0:T(8,128)(2,1)}, bf16[2,3,32,1536]{3,2,1,0:T(8,128)(2,1)}, bf16[480,384]{1,0:T(8,1...) custom-call(s32[5]{0:T(128)} %stack.23.place, ...), custom_call_target="tpu_custom_call" | custom-call | tf_op jit(solution)/shard_map/pack/pallas_call | solution.py:123
  13.0 19.5 %all_to_all.10.refs_0_.q_ref = bf16[4,3,3,128,128]{4,3,2,1,0:T(8,128)(2,1)S(1)} all-to-all(bf16[4,3,3,128,128]{4,3,2,1,0:T(8,128)(2,1)} %get-tuple-element.40), channel_id=1, replica_groups=mesh['batch'=4,'ctx'=16,'tower'=4] {'tower'}, dimensions={0} | all-to-all | bytes 2359296 | tf_op jit(solution)/shard_map/all_to_all | solution.py:490
  32.5 2.9 %collective-permute-start.1 = (bf16[4,2,3,128,128]{4,3,2,1,0:T(8,128)(2,1)S(1)}, bf16[4,2,3,128,128]{4,3,2,1,0:T(8,128)(2,1)S(1)}, u32[]{:S(2)}, u32[]{:S(2)}) collective-permute-start(bf16[4,2,3,128,128]{4,3,2,1,0:T(8,128)(2,1)S(1)} %slice.4.refs_1_.refs_8_), channel_id=1, source_target_pairs={{0,4},{4,0},{8,12},{12,8},{16,20},{20,16},{24,28},{28,24},{32,36},... | collective-permute-start | bytes 2359304 | tf_op jit(solution)/shard_map/ppermute | solution.py:526
  35.4 5.6 %collective-permute-start = (bf16[4,2,3,128,128]{4,3,2,1,0:T(8,128)(2,1)S(1)}, bf16[4,2,3,128,128]{4,3,2,1,0:T(8,128)(2,1)S(1)}, u32[]{:S(2)}, u32[]{:S(2)}) collective-permute-start(bf16[4,2,3,128,128]{4,3,2,1,0:T(8,128)(2,1)S(1)} %slice.4.refs_1_.refs_8_), channel_id=1, source_target_pairs={{0,8},{4,60},{8,16},{12,4},{16,24},{20,12},{24,32},{28,20},{32,40}... | collective-permute-start | bytes 2359304 | tf_op jit(solution)/shard_map/ppermute | solution.py:522
  41.9 2.5 %collective-permute-start.3 = (bf16[480,384]{1,0:T(8,128)(2,1)}, bf16[480,384]{1,0:T(8,128)(2,1)S(1)}, u32[]{:S(2)}, u32[]{:S(2)}) collective-permute-start(bf16[480,384]{1,0:T(8,128)(2,1)} %gate.14), channel_id=1, source_target_pairs={{0,2},{4,6},{8,10},{12,14},{17,19},{21,23},{25,27},{29,31},{34,32}... | collective-permute-start | bytes 1105928 | tf_op jit(solution)/shard_map/ppermute | solution.py:150
  47.2 4.8 %flash.5 = (f32[512,384]{1,0:T(8,128)}, f32[512,384]{1,0:T(8,128)}, f32[512,384]{1,0:T(8,128)}, f32[8,128]{1,0:T(8,128)}) custom-call(bf16[4,3,3,128,128]{4,3,2,1,0:T(8,128)(2,1)} %copy-done.1, bf16[4,2,3,128,128]{4,3,2,1,0:T(8,128)(2,1)} %copy-done.6, bf16[4,2,3,128,128]{4,3,2,1,0:T(8,128)(2,1)} %copy-done.2), custom_call_target="tpu_custom_call" | custom-call | flops 1 | bytes 1 | tf_op jit(solution)/shard_map/flash/pallas_call | solution.py:231
  55.0 3.2 %collective-permute-done.2.refs_2_.refs_1_ = bf16[480,384]{1,0:T(8,128)(2,1)S(1)} collective-permute-done((bf16[480,384]{1,0:T(8,128)(2,1)}, bf16[480,384]{1,0:T(8,128)(2,1)S(1)}, u32[]{:S(2)}, u32[]{:S(2)}) %collective-permute-start.2) | collective-permute-done | bytes 368672 | tf_op jit(solution)/shard_map/ppermute | solution.py:150
  60.5 5.3 %collective-permute-done.9.refs_0_ = bf16[4,2,3,128,128]{4,3,2,1,0:T(8,128)(2,1)S(1)} collective-permute-done((bf16[4,2,3,128,128]{4,3,2,1,0:T(8,128)(2,1)S(1)}, bf16[4,2,3,128,128]{4,3,2,1,0:T(8,128)(2,1)S(1)}, u32[]{:S(2)}, u32[]{:S(2)}) %collective-permute-start.9) | collective-permute-done | bytes 786464 | tf_op jit(solution)/shard_map/ppermute | solution.py:522
  69.1 6.8 %cross.1.refs_1_.own = bf16[4,160,384]{2,1,0:T(8,128)(2,1)} custom-call(s32[5]{0:T(128)} %stack.23.place, s32[64,3]{1,0:T(8,128)} %bitcast.29, bf16[4,3,3,128,128]{4,3,2,1,0:T(8,128)(2,1)} %copy-done.1, bf16[480,384]{1,0:T(8,128)(2,1)} %get-tuple-element.48.refs_0_, bf16[480,384]{1,0:T(8,128)(2,1)} %copy-done.18, bf16[480,384]{1,0:T(8,128)(2,1)} %copy-done.16, ...), custom_call_target="tpu_custom_call" | custom-call | flops 1 | bytes 1 | tf_op jit(solution)/shard_map/cross/pallas_call | solution.py:319
  76.0 4.7 %collective-permute-start.10 = (bf16[4,2,3,128,128]{4,3,2,1,0:T(8,128)(2,1)}, bf16[4,2,3,128,128]{4,3,2,1,0:T(8,128)(2,1)S(1)}, u32[]{:S(2)}, u32[]{:S(2)}) collective-permute-start(bf16[4,2,3,128,128]{4,3,2,1,0:T(8,128)(2,1)} %gate.21.refs_1_), channel_id=1, source_target_pairs={{0,8},{4,60},{8,16},{12,4},{16,24},{20,12},{24,32},{28,20},{32,40}... | collective-permute-start | bytes 2359304 | tf_op jit(solution)/shard_map/ppermute | solution.py:522
  80.7 1.9 %collective-permute-done.15.refs_0_ = bf16[4,2,3,128,128]{4,3,2,1,0:T(8,128)(2,1)S(1)} collective-permute-done((bf16[4,2,3,128,128]{4,3,2,1,0:T(8,128)(2,1)}, bf16[4,2,3,128,128]{4,3,2,1,0:T(8,128)(2,1)S(1)}, u32[]{:S(2)}, u32[]{:S(2)}) %collective-permute-start.15) | collective-permute-done | bytes 786464 | tf_op jit(solution)/shard_map/ppermute | solution.py:522
  83.5 5.5 %collective-permute-start.19 = (bf16[4,2,3,128,128]{4,3,2,1,0:T(8,128)(2,1)}, bf16[4,2,3,128,128]{4,3,2,1,0:T(8,128)(2,1)S(1)}, u32[]{:S(2)}, u32[]{:S(2)}) collective-permute-start(bf16[4,2,3,128,128]{4,3,2,1,0:T(8,128)(2,1)} %gate.23.refs_2_), channel_id=1, source_target_pairs={{0,8},{4,60},{8,16},{12,4},{16,24},{20,12},{24,32},{28,20},{32,40}... | collective-permute-start | bytes 2359304 | tf_op jit(solution)/shard_map/ppermute | solution.py:522
  89.0 6.7 %project_cross.1 = (bf16[320,1536]{1,0:T(8,128)(2,1)}, bf16[320,1536]{1,0:T(8,128)(2,1)}, bf16[320,1536]{1,0:T(8,128)(2,1)}, bf16[160,1536]{1,0:T(8,128)(2,1)}, bf16[160,1536]{1,0:T(8,128)(2,1)}) custom-call(s32[5]{0:T(128)} %stack.23.place, bf16[4,160,384]{2,1,0:T(8,128)(2,1)} %cross.1.refs_1_.own, bf16[4,160,384]{2,1,0:T(8,128)(2,1)} %collective-permute-done.13.sibling, ...), custom_call_target="tpu_custom_call" | custom-call | flops 1 | bytes 1 | tf_op jit(solution)/shard_map/project_cross/pallas_call | solution.py:371
  96.0 7.0 %flash.6 = (f32[512,384]{1,0:T(8,128)}, f32[512,384]{1,0:T(8,128)}, f32[512,384]{1,0:T(8,128)}, f32[8,128]{1,0:T(8,128)}) custom-call(bf16[4,3,3,128,128]{4,3,2,1,0:T(8,128)(2,1)} %copy-done.1, bf16[4,2,3,128,128]{4,3,2,1,0:T(8,128)(2,1)} %gate.19.refs_1_, bf16[4,2,3,128,128]{4,3,2,1,0:T(8,128)(2,1)} %gate.20.refs_10_.refs_2_, ...), custom_call_target="tpu_custom_call" | custom-call | flops 1 | bytes 1 | tf_op jit(solution)/shard_map/flash/pallas_call | solution.py:231
  105.5 2.7 %collective-permute-start.23 = (bf16[160,1536]{1,0:T(8,128)(2,1)}, bf16[160,1536]{1,0:T(8,128)(2,1)}, u32[]{:S(2)}, u32[]{:S(2)}) collective-permute-start(bf16[160,1536]{1,0:T(8,128)(2,1)} %get-tuple-element.66), channel_id=1, source_target_pairs={{0,3},{1,0},{2,1},{3,2},{4,7},{5,4},{6,5},{7,6},{8,11},{9,8},{10,9... | collective-permute-start | bytes 1474568 | tf_op jit(solution)/shard_map/ppermute | solution.py:517
  108.8 6.9 %flash.7 = (f32[512,384]{1,0:T(8,128)}, f32[512,384]{1,0:T(8,128)}, f32[512,384]{1,0:T(8,128)}, f32[8,128]{1,0:T(8,128)}) custom-call(bf16[4,3,3,128,128]{4,3,2,1,0:T(8,128)(2,1)} %copy-done.1, bf16[4,2,3,128,128]{4,3,2,1,0:T(8,128)(2,1)} %gate.21.refs_1_, bf16[4,2,3,128,128]{4,3,2,1,0:T(8,128)(2,1)} %gate.23.refs_2_, ...), custom_call_target="tpu_custom_call" | custom-call | flops 1 | bytes 1 | tf_op jit(solution)/shard_map/flash/pallas_call | solution.py:231
  116.6 2.1 %collective-permute-start.18 = (bf16[4,2,3,128,128]{4,3,2,1,0:T(8,128)(2,1)}, bf16[4,2,3,128,128]{4,3,2,1,0:T(8,128)(2,1)}, u32[]{:S(2)}, u32[]{:S(2)}) collective-permute-start(bf16[4,2,3,128,128]{4,3,2,1,0:T(8,128)(2,1)} %gate.24.refs_1_), channel_id=1, source_target_pairs={{0,4},{4,0},{8,12},{12,8},{16,20},{20,16},{24,28},{28,24},{32,36},... | collective-permute-start | bytes 2359304 | tf_op jit(solution)/shard_map/ppermute | solution.py:526
  118.7 4.6 %collective-permute-done.22.up_first = bf16[160,1536]{1,0:T(8,128)(2,1)S(1)} collective-permute-done((bf16[160,1536]{1,0:T(8,128)(2,1)}, bf16[160,1536]{1,0:T(8,128)(2,1)S(1)}, u32[]{:S(2)}, u32[]{:S(2)}) %collective-permute-start.22) | collective-permute-done | bytes 491552 | tf_op jit(solution)/shard_map/ppermute | solution.py:517
  124.1 3.4 %add_halves.1 = (bf16[320,1536]{1,0:T(8,128)(2,1)}, bf16[320,1536]{1,0:T(8,128)(2,1)}) custom-call(bf16[320,1536]{1,0:T(8,128)(2,1)} %get-tuple-element.63.up, bf16[320,1536]{1,0:T(8,128)(2,1)} %get-tuple-element.64.down, bf16[160,1536]{1,0:T(8,128)(2,1)} %copy-done.22, ...), custom_call_target="tpu_custom_call", output_to_operand_aliasing={{0}: (0, {}), {1}: (1, {})} | custom-call | flops 1 | bytes 1 | tf_op jit(solution)/shard_map/add_halves/pallas_call | solution.py:503
  127.5 2.7 %collective-permute-start.26 = (bf16[320,1536]{1,0:T(8,128)(2,1)}, bf16[320,1536]{1,0:T(8,128)(2,1)S(1)}, u32[]{:S(2)}, u32[]{:S(2)}) collective-permute-start(bf16[320,1536]{1,0:T(8,128)(2,1)} %get-tuple-element.68.refs_9_), channel_id=1, source_target_pairs={{0,3},{1,0},{2,1},{3,2},{4,7},{5,4},{6,5},{7,6},{8,11},{9,8},{10,9... | collective-permute-start | bytes 2949128 | tf_op jit(solution)/shard_map/ppermute | solution.py:517
  131.1 6.8 %flash.8 = (f32[512,384]{1,0:T(8,128)}, f32[512,384]{1,0:T(8,128)}, f32[512,384]{1,0:T(8,128)}, f32[8,128]{1,0:T(8,128)}) custom-call(bf16[4,3,3,128,128]{4,3,2,1,0:T(8,128)(2,1)} %copy-done.1, bf16[4,2,3,128,128]{4,3,2,1,0:T(8,128)(2,1)} %gate.22.refs_1_, bf16[4,2,3,128,128]{4,3,2,1,0:T(8,128)(2,1)} %gate.25.refs_2_, ...), custom_call_target="tpu_custom_call" | custom-call | flops 1 | bytes 1 | tf_op jit(solution)/shard_map/flash/pallas_call | solution.py:231
  137.9 5.3 %flash.9 = bf16[512,384]{1,0:T(8,128)(2,1)} custom-call(bf16[4,3,3,128,128]{4,3,2,1,0:T(8,128)(2,1)} %copy-done.1, bf16[4,2,3,128,128]{4,3,2,1,0:T(8,128)(2,1)} %gate.24.refs_1_, bf16[4,2,3,128,128]{4,3,2,1,0:T(8,128)(2,1)} %collective-permute-done.18.refs_2_, f32[512,384]{1,0:T(8,128)} %get-tuple-element.69.refs_3_, f32[512,384]{1,0:T(8,128)} %get-tuple-element.70.refs_4_, ...), custom_call_target="tpu_custom_call" | custom-call | flops 1 | bytes 1 | tf_op jit(solution)/shard_map/flash/pallas_call | solution.py:231
  143.2 12.8 %all_to_all.11.own = bf16[4,128,384]{2,1,0:T(8,128)(2,1)S(1)} all-to-all(bf16[4,128,384]{2,1,0:T(8,128)(2,1)} %bitcast.20), channel_id=1, replica_groups=mesh['batch'=4,'ctx'=16,'tower'=4] {'tower'}, dimensions={0} | all-to-all | bytes 786432 | tf_op jit(solution)/shard_map/all_to_all | solution.py:490
  159.4 6.7 %project_self.1 = (bf16[128,3072]{1,0:T(8,128)(2,1)}, bf16[24,3072]{1,0:T(8,128)(2,1)}, bf16[160,1536]{1,0:T(8,128)(2,1)}) custom-call(s32[5]{0:T(128)} %stack.23.place, bf16[4,128,384]{2,1,0:T(8,128)(2,1)} %copy-done.15, bf16[4,128,384]{2,1,0:T(8,128)(2,1)} %copy-done.23, bf16[16,3,32,1536]{3,2,1,0:T(8,128)(2,1)} %bitcast.18, ...), custom_call_target="tpu_custom_call" | custom-call | flops 1 | bytes 1 | tf_op jit(solution)/shard_map/project_self/pallas_call | solution.py:422
  (123 shorter events, 27.4 us)
Async XLA Ops:
  7.2 81.8 %all-gather.5.cloned.1.call-start = ((), (), s32[]{:S(2)}) async-start(), calls=%async_computation.2 | async-start | bytes 2949120 | tf_op jit(solution)/shard_map/all_gather | solution.py:540
  12.2 146.4 %all-gather.7.cloned.1.call-start = ((), (), s32[]{:S(2)}) async-start(), calls=%async_computation.3 | async-start | bytes 5013504 | tf_op jit(solution)/shard_map/all_gather | solution.py:541
  32.5 8.5 %collective-permute-start.1 = (bf16[4,2,3,128,128]{4,3,2,1,0:T(8,128)(2,1)S(1)}, bf16[4,2,3,128,128]{4,3,2,1,0:T(8,128)(2,1)S(1)}, u32[]{:S(2)}, u32[]{:S(2)}) collective-permute-start(bf16[4,2,3,128,128]{4,3,2,1,0:T(8,128)(2,1)S(1)} %slice.4.refs_1_.refs_8_), channel_id=1, source_target_pairs={{0,4},{4,0},{8,12},{12,8},{16,20},{20,16},{24,28},{28,24},{32,36},... | collective-permute-start | bytes 2359304 | tf_op jit(solution)/shard_map/ppermute | solution.py:526
  35.4 17.2 %collective-permute-start = (bf16[4,2,3,128,128]{4,3,2,1,0:T(8,128)(2,1)S(1)}, bf16[4,2,3,128,128]{4,3,2,1,0:T(8,128)(2,1)S(1)}, u32[]{:S(2)}, u32[]{:S(2)}) collective-permute-start(bf16[4,2,3,128,128]{4,3,2,1,0:T(8,128)(2,1)S(1)} %slice.4.refs_1_.refs_8_), channel_id=1, source_target_pairs={{0,8},{4,60},{8,16},{12,4},{16,24},{20,12},{24,32},{28,20},{32,40}... | collective-permute-start | bytes 2359304 | tf_op jit(solution)/shard_map/ppermute | solution.py:522
  41.9 13.0 %collective-permute-start.3 = (bf16[480,384]{1,0:T(8,128)(2,1)}, bf16[480,384]{1,0:T(8,128)(2,1)S(1)}, u32[]{:S(2)}, u32[]{:S(2)}) collective-permute-start(bf16[480,384]{1,0:T(8,128)(2,1)} %gate.14), channel_id=1, source_target_pairs={{0,2},{4,6},{8,10},{12,14},{17,19},{21,23},{25,27},{29,31},{34,32}... | collective-permute-start | bytes 1105928 | tf_op jit(solution)/shard_map/ppermute | solution.py:150
  44.4 10.6 %collective-permute-start.4 = (bf16[480,384]{1,0:T(8,128)(2,1)}, bf16[480,384]{1,0:T(8,128)(2,1)S(1)}, u32[]{:S(2)}, u32[]{:S(2)}) collective-permute-start(bf16[480,384]{1,0:T(8,128)(2,1)} %gate.15), channel_id=1, source_target_pairs={{0,3},{4,7},{8,11},{12,15},{17,16},{21,20},{25,24},{29,28},{34,33}... | collective-permute-start | bytes 1105928 | tf_op jit(solution)/shard_map/ppermute | solution.py:150
  45.8 12.4 %collective-permute-start.2 = (bf16[480,384]{1,0:T(8,128)(2,1)}, bf16[480,384]{1,0:T(8,128)(2,1)S(1)}, u32[]{:S(2)}, u32[]{:S(2)}) collective-permute-start(bf16[480,384]{1,0:T(8,128)(2,1)} %gate.13), channel_id=1, source_target_pairs={{0,1},{4,5},{8,9},{12,13},{17,18},{21,22},{25,26},{29,30},{34,35},... | collective-permute-start | bytes 1105928 | tf_op jit(solution)/shard_map/ppermute | solution.py:150
  54.1 11.7 %collective-permute-start.9 = (bf16[4,2,3,128,128]{4,3,2,1,0:T(8,128)(2,1)S(1)}, bf16[4,2,3,128,128]{4,3,2,1,0:T(8,128)(2,1)S(1)}, u32[]{:S(2)}, u32[]{:S(2)}) collective-permute-start(bf16[4,2,3,128,128]{4,3,2,1,0:T(8,128)(2,1)S(1)} %copy-done.3), channel_id=1, source_target_pairs={{0,8},{4,60},{8,16},{12,4},{16,24},{20,12},{24,32},{28,20},{32,40}... | collective-permute-start | bytes 2359304 | tf_op jit(solution)/shard_map/ppermute | solution.py:522
  58.9 17.0 %collective-permute-start.8 = (bf16[4,2,3,128,128]{4,3,2,1,0:T(8,128)(2,1)}, bf16[4,2,3,128,128]{4,3,2,1,0:T(8,128)(2,1)}, u32[]{:S(2)}, u32[]{:S(2)}) collective-permute-start(bf16[4,2,3,128,128]{4,3,2,1,0:T(8,128)(2,1)} %gate.19.refs_1_), channel_id=1, source_target_pairs={{0,8},{4,60},{8,16},{12,4},{16,24},{20,12},{24,32},{28,20},{32,40}... | collective-permute-start | bytes 2359304 | tf_op jit(solution)/shard_map/ppermute | solution.py:522
  66.8 15.8 %collective-permute-start.15 = (bf16[4,2,3,128,128]{4,3,2,1,0:T(8,128)(2,1)}, bf16[4,2,3,128,128]{4,3,2,1,0:T(8,128)(2,1)S(1)}, u32[]{:S(2)}, u32[]{:S(2)}) collective-permute-start(bf16[4,2,3,128,128]{4,3,2,1,0:T(8,128)(2,1)} %gate.20.refs_10_.refs_2_), channel_id=1, source_target_pairs={{0,8},{4,60},{8,16},{12,4},{16,24},{20,12},{24,32},{28,20},{32,40}... | collective-permute-start | bytes 2359304 | tf_op jit(solution)/shard_map/ppermute | solution.py:522
  68.6 27.1 %collective-permute-start.11 = (bf16[4,2,3,128,128]{4,3,2,1,0:T(8,128)(2,1)S(1)}, bf16[4,2,3,128,128]{4,3,2,1,0:T(8,128)(2,1)}, u32[]{:S(2)}, u32[]{:S(2)}) collective-permute-start(bf16[4,2,3,128,128]{4,3,2,1,0:T(8,128)(2,1)S(1)} %copy-done.11), channel_id=1, source_target_pairs={{0,4},{4,0},{8,12},{12,8},{16,20},{20,16},{24,28},{28,24},{32,36},... | collective-permute-start | bytes 2359304 | tf_op jit(solution)/shard_map/ppermute | solution.py:526
  68.6 27.4 %collective-permute-start.12 = (bf16[4,2,3,128,128]{4,3,2,1,0:T(8,128)(2,1)}, bf16[4,2,3,128,128]{4,3,2,1,0:T(8,128)(2,1)}, u32[]{:S(2)}, u32[]{:S(2)}) collective-permute-start(bf16[4,2,3,128,128]{4,3,2,1,0:T(8,128)(2,1)} %gate.20.refs_10_.refs_2_), channel_id=1, source_target_pairs={{0,4},{4,0},{8,12},{12,8},{16,20},{20,16},{24,28},{28,24},{32,36},... | collective-permute-start | bytes 2359304 | tf_op jit(solution)/shard_map/ppermute | solution.py:526
  76.0 27.1 %collective-permute-start.10 = (bf16[4,2,3,128,128]{4,3,2,1,0:T(8,128)(2,1)}, bf16[4,2,3,128,128]{4,3,2,1,0:T(8,128)(2,1)S(1)}, u32[]{:S(2)}, u32[]{:S(2)}) collective-permute-start(bf16[4,2,3,128,128]{4,3,2,1,0:T(8,128)(2,1)} %gate.21.refs_1_), channel_id=1, source_target_pairs={{0,8},{4,60},{8,16},{12,4},{16,24},{20,12},{24,32},{28,20},{32,40}... | collective-permute-start | bytes 2359304 | tf_op jit(solution)/shard_map/ppermute | solution.py:522
  82.6 25.6 %collective-permute-start.16 = (bf16[4,2,3,128,128]{4,3,2,1,0:T(8,128)(2,1)}, bf16[4,2,3,128,128]{4,3,2,1,0:T(8,128)(2,1)}, u32[]{:S(2)}, u32[]{:S(2)}) collective-permute-start(bf16[4,2,3,128,128]{4,3,2,1,0:T(8,128)(2,1)} %gate.21.refs_1_), channel_id=1, source_target_pairs={{0,4},{4,0},{8,12},{12,8},{16,20},{20,16},{24,28},{28,24},{32,36},... | collective-permute-start | bytes 2359304 | tf_op jit(solution)/shard_map/ppermute | solution.py:526
  83.5 22.0 %collective-permute-start.19 = (bf16[4,2,3,128,128]{4,3,2,1,0:T(8,128)(2,1)}, bf16[4,2,3,128,128]{4,3,2,1,0:T(8,128)(2,1)S(1)}, u32[]{:S(2)}, u32[]{:S(2)}) collective-permute-start(bf16[4,2,3,128,128]{4,3,2,1,0:T(8,128)(2,1)} %gate.23.refs_2_), channel_id=1, source_target_pairs={{0,8},{4,60},{8,16},{12,4},{16,24},{20,12},{24,32},{28,20},{32,40}... | collective-permute-start | bytes 2359304 | tf_op jit(solution)/shard_map/ppermute | solution.py:522
  95.7 12.6 %collective-permute-start.17 = (bf16[4,2,3,128,128]{4,3,2,1,0:T(8,128)(2,1)S(1)}, bf16[4,2,3,128,128]{4,3,2,1,0:T(8,128)(2,1)}, u32[]{:S(2)}, u32[]{:S(2)}) collective-permute-start(bf16[4,2,3,128,128]{4,3,2,1,0:T(8,128)(2,1)S(1)} %copy-done.13), channel_id=1, source_target_pairs={{0,4},{4,0},{8,12},{12,8},{16,20},{20,16},{24,28},{28,24},{32,36},... | collective-permute-start | bytes 2359304 | tf_op jit(solution)/shard_map/ppermute | solution.py:526
  103.9 11.8 %collective-permute-start.14 = (bf16[4,2,3,128,128]{4,3,2,1,0:T(8,128)(2,1)}, bf16[4,2,3,128,128]{4,3,2,1,0:T(8,128)(2,1)S(1)}, u32[]{:S(2)}, u32[]{:S(2)}) collective-permute-start(bf16[4,2,3,128,128]{4,3,2,1,0:T(8,128)(2,1)} %gate.22.refs_1_), channel_id=1, source_target_pairs={{0,8},{4,60},{8,16},{12,4},{16,24},{20,12},{24,32},{28,20},{32,40}... | collective-permute-start | bytes 2359304 | tf_op jit(solution)/shard_map/ppermute | solution.py:522
  105.5 17.8 %collective-permute-start.22 = (bf16[160,1536]{1,0:T(8,128)(2,1)}, bf16[160,1536]{1,0:T(8,128)(2,1)S(1)}, u32[]{:S(2)}, u32[]{:S(2)}) collective-permute-start(bf16[160,1536]{1,0:T(8,128)(2,1)} %get-tuple-element.65), channel_id=1, source_target_pairs={{0,1},{1,2},{2,3},{3,0},{4,5},{5,6},{6,7},{7,4},{8,9},{9,10},{10,1... | collective-permute-start | bytes 1474568 | tf_op jit(solution)/shard_map/ppermute | solution.py:517
  105.5 17.8 %collective-permute-start.23 = (bf16[160,1536]{1,0:T(8,128)(2,1)}, bf16[160,1536]{1,0:T(8,128)(2,1)}, u32[]{:S(2)}, u32[]{:S(2)}) collective-permute-start(bf16[160,1536]{1,0:T(8,128)(2,1)} %get-tuple-element.66), channel_id=1, source_target_pairs={{0,3},{1,0},{2,1},{3,2},{4,7},{5,4},{6,5},{7,6},{8,11},{9,8},{10,9... | collective-permute-start | bytes 1474568 | tf_op jit(solution)/shard_map/ppermute | solution.py:517
  108.2 21.9 %collective-permute-start.20 = (bf16[4,2,3,128,128]{4,3,2,1,0:T(8,128)(2,1)S(1)}, bf16[4,2,3,128,128]{4,3,2,1,0:T(8,128)(2,1)}, u32[]{:S(2)}, u32[]{:S(2)}) collective-permute-start(bf16[4,2,3,128,128]{4,3,2,1,0:T(8,128)(2,1)S(1)} %copy-done.8), channel_id=1, source_target_pairs={{0,4},{4,0},{8,12},{12,8},{16,20},{20,16},{24,28},{28,24},{32,36},... | collective-permute-start | bytes 2359304 | tf_op jit(solution)/shard_map/ppermute | solution.py:526
  108.3 21.8 %collective-permute-start.21 = (bf16[4,2,3,128,128]{4,3,2,1,0:T(8,128)(2,1)}, bf16[4,2,3,128,128]{4,3,2,1,0:T(8,128)(2,1)S(1)}, u32[]{:S(2)}, u32[]{:S(2)}) collective-permute-start(bf16[4,2,3,128,128]{4,3,2,1,0:T(8,128)(2,1)} %gate.25.refs_2_), channel_id=1, source_target_pairs={{0,4},{4,0},{8,12},{12,8},{16,20},{20,16},{24,28},{28,24},{32,36},... | collective-permute-start | bytes 2359304 | tf_op jit(solution)/shard_map/ppermute | solution.py:526
  116.6 21.3 %collective-permute-start.18 = (bf16[4,2,3,128,128]{4,3,2,1,0:T(8,128)(2,1)}, bf16[4,2,3,128,128]{4,3,2,1,0:T(8,128)(2,1)}, u32[]{:S(2)}, u32[]{:S(2)}) collective-permute-start(bf16[4,2,3,128,128]{4,3,2,1,0:T(8,128)(2,1)} %gate.24.refs_1_), channel_id=1, source_target_pairs={{0,4},{4,0},{8,12},{12,8},{16,20},{20,16},{24,28},{28,24},{32,36},... | collective-permute-start | bytes 2359304 | tf_op jit(solution)/shard_map/ppermute | solution.py:526
  127.5 29.8 %collective-permute-start.25 = (bf16[320,1536]{1,0:T(8,128)(2,1)}, bf16[320,1536]{1,0:T(8,128)(2,1)S(1)}, u32[]{:S(2)}, u32[]{:S(2)}) collective-permute-start(bf16[320,1536]{1,0:T(8,128)(2,1)} %get-tuple-element.67.refs_8_), channel_id=1, source_target_pairs={{0,1},{1,2},{2,3},{3,0},{4,5},{5,6},{6,7},{7,4},{8,9},{9,10},{10,1... | collective-permute-start | bytes 2949128 | tf_op jit(solution)/shard_map/ppermute | solution.py:517
  127.5 29.8 %collective-permute-start.26 = (bf16[320,1536]{1,0:T(8,128)(2,1)}, bf16[320,1536]{1,0:T(8,128)(2,1)S(1)}, u32[]{:S(2)}, u32[]{:S(2)}) collective-permute-start(bf16[320,1536]{1,0:T(8,128)(2,1)} %get-tuple-element.68.refs_9_), channel_id=1, source_target_pairs={{0,3},{1,0},{2,1},{3,2},{4,7},{5,4},{6,5},{7,6},{8,11},{9,8},{10,9... | collective-permute-start | bytes 2949128 | tf_op jit(solution)/shard_map/ppermute | solution.py:517
  (34 other events, 127.3 us)
Sparse Core Ops, SparseCore 0:
  12.4 39.3 all-gather.4
  54.2 62.5 all-gather.6

commit v11 on v10

--- a/solution.py
+++ b/solution.py
@@ -173,7 +173,7 @@
 
 def flash_kernel(kv_count, first, last, after, *refs):
     q_ref = refs[0]
-    kv_refs = refs[1 : 1 + kv_count]
+    kv_refs = [ref.at[i] for ref in refs[1 : 1 + kv_count] for i in range(ref.shape[0])]
     rest = refs[1 + kv_count :]
     rest = rest[: len(rest) - (1 if last else 4) - after] + rest[len(rest) - (1 if last else 4) :]
     if first:
@@ -214,7 +214,14 @@
 
 
 QUERY = pl.BlockSpec((TOWERS, 1, 1, VBLK, HD), lambda h, *_: (0, 2, h, 0, 0))
-SHARD = pl.BlockSpec((TOWERS, 2, 1, VBLK, HD), lambda h, *_: (0, 0, h, 0, 0))
+
+
+def shards_spec(count):
+    return pl.BlockSpec((count, TOWERS, 2, 1, VBLK, HD), lambda h, *_: (0, 0, 0, h, 0, 0))
+
+
+def shard_spec(which):
+    return pl.BlockSpec((None, TOWERS, 2, 1, VBLK, HD), lambda h, *_: (which, 0, 0, h, 0, 0))
 
 
 def flash(query, kvs, state, last, after=()):
@@ -232,7 +239,7 @@
         functools.partial(flash_kernel, len(kvs), state is None, last, len(after)),
         out_shape=out_shape,
         grid=(LOCAL,),
-        in_specs=[QUERY] + [SHARD] * len(kvs) + ([] if state is None else [head] * 3) + [ANY] * len(after),
+        in_specs=[QUERY] + [shards_spec(kv.shape[0]) for kv in kvs] + ([] if state is None else [head] * 3) + [ANY] * len(after),
         out_specs=out_specs,
         compiler_params=pltpu.CompilerParams(vmem_limit_bytes=60 * MIB),
         cost_estimate=BRIEF,
@@ -314,7 +321,7 @@
         out[r, pl.ds(VBLK, AUDIO_ROWS), :] = padded.astype(jnp.bfloat16)
 
 
-def cross(place, margin, query, mains, halos, own, sibling, third):
+def cross(place, margin, query, mains, halos, here, behind):
     rows = TOWERS * VBLK
     return pl.pallas_call(
         cross_kernel,
@@ -327,13 +334,13 @@
             ]
             + [pl.BlockSpec((HAT, HD), lambda h, *_: (0, h))] * TOWERS
             + [pl.BlockSpec((2 * HALO, HD), lambda h, *_: (0, h))] * TOWERS
-            + [SHARD] * 3,
+            + [shard_spec(0), shard_spec(1), shard_spec(1)],
             out_specs=pl.BlockSpec((TOWERS, BOTH, HD), lambda h, *_: (0, 0, h)),
         ),
         compiler_params=pltpu.CompilerParams(vmem_limit_bytes=60 * MIB),
         cost_estimate=BRIEF,
         name="cross",
-    )(place, margin, query, *mains, *halos, own, sibling, third)
+    )(place, margin, query, *mains, *halos, here, here, behind)
 
 
 def weight_rows(pieces):
@@ -542,14 +549,14 @@
     query = exchange_towers(parts)
     own = query[:, :2]
     sibling = swap_core(own)
-    near, far = hop(own), hop(sibling)
+    here = jnp.stack([own, sibling])
+    ahead = hop(here)
     mains = [audio[0]] + [send_main(gate(audio[step], sibling), step) for step in (1, 2, 3)]
 
-    acc, top, total, token = flash(query, [own, sibling], None, False)
+    acc, top, total, token = flash(query, [here], None, False)
     halos = [audio[4]] + [send_halo(gate(audio[4 + step], token), step) for step in (1, 2, 3)]
-    near, far = gate(near, token, *mains[1:], *halos[1:]), gate(far, token)
-    crossed = cross(place, margins, query, mains, halos, own, sibling, far)
-
+    ahead = gate(ahead, token, *mains[1:], *halos[1:])
+    crossed = cross(place, margins, query, mains, halos, here, ahead)
     rest, up, down, up_first, down_first = project_cross(
         place, crossed, swap_core(crossed), w_rest, (token, token)
     )
@@ -558,18 +565,14 @@
     behind = [crossed]
     after = (rest,)
     for step in range(1, 4):
-        if step == 3:
-            up, down = add_halves(up, down, up_first, down_first)
-            after = (up, down)
-        now = [near, far, swap_core(near), swap_core(far)]
-        near, far = hop(near), (hop(far) if step < 3 else None)
+        now = [ahead, swap_core(ahead)]
+        ahead = hop(ahead if step < 3 else ahead[:1])
         acc, top, total, token = flash(query, now, (acc, top, total), False, after)
         behind.append(token)
         after = ()
-        near = gate(near, behind[step - 1])
-        if step < 3:
-            far = gate(far, behind[step - 1])
-    video_self = flash(query, [near, swap_core(near)], (acc, top, total), True)
+        ahead = gate(ahead, behind[step - 1])
+    up, down = add_halves(gate(up, token), down, up_first, down_first)
+    video_self = flash(query, [ahead, swap_core(ahead)], (acc, top, total), True, (up, down))
     base = (rest, shift_tower(up, 1), shift_tower(down, -1))
 
     self_all = exchange_towers(video_self.reshape(TOWERS, VBLK, GW))

time: 177 us -> 194 us (1.096)
  waiting for transfers between devices: 18.7 us -> 47.8 us
  blocking collectives: 32.3 us -> 18.7 us
  local copies, waits for them, and re-layouts: 8.19 us -> 11.2 us
    all_to_all x0 -> x1, waiting for transfers between devices: none -> 13.9 us  [exchange_towers(): lax.all_to_all(value, 'tower', split_axis=0, concat_axis=0, tiled=True)]
    all_to_all x2 -> x1, blocking collectives: 32.3 us -> 18.7 us  [exchange_towers(): lax.all_to_all(value, 'tower', split_axis=0, concat_axis=0, tiled=True)]
    ppermute x7 -> x4, waiting for transfers between devices: 7.18 us -> 16.1 us  [hop(): lax.ppermute(value, 'ctx', [(i, (i + 2 - 4 * (i % 2)) % total) for i in r...]
    ppermute x7 -> x4, starting transfers between devices: 21 us -> 12.2 us  [hop(): lax.ppermute(value, 'ctx', [(i, (i + 2 - 4 * (i % 2)) % total) for i in r...]
    all_to_all x0 -> x1, starting transfers between devices: none -> 4.87 us  [exchange_towers(): lax.all_to_all(value, 'tower', split_axis=0, concat_axis=0, tiled=True)]
    ppermute x11 -> x8, waiting for transfers between devices: 3.05 us -> 7.34 us  [swap_core(): return lax.ppermute(value, 'ctx', [(i, i ^ 1) for i in range(2 * CHIPS)])]
    ppermute x11 -> x8, starting transfers between devices: 8.94 us -> 11.9 us  [swap_core(): return lax.ppermute(value, 'ctx', [(i, i ^ 1) for i in range(2 * CHIPS)])]
    unnamed x57 -> x47, local copies, waits for them, and re-layouts: 7.52 us -> 9.1 us
  transfers between devices with their start and end apart: 30 -> 25, of which waited for: 6 -> 12; matrix products, arithmetic and copies ran while one was open for 0% -> 1% of each run, Pallas kernels for 27% -> 24%
where the time goes in v11:
time: 194 us; the launch traced here: 193 us
  Pallas kernels  59.6 us (31%)
  waiting for transfers between devices  47.8 us (25%)
  starting transfers between devices  41.1 us (21%)
  blocking collectives  18.7 us (10%)
  between operations  14.4 us (7%)
  local copies, waits for them, and re-layouts  11.2 us (6%)
    pallas_call x5, Pallas kernels, flash(): pl.pallas_call(functools.partial(flash_kernel, len(kvs), state is None, l...  30.6 us
    all_to_all x1, blocking collectives, exchange_towers(): lax.all_to_all(value, 'tower', split_axis=0, concat_axis=0, tiled=True)  18.7 us
    ppermute x4, waiting for transfers between devices, hop(): lax.ppermute(value, 'ctx', [(i, (i + 2 - 4 * (i % 2)) % total) for i in r...  16.1 us
    all_to_all x1, waiting for transfers between devices, exchange_towers(): lax.all_to_all(value, 'tower', split_axis=0, concat_axis=0, tiled=True)  13.9 us
    ppermute x4, starting transfers between devices, hop(): lax.ppermute(value, 'ctx', [(i, (i + 2 - 4 * (i % 2)) % total) for i in r...  12.2 us
    ppermute x8, starting transfers between devices, swap_core(): return lax.ppermute(value, 'ctx', [(i, i ^ 1) for i in range(2 * CHIPS)])  11.9 us
    unnamed x47, local copies, waits for them, and re-layouts  9.1 us
    ppermute x8, waiting for transfers between devices, swap_core(): return lax.ppermute(value, 'ctx', [(i, i ^ 1) for i in range(2 * CHIPS)])  7.34 us
  transfers between devices with their start and end apart: 25, of which 12 were waited for; matrix products, arithmetic and copies ran while one was open for 1% of the time, Pallas kernels for 24%

profile of v11, /device:TPU:1, one launch (start us, length us, event | category | flops | bytes accessed | tf_op | source)
XLA Modules:
  0.0 192.9 jit_solution(15300444400194853828)
XLA Ops:
  7.9 4.3 %pack.1 = (bf16[4,3,3,128,128]{4,3,2,1,0:T(8,128)(2,1)}, bf16[3,32,1536]{2,1,0:T(8,128)(2,1)}, bf16[2,3,32,1536]{3,2,1,0:T(8,128)(2,1)}, bf16[480,384]{1,0:T(8,1...) custom-call(s32[5]{0:T(128)} %stack.32.place, ...), custom_call_target="tpu_custom_call" | custom-call | tf_op jit(solution)/shard_map/pack/pallas_call | solution.py:123
  12.3 4.9 %all-to-all-start = ((bf16[4,3,3,128,128]{4,3,2,1,0:T(8,128)(2,1)}), bf16[4,3,3,128,128]{4,3,2,1,0:T(8,128)(2,1)S(1)}, u32[]{:S(2)}, u32[]{:S(2)}) async-start(bf16[4,3,3,128,128]{4,3,2,1,0:T(8,128)(2,1)} %get-tuple-element.41), calls=%async_computation | async-start | bytes 2359296 | tf_op jit(solution)/shard_map/all_to_all | solution.py:497
  17.9 13.9 %all-to-all-done.refs_0_.q_ref = bf16[4,3,3,128,128]{4,3,2,1,0:T(8,128)(2,1)S(1)} async-done(((bf16[4,3,3,128,128]{4,3,2,1,0:T(8,128)(2,1)}), bf16[4,3,3,128,128]{4,3,2,1,0:T(8,128)(2,1)S(1)}, u32[]{:S(2)}, u32[]{:S(2)}) %all-to-all-start) | async-done | bytes 1179680 | tf_op jit(solution)/shard_map/all_to_all | solution.py:497
  32.0 2.9 %collective-permute-start = (bf16[4,2,3,128,128]{4,3,2,1,0:T(8,128)(2,1)S(1)}, bf16[4,2,3,128,128]{4,3,2,1,0:T(8,128)(2,1)S(1)}, u32[]{:S(2)}, u32[]{:S(2)}) collective-permute-start(bf16[4,2,3,128,128]{4,3,2,1,0:T(8,128)(2,1)S(1)} %get-tuple-element.81), channel_id=1, source_target_pairs={{0,4},{4,0},{8,12},{12,8},{16,20},{20,16},{24,28},{28,24},{32,36},... | collective-permute-start | bytes 2359304 | tf_op jit(solution)/shard_map/ppermute | solution.py:533
  37.7 5.6 %collective-permute-start.1 = (bf16[2,4,2,3,128,128]{5,4,3,2,1,0:T(8,128)(2,1)S(1)}, bf16[2,4,2,3,128,128]{5,4,3,2,1,0:T(8,128)(2,1)}, u32[]{:S(2)}, u32[]{:S(2)}) collective-permute-start(bf16[2,4,2,3,128,128]{5,4,3,2,1,0:T(8,128)(2,1)S(1)} %pad_maximum_fusion.refs_1_.refs_8_.refs_9_), channel_id=1, source_target_pairs={{0,8},{4,60},{8,16},{12,4},{16,24},{20,12},{24,32},{28,20},{32,40}... | collective-permute-start | bytes 4718600 | tf_op jit(solution)/shard_map/ppermute | solution.py:529
  48.1 4.7 %flash.5 = (f32[512,384]{1,0:T(8,128)}, f32[512,384]{1,0:T(8,128)}, f32[512,384]{1,0:T(8,128)}, f32[8,128]{1,0:T(8,128)}) custom-call(bf16[4,3,3,128,128]{4,3,2,1,0:T(8,128)(2,1)} %copy-done.1, bf16[2,4,2,3,128,128]{5,4,3,2,1,0:T(8,128)(2,1)} %copy-done.2), custom_call_target="tpu_custom_call" | custom-call | flops 1 | bytes 1 | tf_op jit(solution)/shard_map/flash/pallas_call | solution.py:238
  55.0 4.2 %collective-permute-done.3.refs_3_.refs_2_ = bf16[480,384]{1,0:T(8,128)(2,1)S(1)} collective-permute-done((bf16[480,384]{1,0:T(8,128)(2,1)}, bf16[480,384]{1,0:T(8,128)(2,1)S(1)}, u32[]{:S(2)}, u32[]{:S(2)}) %collective-permute-start.3) | collective-permute-done | bytes 368672 | tf_op jit(solution)/shard_map/ppermute | solution.py:150
  60.7 3.3 %collective-permute-start.8 = (bf16[2,4,2,3,128,128]{5,4,3,2,1,0:T(8,128)(2,1)}, bf16[2,4,2,3,128,128]{5,4,3,2,1,0:T(8,128)(2,1)S(1)}, u32[]{:S(2)}, u32[]{:S(2)}) collective-permute-start(bf16[2,4,2,3,128,128]{5,4,3,2,1,0:T(8,128)(2,1)} %gate.17.refs_10_.refs_1_), channel_id=1, source_target_pairs={{0,8},{4,60},{8,16},{12,4},{16,24},{20,12},{24,32},{28,20},{32,40}... | collective-permute-start | bytes 4718600 | tf_op jit(solution)/shard_map/ppermute | solution.py:529
  64.7 6.8 %cross.1.refs_1_.own = bf16[4,160,384]{2,1,0:T(8,128)(2,1)} custom-call(s32[5]{0:T(128)} %stack.32.place, s32[64,3]{1,0:T(8,128)} %bitcast.33, bf16[4,3,3,128,128]{4,3,2,1,0:T(8,128)(2,1)} %copy-done.1, bf16[480,384]{1,0:T(8,128)(2,1)} %get-tuple-element.49.refs_0_, bf16[480,384]{1,0:T(8,128)(2,1)} %copy-done.9, bf16[480,384]{1,0:T(8,128)(2,1)} %copy-done.10, ...), custom_call_target="tpu_custom_call" | custom-call | flops 1 | bytes 1 | tf_op jit(solution)/shard_map/cross/pallas_call | solution.py:326
  71.5 10.1 %collective-permute-done.8.refs_0_ = bf16[2,4,2,3,128,128]{5,4,3,2,1,0:T(8,128)(2,1)S(1)} collective-permute-done((bf16[2,4,2,3,128,128]{5,4,3,2,1,0:T(8,128)(2,1)}, bf16[2,4,2,3,128,128]{5,4,3,2,1,0:T(8,128)(2,1)S(1)}, u32[]{:S(2)}, u32[]{:S(2)}) %collective-permute-start.8) | collective-permute-done | bytes 1572896 | tf_op jit(solution)/shard_map/ppermute | solution.py:529
  82.8 3.0 %collective-permute-start.9 = (bf16[2,4,2,3,128,128]{5,4,3,2,1,0:T(8,128)(2,1)}, bf16[2,4,2,3,128,128]{5,4,3,2,1,0:T(8,128)(2,1)S(1)}, u32[]{:S(2)}, u32[]{:S(2)}) collective-permute-start(bf16[2,4,2,3,128,128]{5,4,3,2,1,0:T(8,128)(2,1)} %gate.18.refs_1_), channel_id=1, source_target_pairs={{0,8},{4,60},{8,16},{12,4},{16,24},{20,12},{24,32},{28,20},{32,40}... | collective-permute-start | bytes 4718600 | tf_op jit(solution)/shard_map/ppermute | solution.py:529
  86.3 2.4 %collective-permute-done.11.sibling = bf16[4,160,384]{2,1,0:T(8,128)(2,1)} collective-permute-done((bf16[4,160,384]{2,1,0:T(8,128)(2,1)}, bf16[4,160,384]{2,1,0:T(8,128)(2,1)}, u32[]{:S(2)}, u32[]{:S(2)}) %collective-permute-start.11) | collective-permute-done | bytes 491552 | tf_op jit(solution)/shard_map/ppermute | solution.py:533
  88.7 6.4 %project_cross.1 = (bf16[320,1536]{1,0:T(8,128)(2,1)}, bf16[320,1536]{1,0:T(8,128)(2,1)}, bf16[320,1536]{1,0:T(8,128)(2,1)}, bf16[160,1536]{1,0:T(8,128)(2,1)}, bf16[160,1536]{1,0:T(8,128)(2,1)}) custom-call(s32[5]{0:T(128)} %stack.32.place, bf16[4,160,384]{2,1,0:T(8,128)(2,1)} %cross.1.refs_1_.own, bf16[4,160,384]{2,1,0:T(8,128)(2,1)} %collective-permute-done.11.sibling, ...), custom_call_target="tpu_custom_call" | custom-call | flops 1 | bytes 1 | tf_op jit(solution)/shard_map/project_cross/pallas_call | solution.py:378
  95.1 6.9 %flash.6 = (f32[512,384]{1,0:T(8,128)}, f32[512,384]{1,0:T(8,128)}, f32[512,384]{1,0:T(8,128)}, f32[8,128]{1,0:T(8,128)}) custom-call(bf16[4,3,3,128,128]{4,3,2,1,0:T(8,128)(2,1)} %copy-done.1, bf16[2,4,2,3,128,128]{5,4,3,2,1,0:T(8,128)(2,1)} %gate.17.refs_10_.refs_1_, bf16[2,4,2,3,128,128]{5,4,3,2,1,0:T(8,128)(2,1)} %collective-permute-done.10.refs_2_, ...), custom_call_target="tpu_custom_call" | custom-call | flops 1 | bytes 1 | tf_op jit(solution)/shard_map/flash/pallas_call | solution.py:238
  104.7 3.9 %collective-permute-start.15 = (bf16[2,4,2,3,128,128]{5,4,3,2,1,0:T(8,128)(2,1)}, bf16[2,4,2,3,128,128]{5,4,3,2,1,0:T(8,128)(2,1)}, u32[]{:S(2)}, u32[]{:S(2)}) collective-permute-start(bf16[2,4,2,3,128,128]{5,4,3,2,1,0:T(8,128)(2,1)} %gate.19.refs_1_), channel_id=1, source_target_pairs={{0,4},{4,0},{8,12},{12,8},{16,20},{20,16},{24,28},{28,24},{32,36},... | collective-permute-start | bytes 4718600 | tf_op jit(solution)/shard_map/ppermute | solution.py:533
  111.3 6.8 %flash.7 = (f32[512,384]{1,0:T(8,128)}, f32[512,384]{1,0:T(8,128)}, f32[512,384]{1,0:T(8,128)}, f32[8,128]{1,0:T(8,128)}) custom-call(bf16[4,3,3,128,128]{4,3,2,1,0:T(8,128)(2,1)} %copy-done.1, bf16[2,4,2,3,128,128]{5,4,3,2,1,0:T(8,128)(2,1)} %gate.18.refs_1_, bf16[2,4,2,3,128,128]{5,4,3,2,1,0:T(8,128)(2,1)} %copy-done.8, ...), custom_call_target="tpu_custom_call" | custom-call | flops 1 | bytes 1 | tf_op jit(solution)/shard_map/flash/pallas_call | solution.py:238
  118.1 3.0 %collective-permute-done.12.refs_0_ = bf16[1,4,2,3,128,128]{5,4,3,2,1,0:T(8,128)(2,1)S(1)} collective-permute-done((bf16[1,4,2,3,128,128]{5,4,3,2,1,0:T(8,128)(2,1)S(1)}, bf16[1,4,2,3,128,128]{5,4,3,2,1,0:T(8,128)(2,1)S(1)}, u32[]{:S(2)}, u32[]{:S(2)}) %collective-permute-start.12) | collective-permute-done | bytes 786464 | tf_op jit(solution)/shard_map/ppermute | solution.py:529
  124.4 2.4 %collective-permute-start.17 = (bf16[160,1536]{1,0:T(8,128)(2,1)S(1)}, bf16[160,1536]{1,0:T(8,128)(2,1)S(1)}, u32[]{:S(2)}, u32[]{:S(2)}) collective-permute-start(bf16[160,1536]{1,0:T(8,128)(2,1)S(1)} %copy-done.22), channel_id=1, source_target_pairs={{0,3},{1,0},{2,1},{3,2},{4,7},{5,4},{6,5},{7,6},{8,11},{9,8},{10,9... | collective-permute-start | bytes 1474568 | tf_op jit(solution)/shard_map/ppermute | solution.py:524
  126.8 6.8 %flash.8 = (f32[512,384]{1,0:T(8,128)}, f32[512,384]{1,0:T(8,128)}, f32[512,384]{1,0:T(8,128)}, f32[8,128]{1,0:T(8,128)}) custom-call(bf16[4,3,3,128,128]{4,3,2,1,0:T(8,128)(2,1)} %copy-done.1, bf16[2,4,2,3,128,128]{5,4,3,2,1,0:T(8,128)(2,1)} %gate.19.refs_1_, bf16[2,4,2,3,128,128]{5,4,3,2,1,0:T(8,128)(2,1)} %collective-permute-done.15.refs_2_, ...), custom_call_target="tpu_custom_call" | custom-call | flops 1 | bytes 1 | tf_op jit(solution)/shard_map/flash/pallas_call | solution.py:238
  133.6 4.7 %collective-permute-done.16.up_first = bf16[160,1536]{1,0:T(8,128)(2,1)S(1)} collective-permute-done((bf16[160,1536]{1,0:T(8,128)(2,1)}, bf16[160,1536]{1,0:T(8,128)(2,1)S(1)}, u32[]{:S(2)}, u32[]{:S(2)}) %collective-permute-start.16) | collective-permute-done | bytes 491552 | tf_op jit(solution)/shard_map/ppermute | solution.py:524
  140.0 3.4 %add_halves.1 = (bf16[320,1536]{1,0:T(8,128)(2,1)}, bf16[320,1536]{1,0:T(8,128)(2,1)}) custom-call(bf16[320,1536]{1,0:T(8,128)(2,1)} %gate.21.up, bf16[320,1536]{1,0:T(8,128)(2,1)} %get-tuple-element.69.down, bf16[160,1536]{1,0:T(8,128)(2,1)} %copy-done.15, bf16[160,1536]{1,0:T(8,128)(2,1)} %copy-done.16), custom_call_target="tpu_custom_call", output_to_operand_aliasing={{0}: (0, {}), {1}: (1, {})} | custom-call | flops 1 | bytes 1 | tf_op jit(solution)/shard_map/add_halves/pallas_call | solution.py:510
  147.0 5.3 %flash.9 = bf16[512,384]{1,0:T(8,128)(2,1)} custom-call(bf16[4,3,3,128,128]{4,3,2,1,0:T(8,128)(2,1)} %copy-done.1, bf16[1,4,2,3,128,128]{5,4,3,2,1,0:T(8,128)(2,1)} %gate.20.refs_1_, bf16[1,4,2,3,128,128]{5,4,3,2,1,0:T(8,128)(2,1)} %copy-done.14, f32[512,384]{1,0:T(8,128)} %get-tuple-element.64.refs_3_, f32[512,384]{1,0:T(8,128)} %get-tuple-element.65.refs_4_, ...), custom_call_target="tpu_custom_call" | custom-call | flops 1 | bytes 1 | tf_op jit(solution)/shard_map/flash/pallas_call | solution.py:238
  152.3 18.7 %all_to_all.10.own = bf16[4,128,384]{2,1,0:T(8,128)(2,1)S(1)} all-to-all(bf16[4,128,384]{2,1,0:T(8,128)(2,1)} %bitcast.24), channel_id=1, replica_groups=mesh['batch'=4,'ctx'=16,'tower'=4] {'tower'}, dimensions={0} | all-to-all | bytes 786432 | tf_op jit(solution)/shard_map/all_to_all | solution.py:497
  176.0 6.7 %project_self.1 = (bf16[128,3072]{1,0:T(8,128)(2,1)}, bf16[24,3072]{1,0:T(8,128)(2,1)}, bf16[160,1536]{1,0:T(8,128)(2,1)}) custom-call(s32[5]{0:T(128)} %stack.32.place, bf16[4,128,384]{2,1,0:T(8,128)(2,1)} %copy-done.7, bf16[4,128,384]{2,1,0:T(8,128)(2,1)} %copy-done.17, bf16[16,3,32,1536]{3,2,1,0:T(8,128)(2,1)} %bitcast.22, ...), custom_call_target="tpu_custom_call" | custom-call | flops 1 | bytes 1 | tf_op jit(solution)/shard_map/project_self/pallas_call | solution.py:429
  (102 shorter events, 37.3 us)
Async XLA Ops:
  7.2 79.2 %all-gather.5.cloned.1.call-start = ((), (), s32[]{:S(2)}) async-start(), calls=%async_computation.2 | async-start | bytes 2949120 | tf_op jit(solution)/shard_map/all_gather | solution.py:547
  12.3 19.5 %all-to-all-start = ((bf16[4,3,3,128,128]{4,3,2,1,0:T(8,128)(2,1)}), bf16[4,3,3,128,128]{4,3,2,1,0:T(8,128)(2,1)S(1)}, u32[]{:S(2)}, u32[]{:S(2)}) async-start(bf16[4,3,3,128,128]{4,3,2,1,0:T(8,128)(2,1)} %get-tuple-element.41), calls=%async_computation | async-start | bytes 2359296 | tf_op jit(solution)/shard_map/all_to_all | solution.py:497
  17.2 157.4 %all-gather.7.cloned.1.call-start = ((), (), s32[]{:S(2)}) async-start(), calls=%async_computation.3 | async-start | bytes 5013504 | tf_op jit(solution)/shard_map/all_gather | solution.py:548
  32.0 4.8 %collective-permute-start = (bf16[4,2,3,128,128]{4,3,2,1,0:T(8,128)(2,1)S(1)}, bf16[4,2,3,128,128]{4,3,2,1,0:T(8,128)(2,1)S(1)}, u32[]{:S(2)}, u32[]{:S(2)}) collective-permute-start(bf16[4,2,3,128,128]{4,3,2,1,0:T(8,128)(2,1)S(1)} %get-tuple-element.81), channel_id=1, source_target_pairs={{0,4},{4,0},{8,12},{12,8},{16,20},{20,16},{24,28},{28,24},{32,36},... | collective-permute-start | bytes 2359304 | tf_op jit(solution)/shard_map/ppermute | solution.py:533
  37.7 22.9 %collective-permute-start.1 = (bf16[2,4,2,3,128,128]{5,4,3,2,1,0:T(8,128)(2,1)S(1)}, bf16[2,4,2,3,128,128]{5,4,3,2,1,0:T(8,128)(2,1)}, u32[]{:S(2)}, u32[]{:S(2)}) collective-permute-start(bf16[2,4,2,3,128,128]{5,4,3,2,1,0:T(8,128)(2,1)S(1)} %pad_maximum_fusion.refs_1_.refs_8_.refs_9_), channel_id=1, source_target_pairs={{0,8},{4,60},{8,16},{12,4},{16,24},{20,12},{24,32},{28,20},{32,40}... | collective-permute-start | bytes 4718600 | tf_op jit(solution)/shard_map/ppermute | solution.py:529
  43.3 11.7 %collective-permute-start.2 = (bf16[480,384]{1,0:T(8,128)(2,1)}, bf16[480,384]{1,0:T(8,128)(2,1)S(1)}, u32[]{:S(2)}, u32[]{:S(2)}) collective-permute-start(bf16[480,384]{1,0:T(8,128)(2,1)} %gate.11), channel_id=1, source_target_pairs={{0,1},{4,5},{8,9},{12,13},{17,18},{21,22},{25,26},{29,30},{34,35},... | collective-permute-start | bytes 1105928 | tf_op jit(solution)/shard_map/ppermute | solution.py:150
  45.5 13.7 %collective-permute-start.3 = (bf16[480,384]{1,0:T(8,128)(2,1)}, bf16[480,384]{1,0:T(8,128)(2,1)S(1)}, u32[]{:S(2)}, u32[]{:S(2)}) collective-permute-start(bf16[480,384]{1,0:T(8,128)(2,1)} %gate.12), channel_id=1, source_target_pairs={{0,2},{4,6},{8,10},{12,14},{17,19},{21,23},{25,27},{29,31},{34,32}... | collective-permute-start | bytes 1105928 | tf_op jit(solution)/shard_map/ppermute | solution.py:150
  46.8 12.4 %collective-permute-start.4 = (bf16[480,384]{1,0:T(8,128)(2,1)}, bf16[480,384]{1,0:T(8,128)(2,1)S(1)}, u32[]{:S(2)}, u32[]{:S(2)}) collective-permute-start(bf16[480,384]{1,0:T(8,128)(2,1)} %gate.13), channel_id=1, source_target_pairs={{0,3},{4,7},{8,11},{12,15},{17,16},{21,20},{25,24},{29,28},{34,33}... | collective-permute-start | bytes 1105928 | tf_op jit(solution)/shard_map/ppermute | solution.py:150
  53.6 0.7 collective-permute-start.6
  54.3 0.7 collective-permute-start.5
  60.7 21.0 %collective-permute-start.8 = (bf16[2,4,2,3,128,128]{5,4,3,2,1,0:T(8,128)(2,1)}, bf16[2,4,2,3,128,128]{5,4,3,2,1,0:T(8,128)(2,1)S(1)}, u32[]{:S(2)}, u32[]{:S(2)}) collective-permute-start(bf16[2,4,2,3,128,128]{5,4,3,2,1,0:T(8,128)(2,1)} %gate.17.refs_10_.refs_1_), channel_id=1, source_target_pairs={{0,8},{4,60},{8,16},{12,4},{16,24},{20,12},{24,32},{28,20},{32,40}... | collective-permute-start | bytes 4718600 | tf_op jit(solution)/shard_map/ppermute | solution.py:529
  64.7 30.4 %collective-permute-start.10 = (bf16[2,4,2,3,128,128]{5,4,3,2,1,0:T(8,128)(2,1)}, bf16[2,4,2,3,128,128]{5,4,3,2,1,0:T(8,128)(2,1)}, u32[]{:S(2)}, u32[]{:S(2)}) collective-permute-start(bf16[2,4,2,3,128,128]{5,4,3,2,1,0:T(8,128)(2,1)} %gate.17.refs_10_.refs_1_), channel_id=1, source_target_pairs={{0,4},{4,0},{8,12},{12,8},{16,20},{20,16},{24,28},{28,24},{32,36},... | collective-permute-start | bytes 4718600 | tf_op jit(solution)/shard_map/ppermute | solution.py:533
  82.8 20.7 %collective-permute-start.9 = (bf16[2,4,2,3,128,128]{5,4,3,2,1,0:T(8,128)(2,1)}, bf16[2,4,2,3,128,128]{5,4,3,2,1,0:T(8,128)(2,1)S(1)}, u32[]{:S(2)}, u32[]{:S(2)}) collective-permute-start(bf16[2,4,2,3,128,128]{5,4,3,2,1,0:T(8,128)(2,1)} %gate.18.refs_1_), channel_id=1, source_target_pairs={{0,8},{4,60},{8,16},{12,4},{16,24},{20,12},{24,32},{28,20},{32,40}... | collective-permute-start | bytes 4718600 | tf_op jit(solution)/shard_map/ppermute | solution.py:529
  85.8 2.9 %collective-permute-start.11 = (bf16[4,160,384]{2,1,0:T(8,128)(2,1)}, bf16[4,160,384]{2,1,0:T(8,128)(2,1)}, u32[]{:S(2)}, u32[]{:S(2)}) collective-permute-start(bf16[4,160,384]{2,1,0:T(8,128)(2,1)} %cross.1.refs_1_.own), channel_id=1, source_target_pairs={{0,4},{4,0},{8,12},{12,8},{16,20},{20,16},{24,28},{28,24},{32,36},... | collective-permute-start | bytes 1474568 | tf_op jit(solution)/shard_map/ppermute | solution.py:533
  85.8 24.2 %collective-permute-start.13 = (bf16[2,4,2,3,128,128]{5,4,3,2,1,0:T(8,128)(2,1)}, bf16[2,4,2,3,128,128]{5,4,3,2,1,0:T(8,128)(2,1)S(1)}, u32[]{:S(2)}, u32[]{:S(2)}) collective-permute-start(bf16[2,4,2,3,128,128]{5,4,3,2,1,0:T(8,128)(2,1)} %gate.18.refs_1_), channel_id=1, source_target_pairs={{0,4},{4,0},{8,12},{12,8},{16,20},{20,16},{24,28},{28,24},{32,36},... | collective-permute-start | bytes 4718600 | tf_op jit(solution)/shard_map/ppermute | solution.py:533
  104.7 22.1 %collective-permute-start.15 = (bf16[2,4,2,3,128,128]{5,4,3,2,1,0:T(8,128)(2,1)}, bf16[2,4,2,3,128,128]{5,4,3,2,1,0:T(8,128)(2,1)}, u32[]{:S(2)}, u32[]{:S(2)}) collective-permute-start(bf16[2,4,2,3,128,128]{5,4,3,2,1,0:T(8,128)(2,1)} %gate.19.refs_1_), channel_id=1, source_target_pairs={{0,4},{4,0},{8,12},{12,8},{16,20},{20,16},{24,28},{28,24},{32,36},... | collective-permute-start | bytes 4718600 | tf_op jit(solution)/shard_map/ppermute | solution.py:533
  109.7 11.4 %collective-permute-start.12 = (bf16[1,4,2,3,128,128]{5,4,3,2,1,0:T(8,128)(2,1)S(1)}, bf16[1,4,2,3,128,128]{5,4,3,2,1,0:T(8,128)(2,1)S(1)}, u32[]{:S(2)}, u32[]{:S(2)}) collective-permute-start(bf16[1,4,2,3,128,128]{5,4,3,2,1,0:T(8,128)(2,1)S(1)} %slice.9), channel_id=1, source_target_pairs={{0,8},{4,60},{8,16},{12,4},{16,24},{20,12},{24,32},{28,20},{32,40}... | collective-permute-start | bytes 2359304 | tf_op jit(solution)/shard_map/ppermute | solution.py:529
  122.0 24.0 %collective-permute-start.14 = (bf16[1,4,2,3,128,128]{5,4,3,2,1,0:T(8,128)(2,1)}, bf16[1,4,2,3,128,128]{5,4,3,2,1,0:T(8,128)(2,1)S(1)}, u32[]{:S(2)}, u32[]{:S(2)}) collective-permute-start(bf16[1,4,2,3,128,128]{5,4,3,2,1,0:T(8,128)(2,1)} %gate.20.refs_1_), channel_id=1, source_target_pairs={{0,4},{4,0},{8,12},{12,8},{16,20},{20,16},{24,28},{28,24},{32,36},... | collective-permute-start | bytes 2359304 | tf_op jit(solution)/shard_map/ppermute | solution.py:533
  124.1 14.3 %collective-permute-start.16 = (bf16[160,1536]{1,0:T(8,128)(2,1)}, bf16[160,1536]{1,0:T(8,128)(2,1)S(1)}, u32[]{:S(2)}, u32[]{:S(2)}) collective-permute-start(bf16[160,1536]{1,0:T(8,128)(2,1)} %get-tuple-element.70), channel_id=1, source_target_pairs={{0,1},{1,2},{2,3},{3,0},{4,5},{5,6},{6,7},{7,4},{8,9},{9,10},{10,1... | collective-permute-start | bytes 1474568 | tf_op jit(solution)/shard_map/ppermute | solution.py:524
  124.4 14.7 %collective-permute-start.17 = (bf16[160,1536]{1,0:T(8,128)(2,1)S(1)}, bf16[160,1536]{1,0:T(8,128)(2,1)S(1)}, u32[]{:S(2)}, u32[]{:S(2)}) collective-permute-start(bf16[160,1536]{1,0:T(8,128)(2,1)S(1)} %copy-done.22), channel_id=1, source_target_pairs={{0,3},{1,0},{2,1},{3,2},{4,7},{5,4},{6,5},{7,6},{8,11},{9,8},{10,9... | collective-permute-start | bytes 1474568 | tf_op jit(solution)/shard_map/ppermute | solution.py:524
  143.4 31.2 %collective-permute-start.19 = (bf16[320,1536]{1,0:T(8,128)(2,1)}, bf16[320,1536]{1,0:T(8,128)(2,1)S(1)}, u32[]{:S(2)}, u32[]{:S(2)}) collective-permute-start(bf16[320,1536]{1,0:T(8,128)(2,1)} %get-tuple-element.72.refs_6_), channel_id=1, source_target_pairs={{0,1},{1,2},{2,3},{3,0},{4,5},{5,6},{6,7},{7,4},{8,9},{9,10},{10,1... | collective-permute-start | bytes 2949128 | tf_op jit(solution)/shard_map/ppermute | solution.py:524
  144.5 30.0 %collective-permute-start.20 = (bf16[320,1536]{1,0:T(8,128)(2,1)}, bf16[320,1536]{1,0:T(8,128)(2,1)S(1)}, u32[]{:S(2)}, u32[]{:S(2)}) collective-permute-start(bf16[320,1536]{1,0:T(8,128)(2,1)} %get-tuple-element.73.refs_7_), channel_id=1, source_target_pairs={{0,3},{1,0},{2,1},{3,2},{4,7},{5,4},{6,5},{7,6},{8,11},{9,8},{10,9... | collective-permute-start | bytes 2949128 | tf_op jit(solution)/shard_map/ppermute | solution.py:524
  171.1 3.5 %collective-permute-start.18 = (bf16[4,128,384]{2,1,0:T(8,128)(2,1)S(1)}, bf16[4,128,384]{2,1,0:T(8,128)(2,1)S(1)}, u32[]{:S(2)}, u32[]{:S(2)}) collective-permute-start(bf16[4,128,384]{2,1,0:T(8,128)(2,1)S(1)} %all_to_all.10.own), channel_id=1, source_target_pairs={{0,4},{4,0},{8,12},{12,8},{16,20},{20,16},{24,28},{28,24},{32,36},... | collective-permute-start | bytes 1179656 | tf_op jit(solution)/shard_map/ppermute | solution.py:533
  182.7 2.1 %collective-permute-start.21 = (bf16[160,1536]{1,0:T(8,128)(2,1)}, bf16[160,1536]{1,0:T(8,128)(2,1)S(1)}, u32[]{:S(2)}, u32[]{:S(2)}) collective-permute-start(bf16[160,1536]{1,0:T(8,128)(2,1)} %get-tuple-element.77), channel_id=1, source_target_pairs={{0,4},{4,0},{8,12},{12,8},{16,20},{20,16},{24,28},{28,24},{32,36},... | collective-permute-start | bytes 1474568 | tf_op jit(solution)/shard_map/ppermute | solution.py:533
  (24 other events, 79.0 us)
Sparse Core Ops, SparseCore 0:
  12.4 39.3 all-gather.4
  54.3 59.0 all-gather.6

commit v12 on v11

--- a/solution.py
+++ b/solution.py
@@ -562,17 +562,19 @@
     )
     up_first, down_first = shift_tower(up_first, 1), shift_tower(down_first, -1)
 
-    behind = [crossed]
+    behind = [rest]
     after = (rest,)
     for step in range(1, 4):
+        if step == 3:
+            up, down = add_halves(up, down, up_first, down_first)
+            after = (up, down)
         now = [ahead, swap_core(ahead)]
         ahead = hop(ahead if step < 3 else ahead[:1])
         acc, top, total, token = flash(query, now, (acc, top, total), False, after)
         behind.append(token)
         after = ()
         ahead = gate(ahead, behind[step - 1])
-    up, down = add_halves(gate(up, token), down, up_first, down_first)
-    video_self = flash(query, [ahead, swap_core(ahead)], (acc, top, total), True, (up, down))
+    video_self = flash(query, [ahead, swap_core(ahead)], (acc, top, total), True)
     base = (rest, shift_tower(up, 1), shift_tower(down, -1))
 
     self_all = exchange_towers(video_self.reshape(TOWERS, VBLK, GW))

time: 194 us -> 180 us (0.928)
  waiting for transfers between devices: 47.8 us -> 40.4 us
  blocking collectives: 18.7 us -> 12 us
    all_to_all x1, blocking collectives: 18.7 us -> 12 us  [exchange_towers(): lax.all_to_all(value, 'tower', split_axis=0, concat_axis=0, tiled=True)]
    ppermute x4, waiting for transfers between devices: 5.5 us -> 1.99 us  [shift_tower(): lax.ppermute(value, 'tower', [(i, (i + step) % TOWERS) for i in range(TOW...]
    ppermute x4, waiting for transfers between devices: 16.1 us -> 13 us  [hop(): lax.ppermute(value, 'ctx', [(i, (i + 2 - 4 * (i % 2)) % total) for i in r...]
  transfers between devices with their start and end apart: 25 -> 25, of which waited for: 12 -> 11; matrix products, arithmetic and copies ran while one was open for 1% -> 1% of each run, Pallas kernels for 24% -> 26%
where the time goes in v12:
time: 180 us; the launch traced here: 179 us
  Pallas kernels  59.6 us (33%)
  starting transfers between devices  41.2 us (23%)
  waiting for transfers between devices  40.4 us (22%)
  between operations  14.4 us (8%)
  blocking collectives  12 us (7%)
  local copies, waits for them, and re-layouts  11.2 us (6%)
    pallas_call x5, Pallas kernels, flash(): pl.pallas_call(functools.partial(flash_kernel, len(kvs), state is None, l...  30.5 us
    all_to_all x1, waiting for transfers between devices, exchange_towers(): lax.all_to_all(value, 'tower', split_axis=0, concat_axis=0, tiled=True)  13.9 us
    ppermute x4, waiting for transfers between devices, hop(): lax.ppermute(value, 'ctx', [(i, (i + 2 - 4 * (i % 2)) % total) for i in r...  13 us
    all_to_all x1, blocking collectives, exchange_towers(): lax.all_to_all(value, 'tower', split_axis=0, concat_axis=0, tiled=True)  12 us
    ppermute x4, starting transfers between devices, hop(): lax.ppermute(value, 'ctx', [(i, (i + 2 - 4 * (i % 2)) % total) for i in r...  12 us
    ppermute x8, starting transfers between devices, swap_core(): return lax.ppermute(value, 'ctx', [(i, i ^ 1) for i in range(2 * CHIPS)])  11.7 us
    unnamed x47, local copies, waits for them, and re-layouts  9.16 us
    pallas_call x1, Pallas kernels, cross(): pl.pallas_call(cross_kernel, out_shape=jax.ShapeDtypeStruct((TOWERS, BOTH...  6.85 us
  transfers between devices with their start and end apart: 25, of which 11 were waited for; matrix products, arithmetic and copies ran while one was open for 1% of the time, Pallas kernels for 26%

profile of v12, /device:TPU:1, one launch (start us, length us, event | category | flops | bytes accessed | tf_op | source)
XLA Modules:
  0.0 178.9 jit_solution(5969207264742906603)
XLA Ops:
  7.8 4.3 %pack.1 = (bf16[4,3,3,128,128]{4,3,2,1,0:T(8,128)(2,1)}, bf16[3,32,1536]{2,1,0:T(8,128)(2,1)}, bf16[2,3,32,1536]{3,2,1,0:T(8,128)(2,1)}, bf16[480,384]{1,0:T(8,1...) custom-call(s32[5]{0:T(128)} %stack.32.place, ...), custom_call_target="tpu_custom_call" | custom-call | tf_op jit(solution)/shard_map/pack/pallas_call | solution.py:123
  12.2 4.9 %all-to-all-start = ((bf16[4,3,3,128,128]{4,3,2,1,0:T(8,128)(2,1)}), bf16[4,3,3,128,128]{4,3,2,1,0:T(8,128)(2,1)S(1)}, u32[]{:S(2)}, u32[]{:S(2)}) async-start(bf16[4,3,3,128,128]{4,3,2,1,0:T(8,128)(2,1)} %get-tuple-element.40), calls=%async_computation | async-start | bytes 2359296 | tf_op jit(solution)/shard_map/all_to_all | solution.py:497
  17.8 13.9 %all-to-all-done.refs_0_.q_ref = bf16[4,3,3,128,128]{4,3,2,1,0:T(8,128)(2,1)S(1)} async-done(((bf16[4,3,3,128,128]{4,3,2,1,0:T(8,128)(2,1)}), bf16[4,3,3,128,128]{4,3,2,1,0:T(8,128)(2,1)S(1)}, u32[]{:S(2)}, u32[]{:S(2)}) %all-to-all-start) | async-done | bytes 1179680 | tf_op jit(solution)/shard_map/all_to_all | solution.py:497
  31.9 2.9 %collective-permute-start = (bf16[4,2,3,128,128]{4,3,2,1,0:T(8,128)(2,1)S(1)}, bf16[4,2,3,128,128]{4,3,2,1,0:T(8,128)(2,1)S(1)}, u32[]{:S(2)}, u32[]{:S(2)}) collective-permute-start(bf16[4,2,3,128,128]{4,3,2,1,0:T(8,128)(2,1)S(1)} %get-tuple-element.79), channel_id=1, source_target_pairs={{0,4},{4,0},{8,12},{12,8},{16,20},{20,16},{24,28},{28,24},{32,36},... | collective-permute-start | bytes 2359304 | tf_op jit(solution)/shard_map/ppermute | solution.py:533
  37.6 5.6 %collective-permute-start.1 = (bf16[2,4,2,3,128,128]{5,4,3,2,1,0:T(8,128)(2,1)S(1)}, bf16[2,4,2,3,128,128]{5,4,3,2,1,0:T(8,128)(2,1)}, u32[]{:S(2)}, u32[]{:S(2)}) collective-permute-start(bf16[2,4,2,3,128,128]{5,4,3,2,1,0:T(8,128)(2,1)S(1)} %pad_maximum_fusion.refs_1_.refs_8_.refs_9_), channel_id=1, source_target_pairs={{0,8},{4,60},{8,16},{12,4},{16,24},{20,12},{24,32},{28,20},{32,40}... | collective-permute-start | bytes 4718600 | tf_op jit(solution)/shard_map/ppermute | solution.py:529
  43.2 2.2 %collective-permute-start.2 = (bf16[480,384]{1,0:T(8,128)(2,1)}, bf16[480,384]{1,0:T(8,128)(2,1)S(1)}, u32[]{:S(2)}, u32[]{:S(2)}) collective-permute-start(bf16[480,384]{1,0:T(8,128)(2,1)} %gate.10), channel_id=1, source_target_pairs={{0,1},{4,5},{8,9},{12,13},{17,18},{21,22},{25,26},{29,30},{34,35},... | collective-permute-start | bytes 1105928 | tf_op jit(solution)/shard_map/ppermute | solution.py:150
  48.1 4.7 %flash.5 = (f32[512,384]{1,0:T(8,128)}, f32[512,384]{1,0:T(8,128)}, f32[512,384]{1,0:T(8,128)}, f32[8,128]{1,0:T(8,128)}) custom-call(bf16[4,3,3,128,128]{4,3,2,1,0:T(8,128)(2,1)} %copy-done.1, bf16[2,4,2,3,128,128]{5,4,3,2,1,0:T(8,128)(2,1)} %copy-done.2), custom_call_target="tpu_custom_call" | custom-call | flops 1 | bytes 1 | tf_op jit(solution)/shard_map/flash/pallas_call | solution.py:238
  54.9 4.2 %collective-permute-done.3.refs_3_.refs_2_ = bf16[480,384]{1,0:T(8,128)(2,1)S(1)} collective-permute-done((bf16[480,384]{1,0:T(8,128)(2,1)}, bf16[480,384]{1,0:T(8,128)(2,1)S(1)}, u32[]{:S(2)}, u32[]{:S(2)}) %collective-permute-start.3) | collective-permute-done | bytes 368672 | tf_op jit(solution)/shard_map/ppermute | solution.py:150
  60.6 3.3 %collective-permute-start.8 = (bf16[2,4,2,3,128,128]{5,4,3,2,1,0:T(8,128)(2,1)}, bf16[2,4,2,3,128,128]{5,4,3,2,1,0:T(8,128)(2,1)S(1)}, u32[]{:S(2)}, u32[]{:S(2)}) collective-permute-start(bf16[2,4,2,3,128,128]{5,4,3,2,1,0:T(8,128)(2,1)} %gate.16.refs_10_.refs_1_), channel_id=1, source_target_pairs={{0,8},{4,60},{8,16},{12,4},{16,24},{20,12},{24,32},{28,20},{32,40}... | collective-permute-start | bytes 4718600 | tf_op jit(solution)/shard_map/ppermute | solution.py:529
  64.6 6.8 %cross.1.own = bf16[4,160,384]{2,1,0:T(8,128)(2,1)} custom-call(s32[5]{0:T(128)} %stack.32.place, s32[64,3]{1,0:T(8,128)} %bitcast.33, bf16[4,3,3,128,128]{4,3,2,1,0:T(8,128)(2,1)} %copy-done.1, bf16[480,384]{1,0:T(8,128)(2,1)} %get-tuple-element.48.refs_0_, bf16[480,384]{1,0:T(8,128)(2,1)} %copy-done.9, bf16[480,384]{1,0:T(8,128)(2,1)} %copy-done.10, ...), custom_call_target="tpu_custom_call" | custom-call | flops 1 | bytes 1 | tf_op jit(solution)/shard_map/cross/pallas_call | solution.py:326
  74.4 6.5 %project_cross.1 = (bf16[320,1536]{1,0:T(8,128)(2,1)}, bf16[320,1536]{1,0:T(8,128)(2,1)}, bf16[320,1536]{1,0:T(8,128)(2,1)}, bf16[160,1536]{1,0:T(8,128)(2,1)}, bf16[160,1536]{1,0:T(8,128)(2,1)}) custom-call(s32[5]{0:T(128)} %stack.32.place, bf16[4,160,384]{2,1,0:T(8,128)(2,1)} %cross.1.own, bf16[4,160,384]{2,1,0:T(8,128)(2,1)} %copy-done.17, ...), custom_call_target="tpu_custom_call" | custom-call | flops 1 | bytes 1 | tf_op jit(solution)/shard_map/project_cross/pallas_call | solution.py:378
  82.7 3.0 %collective-permute-start.10 = (bf16[2,4,2,3,128,128]{5,4,3,2,1,0:T(8,128)(2,1)}, bf16[2,4,2,3,128,128]{5,4,3,2,1,0:T(8,128)(2,1)S(1)}, u32[]{:S(2)}, u32[]{:S(2)}) collective-permute-start(bf16[2,4,2,3,128,128]{5,4,3,2,1,0:T(8,128)(2,1)} %gate.17.refs_1_), channel_id=1, source_target_pairs={{0,8},{4,60},{8,16},{12,4},{16,24},{20,12},{24,32},{28,20},{32,40}... | collective-permute-start | bytes 4718600 | tf_op jit(solution)/shard_map/ppermute | solution.py:529
  85.8 6.8 %flash.6 = (f32[512,384]{1,0:T(8,128)}, f32[512,384]{1,0:T(8,128)}, f32[512,384]{1,0:T(8,128)}, f32[8,128]{1,0:T(8,128)}) custom-call(bf16[4,3,3,128,128]{4,3,2,1,0:T(8,128)(2,1)} %copy-done.1, bf16[2,4,2,3,128,128]{5,4,3,2,1,0:T(8,128)(2,1)} %gate.16.refs_10_.refs_1_, bf16[2,4,2,3,128,128]{5,4,3,2,1,0:T(8,128)(2,1)} %collective-permute-done.11.refs_2_, ...), custom_call_target="tpu_custom_call" | custom-call | flops 1 | bytes 1 | tf_op jit(solution)/shard_map/flash/pallas_call | solution.py:238
  92.6 10.8 %collective-permute-done.10.refs_0_ = bf16[2,4,2,3,128,128]{5,4,3,2,1,0:T(8,128)(2,1)S(1)} collective-permute-done((bf16[2,4,2,3,128,128]{5,4,3,2,1,0:T(8,128)(2,1)}, bf16[2,4,2,3,128,128]{5,4,3,2,1,0:T(8,128)(2,1)S(1)}, u32[]{:S(2)}, u32[]{:S(2)}) %collective-permute-start.10) | collective-permute-done | bytes 1572896 | tf_op jit(solution)/shard_map/ppermute | solution.py:529
  104.6 3.9 %collective-permute-start.15 = (bf16[2,4,2,3,128,128]{5,4,3,2,1,0:T(8,128)(2,1)}, bf16[2,4,2,3,128,128]{5,4,3,2,1,0:T(8,128)(2,1)}, u32[]{:S(2)}, u32[]{:S(2)}) collective-permute-start(bf16[2,4,2,3,128,128]{5,4,3,2,1,0:T(8,128)(2,1)} %gate.18.refs_1_), channel_id=1, source_target_pairs={{0,4},{4,0},{8,12},{12,8},{16,20},{20,16},{24,28},{28,24},{32,36},... | collective-permute-start | bytes 4718600 | tf_op jit(solution)/shard_map/ppermute | solution.py:533
  110.3 2.6 %collective-permute-start.17 = (bf16[160,1536]{1,0:T(8,128)(2,1)}, bf16[160,1536]{1,0:T(8,128)(2,1)S(1)}, u32[]{:S(2)}, u32[]{:S(2)}) collective-permute-start(bf16[160,1536]{1,0:T(8,128)(2,1)} %get-tuple-element.66), channel_id=1, source_target_pairs={{0,3},{1,0},{2,1},{3,2},{4,7},{5,4},{6,5},{7,6},{8,11},{9,8},{10,9... | collective-permute-start | bytes 1474568 | tf_op jit(solution)/shard_map/ppermute | solution.py:524
  114.2 6.8 %flash.7 = (f32[512,384]{1,0:T(8,128)}, f32[512,384]{1,0:T(8,128)}, f32[512,384]{1,0:T(8,128)}, f32[8,128]{1,0:T(8,128)}) custom-call(bf16[4,3,3,128,128]{4,3,2,1,0:T(8,128)(2,1)} %copy-done.1, bf16[2,4,2,3,128,128]{5,4,3,2,1,0:T(8,128)(2,1)} %gate.17.refs_1_, bf16[2,4,2,3,128,128]{5,4,3,2,1,0:T(8,128)(2,1)} %copy-done.8, ...), custom_call_target="tpu_custom_call" | custom-call | flops 1 | bytes 1 | tf_op jit(solution)/shard_map/flash/pallas_call | solution.py:238
  121.9 1.9 %collective-permute-start.14 = (bf16[1,4,2,3,128,128]{5,4,3,2,1,0:T(8,128)(2,1)}, bf16[1,4,2,3,128,128]{5,4,3,2,1,0:T(8,128)(2,1)S(1)}, u32[]{:S(2)}, u32[]{:S(2)}) collective-permute-start(bf16[1,4,2,3,128,128]{5,4,3,2,1,0:T(8,128)(2,1)} %gate.19.refs_1_), channel_id=1, source_target_pairs={{0,4},{4,0},{8,12},{12,8},{16,20},{20,16},{24,28},{28,24},{32,36},... | collective-permute-start | bytes 2359304 | tf_op jit(solution)/shard_map/ppermute | solution.py:533
  126.7 3.4 %add_halves.1 = (bf16[320,1536]{1,0:T(8,128)(2,1)}, bf16[320,1536]{1,0:T(8,128)(2,1)}) custom-call(bf16[320,1536]{1,0:T(8,128)(2,1)} %get-tuple-element.63.up, bf16[320,1536]{1,0:T(8,128)(2,1)} %get-tuple-element.64.down, bf16[160,1536]{1,0:T(8,128)(2,1)} %copy-done.15, bf16[160,1536]{1,0:T(8,128)(2,1)} %copy-done.16), custom_call_target="tpu_custom_call", output_to_operand_aliasing={{0}: (0, {}), {1}: (1, {})} | custom-call | flops 1 | bytes 1 | tf_op jit(solution)/shard_map/add_halves/pallas_call | solution.py:510
  132.7 6.8 %flash.8 = (f32[512,384]{1,0:T(8,128)}, f32[512,384]{1,0:T(8,128)}, f32[512,384]{1,0:T(8,128)}, f32[8,128]{1,0:T(8,128)}) custom-call(bf16[4,3,3,128,128]{4,3,2,1,0:T(8,128)(2,1)} %copy-done.1, bf16[2,4,2,3,128,128]{5,4,3,2,1,0:T(8,128)(2,1)} %gate.18.refs_1_, bf16[2,4,2,3,128,128]{5,4,3,2,1,0:T(8,128)(2,1)} %collective-permute-done.15.refs_2_, ...), custom_call_target="tpu_custom_call" | custom-call | flops 1 | bytes 1 | tf_op jit(solution)/shard_map/flash/pallas_call | solution.py:238
  140.5 5.3 %flash.9 = bf16[512,384]{1,0:T(8,128)(2,1)} custom-call(bf16[4,3,3,128,128]{4,3,2,1,0:T(8,128)(2,1)} %copy-done.1, bf16[1,4,2,3,128,128]{5,4,3,2,1,0:T(8,128)(2,1)} %gate.19.refs_1_, bf16[1,4,2,3,128,128]{5,4,3,2,1,0:T(8,128)(2,1)} %copy-done.14, f32[512,384]{1,0:T(8,128)} %get-tuple-element.69.refs_3_, f32[512,384]{1,0:T(8,128)} %get-tuple-element.70.refs_4_, ...), custom_call_target="tpu_custom_call" | custom-call | flops 1 | bytes 1 | tf_op jit(solution)/shard_map/flash/pallas_call | solution.py:238
  145.8 12.0 %all_to_all.10.own = bf16[4,128,384]{2,1,0:T(8,128)(2,1)S(1)} all-to-all(bf16[4,128,384]{2,1,0:T(8,128)(2,1)} %bitcast.24), channel_id=1, replica_groups=mesh['batch'=4,'ctx'=16,'tower'=4] {'tower'}, dimensions={0} | all-to-all | bytes 786432 | tf_op jit(solution)/shard_map/all_to_all | solution.py:497
  157.8 2.0 %collective-permute-start.18 = (bf16[4,128,384]{2,1,0:T(8,128)(2,1)S(1)}, bf16[4,128,384]{2,1,0:T(8,128)(2,1)S(1)}, u32[]{:S(2)}, u32[]{:S(2)}) collective-permute-start(bf16[4,128,384]{2,1,0:T(8,128)(2,1)S(1)} %all_to_all.10.own), channel_id=1, source_target_pairs={{0,4},{4,0},{8,12},{12,8},{16,20},{20,16},{24,28},{28,24},{32,36},... | collective-permute-start | bytes 1179656 | tf_op jit(solution)/shard_map/ppermute | solution.py:533
  162.0 6.7 %project_self.1 = (bf16[128,3072]{1,0:T(8,128)(2,1)}, bf16[24,3072]{1,0:T(8,128)(2,1)}, bf16[160,1536]{1,0:T(8,128)(2,1)}) custom-call(s32[5]{0:T(128)} %stack.32.place, bf16[4,128,384]{2,1,0:T(8,128)(2,1)} %copy-done.7, bf16[4,128,384]{2,1,0:T(8,128)(2,1)} %copy-done.18, bf16[16,3,32,1536]{3,2,1,0:T(8,128)(2,1)} %bitcast.22, ...), custom_call_target="tpu_custom_call" | custom-call | flops 1 | bytes 1 | tf_op jit(solution)/shard_map/project_self/pallas_call | solution.py:429
  (101 shorter events, 33.0 us)
Async XLA Ops:
  7.2 64.9 %all-gather.5.cloned.1.call-start = ((), (), s32[]{:S(2)}) async-start(), calls=%async_computation.2 | async-start | bytes 2949120 | tf_op jit(solution)/shard_map/all_gather | solution.py:547
  12.2 19.5 %all-to-all-start = ((bf16[4,3,3,128,128]{4,3,2,1,0:T(8,128)(2,1)}), bf16[4,3,3,128,128]{4,3,2,1,0:T(8,128)(2,1)S(1)}, u32[]{:S(2)}, u32[]{:S(2)}) async-start(bf16[4,3,3,128,128]{4,3,2,1,0:T(8,128)(2,1)} %get-tuple-element.40), calls=%async_computation | async-start | bytes 2359296 | tf_op jit(solution)/shard_map/all_to_all | solution.py:497
  17.1 144.1 %all-gather.7.cloned.1.call-start = ((), (), s32[]{:S(2)}) async-start(), calls=%async_computation.3 | async-start | bytes 5013504 | tf_op jit(solution)/shard_map/all_gather | solution.py:548
  31.9 4.8 %collective-permute-start = (bf16[4,2,3,128,128]{4,3,2,1,0:T(8,128)(2,1)S(1)}, bf16[4,2,3,128,128]{4,3,2,1,0:T(8,128)(2,1)S(1)}, u32[]{:S(2)}, u32[]{:S(2)}) collective-permute-start(bf16[4,2,3,128,128]{4,3,2,1,0:T(8,128)(2,1)S(1)} %get-tuple-element.79), channel_id=1, source_target_pairs={{0,4},{4,0},{8,12},{12,8},{16,20},{20,16},{24,28},{28,24},{32,36},... | collective-permute-start | bytes 2359304 | tf_op jit(solution)/shard_map/ppermute | solution.py:533
  37.6 22.9 %collective-permute-start.1 = (bf16[2,4,2,3,128,128]{5,4,3,2,1,0:T(8,128)(2,1)S(1)}, bf16[2,4,2,3,128,128]{5,4,3,2,1,0:T(8,128)(2,1)}, u32[]{:S(2)}, u32[]{:S(2)}) collective-permute-start(bf16[2,4,2,3,128,128]{5,4,3,2,1,0:T(8,128)(2,1)S(1)} %pad_maximum_fusion.refs_1_.refs_8_.refs_9_), channel_id=1, source_target_pairs={{0,8},{4,60},{8,16},{12,4},{16,24},{20,12},{24,32},{28,20},{32,40}... | collective-permute-start | bytes 4718600 | tf_op jit(solution)/shard_map/ppermute | solution.py:529
  43.2 11.7 %collective-permute-start.2 = (bf16[480,384]{1,0:T(8,128)(2,1)}, bf16[480,384]{1,0:T(8,128)(2,1)S(1)}, u32[]{:S(2)}, u32[]{:S(2)}) collective-permute-start(bf16[480,384]{1,0:T(8,128)(2,1)} %gate.10), channel_id=1, source_target_pairs={{0,1},{4,5},{8,9},{12,13},{17,18},{21,22},{25,26},{29,30},{34,35},... | collective-permute-start | bytes 1105928 | tf_op jit(solution)/shard_map/ppermute | solution.py:150
  45.4 13.7 %collective-permute-start.3 = (bf16[480,384]{1,0:T(8,128)(2,1)}, bf16[480,384]{1,0:T(8,128)(2,1)S(1)}, u32[]{:S(2)}, u32[]{:S(2)}) collective-permute-start(bf16[480,384]{1,0:T(8,128)(2,1)} %gate.11), channel_id=1, source_target_pairs={{0,2},{4,6},{8,10},{12,14},{17,19},{21,23},{25,27},{29,31},{34,32}... | collective-permute-start | bytes 1105928 | tf_op jit(solution)/shard_map/ppermute | solution.py:150
  46.7 12.4 %collective-permute-start.4 = (bf16[480,384]{1,0:T(8,128)(2,1)}, bf16[480,384]{1,0:T(8,128)(2,1)S(1)}, u32[]{:S(2)}, u32[]{:S(2)}) collective-permute-start(bf16[480,384]{1,0:T(8,128)(2,1)} %gate.12), channel_id=1, source_target_pairs={{0,3},{4,7},{8,11},{12,15},{17,16},{21,20},{25,24},{29,28},{34,33}... | collective-permute-start | bytes 1105928 | tf_op jit(solution)/shard_map/ppermute | solution.py:150
  53.5 0.7 collective-permute-start.6
  54.2 0.7 collective-permute-start.5
  60.6 21.0 %collective-permute-start.8 = (bf16[2,4,2,3,128,128]{5,4,3,2,1,0:T(8,128)(2,1)}, bf16[2,4,2,3,128,128]{5,4,3,2,1,0:T(8,128)(2,1)S(1)}, u32[]{:S(2)}, u32[]{:S(2)}) collective-permute-start(bf16[2,4,2,3,128,128]{5,4,3,2,1,0:T(8,128)(2,1)} %gate.16.refs_10_.refs_1_), channel_id=1, source_target_pairs={{0,8},{4,60},{8,16},{12,4},{16,24},{20,12},{24,32},{28,20},{32,40}... | collective-permute-start | bytes 4718600 | tf_op jit(solution)/shard_map/ppermute | solution.py:529
  71.4 2.2 %collective-permute-start.9 = (bf16[4,160,384]{2,1,0:T(8,128)(2,1)}, bf16[4,160,384]{2,1,0:T(8,128)(2,1)S(1)}, u32[]{:S(2)}, u32[]{:S(2)}) collective-permute-start(bf16[4,160,384]{2,1,0:T(8,128)(2,1)} %cross.1.own), channel_id=1, source_target_pairs={{0,4},{4,0},{8,12},{12,8},{16,20},{20,16},{24,28},{28,24},{32,36},... | collective-permute-start | bytes 1474568 | tf_op jit(solution)/shard_map/ppermute | solution.py:533
  71.5 14.2 %collective-permute-start.11 = (bf16[2,4,2,3,128,128]{5,4,3,2,1,0:T(8,128)(2,1)}, bf16[2,4,2,3,128,128]{5,4,3,2,1,0:T(8,128)(2,1)}, u32[]{:S(2)}, u32[]{:S(2)}) collective-permute-start(bf16[2,4,2,3,128,128]{5,4,3,2,1,0:T(8,128)(2,1)} %gate.16.refs_10_.refs_1_), channel_id=1, source_target_pairs={{0,4},{4,0},{8,12},{12,8},{16,20},{20,16},{24,28},{28,24},{32,36},... | collective-permute-start | bytes 4718600 | tf_op jit(solution)/shard_map/ppermute | solution.py:533
  82.7 20.7 %collective-permute-start.10 = (bf16[2,4,2,3,128,128]{5,4,3,2,1,0:T(8,128)(2,1)}, bf16[2,4,2,3,128,128]{5,4,3,2,1,0:T(8,128)(2,1)S(1)}, u32[]{:S(2)}, u32[]{:S(2)}) collective-permute-start(bf16[2,4,2,3,128,128]{5,4,3,2,1,0:T(8,128)(2,1)} %gate.17.refs_1_), channel_id=1, source_target_pairs={{0,8},{4,60},{8,16},{12,4},{16,24},{20,12},{24,32},{28,20},{32,40}... | collective-permute-start | bytes 4718600 | tf_op jit(solution)/shard_map/ppermute | solution.py:529
  85.7 27.2 %collective-permute-start.13 = (bf16[2,4,2,3,128,128]{5,4,3,2,1,0:T(8,128)(2,1)}, bf16[2,4,2,3,128,128]{5,4,3,2,1,0:T(8,128)(2,1)S(1)}, u32[]{:S(2)}, u32[]{:S(2)}) collective-permute-start(bf16[2,4,2,3,128,128]{5,4,3,2,1,0:T(8,128)(2,1)} %gate.17.refs_1_), channel_id=1, source_target_pairs={{0,4},{4,0},{8,12},{12,8},{16,20},{20,16},{24,28},{28,24},{32,36},... | collective-permute-start | bytes 4718600 | tf_op jit(solution)/shard_map/ppermute | solution.py:533
  104.6 28.1 %collective-permute-start.15 = (bf16[2,4,2,3,128,128]{5,4,3,2,1,0:T(8,128)(2,1)}, bf16[2,4,2,3,128,128]{5,4,3,2,1,0:T(8,128)(2,1)}, u32[]{:S(2)}, u32[]{:S(2)}) collective-permute-start(bf16[2,4,2,3,128,128]{5,4,3,2,1,0:T(8,128)(2,1)} %gate.18.refs_1_), channel_id=1, source_target_pairs={{0,4},{4,0},{8,12},{12,8},{16,20},{20,16},{24,28},{28,24},{32,36},... | collective-permute-start | bytes 4718600 | tf_op jit(solution)/shard_map/ppermute | solution.py:533
  109.7 11.3 %collective-permute-start.12 = (bf16[1,4,2,3,128,128]{5,4,3,2,1,0:T(8,128)(2,1)S(1)}, bf16[1,4,2,3,128,128]{5,4,3,2,1,0:T(8,128)(2,1)S(1)}, u32[]{:S(2)}, u32[]{:S(2)}) collective-permute-start(bf16[1,4,2,3,128,128]{5,4,3,2,1,0:T(8,128)(2,1)S(1)} %slice.9), channel_id=1, source_target_pairs={{0,8},{4,60},{8,16},{12,4},{16,24},{20,12},{24,32},{28,20},{32,40}... | collective-permute-start | bytes 2359304 | tf_op jit(solution)/shard_map/ppermute | solution.py:529
  109.8 14.9 %collective-permute-start.16 = (bf16[160,1536]{1,0:T(8,128)(2,1)}, bf16[160,1536]{1,0:T(8,128)(2,1)S(1)}, u32[]{:S(2)}, u32[]{:S(2)}) collective-permute-start(bf16[160,1536]{1,0:T(8,128)(2,1)} %get-tuple-element.65), channel_id=1, source_target_pairs={{0,1},{1,2},{2,3},{3,0},{4,5},{5,6},{6,7},{7,4},{8,9},{9,10},{10,1... | collective-permute-start | bytes 1474568 | tf_op jit(solution)/shard_map/ppermute | solution.py:524
  110.3 15.5 %collective-permute-start.17 = (bf16[160,1536]{1,0:T(8,128)(2,1)}, bf16[160,1536]{1,0:T(8,128)(2,1)S(1)}, u32[]{:S(2)}, u32[]{:S(2)}) collective-permute-start(bf16[160,1536]{1,0:T(8,128)(2,1)} %get-tuple-element.66), channel_id=1, source_target_pairs={{0,3},{1,0},{2,1},{3,2},{4,7},{5,4},{6,5},{7,6},{8,11},{9,8},{10,9... | collective-permute-start | bytes 1474568 | tf_op jit(solution)/shard_map/ppermute | solution.py:524
  121.9 17.6 %collective-permute-start.14 = (bf16[1,4,2,3,128,128]{5,4,3,2,1,0:T(8,128)(2,1)}, bf16[1,4,2,3,128,128]{5,4,3,2,1,0:T(8,128)(2,1)S(1)}, u32[]{:S(2)}, u32[]{:S(2)}) collective-permute-start(bf16[1,4,2,3,128,128]{5,4,3,2,1,0:T(8,128)(2,1)} %gate.19.refs_1_), channel_id=1, source_target_pairs={{0,4},{4,0},{8,12},{12,8},{16,20},{20,16},{24,28},{28,24},{32,36},... | collective-permute-start | bytes 2359304 | tf_op jit(solution)/shard_map/ppermute | solution.py:533
  130.0 29.8 %collective-permute-start.19 = (bf16[320,1536]{1,0:T(8,128)(2,1)}, bf16[320,1536]{1,0:T(8,128)(2,1)S(1)}, u32[]{:S(2)}, u32[]{:S(2)}) collective-permute-start(bf16[320,1536]{1,0:T(8,128)(2,1)} %get-tuple-element.67.refs_6_), channel_id=1, source_target_pairs={{0,1},{1,2},{2,3},{3,0},{4,5},{5,6},{6,7},{7,4},{8,9},{9,10},{10,1... | collective-permute-start | bytes 2949128 | tf_op jit(solution)/shard_map/ppermute | solution.py:524
  131.3 28.5 %collective-permute-start.20 = (bf16[320,1536]{1,0:T(8,128)(2,1)}, bf16[320,1536]{1,0:T(8,128)(2,1)S(1)}, u32[]{:S(2)}, u32[]{:S(2)}) collective-permute-start(bf16[320,1536]{1,0:T(8,128)(2,1)} %get-tuple-element.68.refs_7_), channel_id=1, source_target_pairs={{0,3},{1,0},{2,1},{3,2},{4,7},{5,4},{6,5},{7,6},{8,11},{9,8},{10,9... | collective-permute-start | bytes 2949128 | tf_op jit(solution)/shard_map/ppermute | solution.py:524
  157.8 3.4 %collective-permute-start.18 = (bf16[4,128,384]{2,1,0:T(8,128)(2,1)S(1)}, bf16[4,128,384]{2,1,0:T(8,128)(2,1)S(1)}, u32[]{:S(2)}, u32[]{:S(2)}) collective-permute-start(bf16[4,128,384]{2,1,0:T(8,128)(2,1)S(1)} %all_to_all.10.own), channel_id=1, source_target_pairs={{0,4},{4,0},{8,12},{12,8},{16,20},{20,16},{24,28},{28,24},{32,36},... | collective-permute-start | bytes 1179656 | tf_op jit(solution)/shard_map/ppermute | solution.py:533
  168.7 2.1 %collective-permute-start.21 = (bf16[160,1536]{1,0:T(8,128)(2,1)}, bf16[160,1536]{1,0:T(8,128)(2,1)S(1)}, u32[]{:S(2)}, u32[]{:S(2)}) collective-permute-start(bf16[160,1536]{1,0:T(8,128)(2,1)} %get-tuple-element.75), channel_id=1, source_target_pairs={{0,4},{4,0},{8,12},{12,8},{16,20},{20,16},{24,28},{28,24},{32,36},... | collective-permute-start | bytes 1474568 | tf_op jit(solution)/shard_map/ppermute | solution.py:533
  (24 other events, 76.8 us)
Sparse Core Ops, SparseCore 0:
  12.3 39.3 all-gather.4
  54.2 59.0 all-gather.6

commit v13 on v12

--- a/solution.py
+++ b/solution.py
@@ -573,7 +573,7 @@
         acc, top, total, token = flash(query, now, (acc, top, total), False, after)
         behind.append(token)
         after = ()
-        ahead = gate(ahead, behind[step - 1])
+        ahead = gate(ahead, behind[0] if step == 1 else behind[2])
     video_self = flash(query, [ahead, swap_core(ahead)], (acc, top, total), True)
     base = (rest, shift_tower(up, 1), shift_tower(down, -1))
 

time: 180 us -> 180 us (level)
    unnamed x47 -> x49, local copies, waits for them, and re-layouts: 9.16 us -> 10.3 us
  transfers between devices with their start and end apart: 25 -> 25, of which waited for: 11 -> 12; matrix products, arithmetic and copies ran while one was open for 1% -> 1% of each run, Pallas kernels for 26% -> 27%
where the time goes in v13:
time: 180 us; the launch traced here: 179 us
  Pallas kernels  60.1 us (33%)
  starting transfers between devices  40.2 us (22%)
  waiting for transfers between devices  39.8 us (22%)
  between operations  14.4 us (8%)
  local copies, waits for them, and re-layouts  12.4 us (7%)
  blocking collectives  12.3 us (7%)
    pallas_call x5, Pallas kernels, flash(): pl.pallas_call(functools.partial(flash_kernel, len(kvs), state is None, l...  31.1 us
    all_to_all x1, waiting for transfers between devices, exchange_towers(): lax.all_to_all(value, 'tower', split_axis=0, concat_axis=0, tiled=True)  13.9 us
    ppermute x4, waiting for transfers between devices, hop(): lax.ppermute(value, 'ctx', [(i, (i + 2 - 4 * (i % 2)) % total) for i in r...  12.8 us
    all_to_all x1, blocking collectives, exchange_towers(): lax.all_to_all(value, 'tower', split_axis=0, concat_axis=0, tiled=True)  12.3 us
    ppermute x8, starting transfers between devices, swap_core(): return lax.ppermute(value, 'ctx', [(i, i ^ 1) for i in range(2 * CHIPS)])  11.9 us
    ppermute x4, starting transfers between devices, hop(): lax.ppermute(value, 'ctx', [(i, (i + 2 - 4 * (i % 2)) % total) for i in r...  10.7 us
    unnamed x49, local copies, waits for them, and re-layouts  10.3 us
    pallas_call x1, Pallas kernels, cross(): pl.pallas_call(cross_kernel, out_shape=jax.ShapeDtypeStruct((TOWERS, BOTH...  6.84 us
  transfers between devices with their start and end apart: 25, of which 12 were waited for; matrix products, arithmetic and copies ran while one was open for 1% of the time, Pallas kernels for 27%

profile of v13, /device:TPU:1, one launch (start us, length us, event | category | flops | bytes accessed | tf_op | source)
XLA Modules:
  0.0 179.3 jit_solution(13941199244728287566)
XLA Ops:
  7.9 4.3 %pack.1 = (bf16[4,3,3,128,128]{4,3,2,1,0:T(8,128)(2,1)}, bf16[3,32,1536]{2,1,0:T(8,128)(2,1)}, bf16[2,3,32,1536]{3,2,1,0:T(8,128)(2,1)}, bf16[480,384]{1,0:T(8,1...) custom-call(s32[5]{0:T(128)} %stack.32.place, ...), custom_call_target="tpu_custom_call" | custom-call | tf_op jit(solution)/shard_map/pack/pallas_call | solution.py:123
  12.3 4.9 %all-to-all-start = ((bf16[4,3,3,128,128]{4,3,2,1,0:T(8,128)(2,1)}), bf16[4,3,3,128,128]{4,3,2,1,0:T(8,128)(2,1)S(1)}, u32[]{:S(2)}, u32[]{:S(2)}) async-start(bf16[4,3,3,128,128]{4,3,2,1,0:T(8,128)(2,1)} %get-tuple-element.39), calls=%async_computation | async-start | bytes 2359296 | tf_op jit(solution)/shard_map/all_to_all | solution.py:497
  17.9 13.9 %all-to-all-done.refs_0_.q_ref = bf16[4,3,3,128,128]{4,3,2,1,0:T(8,128)(2,1)S(1)} async-done(((bf16[4,3,3,128,128]{4,3,2,1,0:T(8,128)(2,1)}), bf16[4,3,3,128,128]{4,3,2,1,0:T(8,128)(2,1)S(1)}, u32[]{:S(2)}, u32[]{:S(2)}) %all-to-all-start) | async-done | bytes 1179680 | tf_op jit(solution)/shard_map/all_to_all | solution.py:497
  32.0 2.9 %collective-permute-start = (bf16[4,2,3,128,128]{4,3,2,1,0:T(8,128)(2,1)S(1)}, bf16[4,2,3,128,128]{4,3,2,1,0:T(8,128)(2,1)S(1)}, u32[]{:S(2)}, u32[]{:S(2)}) collective-permute-start(bf16[4,2,3,128,128]{4,3,2,1,0:T(8,128)(2,1)S(1)} %get-tuple-element.77), channel_id=1, source_target_pairs={{0,4},{4,0},{8,12},{12,8},{16,20},{20,16},{24,28},{28,24},{32,36},... | collective-permute-start | bytes 2359304 | tf_op jit(solution)/shard_map/ppermute | solution.py:533
  37.7 5.6 %collective-permute-start.1 = (bf16[2,4,2,3,128,128]{5,4,3,2,1,0:T(8,128)(2,1)S(1)}, bf16[2,4,2,3,128,128]{5,4,3,2,1,0:T(8,128)(2,1)}, u32[]{:S(2)}, u32[]{:S(2)}) collective-permute-start(bf16[2,4,2,3,128,128]{5,4,3,2,1,0:T(8,128)(2,1)S(1)} %pad_maximum_fusion.refs_1_.refs_8_.refs_9_), channel_id=1, source_target_pairs={{0,8},{4,60},{8,16},{12,4},{16,24},{20,12},{24,32},{28,20},{32,40}... | collective-permute-start | bytes 4718600 | tf_op jit(solution)/shard_map/ppermute | solution.py:529
  43.3 2.2 %collective-permute-start.2 = (bf16[480,384]{1,0:T(8,128)(2,1)}, bf16[480,384]{1,0:T(8,128)(2,1)S(1)}, u32[]{:S(2)}, u32[]{:S(2)}) collective-permute-start(bf16[480,384]{1,0:T(8,128)(2,1)} %gate.10), channel_id=1, source_target_pairs={{0,1},{4,5},{8,9},{12,13},{17,18},{21,22},{25,26},{29,30},{34,35},... | collective-permute-start | bytes 1105928 | tf_op jit(solution)/shard_map/ppermute | solution.py:150
  48.1 4.7 %flash.5 = (f32[512,384]{1,0:T(8,128)}, f32[512,384]{1,0:T(8,128)}, f32[512,384]{1,0:T(8,128)}, f32[8,128]{1,0:T(8,128)}) custom-call(bf16[4,3,3,128,128]{4,3,2,1,0:T(8,128)(2,1)} %copy-done.1, bf16[2,4,2,3,128,128]{5,4,3,2,1,0:T(8,128)(2,1)} %copy-done.2), custom_call_target="tpu_custom_call" | custom-call | flops 1 | bytes 1 | tf_op jit(solution)/shard_map/flash/pallas_call | solution.py:238
  55.0 4.2 %collective-permute-done.3.refs_3_.refs_2_ = bf16[480,384]{1,0:T(8,128)(2,1)S(1)} collective-permute-done((bf16[480,384]{1,0:T(8,128)(2,1)}, bf16[480,384]{1,0:T(8,128)(2,1)S(1)}, u32[]{:S(2)}, u32[]{:S(2)}) %collective-permute-start.3) | collective-permute-done | bytes 368672 | tf_op jit(solution)/shard_map/ppermute | solution.py:150
  60.7 3.3 %collective-permute-start.8 = (bf16[2,4,2,3,128,128]{5,4,3,2,1,0:T(8,128)(2,1)}, bf16[2,4,2,3,128,128]{5,4,3,2,1,0:T(8,128)(2,1)S(1)}, u32[]{:S(2)}, u32[]{:S(2)}) collective-permute-start(bf16[2,4,2,3,128,128]{5,4,3,2,1,0:T(8,128)(2,1)} %gate.16.refs_10_.refs_1_), channel_id=1, source_target_pairs={{0,8},{4,60},{8,16},{12,4},{16,24},{20,12},{24,32},{28,20},{32,40}... | collective-permute-start | bytes 4718600 | tf_op jit(solution)/shard_map/ppermute | solution.py:529
  64.7 6.8 %cross.1.own = bf16[4,160,384]{2,1,0:T(8,128)(2,1)} custom-call(s32[5]{0:T(128)} %stack.32.place, s32[64,3]{1,0:T(8,128)} %bitcast.33, bf16[4,3,3,128,128]{4,3,2,1,0:T(8,128)(2,1)} %copy-done.1, bf16[480,384]{1,0:T(8,128)(2,1)} %get-tuple-element.47.refs_0_, bf16[480,384]{1,0:T(8,128)(2,1)} %copy-done.10, bf16[480,384]{1,0:T(8,128)(2,1)} %copy-done.11, ...), custom_call_target="tpu_custom_call" | custom-call | flops 1 | bytes 1 | tf_op jit(solution)/shard_map/cross/pallas_call | solution.py:326
  74.5 6.4 %project_cross.1 = (bf16[320,1536]{1,0:T(8,128)(2,1)}, bf16[320,1536]{1,0:T(8,128)(2,1)}, bf16[320,1536]{1,0:T(8,128)(2,1)}, bf16[160,1536]{1,0:T(8,128)(2,1)}, bf16[160,1536]{1,0:T(8,128)(2,1)}) custom-call(s32[5]{0:T(128)} %stack.32.place, bf16[4,160,384]{2,1,0:T(8,128)(2,1)} %cross.1.own, bf16[4,160,384]{2,1,0:T(8,128)(2,1)} %copy-done.17, ...), custom_call_target="tpu_custom_call" | custom-call | flops 1 | bytes 1 | tf_op jit(solution)/shard_map/project_cross/pallas_call | solution.py:378
  82.9 2.7 %collective-permute-start.11 = (bf16[2,4,2,3,128,128]{5,4,3,2,1,0:T(8,128)(2,1)}, bf16[2,4,2,3,128,128]{5,4,3,2,1,0:T(8,128)(2,1)S(1)}, u32[]{:S(2)}, u32[]{:S(2)}) collective-permute-start(bf16[2,4,2,3,128,128]{5,4,3,2,1,0:T(8,128)(2,1)} %gate.17.refs_1_), channel_id=1, source_target_pairs={{0,4},{4,0},{8,12},{12,8},{16,20},{20,16},{24,28},{28,24},{32,36},... | collective-permute-start | bytes 4718600 | tf_op jit(solution)/shard_map/ppermute | solution.py:533
  86.9 7.3 %flash.6 = (f32[512,384]{1,0:T(8,128)}, f32[512,384]{1,0:T(8,128)}, f32[512,384]{1,0:T(8,128)}, f32[8,128]{1,0:T(8,128)}) custom-call(bf16[4,3,3,128,128]{4,3,2,1,0:T(8,128)(2,1)} %copy-done.1, bf16[2,4,2,3,128,128]{5,4,3,2,1,0:T(8,128)(2,1)} %gate.16.refs_10_.refs_1_, bf16[2,4,2,3,128,128]{5,4,3,2,1,0:T(8,128)(2,1)} %collective-permute-done.12.refs_2_, ...), custom_call_target="tpu_custom_call" | custom-call | flops 1 | bytes 1 | tf_op jit(solution)/shard_map/flash/pallas_call | solution.py:238
  95.4 6.8 %flash.7 = (f32[512,384]{1,0:T(8,128)}, f32[512,384]{1,0:T(8,128)}, f32[512,384]{1,0:T(8,128)}, f32[8,128]{1,0:T(8,128)}) custom-call(bf16[4,3,3,128,128]{4,3,2,1,0:T(8,128)(2,1)} %copy-done.1, bf16[2,4,2,3,128,128]{5,4,3,2,1,0:T(8,128)(2,1)} %gate.17.refs_1_, bf16[2,4,2,3,128,128]{5,4,3,2,1,0:T(8,128)(2,1)} %copy-done.8, ...), custom_call_target="tpu_custom_call" | custom-call | flops 1 | bytes 1 | tf_op jit(solution)/shard_map/flash/pallas_call | solution.py:238
  102.2 3.3 %collective-permute-done.10.refs_0_ = bf16[2,4,2,3,128,128]{5,4,3,2,1,0:T(8,128)(2,1)S(1)} collective-permute-done((bf16[2,4,2,3,128,128]{5,4,3,2,1,0:T(8,128)(2,1)}, bf16[2,4,2,3,128,128]{5,4,3,2,1,0:T(8,128)(2,1)S(1)}, u32[]{:S(2)}, u32[]{:S(2)}) %collective-permute-start.10) | collective-permute-done | bytes 1572896 | tf_op jit(solution)/shard_map/ppermute | solution.py:529
  106.7 2.0 %collective-permute-start.15 = (bf16[2,4,2,3,128,128]{5,4,3,2,1,0:T(8,128)(2,1)}, bf16[2,4,2,3,128,128]{5,4,3,2,1,0:T(8,128)(2,1)S(1)}, u32[]{:S(2)}, u32[]{:S(2)}) collective-permute-start(bf16[2,4,2,3,128,128]{5,4,3,2,1,0:T(8,128)(2,1)} %gate.18.refs_1_), channel_id=1, source_target_pairs={{0,4},{4,0},{8,12},{12,8},{16,20},{20,16},{24,28},{28,24},{32,36},... | collective-permute-start | bytes 4718600 | tf_op jit(solution)/shard_map/ppermute | solution.py:533
  110.5 3.2 %collective-permute-start.17 = (bf16[160,1536]{1,0:T(8,128)(2,1)S(1)}, bf16[160,1536]{1,0:T(8,128)(2,1)S(1)}, u32[]{:S(2)}, u32[]{:S(2)}) collective-permute-start(bf16[160,1536]{1,0:T(8,128)(2,1)S(1)} %copy-done.23), channel_id=1, source_target_pairs={{0,3},{1,0},{2,1},{3,2},{4,7},{5,4},{6,5},{7,6},{8,11},{9,8},{10,9... | collective-permute-start | bytes 1474568 | tf_op jit(solution)/shard_map/ppermute | solution.py:524
  113.7 7.4 %collective-permute-done.13.refs_0_ = bf16[1,4,2,3,128,128]{5,4,3,2,1,0:T(8,128)(2,1)S(1)} collective-permute-done((bf16[1,4,2,3,128,128]{5,4,3,2,1,0:T(8,128)(2,1)S(1)}, bf16[1,4,2,3,128,128]{5,4,3,2,1,0:T(8,128)(2,1)S(1)}, u32[]{:S(2)}, u32[]{:S(2)}) %collective-permute-start.13) | collective-permute-done | bytes 786464 | tf_op jit(solution)/shard_map/ppermute | solution.py:529
  122.0 2.1 %collective-permute-start.14 = (bf16[1,4,2,3,128,128]{5,4,3,2,1,0:T(8,128)(2,1)}, bf16[1,4,2,3,128,128]{5,4,3,2,1,0:T(8,128)(2,1)S(1)}, u32[]{:S(2)}, u32[]{:S(2)}) collective-permute-start(bf16[1,4,2,3,128,128]{5,4,3,2,1,0:T(8,128)(2,1)} %gate.19.refs_1_), channel_id=1, source_target_pairs={{0,4},{4,0},{8,12},{12,8},{16,20},{20,16},{24,28},{28,24},{32,36},... | collective-permute-start | bytes 2359304 | tf_op jit(solution)/shard_map/ppermute | solution.py:533
  126.5 3.4 %add_halves.1 = (bf16[320,1536]{1,0:T(8,128)(2,1)}, bf16[320,1536]{1,0:T(8,128)(2,1)}) custom-call(bf16[320,1536]{1,0:T(8,128)(2,1)} %get-tuple-element.61.up, bf16[320,1536]{1,0:T(8,128)(2,1)} %get-tuple-element.62.down, bf16[160,1536]{1,0:T(8,128)(2,1)} %copy-done.15, bf16[160,1536]{1,0:T(8,128)(2,1)} %copy-done.16), custom_call_target="tpu_custom_call", output_to_operand_aliasing={{0}: (0, {}), {1}: (1, {})} | custom-call | flops 1 | bytes 1 | tf_op jit(solution)/shard_map/add_halves/pallas_call | solution.py:510
  133.7 6.8 %flash.8 = (f32[512,384]{1,0:T(8,128)}, f32[512,384]{1,0:T(8,128)}, f32[512,384]{1,0:T(8,128)}, f32[8,128]{1,0:T(8,128)}) custom-call(bf16[4,3,3,128,128]{4,3,2,1,0:T(8,128)(2,1)} %copy-done.1, bf16[2,4,2,3,128,128]{5,4,3,2,1,0:T(8,128)(2,1)} %gate.18.refs_1_, bf16[2,4,2,3,128,128]{5,4,3,2,1,0:T(8,128)(2,1)} %copy-done.9, ...), custom_call_target="tpu_custom_call" | custom-call | flops 1 | bytes 1 | tf_op jit(solution)/shard_map/flash/pallas_call | solution.py:238
  141.4 5.3 %flash.9 = bf16[512,384]{1,0:T(8,128)(2,1)} custom-call(bf16[4,3,3,128,128]{4,3,2,1,0:T(8,128)(2,1)} %copy-done.1, bf16[1,4,2,3,128,128]{5,4,3,2,1,0:T(8,128)(2,1)} %gate.19.refs_1_, bf16[1,4,2,3,128,128]{5,4,3,2,1,0:T(8,128)(2,1)} %copy-done.14, f32[512,384]{1,0:T(8,128)} %get-tuple-element.67.refs_3_, f32[512,384]{1,0:T(8,128)} %get-tuple-element.68.refs_4_, ...), custom_call_target="tpu_custom_call" | custom-call | flops 1 | bytes 1 | tf_op jit(solution)/shard_map/flash/pallas_call | solution.py:238
  146.8 12.3 %all_to_all.10.own = bf16[4,128,384]{2,1,0:T(8,128)(2,1)S(1)} all-to-all(bf16[4,128,384]{2,1,0:T(8,128)(2,1)} %bitcast.24), channel_id=1, replica_groups=mesh['batch'=4,'ctx'=16,'tower'=4] {'tower'}, dimensions={0} | all-to-all | bytes 786432 | tf_op jit(solution)/shard_map/all_to_all | solution.py:497
  162.4 6.7 %project_self.1 = (bf16[128,3072]{1,0:T(8,128)(2,1)}, bf16[24,3072]{1,0:T(8,128)(2,1)}, bf16[160,1536]{1,0:T(8,128)(2,1)}) custom-call(s32[5]{0:T(128)} %stack.32.place, bf16[4,128,384]{2,1,0:T(8,128)(2,1)} %copy-done.7, bf16[4,128,384]{2,1,0:T(8,128)(2,1)} %copy-done.18, bf16[16,3,32,1536]{3,2,1,0:T(8,128)(2,1)} %bitcast.22, ...), custom_call_target="tpu_custom_call" | custom-call | flops 1 | bytes 1 | tf_op jit(solution)/shard_map/project_self/pallas_call | solution.py:429
  (103 shorter events, 36.3 us)
Async XLA Ops:
  7.2 65.0 %all-gather.5.cloned.1.call-start = ((), (), s32[]{:S(2)}) async-start(), calls=%async_computation.2 | async-start | bytes 2949120 | tf_op jit(solution)/shard_map/all_gather | solution.py:547
  12.3 19.5 %all-to-all-start = ((bf16[4,3,3,128,128]{4,3,2,1,0:T(8,128)(2,1)}), bf16[4,3,3,128,128]{4,3,2,1,0:T(8,128)(2,1)S(1)}, u32[]{:S(2)}, u32[]{:S(2)}) async-start(bf16[4,3,3,128,128]{4,3,2,1,0:T(8,128)(2,1)} %get-tuple-element.39), calls=%async_computation | async-start | bytes 2359296 | tf_op jit(solution)/shard_map/all_to_all | solution.py:497
  17.2 144.4 %all-gather.7.cloned.1.call-start = ((), (), s32[]{:S(2)}) async-start(), calls=%async_computation.3 | async-start | bytes 5013504 | tf_op jit(solution)/shard_map/all_gather | solution.py:548
  32.0 4.8 %collective-permute-start = (bf16[4,2,3,128,128]{4,3,2,1,0:T(8,128)(2,1)S(1)}, bf16[4,2,3,128,128]{4,3,2,1,0:T(8,128)(2,1)S(1)}, u32[]{:S(2)}, u32[]{:S(2)}) collective-permute-start(bf16[4,2,3,128,128]{4,3,2,1,0:T(8,128)(2,1)S(1)} %get-tuple-element.77), channel_id=1, source_target_pairs={{0,4},{4,0},{8,12},{12,8},{16,20},{20,16},{24,28},{28,24},{32,36},... | collective-permute-start | bytes 2359304 | tf_op jit(solution)/shard_map/ppermute | solution.py:533
  37.7 22.9 %collective-permute-start.1 = (bf16[2,4,2,3,128,128]{5,4,3,2,1,0:T(8,128)(2,1)S(1)}, bf16[2,4,2,3,128,128]{5,4,3,2,1,0:T(8,128)(2,1)}, u32[]{:S(2)}, u32[]{:S(2)}) collective-permute-start(bf16[2,4,2,3,128,128]{5,4,3,2,1,0:T(8,128)(2,1)S(1)} %pad_maximum_fusion.refs_1_.refs_8_.refs_9_), channel_id=1, source_target_pairs={{0,8},{4,60},{8,16},{12,4},{16,24},{20,12},{24,32},{28,20},{32,40}... | collective-permute-start | bytes 4718600 | tf_op jit(solution)/shard_map/ppermute | solution.py:529
  43.3 11.7 %collective-permute-start.2 = (bf16[480,384]{1,0:T(8,128)(2,1)}, bf16[480,384]{1,0:T(8,128)(2,1)S(1)}, u32[]{:S(2)}, u32[]{:S(2)}) collective-permute-start(bf16[480,384]{1,0:T(8,128)(2,1)} %gate.10), channel_id=1, source_target_pairs={{0,1},{4,5},{8,9},{12,13},{17,18},{21,22},{25,26},{29,30},{34,35},... | collective-permute-start | bytes 1105928 | tf_op jit(solution)/shard_map/ppermute | solution.py:150
  45.5 13.7 %collective-permute-start.3 = (bf16[480,384]{1,0:T(8,128)(2,1)}, bf16[480,384]{1,0:T(8,128)(2,1)S(1)}, u32[]{:S(2)}, u32[]{:S(2)}) collective-permute-start(bf16[480,384]{1,0:T(8,128)(2,1)} %gate.11), channel_id=1, source_target_pairs={{0,2},{4,6},{8,10},{12,14},{17,19},{21,23},{25,27},{29,31},{34,32}... | collective-permute-start | bytes 1105928 | tf_op jit(solution)/shard_map/ppermute | solution.py:150
  46.8 12.4 %collective-permute-start.4 = (bf16[480,384]{1,0:T(8,128)(2,1)}, bf16[480,384]{1,0:T(8,128)(2,1)S(1)}, u32[]{:S(2)}, u32[]{:S(2)}) collective-permute-start(bf16[480,384]{1,0:T(8,128)(2,1)} %gate.12), channel_id=1, source_target_pairs={{0,3},{4,7},{8,11},{12,15},{17,16},{21,20},{25,24},{29,28},{34,33}... | collective-permute-start | bytes 1105928 | tf_op jit(solution)/shard_map/ppermute | solution.py:150
  53.6 0.7 collective-permute-start.6
  54.3 0.7 collective-permute-start.5
  60.7 21.0 %collective-permute-start.8 = (bf16[2,4,2,3,128,128]{5,4,3,2,1,0:T(8,128)(2,1)}, bf16[2,4,2,3,128,128]{5,4,3,2,1,0:T(8,128)(2,1)S(1)}, u32[]{:S(2)}, u32[]{:S(2)}) collective-permute-start(bf16[2,4,2,3,128,128]{5,4,3,2,1,0:T(8,128)(2,1)} %gate.16.refs_10_.refs_1_), channel_id=1, source_target_pairs={{0,8},{4,60},{8,16},{12,4},{16,24},{20,12},{24,32},{28,20},{32,40}... | collective-permute-start | bytes 4718600 | tf_op jit(solution)/shard_map/ppermute | solution.py:529
  71.5 2.2 %collective-permute-start.9 = (bf16[4,160,384]{2,1,0:T(8,128)(2,1)}, bf16[4,160,384]{2,1,0:T(8,128)(2,1)S(1)}, u32[]{:S(2)}, u32[]{:S(2)}) collective-permute-start(bf16[4,160,384]{2,1,0:T(8,128)(2,1)} %cross.1.own), channel_id=1, source_target_pairs={{0,4},{4,0},{8,12},{12,8},{16,20},{20,16},{24,28},{28,24},{32,36},... | collective-permute-start | bytes 1474568 | tf_op jit(solution)/shard_map/ppermute | solution.py:533
  71.6 15.2 %collective-permute-start.12 = (bf16[2,4,2,3,128,128]{5,4,3,2,1,0:T(8,128)(2,1)}, bf16[2,4,2,3,128,128]{5,4,3,2,1,0:T(8,128)(2,1)}, u32[]{:S(2)}, u32[]{:S(2)}) collective-permute-start(bf16[2,4,2,3,128,128]{5,4,3,2,1,0:T(8,128)(2,1)} %gate.16.refs_10_.refs_1_), channel_id=1, source_target_pairs={{0,4},{4,0},{8,12},{12,8},{16,20},{20,16},{24,28},{28,24},{32,36},... | collective-permute-start | bytes 4718600 | tf_op jit(solution)/shard_map/ppermute | solution.py:533
  82.9 11.3 %collective-permute-start.11 = (bf16[2,4,2,3,128,128]{5,4,3,2,1,0:T(8,128)(2,1)}, bf16[2,4,2,3,128,128]{5,4,3,2,1,0:T(8,128)(2,1)S(1)}, u32[]{:S(2)}, u32[]{:S(2)}) collective-permute-start(bf16[2,4,2,3,128,128]{5,4,3,2,1,0:T(8,128)(2,1)} %gate.17.refs_1_), channel_id=1, source_target_pairs={{0,4},{4,0},{8,12},{12,8},{16,20},{20,16},{24,28},{28,24},{32,36},... | collective-permute-start | bytes 4718600 | tf_op jit(solution)/shard_map/ppermute | solution.py:533
  85.6 19.9 %collective-permute-start.10 = (bf16[2,4,2,3,128,128]{5,4,3,2,1,0:T(8,128)(2,1)}, bf16[2,4,2,3,128,128]{5,4,3,2,1,0:T(8,128)(2,1)S(1)}, u32[]{:S(2)}, u32[]{:S(2)}) collective-permute-start(bf16[2,4,2,3,128,128]{5,4,3,2,1,0:T(8,128)(2,1)} %gate.17.refs_1_), channel_id=1, source_target_pairs={{0,8},{4,60},{8,16},{12,4},{16,24},{20,12},{24,32},{28,20},{32,40}... | collective-permute-start | bytes 4718600 | tf_op jit(solution)/shard_map/ppermute | solution.py:529
  106.7 25.9 %collective-permute-start.15 = (bf16[2,4,2,3,128,128]{5,4,3,2,1,0:T(8,128)(2,1)}, bf16[2,4,2,3,128,128]{5,4,3,2,1,0:T(8,128)(2,1)S(1)}, u32[]{:S(2)}, u32[]{:S(2)}) collective-permute-start(bf16[2,4,2,3,128,128]{5,4,3,2,1,0:T(8,128)(2,1)} %gate.18.refs_1_), channel_id=1, source_target_pairs={{0,4},{4,0},{8,12},{12,8},{16,20},{20,16},{24,28},{28,24},{32,36},... | collective-permute-start | bytes 4718600 | tf_op jit(solution)/shard_map/ppermute | solution.py:533
  109.8 11.2 %collective-permute-start.13 = (bf16[1,4,2,3,128,128]{5,4,3,2,1,0:T(8,128)(2,1)S(1)}, bf16[1,4,2,3,128,128]{5,4,3,2,1,0:T(8,128)(2,1)S(1)}, u32[]{:S(2)}, u32[]{:S(2)}) collective-permute-start(bf16[1,4,2,3,128,128]{5,4,3,2,1,0:T(8,128)(2,1)S(1)} %slice.9), channel_id=1, source_target_pairs={{0,8},{4,60},{8,16},{12,4},{16,24},{20,12},{24,32},{28,20},{32,40}... | collective-permute-start | bytes 2359304 | tf_op jit(solution)/shard_map/ppermute | solution.py:529
  110.5 14.4 %collective-permute-start.16 = (bf16[160,1536]{1,0:T(8,128)(2,1)}, bf16[160,1536]{1,0:T(8,128)(2,1)S(1)}, u32[]{:S(2)}, u32[]{:S(2)}) collective-permute-start(bf16[160,1536]{1,0:T(8,128)(2,1)} %get-tuple-element.63), channel_id=1, source_target_pairs={{0,1},{1,2},{2,3},{3,0},{4,5},{5,6},{6,7},{7,4},{8,9},{9,10},{10,1... | collective-permute-start | bytes 1474568 | tf_op jit(solution)/shard_map/ppermute | solution.py:524
  110.5 15.2 %collective-permute-start.17 = (bf16[160,1536]{1,0:T(8,128)(2,1)S(1)}, bf16[160,1536]{1,0:T(8,128)(2,1)S(1)}, u32[]{:S(2)}, u32[]{:S(2)}) collective-permute-start(bf16[160,1536]{1,0:T(8,128)(2,1)S(1)} %copy-done.23), channel_id=1, source_target_pairs={{0,3},{1,0},{2,1},{3,2},{4,7},{5,4},{6,5},{7,6},{8,11},{9,8},{10,9... | collective-permute-start | bytes 1474568 | tf_op jit(solution)/shard_map/ppermute | solution.py:524
  122.0 18.6 %collective-permute-start.14 = (bf16[1,4,2,3,128,128]{5,4,3,2,1,0:T(8,128)(2,1)}, bf16[1,4,2,3,128,128]{5,4,3,2,1,0:T(8,128)(2,1)S(1)}, u32[]{:S(2)}, u32[]{:S(2)}) collective-permute-start(bf16[1,4,2,3,128,128]{5,4,3,2,1,0:T(8,128)(2,1)} %gate.19.refs_1_), channel_id=1, source_target_pairs={{0,4},{4,0},{8,12},{12,8},{16,20},{20,16},{24,28},{28,24},{32,36},... | collective-permute-start | bytes 2359304 | tf_op jit(solution)/shard_map/ppermute | solution.py:533
  129.8 30.4 %collective-permute-start.19 = (bf16[320,1536]{1,0:T(8,128)(2,1)}, bf16[320,1536]{1,0:T(8,128)(2,1)S(1)}, u32[]{:S(2)}, u32[]{:S(2)}) collective-permute-start(bf16[320,1536]{1,0:T(8,128)(2,1)} %get-tuple-element.65.refs_6_), channel_id=1, source_target_pairs={{0,1},{1,2},{2,3},{3,0},{4,5},{5,6},{6,7},{7,4},{8,9},{9,10},{10,1... | collective-permute-start | bytes 2949128 | tf_op jit(solution)/shard_map/ppermute | solution.py:524
  131.7 28.5 %collective-permute-start.20 = (bf16[320,1536]{1,0:T(8,128)(2,1)}, bf16[320,1536]{1,0:T(8,128)(2,1)}, u32[]{:S(2)}, u32[]{:S(2)}) collective-permute-start(bf16[320,1536]{1,0:T(8,128)(2,1)} %get-tuple-element.66.refs_7_), channel_id=1, source_target_pairs={{0,3},{1,0},{2,1},{3,2},{4,7},{5,4},{6,5},{7,6},{8,11},{9,8},{10,9... | collective-permute-start | bytes 2949128 | tf_op jit(solution)/shard_map/ppermute | solution.py:524
  159.0 2.6 %collective-permute-start.18 = (bf16[4,128,384]{2,1,0:T(8,128)(2,1)S(1)}, bf16[4,128,384]{2,1,0:T(8,128)(2,1)S(1)}, u32[]{:S(2)}, u32[]{:S(2)}) collective-permute-start(bf16[4,128,384]{2,1,0:T(8,128)(2,1)S(1)} %all_to_all.10.own), channel_id=1, source_target_pairs={{0,4},{4,0},{8,12},{12,8},{16,20},{20,16},{24,28},{28,24},{32,36},... | collective-permute-start | bytes 1179656 | tf_op jit(solution)/shard_map/ppermute | solution.py:533
  169.1 2.1 %collective-permute-start.21 = (bf16[160,1536]{1,0:T(8,128)(2,1)}, bf16[160,1536]{1,0:T(8,128)(2,1)S(1)}, u32[]{:S(2)}, u32[]{:S(2)}) collective-permute-start(bf16[160,1536]{1,0:T(8,128)(2,1)} %get-tuple-element.73), channel_id=1, source_target_pairs={{0,4},{4,0},{8,12},{12,8},{16,20},{20,16},{24,28},{28,24},{32,36},... | collective-permute-start | bytes 1474568 | tf_op jit(solution)/shard_map/ppermute | solution.py:533
  (25 other events, 79.3 us)
Sparse Core Ops, SparseCore 0:
  12.4 39.3 all-gather.4
  54.3 59.0 all-gather.6
